TPU v7x, 32 devices: a whole 2x2x4 slice. The times are simulated.
32 devices in a mesh: seq: 4 (over y, x), dp: 8 (over z, core).
Axes of the slice: x: 2, y: 2, z: 4, core: 2. Of those that a mesh axis runs over, the one named last changes fastest.
Arguments:
- inputs: bfloat16 [32, 1024, 512], P('dp', 'seq'), may hold values from -6 to 6
- cotangent: bfloat16 [32, 1024, 512], P('dp', 'seq'), may hold values from -6 to 6
- timestep: int32 [32], P('dp'), may hold values from 0 to 1023
- unmask_order: int32 [32, 1024], P('dp', 'seq'), may hold values from 0 to 1023, each once within a row
- mask_embed: float32 [512], replicated, may hold values from -5 to 5
- ln1_gain: float32 [512], replicated, may hold values from 0.5 to 1.5
- weight_qkv: bfloat16 [512, 1536], P('dp'), may hold values from -0.25 to 0.25
- weight_out: bfloat16 [512, 512], P('dp'), may hold values from -6 to 6
- ln2_gain: float32 [512], replicated, may hold values from 0.5 to 1.5
- weight_up: bfloat16 [512, 2048], P('dp'), may hold values from -0.25 to 0.25
- weight_down: bfloat16 [2048, 512], P('dp'), may hold values from -0.125 to 0.125
Outputs:
- outputs: bfloat16 [32, 1024, 512], P('dp', 'seq')
- grad_inputs: bfloat16 [32, 1024, 512], P('dp', 'seq')
- grad_mask_embed: float32 [512], P('dp')
- grad_ln1_gain: float32 [512], P('dp')
- grad_weight_qkv: float32 [512, 1536], P('dp', 'seq')
- grad_weight_out: float32 [512, 512], P('dp', 'seq')
- grad_ln2_gain: float32 [512], P('dp')
- grad_weight_up: float32 [512, 2048], P('dp', 'seq')
- grad_weight_down: float32 [2048, 512], P('dp', 'seq')
Inputs may be any that keep to these rules, and one draw needn't show every extreme that they name: Each row of unmask_order holds every number of 0 to 1023 once.
All inputs are finite; a program needn't handle non-finite values.
Results may differ from a plain program's by a relative error of at most 0.018.
Values may be sent and summed in bfloat16 or wider, within the bound.
No kernel may reach another device: no remote copies, remote signals or barrier semaphores. Data moves between devices by JAX's collectives and lax.ppermute only.
A program may use at most 128 MiB of HBM per device.

v0:
```python
import jax
import jax.numpy as jnp
from jax import lax
from jax.sharding import PartitionSpec as P

HEADS = 8
ROWS_MB = 2
MB = 2


EPSILON = 1e-05


def passed_along(value, axis, by):
    count = lax.axis_size(axis)
    return lax.ppermute(value, axis, [(i, (i + by) % count) for i in range(count)])


def layer_norm(tensor, gain_vec):
    center = tensor - jnp.mean(tensor, axis=-1, keepdims=True)
    spread = jnp.mean(center * center, axis=-1, keepdims=True)
    return center * lax.rsqrt(spread + EPSILON) * gain_vec


def smooth_gelu(tensor):
    return jax.nn.gelu(tensor, approximate=True)


def matmul(left, right):
    return jnp.dot(left, right, preferred_element_type=jnp.float32)


def contract_rows(left, right):
    return lax.dot_general(
        left, right, (((0,), (0,)), ((), ())), preferred_element_type=jnp.float32
    )


def contract_cols(left, right):
    return lax.dot_general(
        left, right, (((1,), (1,)), ((), ())), preferred_element_type=jnp.float32
    )


def spread_forward(queries, key_rows, value_rows):
    row_count, segment, head_count, head_width = queries.shape
    scaling = head_width ** (-0.5)
    start_state = (
        jnp.zeros(queries.shape, jnp.float32),
        jnp.zeros((row_count, head_count, segment), jnp.float32),
    )
    key_piece = lax.all_gather(key_rows, "seq", axis=1, tiled=True)
    value_piece = lax.all_gather(value_rows, "seq", axis=1, tiled=True)
    span_size = key_piece.shape[1]
    block_len = min(span_size, segment)

    def advance(position, running):
        numerator, normalizer = running
        key_block = lax.dynamic_slice_in_dim(key_piece, position * block_len, block_len, 1).reshape(
            row_count, block_len, head_count, head_width
        )
        value_block = lax.dynamic_slice_in_dim(
            value_piece, position * block_len, block_len, 1
        ).reshape(row_count, block_len, head_count, head_width)
        logits = (
            jnp.einsum("rshd,rphd->rhsp", queries, key_block, preferred_element_type=jnp.float32)
            * scaling
        )
        weights = jnp.exp(logits).astype(jnp.bfloat16)
        numerator = numerator + jnp.einsum(
            "rhsp,rphd->rshd", weights, value_block, preferred_element_type=jnp.float32
        )
        normalizer = normalizer + jnp.sum(weights, axis=-1, dtype=jnp.float32)
        return (numerator, normalizer)

    numerator, normalizer = lax.fori_loop(0, span_size // block_len, advance, start_state)
    normalizer = jnp.transpose(normalizer, (0, 2, 1))
    return (numerator / normalizer[..., None], normalizer)


def pass_keys(travelling):
    return passed_along(travelling, "seq", 1)


def pass_grads(gathered):
    return passed_along(gathered, "seq", 1)


def spread_backward(queries, key_rows, value_rows, scaled, offsets):
    scaling = queries.shape[3] ** (-0.5)
    own_offsets = jnp.transpose(offsets, (0, 2, 1))[..., None]
    cycle_size = lax.axis_size("seq")

    def visit(grad_query, travelling, gathered):
        far_key = travelling[0]
        far_value = travelling[1]
        logits = (
            jnp.einsum("rshd,rphd->rhsp", queries, far_key, preferred_element_type=jnp.float32)
            * scaling
        )
        exponent = jnp.exp(logits)
        inner_prod = jnp.einsum(
            "rshd,rphd->rhsp", scaled, far_value, preferred_element_type=jnp.float32
        )
        slopes = (exponent * (inner_prod - own_offsets)).astype(jnp.bfloat16)
        grad_query = (
            grad_query
            + jnp.einsum("rhsp,rphd->rshd", slopes, far_key, preferred_element_type=jnp.float32)
            * scaling
        )
        key_part = (
            jnp.einsum("rhsp,rshd->rphd", slopes, queries, preferred_element_type=jnp.float32)
            * scaling
        )
        value_part = jnp.einsum(
            "rhsp,rshd->rphd",
            exponent.astype(jnp.bfloat16),
            scaled,
            preferred_element_type=jnp.float32,
        )
        gathered = gathered + jnp.stack((key_part, value_part))
        return (grad_query, gathered)

    def turn(step, state):
        grad_query, travelling, gathered = state
        grad_query, gathered = visit(grad_query, travelling, gathered)
        return (grad_query, pass_keys(travelling), pass_grads(gathered))

    start_state = (
        jnp.zeros(queries.shape, jnp.float32),
        jnp.stack((key_rows, value_rows)),
        jnp.zeros((2,) + queries.shape, jnp.float32),
    )
    grad_query, travelling, gathered = lax.fori_loop(0, cycle_size - 1, turn, start_state)
    grad_query, gathered = visit(grad_query, travelling, gathered)
    gathered = pass_grads(gathered)
    return (grad_query, gathered[0], gathered[1])


def per_device(
    inputs,
    cotangent,
    timestep,
    unmask_order,
    mask_embed,
    ln1_gain,
    weight_qkv,
    weight_out,
    ln2_gain,
    weight_up,
    weight_down,
):
    row_count = ROWS_MB
    head_count = HEADS
    segment = inputs.shape[1]
    model_width = inputs.shape[2]
    head_width = model_width // head_count
    token_count = row_count * segment
    sum_qkv = jnp.zeros((model_width, 3 * model_width), jnp.float32)
    sum_out = jnp.zeros((model_width, model_width), jnp.float32)
    sum_up = jnp.zeros((model_width, weight_up.shape[1]), jnp.float32)
    sum_down = jnp.zeros((weight_up.shape[1], model_width), jnp.float32)
    sum_embed = jnp.zeros((model_width,), jnp.float32)
    sum_gain_one = jnp.zeros((model_width,), jnp.float32)
    sum_gain_two = jnp.zeros((model_width,), jnp.float32)
    output_parts = []
    grad_parts = []
    for batch_turn in range(MB):
        whole_qkv, whole_out, whole_up, whole_down = (
            lax.all_gather(weight_qkv, "dp", axis=0, tiled=True),
            lax.all_gather(weight_out, "dp", axis=0, tiled=True),
            lax.all_gather(weight_up, "dp", axis=0, tiled=True),
            lax.all_gather(weight_down, "dp", axis=0, tiled=True),
        )
        row_start = batch_turn * row_count
        block_input = inputs[row_start : row_start + row_count].astype(jnp.float32)
        block_grad = cotangent[row_start : row_start + row_count]
        masking = (
            unmask_order[row_start : row_start + row_count]
            <= timestep[row_start : row_start + row_count][:, None]
        ).astype(jnp.float32)
        hidden = block_input + masking[..., None] * mask_embed
        normed_full, pullback_one = jax.vjp(layer_norm, hidden, ln1_gain)
        normed_one = normed_full.astype(jnp.bfloat16).reshape(token_count, model_width)
        projected = (
            matmul(normed_one, whole_qkv)
            .astype(jnp.bfloat16)
            .reshape(row_count, segment, 3 * model_width)
        )
        queries = projected[..., :model_width]
        key_rows = projected[..., model_width : 2 * model_width]
        value_rows = projected[..., 2 * model_width :]
        query_heads = queries.reshape(row_count, segment, head_count, head_width)
        attended_f, normalizer = spread_forward(query_heads, key_rows, value_rows)
        attended = attended_f.reshape(row_count, segment, model_width).astype(jnp.bfloat16)
        flat_attended = attended.reshape(token_count, model_width)
        first = hidden + matmul(flat_attended, whole_out).reshape(row_count, segment, model_width)
        normed_second, pullback_two = jax.vjp(layer_norm, first, ln2_gain)
        normed_two = normed_second.astype(jnp.bfloat16).reshape(token_count, model_width)
        raised = matmul(normed_two, whole_up)
        activated_f, gelu_pullback = jax.vjp(smooth_gelu, raised)
        activated = activated_f.astype(jnp.bfloat16)
        result = first + matmul(activated, whole_down).reshape(row_count, segment, model_width)
        output_parts.append(result.astype(jnp.bfloat16))
        flat_cotangent = block_grad.reshape(token_count, model_width)
        sum_down = sum_down + contract_rows(activated, flat_cotangent)
        grad_activated = contract_cols(flat_cotangent, whole_down)
        grad_raised = gelu_pullback(grad_activated)[0].astype(jnp.bfloat16)
        sum_up = sum_up + contract_rows(normed_two, grad_raised)
        grad_normed_two = contract_cols(grad_raised, whole_up).reshape(
            row_count, segment, model_width
        )
        grad_first_norm, grad_gain_two = pullback_two(grad_normed_two)
        grad_first = block_grad.astype(jnp.float32) + grad_first_norm
        grad_branch = grad_first.astype(jnp.bfloat16).reshape(token_count, model_width)
        sum_out = sum_out + contract_rows(flat_attended, grad_branch)
        grad_attended = contract_cols(grad_branch, whole_out)
        grad_heads = grad_attended.reshape(row_count, segment, head_count, head_width)
        scaled = (grad_heads / normalizer[..., None]).astype(jnp.bfloat16)
        offsets = jnp.sum(grad_heads * attended_f, axis=-1) / normalizer
        grad_query, grad_key, grad_value = spread_backward(
            query_heads,
            key_rows.reshape(query_heads.shape),
            value_rows.reshape(query_heads.shape),
            scaled,
            offsets,
        )
        grad_pieces = [
            grad_part.reshape(row_count, segment, model_width).astype(jnp.bfloat16)
            for grad_part in (grad_query, grad_key, grad_value)
        ]
        grad_projected = jnp.concatenate(grad_pieces, axis=-1).reshape(token_count, 3 * model_width)
        sum_qkv = sum_qkv + contract_rows(normed_one, grad_projected)
        grad_normed_one = contract_cols(grad_projected, whole_qkv).reshape(
            row_count, segment, model_width
        )
        grad_hidden_norm, grad_gain_one = pullback_one(grad_normed_one)
        grad_hidden = grad_first + grad_hidden_norm
        grad_parts.append(grad_hidden.astype(jnp.bfloat16))
        sum_embed = sum_embed + jnp.sum(masking[..., None] * grad_hidden, axis=(0, 1))
        sum_gain_one = sum_gain_one + grad_gain_one
        sum_gain_two = sum_gain_two + grad_gain_two
    row_sums = (
        lax.psum_scatter(
            sum_qkv.astype(jnp.bfloat16), "dp", scatter_dimension=0, tiled=True
        ).astype(jnp.float32),
        lax.psum_scatter(
            sum_out.astype(jnp.bfloat16), "dp", scatter_dimension=0, tiled=True
        ).astype(jnp.float32),
        lax.psum_scatter(sum_up.astype(jnp.bfloat16), "dp", scatter_dimension=0, tiled=True).astype(
            jnp.float32
        ),
        lax.psum_scatter(
            sum_down.astype(jnp.bfloat16), "dp", scatter_dimension=0, tiled=True
        ).astype(jnp.float32),
        lax.psum_scatter(
            sum_embed.astype(jnp.bfloat16), "dp", scatter_dimension=0, tiled=True
        ).astype(jnp.float32),
        lax.psum_scatter(
            sum_gain_one.astype(jnp.bfloat16), "dp", scatter_dimension=0, tiled=True
        ).astype(jnp.float32),
        lax.psum_scatter(
            sum_gain_two.astype(jnp.bfloat16), "dp", scatter_dimension=0, tiled=True
        ).astype(jnp.float32),
    )
    matrix_sums = (
        lax.psum_scatter(
            row_sums[0].astype(jnp.bfloat16), "seq", scatter_dimension=1, tiled=True
        ).astype(jnp.float32),
        lax.psum_scatter(
            row_sums[1].astype(jnp.bfloat16), "seq", scatter_dimension=1, tiled=True
        ).astype(jnp.float32),
        lax.psum_scatter(
            row_sums[2].astype(jnp.bfloat16), "seq", scatter_dimension=1, tiled=True
        ).astype(jnp.float32),
        lax.psum_scatter(
            row_sums[3].astype(jnp.bfloat16), "seq", scatter_dimension=1, tiled=True
        ).astype(jnp.float32),
    )
    vector_sums = lax.psum((row_sums[4], row_sums[5], row_sums[6]), "seq")
    return (
        jnp.concatenate(output_parts, axis=0),
        jnp.concatenate(grad_parts, axis=0),
        vector_sums[0],
        vector_sums[1],
        matrix_sums[0],
        matrix_sums[1],
        vector_sums[2],
        matrix_sums[2],
        matrix_sums[3],
    )


def solution(mesh):
    in_specs = (
        P("dp", "seq", None),
        P("dp", "seq", None),
        P("dp"),
        P("dp", "seq"),
        P(),
        P(),
        P("dp", None),
        P("dp", None),
        P(),
        P("dp", None),
        P("dp", None),
    )
    out_specs = (
        P("dp", "seq", None),
        P("dp", "seq", None),
        P("dp"),
        P("dp"),
        P("dp", "seq"),
        P("dp", "seq"),
        P("dp"),
        P("dp", "seq"),
        P("dp", "seq"),
    )
    return jax.shard_map(
        per_device, mesh=mesh, in_specs=in_specs, out_specs=out_specs, check_vma=False
    )
```

profile of v0, /device:TPU:0, one launch (start us, length us, event | category | flops | bytes accessed | tf_op | source)
XLA Modules:
  0.0 1061.3 jit_solution(14263127145899009491)
XLA Ops:
  17.4 20.0 %all-gather.8.cloned.1.call-done = bf16[512,1536]{1,0:T(8,128)(2,1)} async-done(((bf16[64,1536]{1,0:T(8,128)(2,1)}), bf16[512,1536]{1,0:T(8,128)(2,1)}) %all-gather.8.cloned.1.call-update) | async-done | bytes 1572880 | tf_op jit(solution)/shard_map/all_gather | solution.py:170
  48.0 18.0 %all_gather.31 = bf16[512,512]{1,0:T(8,128)(2,1)} all-gather(bf16[64,512]{1,0:T(8,128)(2,1)S(1)} %copy-done.69), channel_id=1, replica_groups=mesh['seq'=4,'dp'=8] {'dp'}, dimensions={0}, use_global_device_ids=true | all-gather | bytes 589824 | tf_op jit(solution)/shard_map/all_gather | solution.py:171
  73.5 5.0 fusion.135
  78.5 3.3 fusion.137
  81.9 26.6 %all-gather.10.cloned.1.call-done = bf16[2,1024,512]{1,2,0:T(8,128)(2,1)} async-done(((bf16[2,256,512]{1,2,0:T(8,128)(2,1)}), bf16[2,1024,512]{1,2,0:T(8,128)(2,1)}) %all-gather.10.cloned.1.call-update) | async-done | bytes 2097168 | tf_op jit(solution)/shard_map/all_gather | solution.py:53
  108.5 36.9 %all-gather.12.cloned.1.call-done = bf16[2,1024,512]{1,2,0:T(8,128)(2,1)} async-done(((bf16[2,256,512]{1,2,0:T(8,128)(2,1)}), bf16[2,1024,512]{1,2,0:T(8,128)(2,1)}) %all-gather.12.cloned.1.call-update) | async-done | bytes 2097168 | tf_op jit(solution)/shard_map/all_gather | solution.py:52
  145.3 23.3 %while.62 = (s32[]{:T(128)}, f32[2,256,8,64]{1,3,2,0:T(8,128)}, f32[2,8,256]{2,1,0:T(8,128)S(1)}, bf16[2,1024,512]{1,2,0:T(8,128)(2,1)}, bf16[2,1024,512]{1,2,0:...) while((s32[]{:T(128)}, f32[2,256,8,64]{1,3,2,0:T(8,128)}, ...), condition=%wide.region_4.0_spmd.clone, body=%wide.region_2.0_spmd.clone.sunk | while | flops 273158144 | bytes 10027170 | solution.py:76
  168.7 13.6 %all-gather.18.cloned.1.call-done = bf16[2,1024,512]{1,2,0:T(8,128)(2,1)} async-done(((bf16[2,256,512]{1,2,0:T(8,128)(2,1)}), bf16[2,1024,512]{1,2,0:T(8,128)(2,1)}) %all-gather.18.cloned.1.call-update) | async-done | bytes 2097168 | tf_op jit(solution)/shard_map/all_gather | solution.py:53
  182.2 36.9 %all-gather.20.cloned.1.call-done = bf16[2,1024,512]{1,2,0:T(8,128)(2,1)} async-done(((bf16[2,256,512]{1,2,0:T(8,128)(2,1)}), bf16[2,1024,512]{1,2,0:T(8,128)(2,1)}) %all-gather.20.cloned.1.call-update) | async-done | bytes 2097168 | tf_op jit(solution)/shard_map/all_gather | solution.py:52
  219.1 22.9 %while.63 = (s32[]{:T(128)}, f32[2,256,8,64]{1,3,2,0:T(8,128)}, f32[2,8,256]{2,1,0:T(8,128)S(1)}, bf16[2,1024,512]{1,2,0:T(8,128)(2,1)}, bf16[2,1024,512]{1,2,0:...) while((s32[]{:T(128)}, f32[2,256,8,64]{1,3,2,0:T(8,128)}, ...), condition=%wide.region_11.0_spmd.clone, body=%wide.region_9.11_spmd.clone.sunk | while | flops 273158144 | bytes 10027170 | solution.py:76
  249.9 6.8 fusion.44
  261.2 4.2 fusion.51
  279.8 247.6 %while.65 = (s32[]{:T(128)}, f32[2,256,8,64]{1,3,2,0:T(8,128)}, bf16[2,2,256,8,64]{2,4,3,1,0:T(8,128)(2,1)}, f32[2,2,256,8,64]{2,4,3,1,0:T(8,128)}, bf16[2,256,8...) while((s32[]{:T(128)}, f32[2,256,8,64]{1,3,2,0:T(8,128)}, ...), condition=%wide.region_25.26_spmd.clone, body=%wide.region_24.0_spmd.clone.sunk | while | flops 679477248 | bytes 47726776 | solution.py:134
  296.4 66.8 %collective-permute-done.2 = bf16[2,2,256,8,64]{2,4,3,1,0:T(8,128)(2,1)} collective-permute-done((bf16[2,2,256,8,64]{2,4,3,1,0:T(8,128)(2,1)S(1)}, bf16[2,2,256,8,64]{2,4,3,1,0:T(8,128)(2,1)}, u32[]{:S(2)}, u32[]{:S(2)}) %collective-permute-start.2) | collective-permute-done | bytes 1048608 | tf_op jit(solution)/shard_map/while/body/eval_jaxpr/ppermute | solution.py:16
  380.9 64.7 %collective-permute-done.2 = bf16[2,2,256,8,64]{2,4,3,1,0:T(8,128)(2,1)} collective-permute-done((bf16[2,2,256,8,64]{2,4,3,1,0:T(8,128)(2,1)S(1)}, bf16[2,2,256,8,64]{2,4,3,1,0:T(8,128)(2,1)}, u32[]{:S(2)}, u32[]{:S(2)}) %collective-permute-start.2) | collective-permute-done | bytes 1048608 | tf_op jit(solution)/shard_map/while/body/eval_jaxpr/ppermute | solution.py:16
  463.4 63.8 %collective-permute-done.2 = bf16[2,2,256,8,64]{2,4,3,1,0:T(8,128)(2,1)} collective-permute-done((bf16[2,2,256,8,64]{2,4,3,1,0:T(8,128)(2,1)S(1)}, bf16[2,2,256,8,64]{2,4,3,1,0:T(8,128)(2,1)}, u32[]{:S(2)}, u32[]{:S(2)}) %collective-permute-start.2) | collective-permute-done | bytes 1048608 | tf_op jit(solution)/shard_map/while/body/eval_jaxpr/ppermute | solution.py:16
  529.4 3.7 multiply_convert_fusion.2
  539.0 239.3 %while.64 = (s32[]{:T(128)}, f32[2,256,8,64]{1,3,2,0:T(8,128)}, bf16[2,2,256,8,64]{2,4,3,1,0:T(8,128)(2,1)}, f32[2,2,256,8,64]{2,4,3,1,0:T(8,128)}, bf16[2,256,8...) while((s32[]{:T(128)}, f32[2,256,8,64]{1,3,2,0:T(8,128)}, ...), condition=%wide.region_18.0_spmd.clone, body=%wide.region_17.0_spmd.clone.sunk | while | flops 679477248 | bytes 47726776 | solution.py:134
  555.5 64.1 %collective-permute-done = bf16[2,2,256,8,64]{2,4,3,1,0:T(8,128)(2,1)} collective-permute-done((bf16[2,2,256,8,64]{2,4,3,1,0:T(8,128)(2,1)S(1)}, bf16[2,2,256,8,64]{2,4,3,1,0:T(8,128)(2,1)}, u32[]{:S(2)}, u32[]{:S(2)}) %collective-permute-start) | collective-permute-done | bytes 1048608 | tf_op jit(solution)/shard_map/while/body/eval_jaxpr/ppermute | solution.py:16
  637.5 62.0 %collective-permute-done = bf16[2,2,256,8,64]{2,4,3,1,0:T(8,128)(2,1)} collective-permute-done((bf16[2,2,256,8,64]{2,4,3,1,0:T(8,128)(2,1)S(1)}, bf16[2,2,256,8,64]{2,4,3,1,0:T(8,128)(2,1)}, u32[]{:S(2)}, u32[]{:S(2)}) %collective-permute-start) | collective-permute-done | bytes 1048608 | tf_op jit(solution)/shard_map/while/body/eval_jaxpr/ppermute | solution.py:16
  717.2 61.0 %collective-permute-done = bf16[2,2,256,8,64]{2,4,3,1,0:T(8,128)(2,1)} collective-permute-done((bf16[2,2,256,8,64]{2,4,3,1,0:T(8,128)(2,1)S(1)}, bf16[2,2,256,8,64]{2,4,3,1,0:T(8,128)(2,1)}, u32[]{:S(2)}, u32[]{:S(2)}) %collective-permute-start) | collective-permute-done | bytes 1048608 | tf_op jit(solution)/shard_map/while/body/eval_jaxpr/ppermute | solution.py:16
  805.7 11.4 %collective-permute-done.5 = bf16[2,2,256,8,64]{2,4,3,1,0:T(8,128)(2,1)} collective-permute-done((bf16[2,2,256,8,64]{2,4,3,1,0:T(8,128)(2,1)}, bf16[2,2,256,8,64]{2,4,3,1,0:T(8,128)(2,1)}, u32[]{:S(2)}, u32[]{:S(2)}) %collective-permute-start.5) | collective-permute-done | bytes 1048608 | tf_op jit(solution)/shard_map/ppermute | solution.py:16
  818.8 14.5 %collective-permute-done.4 = bf16[2,2,256,8,64]{2,4,3,1,0:T(8,128)(2,1)} collective-permute-done((bf16[2,2,256,8,64]{2,4,3,1,0:T(8,128)(2,1)}, bf16[2,2,256,8,64]{2,4,3,1,0:T(8,128)(2,1)}, u32[]{:S(2)}, u32[]{:S(2)}) %collective-permute-start.4) | collective-permute-done | bytes 1048608 | tf_op jit(solution)/shard_map/ppermute | solution.py:16
  840.3 4.2 fusion.124
  865.5 7.5 reduce-scatter.15.cloned.1.call-done
  877.5 31.6 %reduce-scatter.23.cloned.1.call-done = bf16[256,512]{1,0:T(8,128)(2,1)} async-done(((bf16[2048,512]{1,0:T(8,128)(2,1)}), bf16[256,512]{1,0:T(8,128)(2,1)}) %reduce-scatter.23.cloned.1.call-update) | async-done | bytes 262160 | tf_op jit(solution)/shard_map/reduce_scatter | solution.py:253
  912.9 33.2 %reduce-scatter.19.cloned.1.call-done = bf16[64,2048]{1,0:T(8,128)(2,1)} async-done(((bf16[512,2048]{1,0:T(8,128)(2,1)}), bf16[64,2048]{1,0:T(8,128)(2,1)}) %reduce-scatter.19.cloned.1.call-update) | async-done | bytes 262160 | tf_op jit(solution)/shard_map/reduce_scatter | solution.py:250
  946.2 14.6 %all-reduce.4 = (bf16[512]{0:T(512)(128)(2,1)S(1)}, bf16[512]{0:T(512)(128)(2,1)S(1)}, bf16[512]{0:T(512)(128)(2,1)S(1)}) all-reduce(bf16[512]{0:T(512)(128)(2,1)S(1)} %add_convert_fusion.6, bf16[512]{0:T(512)(128)(2,1)S(1)} %add_convert_fusion.5, bf16[512]{0:T(512)(128)(2,1)S(1)} %add_convert_fusion.4), channel_id=2, replica_groups=mesh['seq'=4,'dp'=8] {'dp'}, use_global_device_ids=true, to_apply=%region_30.0.clone | all-reduce | flops 1536 | bytes 6144
  961.0 10.3 all-reduce.3
  973.8 25.4 %reduce-scatter.25.cloned.1.call-done = bf16[384,64]{1,0:T(8,128)(2,1)} async-done(((bf16[1536,64]{1,0:T(8,128)(2,1)}), bf16[384,64]{1,0:T(8,128)(2,1)}) %reduce-scatter.25.cloned.1.call-update) | async-done | bytes 49168
  1000.8 25.1 %reduce-scatter.29.cloned.1.call-done = bf16[128,256]{1,0:T(8,128)(2,1)} async-done(((bf16[512,256]{1,0:T(8,128)(2,1)}), bf16[128,256]{1,0:T(8,128)(2,1)}) %reduce-scatter.29.cloned.1.call-update) | async-done | bytes 65552
  1027.6 25.3 %reduce-scatter.21.cloned.1.call-done = bf16[64,512]{1,0:T(8,128)(2,1)} async-done(((bf16[64,2048]{1,0:T(8,128)(2,1)}), bf16[64,512]{1,0:T(8,128)(2,1)}) %reduce-scatter.21.cloned.1.call-update) | async-done | bytes 65552 | tf_op jit(solution)/shard_map/reduce_scatter | solution.py:273
  (434 shorter events, 283.5 us)
Async XLA Ops:
  7.2 30.3 %all-gather.8.cloned.1.call-start = ((), (), s32[]{:S(2)}) async-start(), calls=%async_computation.8 | async-start | bytes 1769472 | tf_op jit(solution)/shard_map/all_gather | solution.py:170
  7.9 65.6 %all-gather.16.cloned.1.call-start = ((), (), s32[]{:S(2)}) async-start(), calls=%async_computation.12 | async-start | bytes 2359296 | tf_op jit(solution)/shard_map/all_gather | solution.py:173
  8.7 99.8 %all-gather.10.cloned.1.call-start = ((), (), s32[]{:S(2)}) async-start(), calls=%async_computation.9 | async-start | bytes 2621440 | tf_op jit(solution)/shard_map/all_gather | solution.py:53
  10.4 233.1 %copy-start.67 = (f32[2,256]{1,0:T(2,128)}, f32[2,256]{1,0:T(2,128)S(1)}, u32[]{:S(2)}) copy-start(f32[2,256]{1,0:T(2,128)S(1)} %get-tuple-element.516) | copy-start | bytes 6148
  10.4 235.4 %copy-start.65 = (f32[2,256]{1,0:T(2,128)}, f32[2,256]{1,0:T(2,128)S(1)}, u32[]{:S(2)}) copy-start(f32[2,256]{1,0:T(2,128)S(1)} %get-tuple-element.515) | copy-start | bytes 6148
  41.9 103.4 %all-gather.12.cloned.1.call-start = ((), (), s32[]{:S(2)}) async-start(), calls=%async_computation.10 | async-start | bytes 2621440 | tf_op jit(solution)/shard_map/all_gather | solution.py:52
  43.0 139.2 %all-gather.18.cloned.1.call-start = ((), (), s32[]{:S(2)}) async-start(), calls=%async_computation.13 | async-start | bytes 2621440 | tf_op jit(solution)/shard_map/all_gather | solution.py:53
  46.1 173.0 %all-gather.20.cloned.1.call-start = ((), (), s32[]{:S(2)}) async-start(), calls=%async_computation.14 | async-start | bytes 2621440 | tf_op jit(solution)/shard_map/all_gather | solution.py:52
  47.2 202.7 %all-gather.14.cloned.1.call-start = ((), (), s32[]{:S(2)}) async-start(), calls=%async_computation.11 | async-start | bytes 2359296 | tf_op jit(solution)/shard_map/all_gather | solution.py:172
  47.9 807.9 %reduce-scatter.17.cloned.1.call-start = ((), (), s32[]{:S(2)}) async-start(), calls=%async_computation.16 | async-start | bytes 589824 | tf_op jit(solution)/shard_map/reduce_scatter | solution.py:247
  291.7 71.5 %collective-permute-start.3 = (f32[2,2,256,8,64]{2,4,3,1,0:T(8,128)}, f32[2,2,256,8,64]{2,4,3,1,0:T(8,128)}, u32[]{:S(2)}, u32[]{:S(2)}) collective-permute-start(f32[2,2,256,8,64]{2,4,3,1,0:T(8,128)} %maximum_add_fusion.7), channel_id=1, source_target_pairs={{0,8},{8,16},{16,24},{24,0},{1,9},{9,17},{17,25},{25,1},{2,10},{10... | collective-permute-start | bytes 6291464 | tf_op jit(solution)/shard_map/while/body/eval_jaxpr/ppermute | solution.py:16
  293.1 70.0 %collective-permute-start.2 = (bf16[2,2,256,8,64]{2,4,3,1,0:T(8,128)(2,1)S(1)}, bf16[2,2,256,8,64]{2,4,3,1,0:T(8,128)(2,1)}, u32[]{:S(2)}, u32[]{:S(2)}) collective-permute-start(bf16[2,2,256,8,64]{2,4,3,1,0:T(8,128)(2,1)S(1)} %copy.92), channel_id=1, source_target_pairs={{0,8},{8,16},{16,24},{24,0},{1,9},{9,17},{17,25},{25,1},{2,10},{10... | collective-permute-start | bytes 3145736 | tf_op jit(solution)/shard_map/while/body/eval_jaxpr/ppermute | solution.py:16
  375.0 70.6 %collective-permute-start.3 = (f32[2,2,256,8,64]{2,4,3,1,0:T(8,128)}, f32[2,2,256,8,64]{2,4,3,1,0:T(8,128)}, u32[]{:S(2)}, u32[]{:S(2)}) collective-permute-start(f32[2,2,256,8,64]{2,4,3,1,0:T(8,128)} %maximum_add_fusion.7), channel_id=1, source_target_pairs={{0,8},{8,16},{16,24},{24,0},{1,9},{9,17},{17,25},{25,1},{2,10},{10... | collective-permute-start | bytes 6291464 | tf_op jit(solution)/shard_map/while/body/eval_jaxpr/ppermute | solution.py:16
  375.6 70.1 %collective-permute-start.2 = (bf16[2,2,256,8,64]{2,4,3,1,0:T(8,128)(2,1)S(1)}, bf16[2,2,256,8,64]{2,4,3,1,0:T(8,128)(2,1)}, u32[]{:S(2)}, u32[]{:S(2)}) collective-permute-start(bf16[2,2,256,8,64]{2,4,3,1,0:T(8,128)(2,1)S(1)} %copy.92), channel_id=1, source_target_pairs={{0,8},{8,16},{16,24},{24,0},{1,9},{9,17},{17,25},{25,1},{2,10},{10... | collective-permute-start | bytes 3145736 | tf_op jit(solution)/shard_map/while/body/eval_jaxpr/ppermute | solution.py:16
  457.5 69.7 %collective-permute-start.3 = (f32[2,2,256,8,64]{2,4,3,1,0:T(8,128)}, f32[2,2,256,8,64]{2,4,3,1,0:T(8,128)}, u32[]{:S(2)}, u32[]{:S(2)}) collective-permute-start(f32[2,2,256,8,64]{2,4,3,1,0:T(8,128)} %maximum_add_fusion.7), channel_id=1, source_target_pairs={{0,8},{8,16},{16,24},{24,0},{1,9},{9,17},{17,25},{25,1},{2,10},{10... | collective-permute-start | bytes 6291464 | tf_op jit(solution)/shard_map/while/body/eval_jaxpr/ppermute | solution.py:16
  457.5 69.7 %collective-permute-start.2 = (bf16[2,2,256,8,64]{2,4,3,1,0:T(8,128)(2,1)S(1)}, bf16[2,2,256,8,64]{2,4,3,1,0:T(8,128)(2,1)}, u32[]{:S(2)}, u32[]{:S(2)}) collective-permute-start(bf16[2,2,256,8,64]{2,4,3,1,0:T(8,128)(2,1)S(1)} %copy.92), channel_id=1, source_target_pairs={{0,8},{8,16},{16,24},{24,0},{1,9},{9,17},{17,25},{25,1},{2,10},{10... | collective-permute-start | bytes 3145736 | tf_op jit(solution)/shard_map/while/body/eval_jaxpr/ppermute | solution.py:16
  550.8 68.8 %collective-permute-start.1 = (f32[2,2,256,8,64]{2,4,3,1,0:T(8,128)}, f32[2,2,256,8,64]{2,4,3,1,0:T(8,128)}, u32[]{:S(2)}, u32[]{:S(2)}) collective-permute-start(f32[2,2,256,8,64]{2,4,3,1,0:T(8,128)} %maximum_add_fusion.6), channel_id=1, source_target_pairs={{0,8},{8,16},{16,24},{24,0},{1,9},{9,17},{17,25},{25,1},{2,10},{10... | collective-permute-start | bytes 6291464 | tf_op jit(solution)/shard_map/while/body/eval_jaxpr/ppermute | solution.py:16
  550.8 68.8 %collective-permute-start = (bf16[2,2,256,8,64]{2,4,3,1,0:T(8,128)(2,1)S(1)}, bf16[2,2,256,8,64]{2,4,3,1,0:T(8,128)(2,1)}, u32[]{:S(2)}, u32[]{:S(2)}) collective-permute-start(bf16[2,2,256,8,64]{2,4,3,1,0:T(8,128)(2,1)S(1)} %copy.104), channel_id=1, source_target_pairs={{0,8},{8,16},{16,24},{24,0},{1,9},{9,17},{17,25},{25,1},{2,10},{10... | collective-permute-start | bytes 3145736 | tf_op jit(solution)/shard_map/while/body/eval_jaxpr/ppermute | solution.py:16
  631.5 67.9 %collective-permute-start.1 = (f32[2,2,256,8,64]{2,4,3,1,0:T(8,128)}, f32[2,2,256,8,64]{2,4,3,1,0:T(8,128)}, u32[]{:S(2)}, u32[]{:S(2)}) collective-permute-start(f32[2,2,256,8,64]{2,4,3,1,0:T(8,128)} %maximum_add_fusion.6), channel_id=1, source_target_pairs={{0,8},{8,16},{16,24},{24,0},{1,9},{9,17},{17,25},{25,1},{2,10},{10... | collective-permute-start | bytes 6291464 | tf_op jit(solution)/shard_map/while/body/eval_jaxpr/ppermute | solution.py:16
  631.5 67.9 %collective-permute-start = (bf16[2,2,256,8,64]{2,4,3,1,0:T(8,128)(2,1)S(1)}, bf16[2,2,256,8,64]{2,4,3,1,0:T(8,128)(2,1)}, u32[]{:S(2)}, u32[]{:S(2)}) collective-permute-start(bf16[2,2,256,8,64]{2,4,3,1,0:T(8,128)(2,1)S(1)} %copy.104), channel_id=1, source_target_pairs={{0,8},{8,16},{16,24},{24,0},{1,9},{9,17},{17,25},{25,1},{2,10},{10... | collective-permute-start | bytes 3145736 | tf_op jit(solution)/shard_map/while/body/eval_jaxpr/ppermute | solution.py:16
  711.3 67.0 %collective-permute-start.1 = (f32[2,2,256,8,64]{2,4,3,1,0:T(8,128)}, f32[2,2,256,8,64]{2,4,3,1,0:T(8,128)}, u32[]{:S(2)}, u32[]{:S(2)}) collective-permute-start(f32[2,2,256,8,64]{2,4,3,1,0:T(8,128)} %maximum_add_fusion.6), channel_id=1, source_target_pairs={{0,8},{8,16},{16,24},{24,0},{1,9},{9,17},{17,25},{25,1},{2,10},{10... | collective-permute-start | bytes 6291464 | tf_op jit(solution)/shard_map/while/body/eval_jaxpr/ppermute | solution.py:16
  711.3 67.0 %collective-permute-start = (bf16[2,2,256,8,64]{2,4,3,1,0:T(8,128)(2,1)S(1)}, bf16[2,2,256,8,64]{2,4,3,1,0:T(8,128)(2,1)}, u32[]{:S(2)}, u32[]{:S(2)}) collective-permute-start(bf16[2,2,256,8,64]{2,4,3,1,0:T(8,128)(2,1)S(1)} %copy.104), channel_id=1, source_target_pairs={{0,8},{8,16},{16,24},{24,0},{1,9},{9,17},{17,25},{25,1},{2,10},{10... | collective-permute-start | bytes 3145736 | tf_op jit(solution)/shard_map/while/body/eval_jaxpr/ppermute | solution.py:16
  789.7 27.3 %collective-permute-start.5 = (bf16[2,2,256,8,64]{2,4,3,1,0:T(8,128)(2,1)}, bf16[2,2,256,8,64]{2,4,3,1,0:T(8,128)(2,1)}, u32[]{:S(2)}, u32[]{:S(2)}) collective-permute-start(bf16[2,2,256,8,64]{2,4,3,1,0:T(8,128)(2,1)} %maximum_add_fusion.3), channel_id=1, source_target_pairs={{0,8},{8,16},{16,24},{24,0},{1,9},{9,17},{17,25},{25,1},{2,10},{10... | collective-permute-start | bytes 3145736 | tf_op jit(solution)/shard_map/ppermute | solution.py:16
  794.4 38.9 %collective-permute-start.4 = (bf16[2,2,256,8,64]{2,4,3,1,0:T(8,128)(2,1)}, bf16[2,2,256,8,64]{2,4,3,1,0:T(8,128)(2,1)}, u32[]{:S(2)}, u32[]{:S(2)}) collective-permute-start(bf16[2,2,256,8,64]{2,4,3,1,0:T(8,128)(2,1)} %maximum_add_fusion.2), channel_id=1, source_target_pairs={{0,8},{8,16},{16,24},{24,0},{1,9},{9,17},{17,25},{25,1},{2,10},{10... | collective-permute-start | bytes 3145736 | tf_op jit(solution)/shard_map/ppermute | solution.py:16
  799.1 73.9 %reduce-scatter.15.cloned.1.call-start = ((), (), s32[]{:S(2)}) async-start(), calls=%async_computation.15 | async-start | bytes 1769472 | tf_op jit(solution)/shard_map/reduce_scatter | solution.py:244
  840.2 68.9 %reduce-scatter.23.cloned.1.call-start = ((), (), s32[]{:S(2)}) async-start(), calls=%async_computation.19 | async-start | bytes 2359296 | tf_op jit(solution)/shard_map/reduce_scatter | solution.py:253
  847.5 98.6 %reduce-scatter.19.cloned.1.call-start = ((), (), s32[]{:S(2)}) async-start(), calls=%async_computation.17 | async-start | bytes 2359296 | tf_op jit(solution)/shard_map/reduce_scatter | solution.py:250
  853.4 119.0 %reduce-scatter.27.cloned.1.call-start = ((), (), s32[]{:S(2)}) async-start(), calls=%async_computation.21 | async-start | bytes 163840
  862.9 136.3 %reduce-scatter.25.cloned.1.call-start = ((), (), s32[]{:S(2)}) async-start(), calls=%async_computation.20 | async-start | bytes 491520
  874.9 151.1 %reduce-scatter.29.cloned.1.call-start = ((), (), s32[]{:S(2)}) async-start(), calls=%async_computation.22 | async-start | bytes 327680
  877.5 93.8 %copy-start.47 = (bf16[2,256,512]{2,1,0:T(8,128)(2,1)S(1)}, bf16[2,256,512]{2,1,0:T(8,128)(2,1)}, u32[]{:S(2)}) copy-start(bf16[2,256,512]{2,1,0:T(8,128)(2,1)} %get-tuple-element.482) | copy-start | bytes 1572868
  910.9 141.9 %reduce-scatter.21.cloned.1.call-start = ((), (), s32[]{:S(2)}) async-start(), calls=%async_computation.18 | async-start | bytes 327680 | tf_op jit(solution)/shard_map/reduce_scatter | solution.py:273
  (94 other events, 725.1 us)
Sparse Core Ops, SparseCore 0:
  9.7 27.7 all-gather.7
  39.0 32.8 all-gather.15
  73.8 34.6 all-gather.9
  110.1 35.1 all-gather.11
  147.0 35.1 all-gather.17
  183.9 35.1 all-gather.19
  220.7 29.0 all-gather.13
  799.2 28.4 reduce-scatter.16
  840.3 32.6 reduce-scatter.14
  875.2 33.8 reduce-scatter.22
  911.5 34.5 reduce-scatter.18
  949.5 22.4 reduce-scatter.26
  974.8 24.4 reduce-scatter.24
  1001.8 24.0 reduce-scatter.28
  1028.8 24.0 reduce-scatter.20
where the time goes:
time: 1070 us; the launch traced here: 1060 us
  waiting for transfers between devices  694 us (65%)
  matrix products  175 us (16%)
  other arithmetic  56.4 us (5%)
  local copies, waits for them, and re-layouts  54.2 us (5%)
  blocking collectives  42.9 us (4%)
  starting transfers between devices  21.6 us (2%)
  between operations  16.4 us (2%)
    ppermute x14, waiting for transfers between devices, passed_along(): lax.ppermute(value, axis, [(i, (i + by) % count) for i in range(count)])  408 us
    all_gather x2, waiting for transfers between devices, spread_forward(): key_piece = lax.all_gather(key_rows, 'seq', axis=1, tiled=True)  73.8 us
    unnamed x18, waiting for transfers between devices  52.7 us
    all_gather x2, waiting for transfers between devices, spread_forward(): value_piece = lax.all_gather(value_rows, 'seq', axis=1, tiled=True)  40.2 us
    reduce_scatter x1, waiting for transfers between devices, per_device(): lax.psum_scatter(sum_up.astype(jnp.bfloat16), 'dp', scatter_dimension=0,...  33.2 us
    reduce_scatter x1, waiting for transfers between devices, per_device(): lax.psum_scatter(sum_down.astype(jnp.bfloat16), 'dp', scatter_dimension=0...  31.6 us
    reduce_scatter x1, waiting for transfers between devices, per_device(): lax.psum_scatter(row_sums[2].astype(jnp.bfloat16), 'seq', scatter_dimensi...  25.3 us
    add x8, other arithmetic, visit(): gathered = gathered + jnp.stack((key_part, value_part))  25.2 us
  transfers between devices with their start and end apart: 29, of which 20 were waited for; matrix products, arithmetic and copies ran while one was open for 15% of the time, Pallas kernels for 0%

commit v1 on v0

v1 whole, which is shorter than its diff:
```python
import functools

import jax
import jax.numpy as jnp
from jax import lax
from jax.experimental import pallas as pl
from jax.experimental.pallas import tpu as pltpu
from jax.sharding import PartitionSpec as P

EPSILON = 1e-05
HEADS = 8
F32 = jnp.float32
BF16 = jnp.bfloat16
VMEM_BYTES = 56 * 2**20


def nn(left, right):
    return jnp.dot(left, right, preferred_element_type=F32)


def nt(left, right):
    return lax.dot_general(left, right, (((1,), (1,)), ((), ())), preferred_element_type=F32)


def params(vmem=VMEM_BYTES):
    return pltpu.CompilerParams(vmem_limit_bytes=vmem)


def cost(flops, bytes_accessed):
    return pl.CostEstimate(
        flops=int(flops), bytes_accessed=int(bytes_accessed), transcendentals=0
    )


def attend_kernel(chunk, q_ref, k_ref, v_ref, out_ref, den_ref):
    count = q_ref.shape[0]
    low = lax.broadcasted_iota(jnp.int32, (1, 128), 1) < 64
    keys = k_ref[...]
    values = v_ref[...]
    one = jnp.ones_like(values)
    values_low = jnp.where(low, values, one)
    values_high = jnp.where(low, one, values)
    for start in range(0, count, chunk):
        q = q_ref[start : start + chunk, :] * jnp.asarray(0.125, BF16)
        zero = jnp.zeros_like(q)
        left = nn(jnp.exp(nt(jnp.where(low, q, zero), keys)).astype(BF16), values_low)
        right = nn(jnp.exp(nt(jnp.where(low, zero, q), keys)).astype(BF16), values_high)
        den = pltpu.roll(jnp.where(low, right, left), 64, 1)
        den_ref[start : start + chunk, :] = den
        out_ref[start : start + chunk, :] = jnp.where(low, left, right) / den


def attend(q_source, kv_source, kv_shift):
    count, span = q_source.shape[0], kv_source.shape[0]
    chunk = min(256, count)
    out = jax.ShapeDtypeStruct((count, 512), F32)
    return pl.pallas_call(
        functools.partial(attend_kernel, chunk),
        grid=(4,),
        in_specs=[
            pl.BlockSpec((count, 128), lambda p: (0, p)),
            pl.BlockSpec((span, 128), lambda p: (0, kv_shift + p)),
            pl.BlockSpec((span, 128), lambda p: (0, kv_shift + 4 + p)),
        ],
        out_specs=[pl.BlockSpec((count, 128), lambda p: (0, p))] * 2,
        out_shape=[out, out],
        compiler_params=params(),
        cost_estimate=cost(16 * count * span * 1024, 7 * 2**20),
        name="attend",
    )(q_source, kv_source, kv_source)


def attend_back_kernel(chunk, q_ref, k_ref, v_ref, s_ref, x_ref, dq_ref, dk_ref, dv_ref):
    count, span = q_ref.shape[0], k_ref.shape[0]
    lane = lax.broadcasted_iota(jnp.int32, (1, 128), 1)
    low = lane < 64
    q = q_ref[...] * jnp.asarray(0.125, BF16)
    scaled = s_ref[...]
    extra = x_ref[...]
    zero = jnp.zeros_like(q)
    q_own = (jnp.where(low, q, zero), jnp.where(low, zero, q))
    s_own = (jnp.where(low, scaled, zero), jnp.where(low, zero, scaled))
    s_with = (jnp.where(low, scaled, extra), jnp.where(low, extra, scaled))
    minus = (
        jnp.where((lane == 64) | (lane == 65), -1.0, 0.0).astype(BF16),
        jnp.where((lane == 0) | (lane == 1), -1.0, 0.0).astype(BF16),
    )
    total = jnp.zeros((128, count), F32)
    for start in range(0, span, chunk):
        keys = k_ref[start : start + chunk, :]
        values = v_ref[start : start + chunk, :]
        none = jnp.zeros_like(keys)
        k_own = (jnp.where(low, keys, none), jnp.where(low, none, keys))
        v_with = (jnp.where(low, values, minus[0]), jnp.where(low, minus[1], values))
        dk = dv = 0.0
        for head in range(2):
            weights = jnp.exp(nt(keys, q_own[head]))
            slopes = (weights * nt(v_with[head], s_with[head])).astype(BF16)
            dv = dv + nn(weights.astype(BF16), s_own[head])
            dk = dk + nn(slopes, q_own[head])
            total = total + nn(k_own[head].T, slopes)
        dk_ref[start : start + chunk, :] = dk.astype(BF16)
        dv_ref[start : start + chunk, :] = dv.astype(BF16)
    dq_ref[...] = (total.T * 0.125).astype(BF16)


def attend_back(q_source, kv_source, kv_shift, scaled, extra):
    count, span = q_source.shape[0], kv_source.shape[0]
    chunk = min(512, span)
    own = pl.BlockSpec((count, 128), lambda p: (0, p))
    far = pl.BlockSpec((span, 128), lambda p: (0, p))
    return pl.pallas_call(
        functools.partial(attend_back_kernel, chunk),
        grid=(4,),
        in_specs=[
            own,
            pl.BlockSpec((span, 128), lambda p: (0, kv_shift + p)),
            pl.BlockSpec((span, 128), lambda p: (0, kv_shift + 4 + p)),
            own,
            own,
        ],
        out_specs=[own, far, far],
        out_shape=[
            jax.ShapeDtypeStruct((count, 512), BF16),
            jax.ShapeDtypeStruct((span, 512), BF16),
            jax.ShapeDtypeStruct((span, 512), BF16),
        ],
        compiler_params=params(),
        cost_estimate=cost(32 * count * span * 1024, 8 * 2**20),
        name="attend_back",
    )(q_source, kv_source, kv_source, scaled, extra)


def norm_parts(tensor):
    center = tensor - jnp.mean(tensor, axis=-1, keepdims=True)
    scale = lax.rsqrt(jnp.mean(center * center, axis=-1, keepdims=True) + EPSILON)
    return center * scale, scale


def norm_back(q, normed, scale):
    return scale * (
        q - jnp.mean(q, axis=-1, keepdims=True) - normed * jnp.mean(q * normed, axis=-1, keepdims=True)
    )


def feed_kernel(
    hidden_ref,
    att_ref,
    den_ref,
    cot_ref,
    gain_ref,
    w_out_ref,
    w_up_ref,
    w_down_ref,
    out_ref,
    att_bf_ref,
    normed_ref,
    act_ref,
    raise_ref,
    first_ref,
    branch_ref,
    scaled_ref,
    extra_ref,
    gain_sum_ref,
):
    step = pl.program_id(0)
    att = att_ref[...]
    den = den_ref[...]
    cot = cot_ref[...]
    gain = gain_ref[...]
    att_bf = att.astype(BF16)
    att_bf_ref[...] = att_bf
    first = hidden_ref[...] + nn(att_bf, w_out_ref[...])
    normed, scale = norm_parts(first)
    normed_two = (normed * gain).astype(BF16)
    normed_ref[...] = normed_two
    total = first
    back = jnp.zeros_like(first)
    for start in range(0, w_up_ref.shape[1], 512):
        stop = start + 512
        up = w_up_ref[:, start:stop]
        down = w_down_ref[start:stop, :]
        v = nn(normed_two, up)
        square = v * v
        t = jnp.tanh(v * (0.7978845608028654 + 0.035677408136300125 * square))
        half = 0.5 + 0.5 * t
        act = (v * half).astype(BF16)
        slope = half + v * (0.5 - 0.5 * t * t) * (
            0.7978845608028654 + 0.10703222440890037 * square
        )
        act_ref[:, start:stop] = act
        total = total + nn(act, down)
        grad_raised = (nt(cot, down) * slope).astype(BF16)
        raise_ref[:, start:stop] = grad_raised
        back = back + nt(grad_raised, up)
    out_ref[...] = total.astype(BF16)

    @pl.when(step == 0)
    def _():
        gain_sum_ref[...] = jnp.zeros_like(gain_sum_ref)

    gain_sum_ref[...] += jnp.sum(back * normed, axis=0, keepdims=True)
    grad_first = cot.astype(F32) + norm_back(back * gain, normed, scale)
    first_ref[...] = grad_first
    branch = grad_first.astype(BF16)
    branch_ref[...] = branch
    ratio = nt(branch, w_out_ref[...]) / den
    scaled_ref[...] = ratio.astype(BF16)
    row = lax.broadcasted_iota(jnp.int32, (128, 128), 0)
    col = lax.broadcasted_iota(jnp.int32, (128, 128), 1)
    swap = jnp.where((row < 64) != (col < 64), 1.0, 0.0).astype(BF16)
    even = lax.broadcasted_iota(jnp.int32, (1, 128), 1) % 2 == 0
    product = ratio * att
    coarse = product.astype(BF16)
    fine = (product - coarse.astype(F32)).astype(BF16)
    for start in range(0, 512, 128):
        offset = nn(coarse[:, start : start + 128], swap) + nn(fine[:, start : start + 128], swap)
        upper = offset.astype(BF16)
        lower = (offset - upper.astype(F32)).astype(BF16)
        extra_ref[:, start : start + 128] = jnp.where(even, upper, lower)


def feed(hidden, att, den, cot, gain, w_out, w_up, w_down):
    count, width = hidden.shape
    raised = w_up.shape[1]
    chunk = min(256, count)
    blk = pl.BlockSpec((chunk, width), lambda i: (i, 0))
    wide = pl.BlockSpec((chunk, raised), lambda i: (i, 0))

    def whole(shape):
        return pl.BlockSpec(shape, lambda i: (0, 0), pipeline_mode=pl.Buffered(1))

    def sds(cols, dtype):
        return jax.ShapeDtypeStruct((count, cols), dtype)

    return pl.pallas_call(
        feed_kernel,
        grid=(count // chunk,),
        in_specs=[
            blk,
            blk,
            blk,
            blk,
            whole((1, width)),
            whole((width, width)),
            whole((width, raised)),
            whole((raised, width)),
        ],
        out_specs=[blk, blk, blk, wide, wide, blk, blk, blk, blk, whole((1, width))],
        out_shape=[
            sds(width, BF16),
            sds(width, BF16),
            sds(width, BF16),
            sds(raised, BF16),
            sds(raised, BF16),
            sds(width, F32),
            sds(width, BF16),
            sds(width, BF16),
            sds(width, BF16),
            jax.ShapeDtypeStruct((1, width), F32),
        ],
        compiler_params=params(),
        cost_estimate=cost(10 * 2**30, 30 * 2**20),
        name="feed",
    )(hidden, att, den, cot, gain, w_out, w_up, w_down)


def product_kernel(blocks, own_ref, left_ref, right_ref, out_ref, turned):
    @pl.when(pl.program_id(0) == 0)
    def _():
        turned[...] = left_ref[...].T

    result = nn(turned[...], right_ref[...]).astype(BF16)
    rows = result.shape[0] // blocks
    for block in range(blocks):
        piece = result[block * rows : (block + 1) * rows, :]
        if out_ref.shape[0] == 2:
            core = (block % 2) ^ own_ref[2]
            out_ref[core, 0, (block // 2) ^ own_ref[1]] = piece
        else:
            out_ref[0, block ^ own_ref[0], 0] = piece


def grad_pieces(own, left, right, seq_count, dp_count, flipped):
    count, left_cols = left.shape
    right_cols = right.shape[1]
    z_count = dp_count // 2
    left_blocks, right_blocks = (seq_count, dp_count) if flipped else (dp_count, seq_count)
    rows, cols = left_cols // left_blocks, right_cols // right_blocks
    if cols % 128 or rows % 16:
        whole = lax.dot_general(
            left, right, (((0,), (0,)), ((), ())), preferred_element_type=F32
        ).astype(BF16)
        whole = whole.reshape(left_blocks, rows, right_blocks, cols)
        whole = jnp.transpose(whole, (0, 2, 1, 3) if flipped else (2, 0, 1, 3))
        whole = whole.reshape(seq_count, z_count, 2, rows, cols)
        whole = jnp.take(whole, jnp.arange(seq_count) ^ own[0], axis=0)
        whole = jnp.take(whole, jnp.arange(z_count) ^ own[1], axis=1)
        whole = jnp.take(whole, jnp.arange(2) ^ own[2], axis=2)
        return jnp.transpose(whole, (2, 0, 1, 3, 4))
    if flipped:
        out_spec = pl.BlockSpec(
            (1, seq_count, 1, rows, cols),
            lambda i, own: ((i % 2) ^ own[2], 0, (i // 2) ^ own[1], 0, 0),
        )
    else:
        out_spec = pl.BlockSpec(
            (2, 1, z_count, rows, cols), lambda i, own: (0, i ^ own[0], 0, 0, 0)
        )
    return pl.pallas_call(
        functools.partial(product_kernel, left_blocks),
        grid_spec=pltpu.PrefetchScalarGridSpec(
            num_scalar_prefetch=1,
            grid=(right_blocks,),
            in_specs=[
                pl.BlockSpec((count, left_cols), lambda i, own: (0, 0)),
                pl.BlockSpec((count, cols), lambda i, own: (0, i)),
            ],
            out_specs=out_spec,
            scratch_shapes=[pltpu.VMEM((left_cols, count), BF16)],
        ),
        out_shape=jax.ShapeDtypeStruct((2, seq_count, z_count, rows, cols), BF16),
        compiler_params=params(),
        cost_estimate=cost(2 * count * left_cols * right_cols, 2 * count * (left_cols + right_cols)),
        name="grad_product",
    )(own, left, right)


def last_kernel(
    hidden_ref, first_ref, gain_ref, mask_ref, dq_ref, dk_ref, dv_ref, w_ref, out_ref, sums_ref
):
    width = hidden_ref.shape[1]
    back = nt(dq_ref[...], w_ref[:, :width])
    back = back + nt(dk_ref[...], w_ref[:, width : 2 * width])
    back = back + nt(dv_ref[...], w_ref[:, 2 * width :])
    normed, scale = norm_parts(hidden_ref[...])
    grad = first_ref[...] + norm_back(back * gain_ref[...], normed, scale)
    out_ref[...] = grad.astype(BF16)

    @pl.when(pl.program_id(0) == 0)
    def _():
        sums_ref[...] = jnp.zeros_like(sums_ref)

    mask = mask_ref[...].astype(BF16)
    coarse = grad.astype(BF16)
    fine = (grad - coarse.astype(F32)).astype(BF16)
    masked = nn(mask, coarse) + nn(mask, fine)
    sums_ref[0:1, :] += masked[0:1, :]
    sums_ref[1:2, :] += jnp.sum(back * normed, axis=0, keepdims=True)


def last(hidden, grad_first, gain, mask, dq, dk, dv, w_qkv):
    count, width = hidden.shape
    chunk = min(256, count)
    blk = pl.BlockSpec((chunk, width), lambda i: (i, 0))

    def whole(shape):
        return pl.BlockSpec(shape, lambda i: (0, 0), pipeline_mode=pl.Buffered(1))

    return pl.pallas_call(
        last_kernel,
        grid=(count // chunk,),
        in_specs=[
            blk,
            blk,
            whole((1, width)),
            pl.BlockSpec((8, chunk), lambda i: (0, i)),
            blk,
            blk,
            blk,
            whole(w_qkv.shape),
        ],
        out_specs=[blk, whole((8, width))],
        out_shape=[
            jax.ShapeDtypeStruct((count, width), BF16),
            jax.ShapeDtypeStruct((8, width), F32),
        ],
        compiler_params=params(),
        cost_estimate=cost(6 * count * width * width, 12 * 2**20),
        name="last",
    )(hidden, grad_first, gain, mask, dq, dk, dv, w_qkv)


def swap_along(value, axis, mask):
    count = lax.axis_size(axis)
    return lax.ppermute(value, axis, [(i, i ^ mask) for i in range(count)])


def add_up(values):
    total = values[0].astype(F32)
    for value in values[1:]:
        total = total + value.astype(F32)
    return total


def scatter_sum(pieces):
    seq_count, z_count = pieces.shape[1], pieces.shape[2]
    mine = add_up((pieces[0], swap_along(pieces[1], "dp", 1))).astype(BF16)
    plane = [mine[0]] + [swap_along(mine[j], "seq", j) for j in range(1, seq_count)]
    plane = add_up(plane).astype(BF16)
    line = [plane[0]] + [swap_along(plane[j], "dp", 2 * j) for j in range(1, z_count)]
    return add_up(line)


def vector_sum(vectors, own):
    seq_count, dp_count = lax.axis_size("seq"), lax.axis_size("dp")
    total = add_up([vectors] + [swap_along(vectors, "seq", j) for j in range(1, seq_count)])
    total = add_up([total] + [swap_along(total, "dp", 2 * j) for j in range(1, dp_count // 2)])
    total = total + swap_along(total, "dp", 1)
    width = vectors.shape[1] // dp_count
    return lax.dynamic_slice_in_dim(total, lax.axis_index("dp") * width, width, 1)


def per_device(
    inputs,
    cotangent,
    timestep,
    unmask_order,
    mask_embed,
    ln1_gain,
    weight_qkv,
    weight_out,
    ln2_gain,
    weight_up,
    weight_down,
):
    rows, segment, width = inputs.shape
    seq_count, dp_count = lax.axis_size("seq"), lax.axis_size("dp")
    outer = seq_count // rows
    place = lax.axis_index("seq")
    dp_place = lax.axis_index("dp")
    row = place % rows
    own = jnp.stack([place, dp_place // 2, dp_place % 2]).astype(jnp.int32)

    def to_rows(value):
        parts = [
            lax.dynamic_index_in_dim(value, row ^ j, 0, keepdims=False) for j in range(rows)
        ]
        return [parts[0]] + [swap_along(parts[j], "seq", j) for j in range(1, rows)]

    def from_rows(value):
        parts = [value[j * segment : (j + 1) * segment] for j in range(rows)]
        parts = [parts[0]] + [swap_along(parts[j], "seq", j) for j in range(1, rows)]
        bit = 1
        while bit < rows:
            odd = (row & bit) != 0
            parts = [jnp.where(odd, parts[j ^ bit], parts[j]) for j in range(rows)]
            bit *= 2
        return jnp.stack(parts)

    masked = (unmask_order <= timestep[:, None]).astype(F32)
    mask_row = jnp.concatenate(to_rows(masked))
    block = jnp.concatenate(to_rows(inputs)).astype(F32)
    cot = jnp.concatenate(to_rows(cotangent))
    whole_qkv = lax.all_gather(weight_qkv, "dp", axis=0, tiled=True)
    whole_up = lax.all_gather(
        jnp.concatenate((weight_out, weight_up), axis=1), "dp", axis=0, tiled=True
    )
    whole_down = lax.all_gather(weight_down, "dp", axis=0, tiled=True)
    whole_out, whole_up = whole_up[:, :width], whole_up[:, width:]

    hidden = block + mask_row[:, None] * mask_embed
    normed = norm_parts(hidden)[0]
    normed_one = (normed * ln1_gain).astype(BF16)
    projected = nn(normed_one, whole_qkv).astype(BF16)
    if outer > 1:
        groups = [[j * rows + i for j in range(outer)] for i in range(rows)]
        far = lax.all_gather(
            projected[:, width:], "seq", axis=0, tiled=True, axis_index_groups=groups
        )
        shift = 0
    else:
        far, shift = projected, 4
    attended, denominators = attend(projected, far, shift)
    (
        outputs,
        attended_bf,
        normed_two,
        activated,
        grad_raised,
        grad_first,
        grad_branch,
        scaled,
        extra,
        sum_gain_two,
    ) = feed(
        hidden,
        attended,
        denominators,
        cot,
        ln2_gain[None, :],
        whole_out,
        whole_up,
        whole_down,
    )
    result = from_rows(outputs)
    pieces = functools.partial(grad_pieces, own, seq_count=seq_count, dp_count=dp_count)
    pieces_down = pieces(cot, activated, flipped=True)
    pieces_up = pieces(normed_two, grad_raised, flipped=False)
    pieces_out = pieces(attended_bf, grad_branch, flipped=False)
    dq, dk, dv = attend_back(projected, far, shift, scaled, extra)
    if outer > 1:
        both = jnp.concatenate((dk, dv), axis=1)
        both = lax.psum_scatter(
            both, "seq", scatter_dimension=0, tiled=True, axis_index_groups=groups
        )
        dk, dv = both[:, :width], both[:, width:]
    pieces_qkv = pieces(normed_one, jnp.concatenate((dq, dk, dv), axis=1), flipped=False)
    mask_rows = jnp.broadcast_to(mask_row[None, :], (8, mask_row.shape[0]))
    grad_hidden, sums = last(
        hidden, grad_first, ln1_gain[None, :], mask_rows, dq, dk, dv, whole_qkv
    )
    grad_inputs = from_rows(grad_hidden)
    vectors = vector_sum(
        jnp.concatenate((sums[0:2], sum_gain_two, jnp.zeros((5, width), F32)), axis=0), own
    )
    return (
        result,
        grad_inputs,
        vectors[0],
        vectors[1],
        scatter_sum(pieces_qkv),
        scatter_sum(pieces_out),
        vectors[2],
        scatter_sum(pieces_up),
        scatter_sum(pieces_down).T,
    )


def solution(mesh):
    in_specs = (
        P("dp", "seq", None),
        P("dp", "seq", None),
        P("dp"),
        P("dp", "seq"),
        P(),
        P(),
        P("dp", None),
        P("dp", None),
        P(),
        P("dp", None),
        P("dp", None),
    )
    out_specs = (
        P("dp", "seq", None),
        P("dp", "seq", None),
        P("dp"),
        P("dp"),
        P("dp", "seq"),
        P("dp", "seq"),
        P("dp"),
        P("dp", "seq"),
        P("dp", "seq"),
    )
    return jax.shard_map(
        per_device, mesh=mesh, in_specs=in_specs, out_specs=out_specs, check_vma=False
    )
```

time: 1070 us -> 299 us (0.28)
  waiting for transfers between devices: 694 us -> 88.2 us
  matrix products: 175 us -> 5.3 us
  Pallas kernels: 0 us -> 94.5 us
  blocking collectives: 42.9 us -> 0 us
  starting transfers between devices: 21.6 us -> 62.9 us
  local copies, waits for them, and re-layouts: 54.2 us -> 14.5 us
  other arithmetic: 56.4 us -> 18.2 us
    ppermute x14 -> x50, waiting for transfers between devices: 408 us -> 52.2 us  [swap_along(): return lax.ppermute(value, axis, [(i, i ^ mask) for i in range(count)])]
    dot_general x80 -> x1, matrix products: 175 us -> 5.3 us  [nn(): return jnp.dot(left, right, preferred_element_type=F32)]
    all_gather x7 -> x3, waiting for transfers between devices: 136 us -> 35.3 us  [the longest x1 24.6 us: per_device(): whole_down = lax.all_gather(weight_down, 'dp', axis=0, tiled=True)]
    reduce_scatter x5 -> x0, waiting for transfers between devices: 97.7 us -> none  [the longest x1 33.2 us: per_device(): lax.psum_scatter(sum_up.astype(jnp.bfloat16), 'dp', scatter_dimension=0,...]
    pallas_call x0 -> x8, Pallas kernels: none -> 94.5 us  [the longest x4 28.6 us: grad_pieces(): pl.pallas_call(functools.partial(product_kernel, left_blocks), grid_spec=...]
    unnamed x18 -> x3, waiting for transfers between devices: 52.7 us -> 0.71 us
    ppermute x14 -> x50, starting transfers between devices: 20.7 us -> 62.8 us  [swap_along(): return lax.ppermute(value, axis, [(i, i ^ mask) for i in range(count)])]
    add x16 -> x6, other arithmetic: 25.3 us -> 2.13 us  [the longest x5 2.06 us: add_up(): total = total + value.astype(F32)]
  transfers between devices with their start and end apart: 29 -> 53, of which waited for: 20 -> 24; matrix products, arithmetic and copies ran while one was open for 15% -> 11% of each run, Pallas kernels for 0% -> 14%
where the time goes in v1:
time: 299 us; the launch traced here: 298 us
  Pallas kernels  94.5 us (32%)
  waiting for transfers between devices  88.2 us (29%)
  starting transfers between devices  62.9 us (21%)
  other arithmetic  18.2 us (6%)
  local copies, waits for them, and re-layouts  14.5 us (5%)
  between operations  14.2 us (5%)
  matrix products  5.3 us (2%)
    ppermute x50, starting transfers between devices, swap_along(): return lax.ppermute(value, axis, [(i, i ^ mask) for i in range(count)])  62.8 us
    ppermute x50, waiting for transfers between devices, swap_along(): return lax.ppermute(value, axis, [(i, i ^ mask) for i in range(count)])  52.2 us
    pallas_call x4, Pallas kernels, grad_pieces(): pl.pallas_call(functools.partial(product_kernel, left_blocks), grid_spec=...  28.6 us
    all_gather x1, waiting for transfers between devices, per_device(): whole_down = lax.all_gather(weight_down, 'dp', axis=0, tiled=True)  24.6 us
    pallas_call x1, Pallas kernels, attend_back(): pl.pallas_call(functools.partial(attend_back_kernel, chunk), grid=(4,), i...  23.3 us
    pallas_call x1, Pallas kernels, feed(): pl.pallas_call(feed_kernel, grid=(count // chunk,), in_specs=[blk, blk, b...  23.2 us
    pallas_call x1, Pallas kernels, attend(): pl.pallas_call(functools.partial(attend_kernel, chunk), grid=(4,), in_spe...  12.2 us
    all_gather x1, waiting for transfers between devices, per_device(): lax.all_gather(jnp.concatenate((weight_out, weight_up), axis=1), 'dp', ax...  10.7 us
  transfers between devices with their start and end apart: 53, of which 24 were waited for; matrix products, arithmetic and copies ran while one was open for 11% of the time, Pallas kernels for 14%

profile of v1, /device:TPU:0, one launch (start us, length us, event | category | flops | bytes accessed | tf_op | source)
XLA Modules:
  0.0 297.8 jit_solution(13714426946079238904)
XLA Ops:
  11.1 3.0 %collective-permute-start.6 = (bf16[256,512]{1,0:T(8,128)(2,1)S(1)}, bf16[256,512]{1,0:T(8,128)(2,1)S(1)}, u32[]{:S(2)}, u32[]{:S(2)}) collective-permute-start(bf16[256,512]{1,0:T(8,128)(2,1)S(1)} %get-tuple-element.75), channel_id=1, source_target_pairs={{0,8},{8,0},{16,24},{24,16},{1,9},{9,1},{17,25},{25,17},{2,10},{10... | collective-permute-start | bytes 786440 | tf_op jit(solution)/shard_map/ppermute | solution.py:386
  16.3 2.9 collective-permute-start.8
  21.3 3.0 %collective-permute-start.5 = (f32[256]{0:T(256)S(1)}, f32[256]{0:T(256)S(1)}, u32[]{:S(2)}, u32[]{:S(2)}) collective-permute-start(f32[256]{0:T(256)S(1)} %bitcast.169), channel_id=1, source_target_pairs={{0,24},{8,16},{16,8},{24,0},{1,25},{9,17},{17,9},{25,1},{2,26},{10... | collective-permute-start | bytes 3080 | tf_op jit(solution)/shard_map/ppermute | solution.py:386
  24.8 3.7 %collective-permute-done.5 = f32[256]{0:T(256)S(1)} collective-permute-done((f32[256]{0:T(256)S(1)}, f32[256]{0:T(256)S(1)}, u32[]{:S(2)}, u32[]{:S(2)}) %collective-permute-start.5) | collective-permute-done | bytes 1056 | tf_op jit(solution)/shard_map/ppermute | solution.py:386
  28.6 2.9 collective-permute-start.2
  34.3 6.1 %collective-permute-done.1 = bf16[256,512]{1,0:T(8,128)(2,1)S(1)} collective-permute-done((bf16[256,512]{1,0:T(8,128)(2,1)S(1)}, bf16[256,512]{1,0:T(8,128)(2,1)S(1)}, u32[]{:S(2)}, u32[]{:S(2)}) %collective-permute-start.1) | collective-permute-done | bytes 262176 | tf_op jit(solution)/shard_map/ppermute | solution.py:386
  41.8 3.2 %multiply_convert_fusion = (bf16[1024,512]{1,0:T(8,128)(2,1)S(1)}, f32[1024,512]{1,0:T(8,128)}) fusion(f32[512]{0:T(512)S(1)} %copy-done.9, f32[1024]{0:T(1024)S(1)} %add_rsqrt_fusion, f32[1024]{0:T(1024)S(1)} %broadcast_multiply_fusion, f32[512]{0:T(512)S(1)} %copy-done.8, f32[1024]{0:T(1024)S(1)} %pad_maximum_fusion.5, ...), kind=kLoop, calls=%fused_computation.6 | loop fusion | flops 7340032 | bytes 4210688 | tf_op jit(solution)/shard_map/convert_element_type | solution.py:464
  45.0 5.3 %convolution_convert_fusion.q_ref.k_ref.v_ref = bf16[1024,1536]{1,0:T(8,128)(2,1)} fusion(bf16[1024,512]{1,0:T(8,128)(2,1)S(1)} %get-tuple-element.60.left_ref, bf16[512,1536]{1,0:T(8,128)(2,1)} %all-gather.4.cloned.1.call-done.w_ref), kind=kOutput, calls=%fused_computation | convolution fusion | flops 1612185600 | bytes 5767168 | tf_op jit(solution)/shard_map/dot_general | solution.py:18
  50.3 12.2 %attend.1 = (f32[1024,512]{1,0:T(8,128)}, f32[1024,512]{1,0:T(8,128)}) custom-call(bf16[1024,1536]{1,0:T(8,128)(2,1)} %convolution_convert_fusion.q_ref.k_ref.v_ref, bf16[1024,1536]{1,0:T(8,128)(2,1)} %convolution_convert_fusion.q_ref.k_ref.v_ref, bf16[1024,1536]{1,0:T(8,128)(2,1)} %convolution_convert_fusion.q_ref.k_ref.v_ref), custom_call_target="tpu_custom_call" | custom-call | flops 17179869184 | bytes 7340032 | tf_op jit(solution)/shard_map/attend/pallas_call | solution.py:57
  62.4 10.7 %all-gather.6.cloned.1.call-done = bf16[512,2560]{1,0:T(8,128)(2,1)} async-done(((bf16[64,2560]{1,0:T(8,128)(2,1)}), bf16[512,2560]{1,0:T(8,128)(2,1)}) %all-gather.6.cloned.1.call-update) | async-done | bytes 2621456 | tf_op jit(solution)/shard_map/all_gather | solution.py:456
  73.1 3.2 %slice.217.w_up_ref = bf16[512,2048]{1,0:T(8,128)(2,1)} slice(bf16[512,2560]{1,0:T(8,128)(2,1)} %all-gather.6.cloned.1.call-done), slice={[0:512], [512:2560]} | slice | bytes 4194304 | tf_op jit(solution)/shard_map/slice | solution.py:460
  78.2 24.6 %all-gather.8.cloned.1.call-done.w_down_ref = bf16[2048,512]{1,0:T(8,128)(2,1)} async-done(((bf16[256,512]{1,0:T(8,128)(2,1)}), bf16[2048,512]{1,0:T(8,128)(2,1)}) %all-gather.8.cloned.1.call-update) | async-done | bytes 2097168 | tf_op jit(solution)/shard_map/all_gather | solution.py:459
  102.9 23.2 %feed.1 = (bf16[1024,512]{1,0:T(8,128)(2,1)}, bf16[1024,512]{1,0:T(8,128)(2,1)}, bf16[1024,512]{1,0:T(8,128)(2,1)}, bf16[1024,2048]{1,0:T(8,128)(2,1)}, bf16[102...) custom-call(f32[1024,512]{1,0:T(8,128)} %get-tuple-element.61.hidden, ...), custom_call_target="tpu_custom_call" | custom-call | flops 10737418240 | bytes 31457280 | tf_op jit(solution)/shard_map/feed/pallas_call | solution.py:236
  126.1 23.3 %attend_back.1 = (bf16[1024,512]{1,0:T(8,128)(2,1)}, bf16[1024,512]{1,0:T(8,128)(2,1)}, bf16[1024,512]{1,0:T(8,128)(2,1)}) custom-call(bf16[1024,1536]{1,0:T(8,128)(2,1)} %convolution_convert_fusion.q_ref.k_ref.v_ref, bf16[1024,1536]{1,0:T(8,128)(2,1)} %convolution_convert_fusion.q_ref.k_ref.v_ref, ...), custom_call_target="tpu_custom_call" | custom-call | flops 34359738368 | bytes 8388608 | tf_op jit(solution)/shard_map/attend_back/pallas_call | solution.py:112
  149.4 3.1 %pad_maximum_fusion.right_ref = bf16[1024,1536]{1,0:T(8,128)(2,1)} fusion(bf16[1024,512]{1,0:T(8,128)(2,1)} %get-tuple-element.34.dv_ref, bf16[1024,512]{1,0:T(8,128)(2,1)} %get-tuple-element.33.dk_ref, bf16[1024,512]{1,0:T(8,128)(2,1)} %get-tuple-element.32.dq_ref), kind=kLoop, calls=%fused_computation.1 | loop fusion | flops 9437184 | bytes 6291456 | tf_op jit(solution)/shard_map/concatenate | solution.py:508
  153.1 7.2 %last.1 = (bf16[1024,512]{1,0:T(8,128)(2,1)}, f32[8,512]{1,0:T(8,128)}) custom-call(f32[1024,512]{1,0:T(8,128)} %get-tuple-element.61.hidden_ref, f32[1024,512]{1,0:T(8,128)} %get-tuple-element.29.first_ref, f32[1,512]{1,0:T(1,128)} %bitcast.167, f32[8,1024]{1,0:T(8,128)} %broadcast_in_dim.10.mask_ref, bf16[1024,512]{1,0:T(8,128)(2,1)} %get-tuple-element.32.dq_ref, ...), custom_call_target="tpu_custom_call" | custom-call | flops 1610612736 | bytes 12582912 | tf_op jit(solution)/shard_map/last/pallas_call | solution.py:360
  164.7 9.1 %grad_product.7 = bf16[2,4,4,128,256]{4,3,2,1,0:T(8,128)(2,1)} custom-call(s32[3]{0:T(128)} %pad_add_fusion.own_ref, bf16[1024,512]{1,0:T(8,128)(2,1)} %pad_maximum_fusion.1.cot_ref.left_ref, bf16[1024,2048]{1,0:T(8,128)(2,1)} %get-tuple-element.42.right_ref), custom_call_target="tpu_custom_call" | custom-call | flops 2147483648 | bytes 5242880 | tf_op jit(solution)/shard_map/grad_product/pallas_call | solution.py:310
  175.2 7.0 %grad_product.6 = bf16[2,4,4,64,512]{4,3,2,1,0:T(8,128)(2,1)} custom-call(s32[3]{0:T(128)} %pad_add_fusion.own_ref, bf16[1024,512]{1,0:T(8,128)(2,1)} %get-tuple-element.40.left_ref, bf16[1024,2048]{1,0:T(8,128)(2,1)} %get-tuple-element.41.right_ref), custom_call_target="tpu_custom_call" | custom-call | flops 2147483648 | bytes 5242880 | tf_op jit(solution)/shard_map/grad_product/pallas_call | solution.py:310
  183.5 5.5 %grad_product.5 = bf16[2,4,4,64,128]{4,3,2,1,0:T(8,128)(2,1)} custom-call(s32[3]{0:T(128)} %pad_add_fusion.own_ref, bf16[1024,512]{1,0:T(8,128)(2,1)} %get-tuple-element.38.left_ref, bf16[1024,512]{1,0:T(8,128)(2,1)} %get-tuple-element.39.right_ref), custom_call_target="tpu_custom_call" | custom-call | flops 536870912 | bytes 2097152 | tf_op jit(solution)/shard_map/grad_product/pallas_call | solution.py:310
  190.6 6.9 %grad_product.4 = bf16[2,4,4,64,384]{4,3,2,1,0:T(8,128)(2,1)} custom-call(s32[3]{0:T(128)} %pad_add_fusion.own_ref, bf16[1024,512]{1,0:T(8,128)(2,1)} %copy-done.7, bf16[1024,1536]{1,0:T(8,128)(2,1)} %pad_maximum_fusion.right_ref), custom_call_target="tpu_custom_call" | custom-call | flops 1610612736 | bytes 4194304 | tf_op jit(solution)/shard_map/grad_product/pallas_call | solution.py:310
  203.4 2.4 collective-permute-start.12
  211.9 2.3 collective-permute-start.10
  214.1 3.3 %collective-permute-done.13 = bf16[256,512]{1,0:T(8,128)(2,1)S(1)} collective-permute-done((bf16[256,512]{1,0:T(8,128)(2,1)S(1)}, bf16[256,512]{1,0:T(8,128)(2,1)S(1)}, u32[]{:S(2)}, u32[]{:S(2)}) %collective-permute-start.13) | collective-permute-done | bytes 262176 | tf_op jit(solution)/shard_map/ppermute | solution.py:386
  224.5 2.2 collective-permute-done.11
  228.1 4.8 %collective-permute-done.9 = bf16[256,512]{1,0:T(8,128)(2,1)S(1)} collective-permute-done((bf16[256,512]{1,0:T(8,128)(2,1)S(1)}, bf16[256,512]{1,0:T(8,128)(2,1)S(1)}, u32[]{:S(2)}, u32[]{:S(2)}) %collective-permute-start.9) | collective-permute-done | bytes 262176 | tf_op jit(solution)/shard_map/ppermute | solution.py:386
  235.6 2.5 collective-permute-done.32
  242.1 3.4 %collective-permute-done.23 = bf16[4,64,384]{2,1,0:T(8,128)(2,1)S(1)} collective-permute-done((bf16[4,64,384]{2,1,0:T(8,128)(2,1)S(1)}, bf16[4,64,384]{2,1,0:T(8,128)(2,1)S(1)}, u32[]{:S(2)}, u32[]{:S(2)}) %collective-permute-start.23) | collective-permute-done | bytes 196640 | tf_op jit(solution)/shard_map/ppermute | solution.py:386
  246.1 3.1 %collective-permute-done.24 = bf16[4,64,384]{2,1,0:T(8,128)(2,1)S(1)} collective-permute-done((bf16[4,64,384]{2,1,0:T(8,128)(2,1)S(1)}, bf16[4,64,384]{2,1,0:T(8,128)(2,1)S(1)}, u32[]{:S(2)}, u32[]{:S(2)}) %collective-permute-start.24) | collective-permute-done | bytes 196640 | tf_op jit(solution)/shard_map/ppermute | solution.py:386
  259.4 2.3 collective-permute-done.28
  268.5 3.5 %collective-permute-done.44 = bf16[4,128,256]{2,1,0:T(8,128)(2,1)S(1)} collective-permute-done((bf16[4,128,256]{2,1,0:T(8,128)(2,1)S(1)}, bf16[4,128,256]{2,1,0:T(8,128)(2,1)S(1)}, u32[]{:S(2)}, u32[]{:S(2)}) %collective-permute-start.44) | collective-permute-done | bytes 262176 | tf_op jit(solution)/shard_map/ppermute | solution.py:386
  273.2 3.3 %collective-permute-done.45 = bf16[4,128,256]{2,1,0:T(8,128)(2,1)S(1)} collective-permute-done((bf16[4,128,256]{2,1,0:T(8,128)(2,1)S(1)}, bf16[4,128,256]{2,1,0:T(8,128)(2,1)S(1)}, u32[]{:S(2)}, u32[]{:S(2)}) %collective-permute-start.45) | collective-permute-done | bytes 262176 | tf_op jit(solution)/shard_map/ppermute | solution.py:386
  287.6 3.0 %collective-permute-done.42 = bf16[64,512]{1,0:T(8,128)(2,1)S(1)} collective-permute-done((bf16[64,512]{1,0:T(8,128)(2,1)S(1)}, bf16[64,512]{1,0:T(8,128)(2,1)S(1)}, u32[]{:S(2)}, u32[]{:S(2)}) %collective-permute-start.42) | collective-permute-done | bytes 65568 | tf_op jit(solution)/shard_map/ppermute | solution.py:386
  (168 shorter events, 81.1 us)
Async XLA Ops:
  7.2 37.7 %all-gather.4.cloned.1.call-start = ((), (), s32[]{:S(2)}) async-start(), calls=%async_computation | async-start | bytes 1769472 | tf_op jit(solution)/shard_map/all_gather | solution.py:455
  7.9 65.2 %all-gather.6.cloned.1.call-start = ((), (), s32[]{:S(2)}) async-start(), calls=%async_computation.1 | async-start | bytes 2949120 | tf_op jit(solution)/shard_map/all_gather | solution.py:456
  9.7 93.2 %all-gather.8.cloned.1.call-start = ((), (), s32[]{:S(2)}) async-start(), calls=%async_computation.2 | async-start | bytes 2359296 | tf_op jit(solution)/shard_map/all_gather | solution.py:459
  11.1 17.5 %collective-permute-start.6 = (bf16[256,512]{1,0:T(8,128)(2,1)S(1)}, bf16[256,512]{1,0:T(8,128)(2,1)S(1)}, u32[]{:S(2)}, u32[]{:S(2)}) collective-permute-start(bf16[256,512]{1,0:T(8,128)(2,1)S(1)} %get-tuple-element.75), channel_id=1, source_target_pairs={{0,8},{8,0},{16,24},{24,16},{1,9},{9,1},{17,25},{25,17},{2,10},{10... | collective-permute-start | bytes 786440 | tf_op jit(solution)/shard_map/ppermute | solution.py:386
  14.3 10.0 %collective-permute-start.4 = (f32[256]{0:T(256)S(1)}, f32[256]{0:T(256)S(1)}, u32[]{:S(2)}, u32[]{:S(2)}) collective-permute-start(f32[256]{0:T(256)S(1)} %bitcast.170), channel_id=1, source_target_pairs={{0,16},{8,24},{16,0},{24,8},{1,17},{9,25},{17,1},{25,9},{2,18},{10... | collective-permute-start | bytes 3080 | tf_op jit(solution)/shard_map/ppermute | solution.py:386
  16.3 15.9 %collective-permute-start.7 = (bf16[256,512]{1,0:T(8,128)(2,1)S(1)}, bf16[256,512]{1,0:T(8,128)(2,1)}, u32[]{:S(2)}, u32[]{:S(2)}) collective-permute-start(bf16[256,512]{1,0:T(8,128)(2,1)S(1)} %get-tuple-element.77), channel_id=1, source_target_pairs={{0,16},{8,24},{16,0},{24,8},{1,17},{9,25},{17,1},{25,9},{2,18},{10... | collective-permute-start | bytes 786440 | tf_op jit(solution)/shard_map/ppermute | solution.py:386
  16.3 15.8 %collective-permute-start.8 = (bf16[256,512]{1,0:T(8,128)(2,1)S(1)}, bf16[256,512]{1,0:T(8,128)(2,1)}, u32[]{:S(2)}, u32[]{:S(2)}) collective-permute-start(bf16[256,512]{1,0:T(8,128)(2,1)S(1)} %get-tuple-element.76), channel_id=1, source_target_pairs={{0,24},{8,16},{16,8},{24,0},{1,25},{9,17},{17,9},{25,1},{2,26},{10... | collective-permute-start | bytes 786440 | tf_op jit(solution)/shard_map/ppermute | solution.py:386
  24.3 10.0 %collective-permute-start = (bf16[256,512]{1,0:T(8,128)(2,1)S(1)}, bf16[256,512]{1,0:T(8,128)(2,1)S(1)}, u32[]{:S(2)}, u32[]{:S(2)}) collective-permute-start(bf16[256,512]{1,0:T(8,128)(2,1)S(1)} %get-tuple-element.79), channel_id=1, source_target_pairs={{0,8},{8,0},{16,24},{24,16},{1,9},{9,1},{17,25},{25,17},{2,10},{10... | collective-permute-start | bytes 786440 | tf_op jit(solution)/shard_map/ppermute | solution.py:386
  28.5 11.9 %collective-permute-start.1 = (bf16[256,512]{1,0:T(8,128)(2,1)S(1)}, bf16[256,512]{1,0:T(8,128)(2,1)S(1)}, u32[]{:S(2)}, u32[]{:S(2)}) collective-permute-start(bf16[256,512]{1,0:T(8,128)(2,1)S(1)} %get-tuple-element.81), channel_id=1, source_target_pairs={{0,16},{8,24},{16,0},{24,8},{1,17},{9,25},{17,1},{25,9},{2,18},{10... | collective-permute-start | bytes 786440 | tf_op jit(solution)/shard_map/ppermute | solution.py:386
  28.6 11.8 %collective-permute-start.2 = (bf16[256,512]{1,0:T(8,128)(2,1)S(1)}, bf16[256,512]{1,0:T(8,128)(2,1)S(1)}, u32[]{:S(2)}, u32[]{:S(2)}) collective-permute-start(bf16[256,512]{1,0:T(8,128)(2,1)S(1)} %get-tuple-element.80), channel_id=1, source_target_pairs={{0,24},{8,16},{16,8},{24,0},{1,25},{9,17},{17,9},{25,1},{2,26},{10... | collective-permute-start | bytes 786440 | tf_op jit(solution)/shard_map/ppermute | solution.py:386
  161.2 37.7 %collective-permute-start.15 = (f32[8,512]{1,0:T(8,128)S(1)}, f32[8,512]{1,0:T(8,128)S(1)}, u32[]{:S(2)}, u32[]{:S(2)}) collective-permute-start(f32[8,512]{1,0:T(8,128)S(1)} %maximum_maximum_fusion), channel_id=1, source_target_pairs={{0,8},{8,0},{16,24},{24,16},{1,9},{9,1},{17,25},{25,17},{2,10},{10... | collective-permute-start | bytes 49160 | tf_op jit(solution)/shard_map/ppermute | solution.py:386
  162.7 36.2 %collective-permute-start.16 = (f32[8,512]{1,0:T(8,128)S(1)}, f32[8,512]{1,0:T(8,128)S(1)}, u32[]{:S(2)}, u32[]{:S(2)}) collective-permute-start(f32[8,512]{1,0:T(8,128)S(1)} %maximum_maximum_fusion), channel_id=1, source_target_pairs={{0,16},{8,24},{16,0},{24,8},{1,17},{9,25},{17,1},{25,9},{2,18},{10... | collective-permute-start | bytes 49160 | tf_op jit(solution)/shard_map/ppermute | solution.py:386
  164.1 34.7 %collective-permute-start.17 = (f32[8,512]{1,0:T(8,128)S(1)}, f32[8,512]{1,0:T(8,128)S(1)}, u32[]{:S(2)}, u32[]{:S(2)}) collective-permute-start(f32[8,512]{1,0:T(8,128)S(1)} %maximum_maximum_fusion), channel_id=1, source_target_pairs={{0,24},{8,16},{16,8},{24,0},{1,25},{9,17},{17,9},{25,1},{2,26},{10... | collective-permute-start | bytes 49160 | tf_op jit(solution)/shard_map/ppermute | solution.py:386
  175.1 87.3 %collective-permute-start.43 = (bf16[4,4,128,256]{3,2,1,0:T(8,128)(2,1)S(1)}, bf16[4,4,128,256]{3,2,1,0:T(8,128)(2,1)S(1)}, u32[]{:S(2)}, u32[]{:S(2)}) collective-permute-start(bf16[4,4,128,256]{3,2,1,0:T(8,128)(2,1)S(1)} %slice_bitcast_fusion), channel_id=1, source_target_pairs={{0,1},{1,0},{2,3},{3,2},{4,5},{5,4},{6,7},{7,6},{8,9},{9,8},{10,11... | collective-permute-start | bytes 3145736 | tf_op jit(solution)/shard_map/ppermute | solution.py:386
  190.0 20.2 %collective-permute-start.29 = (bf16[4,4,64,128]{3,2,1,0:T(8,128)(2,1)S(1)}, bf16[4,4,64,128]{3,2,1,0:T(8,128)(2,1)S(1)}, u32[]{:S(2)}, u32[]{:S(2)}) collective-permute-start(bf16[4,4,64,128]{3,2,1,0:T(8,128)(2,1)S(1)} %slice_bitcast_fusion.14), channel_id=1, source_target_pairs={{0,1},{1,0},{2,3},{3,2},{4,5},{5,4},{6,7},{7,6},{8,9},{9,8},{10,11... | collective-permute-start | bytes 786440 | tf_op jit(solution)/shard_map/ppermute | solution.py:386
  205.8 11.6 %collective-permute-start.13 = (bf16[256,512]{1,0:T(8,128)(2,1)S(1)}, bf16[256,512]{1,0:T(8,128)(2,1)S(1)}, u32[]{:S(2)}, u32[]{:S(2)}) collective-permute-start(bf16[256,512]{1,0:T(8,128)(2,1)S(1)} %get-tuple-element.69), channel_id=1, source_target_pairs={{0,16},{8,24},{16,0},{24,8},{1,17},{9,25},{17,1},{25,9},{2,18},{10... | collective-permute-start | bytes 786440 | tf_op jit(solution)/shard_map/ppermute | solution.py:386
  208.2 10.8 %collective-permute-start.14 = (bf16[256,512]{1,0:T(8,128)(2,1)S(1)}, bf16[256,512]{1,0:T(8,128)(2,1)S(1)}, u32[]{:S(2)}, u32[]{:S(2)}) collective-permute-start(bf16[256,512]{1,0:T(8,128)(2,1)S(1)} %get-tuple-element.68), channel_id=1, source_target_pairs={{0,8},{8,0},{16,24},{24,16},{1,9},{9,1},{17,25},{25,17},{2,10},{10... | collective-permute-start | bytes 786440 | tf_op jit(solution)/shard_map/ppermute | solution.py:386
  210.2 28.0 %collective-permute-start.22 = (bf16[4,4,64,384]{3,2,1,0:T(8,128)(2,1)S(1)}, bf16[4,4,64,384]{3,2,1,0:T(8,128)(2,1)S(1)}, u32[]{:S(2)}, u32[]{:S(2)}) collective-permute-start(bf16[4,4,64,384]{3,2,1,0:T(8,128)(2,1)S(1)} %slice_bitcast_fusion.4), channel_id=1, source_target_pairs={{0,1},{1,0},{2,3},{3,2},{4,5},{5,4},{6,7},{7,6},{8,9},{9,8},{10,11... | collective-permute-start | bytes 2359304 | tf_op jit(solution)/shard_map/ppermute | solution.py:386
  211.9 11.1 %collective-permute-start.10 = (bf16[256,512]{1,0:T(8,128)(2,1)S(1)}, bf16[256,512]{1,0:T(8,128)(2,1)S(1)}, u32[]{:S(2)}, u32[]{:S(2)}) collective-permute-start(bf16[256,512]{1,0:T(8,128)(2,1)S(1)} %get-tuple-element.72), channel_id=1, source_target_pairs={{0,16},{8,24},{16,0},{24,8},{1,17},{9,25},{17,1},{25,9},{2,18},{10... | collective-permute-start | bytes 786440 | tf_op jit(solution)/shard_map/ppermute | solution.py:386
  217.5 9.2 %collective-permute-start.11 = (bf16[256,512]{1,0:T(8,128)(2,1)S(1)}, bf16[256,512]{1,0:T(8,128)(2,1)S(1)}, u32[]{:S(2)}, u32[]{:S(2)}) collective-permute-start(bf16[256,512]{1,0:T(8,128)(2,1)S(1)} %get-tuple-element.71), channel_id=1, source_target_pairs={{0,8},{8,0},{16,24},{24,16},{1,9},{9,1},{17,25},{25,17},{2,10},{10... | collective-permute-start | bytes 786440 | tf_op jit(solution)/shard_map/ppermute | solution.py:386
  218.9 14.0 %collective-permute-start.9 = (bf16[256,512]{1,0:T(8,128)(2,1)S(1)}, bf16[256,512]{1,0:T(8,128)(2,1)S(1)}, u32[]{:S(2)}, u32[]{:S(2)}) collective-permute-start(bf16[256,512]{1,0:T(8,128)(2,1)S(1)} %get-tuple-element.73), channel_id=1, source_target_pairs={{0,24},{8,16},{16,8},{24,0},{1,25},{9,17},{17,9},{25,1},{2,26},{10... | collective-permute-start | bytes 786440 | tf_op jit(solution)/shard_map/ppermute | solution.py:386
  223.0 12.6 %collective-permute-start.30 = (bf16[4,64,128]{2,1,0:T(8,128)(2,1)S(1)}, bf16[4,64,128]{2,1,0:T(8,128)(2,1)S(1)}, u32[]{:S(2)}, u32[]{:S(2)}) collective-permute-start(bf16[4,64,128]{2,1,0:T(8,128)(2,1)S(1)} %get-tuple-element.91), channel_id=1, source_target_pairs={{0,8},{8,0},{16,24},{24,16},{1,9},{9,1},{17,25},{25,17},{2,10},{10... | collective-permute-start | bytes 196616 | tf_op jit(solution)/shard_map/ppermute | solution.py:386
  235.6 30.7 %collective-permute-start.36 = (bf16[4,4,64,512]{3,2,1,0:T(8,128)(2,1)S(1)}, bf16[4,4,64,512]{3,2,1,0:T(8,128)(2,1)S(1)}, u32[]{:S(2)}, u32[]{:S(2)}) collective-permute-start(bf16[4,4,64,512]{3,2,1,0:T(8,128)(2,1)S(1)} %slice_bitcast_fusion.2), channel_id=1, source_target_pairs={{0,1},{1,0},{2,3},{3,2},{4,5},{5,4},{6,7},{7,6},{8,9},{9,8},{10,11... | collective-permute-start | bytes 3145736 | tf_op jit(solution)/shard_map/ppermute | solution.py:386
  240.0 9.2 %collective-permute-start.24 = (bf16[4,64,384]{2,1,0:T(8,128)(2,1)S(1)}, bf16[4,64,384]{2,1,0:T(8,128)(2,1)S(1)}, u32[]{:S(2)}, u32[]{:S(2)}) collective-permute-start(bf16[4,64,384]{2,1,0:T(8,128)(2,1)S(1)} %get-tuple-element.84), channel_id=1, source_target_pairs={{0,16},{8,24},{16,0},{24,8},{1,17},{9,25},{17,1},{25,9},{2,18},{10... | collective-permute-start | bytes 589832 | tf_op jit(solution)/shard_map/ppermute | solution.py:386
  240.6 9.7 %collective-permute-start.25 = (bf16[4,64,384]{2,1,0:T(8,128)(2,1)S(1)}, bf16[4,64,384]{2,1,0:T(8,128)(2,1)S(1)}, u32[]{:S(2)}, u32[]{:S(2)}) collective-permute-start(bf16[4,64,384]{2,1,0:T(8,128)(2,1)S(1)} %get-tuple-element.83), channel_id=1, source_target_pairs={{0,24},{8,16},{16,8},{24,0},{1,25},{9,17},{17,9},{25,1},{2,26},{10... | collective-permute-start | bytes 589832 | tf_op jit(solution)/shard_map/ppermute | solution.py:386
  262.7 9.3 %collective-permute-start.44 = (bf16[4,128,256]{2,1,0:T(8,128)(2,1)S(1)}, bf16[4,128,256]{2,1,0:T(8,128)(2,1)S(1)}, u32[]{:S(2)}, u32[]{:S(2)}) collective-permute-start(bf16[4,128,256]{2,1,0:T(8,128)(2,1)S(1)} %get-tuple-element.62), channel_id=1, source_target_pairs={{0,8},{8,0},{16,24},{24,16},{1,9},{9,1},{17,25},{25,17},{2,10},{10... | collective-permute-start | bytes 786440 | tf_op jit(solution)/shard_map/ppermute | solution.py:386
  263.2 13.3 %collective-permute-start.45 = (bf16[4,128,256]{2,1,0:T(8,128)(2,1)S(1)}, bf16[4,128,256]{2,1,0:T(8,128)(2,1)S(1)}, u32[]{:S(2)}, u32[]{:S(2)}) collective-permute-start(bf16[4,128,256]{2,1,0:T(8,128)(2,1)S(1)} %get-tuple-element.64), channel_id=1, source_target_pairs={{0,16},{8,24},{16,0},{24,8},{1,17},{9,25},{17,1},{25,9},{2,18},{10... | collective-permute-start | bytes 786440 | tf_op jit(solution)/shard_map/ppermute | solution.py:386
  264.6 11.9 %collective-permute-start.46 = (bf16[4,128,256]{2,1,0:T(8,128)(2,1)S(1)}, bf16[4,128,256]{2,1,0:T(8,128)(2,1)S(1)}, u32[]{:S(2)}, u32[]{:S(2)}) collective-permute-start(bf16[4,128,256]{2,1,0:T(8,128)(2,1)S(1)} %get-tuple-element.63), channel_id=1, source_target_pairs={{0,24},{8,16},{16,8},{24,0},{1,25},{9,17},{17,9},{25,1},{2,26},{10... | collective-permute-start | bytes 786440 | tf_op jit(solution)/shard_map/ppermute | solution.py:386
  266.7 12.6 %collective-permute-start.37 = (bf16[4,64,512]{2,1,0:T(8,128)(2,1)S(1)}, bf16[4,64,512]{2,1,0:T(8,128)(2,1)S(1)}, u32[]{:S(2)}, u32[]{:S(2)}) collective-permute-start(bf16[4,64,512]{2,1,0:T(8,128)(2,1)S(1)} %get-tuple-element.65), channel_id=1, source_target_pairs={{0,8},{8,0},{16,24},{24,16},{1,9},{9,1},{17,25},{25,17},{2,10},{10... | collective-permute-start | bytes 786440 | tf_op jit(solution)/shard_map/ppermute | solution.py:386
  267.2 14.9 %collective-permute-start.38 = (bf16[4,64,512]{2,1,0:T(8,128)(2,1)S(1)}, bf16[4,64,512]{2,1,0:T(8,128)(2,1)S(1)}, u32[]{:S(2)}, u32[]{:S(2)}) collective-permute-start(bf16[4,64,512]{2,1,0:T(8,128)(2,1)S(1)} %get-tuple-element.67), channel_id=1, source_target_pairs={{0,16},{8,24},{16,0},{24,8},{1,17},{9,25},{17,1},{25,9},{2,18},{10... | collective-permute-start | bytes 786440 | tf_op jit(solution)/shard_map/ppermute | solution.py:386
  272.1 10.1 %collective-permute-start.39 = (bf16[4,64,512]{2,1,0:T(8,128)(2,1)S(1)}, bf16[4,64,512]{2,1,0:T(8,128)(2,1)S(1)}, u32[]{:S(2)}, u32[]{:S(2)}) collective-permute-start(bf16[4,64,512]{2,1,0:T(8,128)(2,1)S(1)} %get-tuple-element.66), channel_id=1, source_target_pairs={{0,24},{8,16},{16,8},{24,0},{1,25},{9,17},{17,9},{25,1},{2,26},{10... | collective-permute-start | bytes 786440 | tf_op jit(solution)/shard_map/ppermute | solution.py:386
  276.7 10.0 %collective-permute-start.48 = (bf16[128,256]{1,0:T(8,128)(2,1)S(1)}, bf16[128,256]{1,0:T(8,128)(2,1)S(1)}, u32[]{:S(2)}, u32[]{:S(2)}) collective-permute-start(bf16[128,256]{1,0:T(8,128)(2,1)S(1)} %get-tuple-element.87), channel_id=1, source_target_pairs={{0,4},{1,5},{2,6},{3,7},{4,0},{5,1},{6,2},{7,3},{8,12},{9,13},{10,... | collective-permute-start | bytes 196616 | tf_op jit(solution)/shard_map/ppermute | solution.py:386
  (34 other events, 265.0 us)
Sparse Core Ops, SparseCore 0:
  9.7 27.7 all-gather.3
  39.7 33.3 all-gather.5
  74.7 28.0 all-gather.7

commit v2 on v1

v2 whole, which is shorter than its diff:
```python
import functools

import jax
import jax.numpy as jnp
from jax import lax
from jax.experimental import pallas as pl
from jax.experimental.pallas import tpu as pltpu
from jax.sharding import PartitionSpec as P

EPSILON = 1e-05
HEADS = 8
F32 = jnp.float32
BF16 = jnp.bfloat16
LIGHT = 2**20


def nn(left, right):
    return jnp.dot(left, right, preferred_element_type=F32)


def nt(left, right):
    return lax.dot_general(left, right, (((1,), (1,)), ((), ())), preferred_element_type=F32)


def params(vmem):
    return pltpu.CompilerParams(vmem_limit_bytes=vmem * 2**20)


def cost(flops, bytes_accessed):
    return pl.CostEstimate(
        flops=int(flops) // LIGHT, bytes_accessed=int(bytes_accessed) // LIGHT, transcendentals=0
    )


def attend_kernel(chunk, q_ref, k_ref, v_ref, out_ref, den_ref):
    count = q_ref.shape[0]
    pair = pl.program_id(0)
    lane = lax.broadcasted_iota(jnp.int32, (1, 128), 1)
    low = lane < 64
    keys = k_ref[...]
    values = v_ref[...]
    one = jnp.ones_like(values)
    values_low = jnp.where(low, values, one)
    values_high = jnp.where(low, one, values)
    for start in range(0, count, chunk):
        at = slice(start, start + chunk)
        q = q_ref[at, :] * jnp.asarray(0.125, BF16)
        zero = jnp.zeros_like(q)
        left = nn(jnp.exp(nt(jnp.where(low, q, zero), keys)).astype(BF16), values_low)
        right = nn(jnp.exp(nt(jnp.where(low, zero, q), keys)).astype(BF16), values_high)
        swapped = jnp.where(low, right, left)
        den = pltpu.roll(swapped, 64, 1)
        out_ref[at, :] = (jnp.where(low, left, right) / den).astype(BF16)
        first = lane // 16 == 2 * pair
        second = lane // 16 == 2 * pair + 1
        mine = jnp.where(
            first, jnp.where(low, den, swapped), jnp.where(low, swapped, den)
        )
        den_ref[at, :] = jnp.where(first | second, mine, den_ref[at, :])


def attend(q_source, kv_source, kv_shift):
    count, span = q_source.shape[0], kv_source.shape[0]
    chunk = min(256, count)
    return pl.pallas_call(
        functools.partial(attend_kernel, chunk),
        grid=(4,),
        in_specs=[
            pl.BlockSpec((count, 128), lambda p: (0, p)),
            pl.BlockSpec((span, 128), lambda p: (0, kv_shift + p)),
            pl.BlockSpec((span, 128), lambda p: (0, kv_shift + 4 + p)),
        ],
        out_specs=[
            pl.BlockSpec((count, 128), lambda p: (0, p)),
            pl.BlockSpec((count, 128), lambda p: (0, 0)),
        ],
        out_shape=[
            jax.ShapeDtypeStruct((count, 512), BF16),
            jax.ShapeDtypeStruct((count, 128), F32),
        ],
        compiler_params=params(20),
        cost_estimate=cost(16 * count * span * 1024, 5 * 2**20),
        name="attend",
    )(q_source, kv_source, kv_source)


def head_pair_back(chunk, q_ref, k_ref, v_ref, s_ref, x_ref, dk_ref, dv_ref):
    count, span = q_ref.shape[0], k_ref.shape[0]
    lane = lax.broadcasted_iota(jnp.int32, (1, 128), 1)
    low = lane < 64
    q = q_ref[...] * jnp.asarray(0.125, BF16)
    scaled = s_ref[...]
    extra = x_ref[...]
    zero = jnp.zeros_like(q)
    q_own = (jnp.where(low, q, zero), jnp.where(low, zero, q))
    s_own = (jnp.where(low, scaled, zero), jnp.where(low, zero, scaled))
    s_with = (jnp.where(low, scaled, extra), jnp.where(low, extra, scaled))
    minus = (
        jnp.where((lane == 64) | (lane == 65), -1.0, 0.0).astype(BF16),
        jnp.where((lane == 0) | (lane == 1), -1.0, 0.0).astype(BF16),
    )
    total = jnp.zeros((128, count), F32)
    for start in range(0, span, chunk):
        keys = k_ref[start : start + chunk, :]
        values = v_ref[start : start + chunk, :]
        none = jnp.zeros_like(keys)
        k_own = (jnp.where(low, keys, none), jnp.where(low, none, keys))
        v_with = (jnp.where(low, values, minus[0]), jnp.where(low, minus[1], values))
        dk = dv = 0.0
        for head in range(2):
            weights = jnp.exp(nt(keys, q_own[head]))
            slopes = (weights * nt(v_with[head], s_with[head])).astype(BF16)
            dv = dv + nn(weights.astype(BF16), s_own[head])
            dk = dk + nn(slopes, q_own[head])
            total = total + nn(k_own[head].T, slopes)
        dk_ref[start : start + chunk, :] = dk.astype(BF16)
        dv_ref[start : start + chunk, :] = dv.astype(BF16)
    return (total.T * 0.125).astype(BF16)


def attend_back_kernel(chunk, q_ref, k_ref, v_ref, s_ref, x_ref, dq_ref, dk_ref, dv_ref):
    dq_ref[...] = head_pair_back(chunk, q_ref, k_ref, v_ref, s_ref, x_ref, dk_ref, dv_ref)


def attend_back_half(projected, scaled, extra):
    count, width = scaled.shape

    def at(shift):
        return pl.BlockSpec((count, 128), lambda p: (0, shift + p))

    return pl.pallas_call(
        functools.partial(attend_back_kernel, min(512, count)),
        grid=(2,),
        in_specs=[at(0), at(4), at(8), at(0), at(0)],
        out_specs=[at(0)] * 3,
        out_shape=[jax.ShapeDtypeStruct((count, width // 2), BF16)] * 3,
        compiler_params=params(20),
        cost_estimate=cost(16 * count * count * 1024, 6 * 2**20),
        name="attend_back_half",
    )(projected, projected, projected, scaled, extra)


def attend_back_sum_kernel(
    chunk,
    dp_count,
    own_ref,
    q_ref,
    k_ref,
    v_ref,
    s_ref,
    x_ref,
    normed_ref,
    dq_first,
    dk_first,
    dv_first,
    dq_ref,
    dk_ref,
    dv_ref,
    mine_out,
    other_out,
    normed_t,
    joined,
    grad_ref,
    sem,
):
    step = pl.program_id(0)
    grad_outs = (mine_out, other_out)

    @pl.when(step == 0)
    def _():
        normed_t[...] = normed_ref[...].T

    def weight_part(pair):
        result = nn(normed_t[...], joined[...]).astype(BF16)
        rows = result.shape[0] // dp_count
        per = grad_ref.shape[3]
        for kind in range(3):
            block = pair + 4 * kind
            col, part = (block // per) ^ own_ref[0], block % per
            for d in range(dp_count):
                grad_ref[(d % 2) ^ own_ref[2], col, (d // 2) ^ own_ref[1], part] = result[
                    d * rows : (d + 1) * rows, kind * 128 : (kind + 1) * 128
                ]

    for kind, ref in enumerate((dq_first, dk_first, dv_first)):
        joined[:, kind * 128 : (kind + 1) * 128] = ref[...]
    weight_part(step)
    dq = head_pair_back(chunk, q_ref, k_ref, v_ref, s_ref, x_ref, dk_ref, dv_ref)
    dq_ref[...] = dq
    joined[:, :128] = dq
    joined[:, 128:256] = dk_ref[...]
    joined[:, 256:] = dv_ref[...]
    weight_part(step + 2)

    @pl.when(step == 1)
    def _():
        hand_out(grad_ref, grad_outs, sem)


def attend_back_sum(own, projected, scaled, extra, normed, first_half, seq_count, dp_count):
    count, width = scaled.shape
    pieces = (2, seq_count, dp_count // 2, 12 // seq_count, width // dp_count, 128)

    def at(shift):
        return pl.BlockSpec((count, 128), lambda p, own: (0, shift + p))

    return pl.pallas_call(
        functools.partial(attend_back_sum_kernel, min(512, count), dp_count),
        grid_spec=pltpu.PrefetchScalarGridSpec(
            num_scalar_prefetch=1,
            grid=(2,),
            in_specs=[
                at(2),
                at(6),
                at(10),
                at(2),
                at(2),
                pl.BlockSpec((count, width), lambda p, own: (0, 0)),
                at(0),
                at(0),
                at(0),
            ],
            out_specs=[at(0)] * 3 + [pl.BlockSpec(memory_space=pl.ANY)] * 2,
            scratch_shapes=[
                pltpu.VMEM((width, count), BF16),
                pltpu.VMEM((count, 384), BF16),
                pltpu.VMEM(pieces, BF16),
                pltpu.SemaphoreType.DMA((2,)),
            ],
        ),
        out_shape=[jax.ShapeDtypeStruct((count, width // 2), BF16)] * 3
        + outs_of(pieces, True),
        compiler_params=params(24),
        cost_estimate=cost(20 * count * count * 1024, 10 * 2**20),
        name="attend_back_sum",
    )(own, projected, projected, projected, scaled, extra, normed, *first_half)


def attend_back(q_source, kv_source, scaled, extra):
    count, span = q_source.shape[0], kv_source.shape[0]
    chunk = min(512, span)
    own = pl.BlockSpec((count, 128), lambda p: (0, p))
    far = pl.BlockSpec((span, 128), lambda p: (0, p))
    return pl.pallas_call(
        functools.partial(attend_back_kernel, chunk),
        grid=(4,),
        in_specs=[
            own,
            pl.BlockSpec((span, 128), lambda p: (0, p)),
            pl.BlockSpec((span, 128), lambda p: (0, 4 + p)),
            own,
            own,
        ],
        out_specs=[own, far, far],
        out_shape=[
            jax.ShapeDtypeStruct((count, 512), BF16),
            jax.ShapeDtypeStruct((span, 512), BF16),
            jax.ShapeDtypeStruct((span, 512), BF16),
        ],
        compiler_params=params(40),
        cost_estimate=cost(32 * count * span * 1024, 8 * 2**20),
        name="attend_back",
    )(q_source, kv_source, kv_source, scaled, extra)


def norm_parts(tensor):
    center = tensor - jnp.mean(tensor, axis=-1, keepdims=True)
    scale = lax.rsqrt(jnp.mean(center * center, axis=-1, keepdims=True) + EPSILON)
    return center * scale, scale


def norm_back(q, normed, scale):
    return scale * (
        q - jnp.mean(q, axis=-1, keepdims=True) - normed * jnp.mean(q * normed, axis=-1, keepdims=True)
    )


def place_blocks(own_ref, sources, target, sems):
    copies = []
    for core in range(2):
        source = sources[core]
        by_seq = len(source.shape) == 4
        seq_count = source.shape[0] if by_seq else 1
        z_count, rows, cols = source.shape[-3:]
        by_rows = by_seq and cols == target.shape[1]
        for j in range(seq_count):
            for i in range(z_count):
                block = 2 * (own_ref[1] ^ i) + (own_ref[2] ^ core)
                across = slice(None)
                if by_rows:
                    block = block * seq_count + (own_ref[0] ^ j)
                elif by_seq:
                    across = pl.ds(pl.multiple_of((own_ref[0] ^ j) * cols, cols), cols)
                down = pl.ds(pl.multiple_of(block * rows, rows), rows)
                piece = source.at[j, i] if by_seq else source.at[i]
                copy = pltpu.make_async_copy(piece, target.at[down, across], sems.at[len(copies)])
                copies.append(copy)
    return copies


def fetches(own_ref, refs, target, sems):
    if len(refs) == 2:
        return place_blocks(own_ref, refs, target, sems)
    return [pltpu.make_async_copy(refs[0], target, sems.at[0])]


def launch(copies):
    for copy in copies:
        copy.start()


def finish(copies):
    for copy in copies:
        copy.wait()


def hand_out(held, outs, sems):
    sources = [held] if len(outs) == 1 else [held.at[0], held.at[1]]
    copies = [
        pltpu.make_async_copy(source, out, sems.at[i])
        for i, (source, out) in enumerate(zip(sources, outs))
    ]
    launch(copies)
    finish(copies)


def outs_of(shape, split):
    if split:
        return [jax.ShapeDtypeStruct(shape[1:], BF16)] * 2
    return [jax.ShapeDtypeStruct(shape, BF16)]


def copies_of(parts):
    count = 1
    for size in parts[0].shape[:-2]:
        count *= size
    return max(1, count * len(parts))


def project_kernel(parts, own_ref, hidden_ref, gain_ref, *refs):
    sources, (normed_ref, out_ref, whole_ref, sems) = refs[:parts], refs[parts:]

    @pl.when(pl.program_id(0) == 0)
    def _():
        launch(fetches(own_ref, sources, whole_ref, sems))

    normed = (norm_parts(hidden_ref[...])[0] * gain_ref[...]).astype(BF16)
    normed_ref[...] = normed

    @pl.when(pl.program_id(0) == 0)
    def _():
        finish(fetches(own_ref, sources, whole_ref, sems))

    out_ref[...] = nn(normed, whole_ref[...]).astype(BF16)


def project(own, hidden, gain, parts, cols):
    count, width = hidden.shape
    chunk = min(512, count)

    def rows(cols):
        return pl.BlockSpec((chunk, cols), lambda i, own: (i, 0))

    return pl.pallas_call(
        functools.partial(project_kernel, len(parts)),
        grid_spec=pltpu.PrefetchScalarGridSpec(
            num_scalar_prefetch=1,
            grid=(count // chunk,),
            in_specs=[rows(width), pl.BlockSpec((1, width), lambda i, own: (0, 0))]
            + [pl.BlockSpec(memory_space=pl.ANY)] * len(parts),
            out_specs=[
                rows(width),
                rows(cols),
                pl.BlockSpec((width, cols), lambda i, own: (0, 0)),
            ],
            scratch_shapes=[pltpu.SemaphoreType.DMA((copies_of(parts),))],
        ),
        out_shape=[
            jax.ShapeDtypeStruct((count, width), BF16),
            jax.ShapeDtypeStruct((count, cols), BF16),
            jax.ShapeDtypeStruct((width, cols), BF16),
        ],
        compiler_params=params(16),
        cost_estimate=cost(2 * count * width * cols, 8 * 2**20),
        name="project",
    )(own, hidden, gain, *parts)


def rise_kernel(cfg, own_ref, hidden_ref, att_ref, cot_ref, gain_ref, *refs):
    seq_count, dp_count, split, up_parts, down_parts = cfg
    up_sources, refs = refs[:up_parts], refs[up_parts:]
    down_sources, refs = refs[:down_parts], refs[down_parts:]
    outs = 2 if split else 1
    out_ref, normed_ref, scale_ref, slope_ref, w_up, w_down, *refs = refs
    grad_outs, refs = refs[:outs], refs[outs:]
    (
        act_ref,
        cot_t,
        grad_ref,
        up_sems,
        down_sems,
        out_sem,
    ) = refs
    step = pl.program_id(0)
    chunk, width = hidden_ref.shape
    count, raised = act_ref.shape
    steps = count // chunk

    def tokens():
        at = pl.ds(pl.multiple_of(step * chunk, chunk), chunk)
        first = hidden_ref[...] + nn(att_ref[...], w_up[:, :width])
        normed, scale = norm_parts(first)
        normed_ref[...] = normed
        scale_ref[...] = jnp.broadcast_to(scale, scale_ref.shape)
        normed_two = (normed * gain_ref[...]).astype(BF16)
        cot_t[:, at] = cot_ref[...].T
        total = first
        for start in range(0, raised, 512):
            stop = start + 512
            v = nn(normed_two, w_up[:, width + start : width + stop])
            square = v * v
            t = jnp.tanh(v * (0.7978845608028654 + 0.035677408136300125 * square))
            half = 0.5 + 0.5 * t
            act = (v * half).astype(BF16)
            slope = half + v * (0.5 - 0.5 * t * t) * (
                0.7978845608028654 + 0.10703222440890037 * square
            )
            act_ref[at, start:stop] = act
            slope_ref[:, start:stop] = slope.astype(BF16)
            total = total + nn(act, w_down[start:stop, :])
        out_ref[...] = total.astype(BF16)

    @pl.when(step == 0)
    def _():
        copies = fetches(own_ref, up_sources, w_up, up_sems)
        copies += fetches(own_ref, down_sources, w_down, down_sems)
        launch(copies)
        finish(copies)

    pl.when(step < steps)(tokens)

    @pl.when(step == steps)
    def _():
        if split:
            cols = width // seq_count
            rows = raised // dp_count
            for d in range(dp_count):
                result = nn(cot_t[...], act_ref[:, d * rows : (d + 1) * rows]).astype(BF16)
                for s in range(seq_count):
                    piece = result[s * cols : (s + 1) * cols, :]
                    for part in range(rows // 128):
                        grad_ref[
                            (d % 2) ^ own_ref[2], (d // 2) ^ own_ref[1], s ^ own_ref[0], part
                        ] = piece[:, part * 128 : (part + 1) * 128]
        else:
            for start in range(0, raised, 512):
                grad_ref[:, start : start + 512] = nn(
                    cot_t[...], act_ref[:, start : start + 512]
                ).astype(BF16)
        hand_out(grad_ref, grad_outs, out_sem)


def rise(own, hidden, att, cot, gain, up_parts, down_parts, raised, seq_count, dp_count, split):
    count, width = hidden.shape
    chunk = min(256, count)
    steps = count // chunk

    def rows(cols):
        return pl.BlockSpec((chunk, cols), lambda i, own: (jnp.minimum(i, steps - 1), 0))

    def whole(shape):
        return pl.BlockSpec(shape, lambda i, own: (0, 0), pipeline_mode=pl.Buffered(1))

    anywhere = pl.BlockSpec(memory_space=pl.ANY)
    if split:
        parts = raised // dp_count // 128
        grad_shape = (2, dp_count // 2, seq_count, parts, width // seq_count, 128)
    else:
        grad_shape = (width, raised)
    cfg = (seq_count, dp_count, split, len(up_parts), len(down_parts))
    grads = outs_of(grad_shape, split)
    up_shape, down_shape = (width, width + raised), (raised, width)
    return pl.pallas_call(
        functools.partial(rise_kernel, cfg),
        grid_spec=pltpu.PrefetchScalarGridSpec(
            num_scalar_prefetch=1,
            grid=(steps + 1,),
            in_specs=[rows(width), rows(width), rows(width), whole((1, width))]
            + [anywhere] * (len(up_parts) + len(down_parts)),
            out_specs=[
                rows(width),
                rows(width),
                rows(128),
                rows(raised),
                whole(up_shape),
                whole(down_shape),
            ]
            + [anywhere] * len(grads),
            scratch_shapes=[
                pltpu.VMEM((count, raised), BF16),
                pltpu.VMEM((width, count), BF16),
                pltpu.VMEM(grad_shape, BF16),
                pltpu.SemaphoreType.DMA((copies_of(up_parts),)),
                pltpu.SemaphoreType.DMA((copies_of(down_parts),)),
                pltpu.SemaphoreType.DMA((2,)),
            ],
        ),
        out_shape=[
            jax.ShapeDtypeStruct((count, width), BF16),
            jax.ShapeDtypeStruct((count, width), F32),
            jax.ShapeDtypeStruct((count, 128), F32),
            jax.ShapeDtypeStruct((count, raised), BF16),
            jax.ShapeDtypeStruct(up_shape, BF16),
            jax.ShapeDtypeStruct(down_shape, BF16),
        ]
        + grads,
        compiler_params=params(32),
        cost_estimate=cost(7 * 2**30, 24 * 2**20),
        name="rise",
    )(own, hidden, att, cot, gain, *up_parts, *down_parts)


def fall_kernel(
    cfg,
    own_ref,
    cot_ref,
    slope_ref,
    normed_ref,
    scale_ref,
    att_ref,
    den_ref,
    gain_ref,
    w_up,
    w_down,
    first_ref,
    scaled_ref,
    extra_ref,
    gain_sum_ref,
    *refs,
):
    seq_count, dp_count, split = cfg
    outs = 2 if split else 1
    grad_outs, (raise_ref, normed_t, att_t, branch_ref, grad_ref, out_sem) = refs[:outs], refs[outs:]
    step = pl.program_id(0)
    chunk, width = cot_ref.shape
    count, raised = raise_ref.shape
    steps = count // chunk

    def tokens():
        at = pl.ds(pl.multiple_of(step * chunk, chunk), chunk)
        att = att_ref[...]
        cot = cot_ref[...]
        normed = normed_ref[...]
        gain = gain_ref[...]
        normed_t[:, at] = (normed * gain).astype(BF16).T
        att_t[:, at] = att.T
        back = jnp.zeros((chunk, width), F32)
        for start in range(0, raised, 512):
            stop = start + 512
            grad_raised = (nt(cot, w_down[start:stop, :]) * slope_ref[:, start:stop]).astype(BF16)
            raise_ref[at, start:stop] = grad_raised
            back = back + nt(grad_raised, w_up[:, width + start : width + stop])
        gain_sum_ref[...] += jnp.sum(back * normed, axis=0, keepdims=True)
        grad_first = cot.astype(F32) + norm_back(back * gain, normed, scale_ref[:, :1])
        first_ref[...] = grad_first
        branch = grad_first.astype(BF16)
        branch_ref[at, :] = branch
        inverse = 1.0 / den_ref[...]
        row = lax.broadcasted_iota(jnp.int32, (128, width), 0)
        col = lax.broadcasted_iota(jnp.int32, (128, width), 1)
        spread = jnp.where(row == 16 * (col // 64), 1.0, 0.0).astype(BF16)
        coarse = inverse.astype(BF16)
        fine = (inverse - coarse.astype(F32)).astype(BF16)
        ratio = nt(branch, w_up[:, :width]) * (nn(coarse, spread) + nn(fine, spread))
        scaled_ref[...] = ratio.astype(BF16)
        row = lax.broadcasted_iota(jnp.int32, (128, 128), 0)
        col = lax.broadcasted_iota(jnp.int32, (128, 128), 1)
        swap = jnp.where((row < 64) != (col < 64), 1.0, 0.0).astype(BF16)
        even = lax.broadcasted_iota(jnp.int32, (1, 128), 1) % 2 == 0
        product = ratio * att
        coarse = product.astype(BF16)
        fine = (product - coarse.astype(F32)).astype(BF16)
        for start in range(0, width, 128):
            stop = start + 128
            offset = nn(coarse[:, start:stop], swap) + nn(fine[:, start:stop], swap)
            upper = offset.astype(BF16)
            lower = (offset - upper.astype(F32)).astype(BF16)
            extra_ref[:, start:stop] = jnp.where(even, upper, lower)

    @pl.when(step == 0)
    def _():
        gain_sum_ref[...] = jnp.zeros_like(gain_sum_ref)

    pl.when(step < steps)(tokens)

    @pl.when(step == steps)
    def _():
        if split:
            cols = raised // seq_count
            wide = width // seq_count
            rows = width // dp_count
            for s in range(seq_count):
                result = nn(normed_t[...], raise_ref[:, s * cols : (s + 1) * cols]).astype(BF16)
                for d in range(dp_count):
                    grad_ref[
                        (d % 2) ^ own_ref[2], s ^ own_ref[0], (d // 2) ^ own_ref[1], :, wide:
                    ] = result[d * rows : (d + 1) * rows, :]
            result = nn(att_t[...], branch_ref[...]).astype(BF16)
            for s in range(seq_count):
                for d in range(dp_count):
                    grad_ref[
                        (d % 2) ^ own_ref[2], s ^ own_ref[0], (d // 2) ^ own_ref[1], :, :wide
                    ] = result[d * rows : (d + 1) * rows, s * wide : (s + 1) * wide]
        else:
            grad_ref[:, :width] = nn(att_t[...], branch_ref[...]).astype(BF16)
            for start in range(0, raised, 512):
                grad_ref[:, width + start : width + start + 512] = nn(
                    normed_t[...], raise_ref[:, start : start + 512]
                ).astype(BF16)
        hand_out(grad_ref, grad_outs, out_sem)


def fall(own, cot, slope, normed, scale, att, den, gain, w_up, w_down, seq_count, dp_count, split):
    count, width = cot.shape
    raised = w_down.shape[0]
    chunk = min(256, count)
    steps = count // chunk

    def rows(cols):
        return pl.BlockSpec((chunk, cols), lambda i, own: (jnp.minimum(i, steps - 1), 0))

    def whole(shape):
        return pl.BlockSpec(shape, lambda i, own: (0, 0), pipeline_mode=pl.Buffered(1))

    if split:
        grad_shape = (2, seq_count, dp_count // 2, width // dp_count, (width + raised) // seq_count)
    else:
        grad_shape = (width, width + raised)
    block = rows(width)
    grads = outs_of(grad_shape, split)

    def sds(dtype):
        return jax.ShapeDtypeStruct((count, width), dtype)

    return pl.pallas_call(
        functools.partial(fall_kernel, (seq_count, dp_count, split)),
        grid_spec=pltpu.PrefetchScalarGridSpec(
            num_scalar_prefetch=1,
            grid=(steps + 1,),
            in_specs=[
                block,
                rows(raised),
                block,
                rows(128),
                block,
                rows(128),
                whole((1, width)),
                whole(w_up.shape),
                whole(w_down.shape),
            ],
            out_specs=[
                block,
                block,
                block,
                whole((1, width)),
            ]
            + [pl.BlockSpec(memory_space=pl.ANY)] * len(grads),
            scratch_shapes=[
                pltpu.VMEM((count, raised), BF16),
                pltpu.VMEM((width, count), BF16),
                pltpu.VMEM((width, count), BF16),
                pltpu.VMEM((count, width), BF16),
                pltpu.VMEM(grad_shape, BF16),
                pltpu.SemaphoreType.DMA((2,)),
            ],
        ),
        out_shape=[
            sds(F32),
            sds(BF16),
            sds(BF16),
            jax.ShapeDtypeStruct((1, width), F32),
        ]
        + grads,
        compiler_params=params(32),
        cost_estimate=cost(8 * 2**30, 24 * 2**20),
        name="fall",
    )(own, cot, slope, normed, scale, att, den, gain, w_up, w_down)


def last_kernel(parts, hidden_ref, first_ref, gain_ref, mask_ref, w_ref, *refs):
    grads, (out_ref, sums_ref) = refs[:parts], refs[parts:]
    back = 0.0
    start = 0
    for ref in grads:
        stop = start + ref.shape[1]
        back = back + nt(ref[...], w_ref[:, start:stop])
        start = stop
    normed, scale = norm_parts(hidden_ref[...])
    grad = first_ref[...] + norm_back(back * gain_ref[...], normed, scale)
    out_ref[...] = grad.astype(BF16)

    @pl.when(pl.program_id(0) == 0)
    def _():
        sums_ref[...] = jnp.zeros_like(sums_ref)

    mask = mask_ref[...].astype(BF16)
    coarse = grad.astype(BF16)
    fine = (grad - coarse.astype(F32)).astype(BF16)
    masked = nn(mask, coarse) + nn(mask, fine)
    sums_ref[0:1, :] += masked[0:1, :]
    sums_ref[1:2, :] += jnp.sum(back * normed, axis=0, keepdims=True)


def last(hidden, grad_first, gain, mask, w_qkv, grads):
    count, width = hidden.shape
    chunk = min(256, count)
    blk = pl.BlockSpec((chunk, width), lambda i: (i, 0))

    def whole(shape):
        return pl.BlockSpec(shape, lambda i: (0, 0), pipeline_mode=pl.Buffered(1))

    return pl.pallas_call(
        functools.partial(last_kernel, len(grads)),
        grid=(count // chunk,),
        in_specs=[
            blk,
            blk,
            whole((1, width)),
            pl.BlockSpec((8, chunk), lambda i: (0, i)),
            whole(w_qkv.shape),
        ]
        + [pl.BlockSpec((chunk, g.shape[1]), lambda i: (i, 0)) for g in grads],
        out_specs=[blk, whole((8, width))],
        out_shape=[
            jax.ShapeDtypeStruct((count, width), BF16),
            jax.ShapeDtypeStruct((8, width), F32),
        ],
        compiler_params=params(16),
        cost_estimate=cost(6 * count * width * width, 12 * 2**20),
        name="last",
    )(hidden, grad_first, gain, mask, w_qkv, *grads)


def swap_along(value, axis, mask):
    count = lax.axis_size(axis)
    return lax.ppermute(value, axis, [(i, i ^ mask) for i in range(count)])


def add_up(values):
    total = values[0].astype(F32)
    for value in values[1:]:
        total = total + value.astype(F32)
    return total


def together(*values):
    return lax.optimization_barrier(values)


def from_plane(values):
    return [values[0]] + [swap_along(values[j], "seq", j) for j in range(1, len(values))]


def from_line(values):
    return [values[0]] + [swap_along(values[j], "dp", 2 * j) for j in range(1, len(values))]


def other_core(value):
    return swap_along(value, "dp", 1)


def add_split(left, right):
    return [add_up((left[j], right[j])).astype(BF16) for j in range(left.shape[0])]


def split_first(value):
    return [value[j] for j in range(value.shape[0])]


def halve_line(value):
    half = value.shape[0] // 2
    while half:
        came = swap_along(value[half:], "dp", 2 * half)
        value = add_up((value[:half], came))
        half //= 2
        if half:
            value = value.astype(BF16)
    return value[0]


def gather_line(value):
    return jnp.stack(from_line([value] * (lax.axis_size("dp") // 2)))


def gather_plane(value):
    return jnp.stack(from_plane([value] * lax.axis_size("seq")))


def own_columns(weight):
    cols = weight.shape[1] // lax.axis_size("seq")
    return lax.dynamic_slice_in_dim(weight, lax.axis_index("seq") * cols, cols, 1)


def pieces_of(whole, own, seq_count, dp_count, flipped):
    row_blocks, col_blocks = (seq_count, dp_count) if flipped else (dp_count, seq_count)
    rows, cols = whole.shape[0] // row_blocks, whole.shape[1] // col_blocks
    whole = whole.reshape(row_blocks, rows, col_blocks, cols)
    whole = jnp.transpose(whole, (0, 2, 1, 3) if flipped else (2, 0, 1, 3))
    whole = whole.reshape(seq_count, dp_count // 2, 2, rows, cols)
    whole = jnp.take(whole, jnp.arange(seq_count) ^ own[0], axis=0)
    whole = jnp.take(whole, jnp.arange(dp_count // 2) ^ own[1], axis=1)
    whole = jnp.take(whole, jnp.arange(2) ^ own[2], axis=2)
    return jnp.transpose(whole, (2, 0, 1, 3, 4))


def per_device(
    inputs,
    cotangent,
    timestep,
    unmask_order,
    mask_embed,
    ln1_gain,
    weight_qkv,
    weight_out,
    ln2_gain,
    weight_up,
    weight_down,
):
    rows, segment, width = inputs.shape
    raised = weight_up.shape[1]
    seq_count, dp_count = lax.axis_size("seq"), lax.axis_size("dp")
    outer = seq_count // rows
    split = outer == 1 and (width // seq_count) % 128 == 0 and (width // dp_count) % 16 == 0
    place = lax.axis_index("seq")
    dp_place = lax.axis_index("dp")
    row = place % rows
    own = jnp.stack([place, dp_place // 2, dp_place % 2]).astype(jnp.int32)

    def by_partner(value):
        return [lax.dynamic_index_in_dim(value, row ^ j, 0, keepdims=False) for j in range(rows)]

    def to_rows(value):
        return jnp.concatenate(from_plane(by_partner(value)))

    def to_partners(value):
        return from_plane([value[j * segment : (j + 1) * segment] for j in range(rows)])

    def by_row(parts):
        bit = 1
        while bit < rows:
            odd = (row & bit) != 0
            parts = [jnp.where(odd, parts[j ^ bit], parts[j]) for j in range(rows)]
            bit *= 2
        return jnp.stack(parts)

    masked = (unmask_order <= timestep[:, None]).astype(BF16)
    masked = jnp.pad(masked[:, None, :], ((0, 0), (0, 15), (0, width - segment)))
    came = from_plane(by_partner(jnp.concatenate((inputs, masked), axis=1)))
    block = jnp.concatenate([part[:segment] for part in came]).astype(F32)
    mask_row = jnp.concatenate([part[segment, :segment] for part in came])
    up_and_out = jnp.concatenate((weight_out, weight_up), axis=1)
    if split:
        down_rows = weight_down.shape[0] // seq_count
        own_down = lax.dynamic_slice_in_dim(weight_down, place * down_rows, down_rows, 0)
        own_parts = jnp.concatenate((own_columns(weight_qkv), own_down), axis=1)
        line = gather_line(own_parts)
        line, up_and_out = together(line, up_and_out)
        line_up = from_line([up_and_out] * (dp_count // 2))
        plane_qkv = gather_plane(line[..., : -width])
        line_down = line[..., -width:].reshape(-1, width)
        plane_qkv, line_down, cot = together(plane_qkv, line_down, cotangent)
        parts_qkv = [plane_qkv, other_core(plane_qkv)]
        cot = by_partner(cot)
        cot = from_plane([jnp.concatenate((part, line_down)) for part in cot])
    else:
        cot = from_plane(by_partner(cotangent))
        parts_qkv, parts_up, parts_down = (
            [lax.all_gather(weight, "dp", axis=0, tiled=True)]
            for weight in (weight_qkv, up_and_out, weight_down)
        )

    hidden = block + mask_row.astype(F32)[:, None] * mask_embed
    normed_one, projected, whole_qkv = project(
        own, hidden, ln1_gain[None, :], parts_qkv, 3 * width
    )
    if outer > 1:
        groups = [[j * rows + i for j in range(outer)] for i in range(rows)]
        far = lax.all_gather(
            projected[:, width:], "seq", axis=0, tiled=True, axis_index_groups=groups
        )
        shift = 0
    else:
        far, shift = projected, 4
    attended, denominators = attend(projected, far, shift)
    if split:
        cot, line_up, attended = together(cot, line_up, attended)
        plane_down = jnp.stack([part[segment:] for part in cot])
        plane_down = plane_down.reshape(seq_count, dp_count // 2, -1, width)
        line_up = jnp.stack(line_up)
        parts_up = [line_up, other_core(line_up)]
        parts_down = [plane_down, other_core(plane_down)]
    cot = jnp.concatenate([part[:segment] for part in cot])
    outputs, normed, scale, slope, whole_up, whole_down, *grad_down = rise(
        own,
        hidden,
        attended,
        cot,
        ln2_gain[None, :],
        parts_up,
        parts_down,
        raised,
        seq_count,
        dp_count,
        split,
    )
    result = to_partners(outputs)
    grad_first, scaled, extra, sum_gain_two, *grad_up = fall(
        own,
        cot,
        slope,
        normed,
        scale,
        attended,
        denominators,
        ln2_gain[None, :],
        whole_up,
        whole_down,
        seq_count,
        dp_count,
        split,
    )
    mask_rows = jnp.broadcast_to(mask_row[None, :], (8, mask_row.shape[0]))
    if split:
        grad_down[1] = other_core(grad_down[1])
        grad_down, scaled, grad_up, result = together(grad_down, scaled, grad_up, result)
        line_down = from_line(add_split(*grad_down))
        grad_up[1] = other_core(grad_up[1])
        half = attend_back_half(projected, scaled, extra)
        grad_up, half, line_down[1] = together(grad_up, half, line_down[1])
        plane_up = from_plane(add_split(*grad_up))
        *rest, mine_qkv, other_qkv = attend_back_sum(
            own, projected, scaled, extra, normed_one, half, seq_count, dp_count
        )
        plane_up, line_down, rest, mine_qkv, other_qkv = together(
            plane_up, line_down, rest, mine_qkv, other_qkv
        )
        grads = [part for pair in zip(half, rest) for part in pair]
        both_qkv = (mine_qkv, other_core(other_qkv))
        line_up = add_up(plane_up).astype(BF16)
        z_half = line_up.shape[0] // 2
        line_came = swap_along(line_up[z_half:], "dp", 2 * z_half)
        both_qkv, mask_rows = together(both_qkv, mask_rows)
        tall = width // dp_count
        down = add_up(line_down).astype(BF16).reshape(seq_count, -1, tall, 128)
        mine_qkv = [part.reshape(-1, tall, 128) for part in add_split(*both_qkv)]
        plane_last = from_plane([jnp.concatenate((mine_qkv[j], down[j])) for j in range(seq_count)])
    else:
        dq, dk, dv = attend_back(projected, far, scaled, extra)
        both = jnp.concatenate((dk, dv), axis=1)
        both = lax.psum_scatter(
            both, "seq", scatter_dimension=0, tiled=True, axis_index_groups=groups
        )
        grads = [dq, both]
        grad_qkv = lax.dot_general(
            normed_one,
            jnp.concatenate(grads, axis=1),
            (((0,), (0,)), ((), ())),
            preferred_element_type=F32,
        ).astype(BF16)
        cut = functools.partial(pieces_of, own=own, seq_count=seq_count, dp_count=dp_count)
        (grad_up,), (grad_down,) = grad_up, grad_down
        grad_out, grad_up = (
            cut(part, flipped=False) for part in (grad_up[:, :width], grad_up[:, width:])
        )
        grad_up = jnp.concatenate((grad_out, grad_up), axis=-1)
        grad_qkv = cut(grad_qkv, flipped=False)
        grad_down = cut(grad_down, flipped=True)
        sums = []
        for pieces in (grad_qkv, grad_up, grad_down):
            mine = add_up((pieces[0], other_core(pieces[1]))).astype(BF16)
            plane = add_up(from_plane(split_first(mine))).astype(BF16)
            sums.append(add_up(from_line(split_first(plane))))
        sum_qkv, sum_up, sum_down = sums
        sum_down = sum_down.T
    grad_hidden, sums = last(
        hidden, grad_first, ln1_gain[None, :], mask_rows, whole_qkv, grads
    )
    vectors = jnp.concatenate((sums[0:2], sum_gain_two, jnp.zeros((13, width), F32)), axis=0)
    vectors = vectors + other_core(vectors)
    bit = 1
    while bit < seq_count:
        vectors = vectors + swap_along(vectors, "seq", bit)
        bit *= 2
    if split:
        grad_hidden, vectors, line_came, plane_last = together(
            grad_hidden, vectors, line_came, plane_last
        )
        grad_inputs = to_partners(grad_hidden)
        sum_up = halve_line(add_up((line_up[:z_half], line_came)).astype(BF16))
        plane = add_up(plane_last)
        kinds = mine_qkv[0].shape[0]
        sum_down = plane[kinds:].reshape(-1, width // seq_count, 128)
        sum_down = jnp.transpose(sum_down, (0, 2, 1)).reshape(-1, width // seq_count)
        z_count = dp_count // 2
        plane = plane[:kinds].astype(BF16).reshape((z_count, -1) + plane.shape[1:])
        flat = jnp.transpose(vectors.reshape(16, -1, 128), (1, 0, 2)).astype(BF16)
        flat = jnp.broadcast_to(flat.reshape(1, -1, tall, 128), (z_count, 1, tall, 128))
        line = halve_line(jnp.concatenate((plane, flat), axis=1))
        sum_qkv = jnp.transpose(line[:-1], (1, 0, 2)).reshape(tall, -1)
        vectors = jnp.transpose(line[-1].reshape(-1, 16, 128), (1, 0, 2)).reshape(16, -1)
    else:
        grad_inputs = to_partners(grad_hidden)
        vectors = add_up(from_line([vectors] * (dp_count // 2)))
    block_width = width // dp_count
    vectors = lax.dynamic_slice_in_dim(vectors, dp_place * block_width, block_width, 1)
    out_cols = width // seq_count
    return (
        by_row(result),
        by_row(grad_inputs),
        vectors[0],
        vectors[1],
        sum_qkv,
        sum_up[:, :out_cols],
        vectors[2],
        sum_up[:, out_cols:],
        sum_down,
    )


def solution(mesh):
    in_specs = (
        P("dp", "seq", None),
        P("dp", "seq", None),
        P("dp"),
        P("dp", "seq"),
        P(),
        P(),
        P("dp", None),
        P("dp", None),
        P(),
        P("dp", None),
        P("dp", None),
    )
    out_specs = (
        P("dp", "seq", None),
        P("dp", "seq", None),
        P("dp"),
        P("dp"),
        P("dp", "seq"),
        P("dp", "seq"),
        P("dp"),
        P("dp", "seq"),
        P("dp", "seq"),
    )
    return jax.shard_map(
        per_device, mesh=mesh, in_specs=in_specs, out_specs=out_specs, check_vma=False
    )
```

time: 299 us -> 212 us (0.71)
  waiting for transfers between devices: 88.2 us -> 39.4 us
  Pallas kernels: 94.5 us -> 79.3 us
  between operations: 14.2 us -> 1.5 us
  local copies, waits for them, and re-layouts: 14.5 us -> 25 us
  starting transfers between devices: 62.9 us -> 52.6 us
  matrix products: 5.3 us -> 0 us
  other arithmetic: 18.2 us -> 13.8 us
    all_gather x3 -> x0, waiting for transfers between devices: 35.3 us -> none  [the longest x1 24.6 us: per_device(): whole_down = lax.all_gather(weight_down, 'dp', axis=0, tiled=True)]
    unnamed x27 -> x74, local copies, waits for them, and re-layouts: 0.81 us -> 15.4 us
    pallas_call x7 -> x6, Pallas kernels: 82.3 us -> 68.6 us  [the longest x1 20.2 us: rise(): pl.pallas_call(functools.partial(rise_kernel, cfg), grid_spec=pltpu.Prefe...]
    ppermute x50 -> x43, waiting for transfers between devices: 52.2 us -> 39.4 us  [swap_along(): return lax.ppermute(value, axis, [(i, i ^ mask) for i in range(count)])]
    ppermute x50 -> x43, starting transfers between devices: 62.8 us -> 52.6 us  [swap_along(): return lax.ppermute(value, axis, [(i, i ^ mask) for i in range(count)])]
    squeeze x14 -> x1, local copies, waits for them, and re-layouts: 6.5 us -> 0.07 us  [by_partner(): lax.dynamic_index_in_dim(value, row ^ j, 0, keepdims=False)]
    dot_general x1 -> x0, matrix products: 5.3 us -> none  [nn(): return jnp.dot(left, right, preferred_element_type=F32)]
    concatenate x5 -> x11, other arithmetic: 6.99 us -> 2.56 us  [the longest x1 2.11 us: per_device(): came = from_plane(by_partner(jnp.concatenate((inputs, masked), axis=1)))]
  transfers between devices with their start and end apart: 53 -> 43, of which waited for: 24 -> 12; matrix products, arithmetic and copies ran while one was open for 11% -> 9% of each run, Pallas kernels for 14% -> 28%
where the time goes in v2:
time: 212 us
  Pallas kernels  79.3 us (37%)
  starting transfers between devices  52.6 us (25%)
  waiting for transfers between devices  39.4 us (19%)
  local copies, waits for them, and re-layouts  25 us (12%)
  other arithmetic  13.8 us (7%)
    ppermute x43, starting transfers between devices, swap_along(): return lax.ppermute(value, axis, [(i, i ^ mask) for i in range(count)])  52.6 us
    ppermute x43, waiting for transfers between devices, swap_along(): return lax.ppermute(value, axis, [(i, i ^ mask) for i in range(count)])  39.4 us
    pallas_call x1, Pallas kernels, rise(): pl.pallas_call(functools.partial(rise_kernel, cfg), grid_spec=pltpu.Prefe...  20.2 us
    pallas_call x1, Pallas kernels, attend_back_sum(): pl.pallas_call(functools.partial(attend_back_sum_kernel, min(512, count),...  15.6 us
    unnamed x74, local copies, waits for them, and re-layouts  15.4 us
    pallas_call x1, Pallas kernels, fall(): pl.pallas_call(functools.partial(fall_kernel, (seq_count, dp_count, split...  13.5 us
    pallas_call x1, Pallas kernels, attend_back_half(): pl.pallas_call(functools.partial(attend_back_kernel, min(512, count)), gr...  11.2 us
    pallas_call x1, Pallas kernels, attend(): pl.pallas_call(functools.partial(attend_kernel, chunk), grid=(4,), in_spe...  10.7 us
  transfers between devices with their start and end apart: 43, of which 12 were waited for; matrix products, arithmetic and copies ran while one was open for 9% of the time, Pallas kernels for 28%

profile of v2, /device:TPU:0, one launch (start us, length us, event | category | flops | bytes accessed | tf_op | source)
XLA Modules:
  0.0 211.7 jit_solution(13231887751416429535)
XLA Ops:
  2.4 3.1 %collective-permute-start.3 = (bf16[64,896]{1,0:T(8,128)(2,1)S(1)}, bf16[64,896]{1,0:T(8,128)(2,1)S(1)}, u32[]{:S(2)}, u32[]{:S(2)}) collective-permute-start(bf16[64,896]{1,0:T(8,128)(2,1)S(1)} %get-tuple-element.225), channel_id=1, source_target_pairs={{0,2},{1,3},{2,0},{3,1},{4,6},{5,7},{6,4},{7,5},{8,10},{9,11},{10,... | collective-permute-start | bytes 344072 | tf_op jit(solution)/shard_map/ppermute | solution.py:746
  5.5 2.6 %collective-permute-start.4 = (bf16[64,896]{1,0:T(8,128)(2,1)S(1)}, bf16[64,896]{1,0:T(8,128)(2,1)S(1)}, u32[]{:S(2)}, u32[]{:S(2)}) collective-permute-start(bf16[64,896]{1,0:T(8,128)(2,1)S(1)} %get-tuple-element.225), channel_id=1, source_target_pairs={{0,4},{1,5},{2,6},{3,7},{4,0},{5,1},{6,2},{7,3},{8,12},{9,13},{10,... | collective-permute-start | bytes 344072 | tf_op jit(solution)/shard_map/ppermute | solution.py:746
  8.9 2.1 fusion.6
  11.0 2.7 %collective-permute-start.2 = (bf16[272,512]{1,0:T(8,128)(2,1)S(1)}, bf16[272,512]{1,0:T(8,128)(2,1)}, u32[]{:S(2)}, u32[]{:S(2)}) collective-permute-start(bf16[272,512]{1,0:T(8,128)(2,1)S(1)} %get-tuple-element.190), channel_id=1, source_target_pairs={{0,24},{8,16},{16,8},{24,0},{1,25},{9,17},{17,9},{25,1},{2,26},{10... | collective-permute-start | bytes 835592 | tf_op jit(solution)/shard_map/ppermute | solution.py:746
  14.3 2.9 %collective-permute-done.4 = bf16[64,896]{1,0:T(8,128)(2,1)S(1)} collective-permute-done((bf16[64,896]{1,0:T(8,128)(2,1)S(1)}, bf16[64,896]{1,0:T(8,128)(2,1)S(1)}, u32[]{:S(2)}, u32[]{:S(2)}) %collective-permute-start.4) | collective-permute-done | bytes 114720 | tf_op jit(solution)/shard_map/ppermute | solution.py:746
  17.3 1.6 collective-permute-start.6
  18.9 1.5 collective-permute-start.7
  20.9 5.1 %collective-permute-done.6 = bf16[4,64,384]{2,1,0:T(8,128)(2,1)S(1)} collective-permute-done((bf16[4,64,384]{2,1,0:T(8,128)(2,1)S(1)}, bf16[4,64,384]{2,1,0:T(8,128)(2,1)S(1)}, u32[]{:S(2)}, u32[]{:S(2)}) %collective-permute-start.6) | collective-permute-done | bytes 196640 | tf_op jit(solution)/shard_map/ppermute | solution.py:746
  27.5 6.7 %collective-permute-done.7 = bf16[4,64,384]{2,1,0:T(8,128)(2,1)S(1)} collective-permute-done((bf16[4,64,384]{2,1,0:T(8,128)(2,1)S(1)}, bf16[4,64,384]{2,1,0:T(8,128)(2,1)S(1)}, u32[]{:S(2)}, u32[]{:S(2)}) %collective-permute-start.7) | collective-permute-done | bytes 196640 | tf_op jit(solution)/shard_map/ppermute | solution.py:746
  36.1 1.6 collective-permute-start.10
  40.4 4.3 %collective-permute-done.12 = bf16[64,2560]{1,0:T(8,128)(2,1)S(1)} collective-permute-done((bf16[64,2560]{1,0:T(8,128)(2,1)S(1)}, bf16[64,2560]{1,0:T(8,128)(2,1)S(1)}, u32[]{:S(2)}, u32[]{:S(2)}) %collective-permute-start.12) | collective-permute-done | bytes 327712 | tf_op jit(solution)/shard_map/ppermute | solution.py:746
  44.6 2.4 %collective-permute-start.13 = (bf16[64,2560]{1,0:T(8,128)(2,1)S(1)}, bf16[64,2560]{1,0:T(8,128)(2,1)S(1)}, u32[]{:S(2)}, u32[]{:S(2)}) collective-permute-start(bf16[64,2560]{1,0:T(8,128)(2,1)S(1)} %pad_maximum_fusion.11), channel_id=1, source_target_pairs={{0,4},{1,5},{2,6},{3,7},{4,0},{5,1},{6,2},{7,3},{8,12},{9,13},{10,... | collective-permute-start | bytes 983048 | tf_op jit(solution)/shard_map/ppermute | solution.py:746
  49.2 1.7 slice.305
  52.1 4.1 %project.1 = (bf16[1024,512]{1,0:T(8,128)(2,1)S(1)}, bf16[1024,1536]{1,0:T(8,128)(2,1)S(1)}, bf16[512,1536]{1,0:T(8,128)(2,1)S(1)}) custom-call(s32[3]{0:T(128)S(1)} %pad_add_fusion.own_ref, f32[1024,512]{1,0:T(8,128)S(1)} %multiply_add_fusion.hidden_ref, f32[1,512]{1,0:T(1,128)S(1)} %bitcast.113, bf16[4,4,64,384]{3,2,1,0:T(8,128)(2,1)S(1)} %pad_maximum_fusion.5.refs_0_, ...), custom_call_target="tpu_custom_call" | custom-call | flops 1536 | bytes 8 | tf_op jit(solution)/shard_map/project/pallas_call | solution.py:364
  58.5 10.7 %attend.1 = (bf16[1024,512]{1,0:T(8,128)(2,1)S(1)}, f32[1024,128]{1,0:T(8,128)S(1)}) custom-call(bf16[1024,1536]{1,0:T(8,128)(2,1)S(1)} %get-tuple-element.95.q_ref.k_ref.v_ref, bf16[1024,1536]{1,0:T(8,128)(2,1)S(1)} %get-tuple-element.95.q_ref.k_ref.v_ref, bf16[1024,1536]{1,0:T(8,128)(2,1)S(1)} %get-tuple-element.95.q_ref.k_ref.v_ref), custom_call_target="tpu_custom_call" | custom-call | flops 16384 | bytes 5 | tf_op jit(solution)/shard_map/attend/pallas_call | solution.py:65
  71.2 3.6 %collective-permute-done.17.refs_3_ = bf16[4,4,64,512]{3,2,1,0:T(8,128)(2,1)S(1)} collective-permute-done((bf16[4,4,64,512]{3,2,1,0:T(8,128)(2,1)S(1)}, bf16[4,4,64,512]{3,2,1,0:T(8,128)(2,1)S(1)}, u32[]{:S(2)}, u32[]{:S(2)}) %collective-permute-start.17) | collective-permute-done | bytes 1048608 | tf_op jit(solution)/shard_map/ppermute | solution.py:746
  74.8 20.2 %rise.1 = (bf16[1024,512]{1,0:T(8,128)(2,1)S(1)}, f32[1024,512]{1,0:T(8,128)S(1)}, f32[1024,128]{1,0:T(8,128)S(1)}, bf16[1024,2048]{1,0:T(8,128)(2,1)}, bf16[512...) custom-call(s32[3]{0:T(128)S(1)} %pad_add_fusion.own_ref, ...), custom_call_target="tpu_custom_call" | custom-call | flops 7168 | bytes 24 | tf_op jit(solution)/shard_map/rise/pallas_call | solution.py:483
  99.5 2.2 %copy-done.4 = bf16[1024,2048]{1,0:T(8,128)(2,1)S(1)} copy-done((bf16[1024,2048]{1,0:T(8,128)(2,1)S(1)}, bf16[1024,2048]{1,0:T(8,128)(2,1)}, u32[]{:S(2)}) %copy-start.4) | copy-done | bytes 4194328
  101.7 13.5 %fall.1 = (f32[1024,512]{1,0:T(8,128)S(1)}, bf16[1024,512]{1,0:T(8,128)(2,1)S(1)}, bf16[1024,512]{1,0:T(8,128)(2,1)S(1)}, f32[1,512]{1,0:T(1,128)S(1)}, bf16[4,4...) custom-call(s32[3]{0:T(128)S(1)} %pad_add_fusion.own_ref, ...), custom_call_target="tpu_custom_call" | custom-call | flops 8192 | bytes 24 | tf_op jit(solution)/shard_map/fall/pallas_call | solution.py:645
  116.1 1.7 fusion.14
  117.7 6.6 %collective-permute-start.23 = (bf16[4,2,128,128]{3,2,1,0:T(8,128)(2,1)S(1)}, bf16[4,2,128,128]{3,2,1,0:T(8,128)(2,1)S(1)}, u32[]{:S(2)}, u32[]{:S(2)}) collective-permute-start(bf16[4,2,128,128]{3,2,1,0:T(8,128)(2,1)S(1)} %get-tuple-element.178), channel_id=1, source_target_pairs={{0,2},{1,3},{2,0},{3,1},{4,6},{5,7},{6,4},{7,5},{8,10},{9,11},{10,... | collective-permute-start | bytes 786440 | tf_op jit(solution)/shard_map/ppermute | solution.py:746
  124.4 11.2 %attend_back_half.1 = (bf16[1024,256]{1,0:T(8,128)(2,1)S(1)}, bf16[1024,256]{1,0:T(8,128)(2,1)S(1)}, bf16[1024,256]{1,0:T(8,128)(2,1)S(1)}) custom-call(bf16[1024,1536]{1,0:T(8,128)(2,1)S(1)} %get-tuple-element.95.q_ref.k_ref.v_ref, bf16[1024,1536]{1,0:T(8,128)(2,1)S(1)} %get-tuple-element.95.q_ref.k_ref.v_ref, ...), custom_call_target="tpu_custom_call" | custom-call | flops 16384 | bytes 6 | tf_op jit(solution)/shard_map/attend_back_half/pallas_call | solution.py:131
  142.8 1.9 collective-permute-start.27
  153.1 15.6 %attend_back_sum.1 = (bf16[1024,256]{1,0:T(8,128)(2,1)S(1)}, bf16[1024,256]{1,0:T(8,128)(2,1)S(1)}, bf16[1024,256]{1,0:T(8,128)(2,1)S(1)}, bf16[4,4,3,64,128]{4,...) custom-call(s32[3]{0:T(128)S(1)} %pad_add_fusion.own_ref, bf16[1024,1536]{1,0:T(8,128)(2,1)S(1)} %get-tuple-element.95.q_ref.k_ref.v_ref, ...), custom_call_target="tpu_custom_call" | custom-call | flops 20480 | bytes 10 | tf_op jit(solution)/shard_map/attend_back_sum/pallas_call | solution.py:207
  170.5 2.1 collective-permute-start.33
  174.3 2.0 collective-permute-start.36
  177.4 3.9 %last.1 = (bf16[1024,512]{1,0:T(8,128)(2,1)S(1)}, f32[8,512]{1,0:T(8,128)S(1)}) custom-call(f32[1024,512]{1,0:T(8,128)S(1)} %copy-done.3, f32[1024,512]{1,0:T(8,128)S(1)} %copy-done.10, f32[1,512]{1,0:T(1,128)S(1)} %bitcast.114, bf16[8,1024]{1,0:T(8,128)(2,1)S(1)} %broadcast_in_dim.34.mask_ref, bf16[512,1536]{1,0:T(8,128)(2,1)S(1)} %copy-done.18, ...), custom_call_target="tpu_custom_call" | custom-call | flops 1536 | bytes 12 | tf_op jit(solution)/shard_map/last/pallas_call | solution.py:722
  184.7 6.2 %collective-permute-done.31 = f32[16,512]{1,0:T(8,128)S(1)} collective-permute-done((f32[16,512]{1,0:T(8,128)S(1)}, f32[16,512]{1,0:T(8,128)S(1)}, u32[]{:S(2)}, u32[]{:S(2)}) %collective-permute-start.31) | collective-permute-done | bytes 32800 | tf_op jit(solution)/shard_map/ppermute | solution.py:746
  192.0 2.8 %collective-permute-done.32 = f32[16,512]{1,0:T(8,128)S(1)} collective-permute-done((f32[16,512]{1,0:T(8,128)S(1)}, f32[16,512]{1,0:T(8,128)S(1)}, u32[]{:S(2)}, u32[]{:S(2)}) %collective-permute-start.32) | collective-permute-done | bytes 32800 | tf_op jit(solution)/shard_map/ppermute | solution.py:746
  197.7 1.6 collective-permute-start.37
  201.2 2.5 %collective-permute-done.40 = bf16[2,4,64,128]{3,2,1,0:T(8,128)(2,1)S(1)} collective-permute-done((bf16[2,4,64,128]{3,2,1,0:T(8,128)(2,1)S(1)}, bf16[2,4,64,128]{3,2,1,0:T(8,128)(2,1)S(1)}, u32[]{:S(2)}, u32[]{:S(2)}) %collective-permute-start.40) | collective-permute-done | bytes 131104 | tf_op jit(solution)/shard_map/ppermute | solution.py:746
  205.2 2.9 %collective-permute-done.41 = bf16[1,4,64,128]{3,2,1,0:T(8,128)(2,1)S(1)} collective-permute-done((bf16[1,4,64,128]{3,2,1,0:T(8,128)(2,1)S(1)}, bf16[1,4,64,128]{3,2,1,0:T(8,128)(2,1)S(1)}, u32[]{:S(2)}, u32[]{:S(2)}) %collective-permute-start.41) | collective-permute-done | bytes 65568 | tf_op jit(solution)/shard_map/ppermute | solution.py:746
  (210 shorter events, 56.6 us)
Async XLA Ops:
  2.4 11.8 %collective-permute-start.3 = (bf16[64,896]{1,0:T(8,128)(2,1)S(1)}, bf16[64,896]{1,0:T(8,128)(2,1)S(1)}, u32[]{:S(2)}, u32[]{:S(2)}) collective-permute-start(bf16[64,896]{1,0:T(8,128)(2,1)S(1)} %get-tuple-element.225), channel_id=1, source_target_pairs={{0,2},{1,3},{2,0},{3,1},{4,6},{5,7},{6,4},{7,5},{8,10},{9,11},{10,... | collective-permute-start | bytes 344072 | tf_op jit(solution)/shard_map/ppermute | solution.py:746
  5.5 11.7 %collective-permute-start.4 = (bf16[64,896]{1,0:T(8,128)(2,1)S(1)}, bf16[64,896]{1,0:T(8,128)(2,1)S(1)}, u32[]{:S(2)}, u32[]{:S(2)}) collective-permute-start(bf16[64,896]{1,0:T(8,128)(2,1)S(1)} %get-tuple-element.225), channel_id=1, source_target_pairs={{0,4},{1,5},{2,6},{3,7},{4,0},{5,1},{6,2},{7,3},{8,12},{9,13},{10,... | collective-permute-start | bytes 344072 | tf_op jit(solution)/shard_map/ppermute | solution.py:746
  11.0 24.1 %collective-permute-start.2 = (bf16[272,512]{1,0:T(8,128)(2,1)S(1)}, bf16[272,512]{1,0:T(8,128)(2,1)}, u32[]{:S(2)}, u32[]{:S(2)}) collective-permute-start(bf16[272,512]{1,0:T(8,128)(2,1)S(1)} %get-tuple-element.190), channel_id=1, source_target_pairs={{0,24},{8,16},{16,8},{24,0},{1,25},{9,17},{17,9},{25,1},{2,26},{10... | collective-permute-start | bytes 835592 | tf_op jit(solution)/shard_map/ppermute | solution.py:746
  13.7 24.0 %collective-permute-start.1 = (bf16[272,512]{1,0:T(8,128)(2,1)}, bf16[272,512]{1,0:T(8,128)(2,1)}, u32[]{:S(2)}, u32[]{:S(2)}) collective-permute-start(bf16[272,512]{1,0:T(8,128)(2,1)} %get-tuple-element.189), channel_id=1, source_target_pairs={{0,16},{8,24},{16,0},{24,8},{1,17},{9,25},{17,1},{25,9},{2,18},{10... | collective-permute-start | bytes 835592 | tf_op jit(solution)/shard_map/ppermute | solution.py:746
  18.9 15.3 %collective-permute-start.7 = (bf16[4,64,384]{2,1,0:T(8,128)(2,1)S(1)}, bf16[4,64,384]{2,1,0:T(8,128)(2,1)S(1)}, u32[]{:S(2)}, u32[]{:S(2)}) collective-permute-start(bf16[4,64,384]{2,1,0:T(8,128)(2,1)S(1)} %get-tuple-element.215), channel_id=1, source_target_pairs={{0,16},{8,24},{16,0},{24,8},{1,17},{9,25},{17,1},{25,9},{2,18},{10... | collective-permute-start | bytes 589832 | tf_op jit(solution)/shard_map/ppermute | solution.py:746
  20.4 13.7 %collective-permute-start.8 = (bf16[4,64,384]{2,1,0:T(8,128)(2,1)S(1)}, bf16[4,64,384]{2,1,0:T(8,128)(2,1)S(1)}, u32[]{:S(2)}, u32[]{:S(2)}) collective-permute-start(bf16[4,64,384]{2,1,0:T(8,128)(2,1)S(1)} %get-tuple-element.215), channel_id=1, source_target_pairs={{0,24},{8,16},{16,8},{24,0},{1,25},{9,17},{17,9},{25,1},{2,26},{10... | collective-permute-start | bytes 589832 | tf_op jit(solution)/shard_map/ppermute | solution.py:746
  26.1 13.1 %collective-permute-start = (bf16[272,512]{1,0:T(8,128)(2,1)}, bf16[272,512]{1,0:T(8,128)(2,1)S(1)}, u32[]{:S(2)}, u32[]{:S(2)}) collective-permute-start(bf16[272,512]{1,0:T(8,128)(2,1)} %get-tuple-element.188), channel_id=1, source_target_pairs={{0,8},{8,0},{16,24},{24,16},{1,9},{9,1},{17,25},{25,17},{2,10},{10... | collective-permute-start | bytes 835592 | tf_op jit(solution)/shard_map/ppermute | solution.py:746
  34.3 12.7 %collective-permute-start.15 = (bf16[4,4,64,384]{3,2,1,0:T(8,128)(2,1)S(1)}, bf16[4,4,64,384]{3,2,1,0:T(8,128)(2,1)S(1)}, u32[]{:S(2)}, u32[]{:S(2)}) collective-permute-start(bf16[4,4,64,384]{3,2,1,0:T(8,128)(2,1)S(1)} %pad_maximum_fusion.5.refs_0_), channel_id=1, source_target_pairs={{0,1},{1,0},{2,3},{3,2},{4,5},{5,4},{6,7},{7,6},{8,9},{9,8},{10,11... | collective-permute-start | bytes 2359304 | tf_op jit(solution)/shard_map/ppermute | solution.py:746
  34.5 10.2 %collective-permute-start.12 = (bf16[64,2560]{1,0:T(8,128)(2,1)S(1)}, bf16[64,2560]{1,0:T(8,128)(2,1)S(1)}, u32[]{:S(2)}, u32[]{:S(2)}) collective-permute-start(bf16[64,2560]{1,0:T(8,128)(2,1)S(1)} %pad_maximum_fusion.11), channel_id=1, source_target_pairs={{0,2},{1,3},{2,0},{3,1},{4,6},{5,7},{6,4},{7,5},{8,10},{9,11},{10,... | collective-permute-start | bytes 983048 | tf_op jit(solution)/shard_map/ppermute | solution.py:746
  36.1 33.8 %collective-permute-start.10 = (bf16[512,512]{1,0:T(8,128)(2,1)S(1)}, bf16[512,512]{1,0:T(8,128)(2,1)S(1)}, u32[]{:S(2)}, u32[]{:S(2)}) collective-permute-start(bf16[512,512]{1,0:T(8,128)(2,1)S(1)} %get-tuple-element.222), channel_id=1, source_target_pairs={{0,16},{8,24},{16,0},{24,8},{1,17},{9,25},{17,1},{25,9},{2,18},{10... | collective-permute-start | bytes 1572872 | tf_op jit(solution)/shard_map/ppermute | solution.py:746
  37.7 32.3 %collective-permute-start.11 = (bf16[512,512]{1,0:T(8,128)(2,1)S(1)}, bf16[512,512]{1,0:T(8,128)(2,1)S(1)}, u32[]{:S(2)}, u32[]{:S(2)}) collective-permute-start(bf16[512,512]{1,0:T(8,128)(2,1)S(1)} %get-tuple-element.220), channel_id=1, source_target_pairs={{0,24},{8,16},{16,8},{24,0},{1,25},{9,17},{17,9},{25,1},{2,26},{10... | collective-permute-start | bytes 1572872 | tf_op jit(solution)/shard_map/ppermute | solution.py:746
  39.1 30.8 %collective-permute-start.9 = (bf16[512,512]{1,0:T(8,128)(2,1)S(1)}, bf16[512,512]{1,0:T(8,128)(2,1)S(1)}, u32[]{:S(2)}, u32[]{:S(2)}) collective-permute-start(bf16[512,512]{1,0:T(8,128)(2,1)S(1)} %get-tuple-element.221), channel_id=1, source_target_pairs={{0,8},{8,0},{16,24},{24,16},{1,9},{9,1},{17,25},{25,17},{2,10},{10... | collective-permute-start | bytes 1572872 | tf_op jit(solution)/shard_map/ppermute | solution.py:746
  44.6 25.3 %collective-permute-start.13 = (bf16[64,2560]{1,0:T(8,128)(2,1)S(1)}, bf16[64,2560]{1,0:T(8,128)(2,1)S(1)}, u32[]{:S(2)}, u32[]{:S(2)}) collective-permute-start(bf16[64,2560]{1,0:T(8,128)(2,1)S(1)} %pad_maximum_fusion.11), channel_id=1, source_target_pairs={{0,4},{1,5},{2,6},{3,7},{4,0},{5,1},{6,2},{7,3},{8,12},{9,13},{10,... | collective-permute-start | bytes 983048 | tf_op jit(solution)/shard_map/ppermute | solution.py:746
  47.0 22.9 %collective-permute-start.14 = (bf16[64,2560]{1,0:T(8,128)(2,1)S(1)}, bf16[64,2560]{1,0:T(8,128)(2,1)S(1)}, u32[]{:S(2)}, u32[]{:S(2)}) collective-permute-start(bf16[64,2560]{1,0:T(8,128)(2,1)S(1)} %pad_maximum_fusion.11), channel_id=1, source_target_pairs={{0,6},{1,7},{2,4},{3,5},{4,2},{5,3},{6,0},{7,1},{8,14},{9,15},{10,... | collective-permute-start | bytes 983048 | tf_op jit(solution)/shard_map/ppermute | solution.py:746
  95.0 20.3 %collective-permute-start.18 = (bf16[4,4,2,128,128]{4,3,2,1,0:T(8,128)(2,1)S(1)}, bf16[4,4,2,128,128]{4,3,2,1,0:T(8,128)(2,1)S(1)}, u32[]{:S(2)}, u32[]{:S(2)}) collective-permute-start(bf16[4,4,2,128,128]{4,3,2,1,0:T(8,128)(2,1)S(1)} %get-tuple-element.107), channel_id=1, source_target_pairs={{0,1},{1,0},{2,3},{3,2},{4,5},{5,4},{6,7},{7,6},{8,9},{9,8},{10,11... | collective-permute-start | bytes 3145736 | tf_op jit(solution)/shard_map/ppermute | solution.py:746
  96.0 19.3 %collective-permute-start.19 = (bf16[256,512]{1,0:T(8,128)(2,1)S(1)}, bf16[256,512]{1,0:T(8,128)(2,1)S(1)}, u32[]{:S(2)}, u32[]{:S(2)}) collective-permute-start(bf16[256,512]{1,0:T(8,128)(2,1)S(1)} %get-tuple-element.200), channel_id=1, source_target_pairs={{0,8},{8,0},{16,24},{24,16},{1,9},{9,1},{17,25},{25,17},{2,10},{10... | collective-permute-start | bytes 786440 | tf_op jit(solution)/shard_map/ppermute | solution.py:746
  97.5 17.8 %collective-permute-start.20 = (bf16[256,512]{1,0:T(8,128)(2,1)S(1)}, bf16[256,512]{1,0:T(8,128)(2,1)S(1)}, u32[]{:S(2)}, u32[]{:S(2)}) collective-permute-start(bf16[256,512]{1,0:T(8,128)(2,1)S(1)} %get-tuple-element.199), channel_id=1, source_target_pairs={{0,16},{8,24},{16,0},{24,8},{1,17},{9,25},{17,1},{25,9},{2,18},{10... | collective-permute-start | bytes 786440 | tf_op jit(solution)/shard_map/ppermute | solution.py:746
  98.5 16.8 %collective-permute-start.21 = (bf16[256,512]{1,0:T(8,128)(2,1)S(1)}, bf16[256,512]{1,0:T(8,128)(2,1)S(1)}, u32[]{:S(2)}, u32[]{:S(2)}) collective-permute-start(bf16[256,512]{1,0:T(8,128)(2,1)S(1)} %get-tuple-element.198), channel_id=1, source_target_pairs={{0,24},{8,16},{16,8},{24,0},{1,25},{9,17},{17,9},{25,1},{2,26},{10... | collective-permute-start | bytes 786440 | tf_op jit(solution)/shard_map/ppermute | solution.py:746
  116.1 22.0 %collective-permute-start.22 = (bf16[4,4,64,640]{3,2,1,0:T(8,128)(2,1)S(1)}, bf16[4,4,64,640]{3,2,1,0:T(8,128)(2,1)S(1)}, u32[]{:S(2)}, u32[]{:S(2)}) collective-permute-start(bf16[4,4,64,640]{3,2,1,0:T(8,128)(2,1)S(1)} %get-tuple-element.124), channel_id=1, source_target_pairs={{0,1},{1,0},{2,3},{3,2},{4,5},{5,4},{6,7},{7,6},{8,9},{9,8},{10,11... | collective-permute-start | bytes 3932168 | tf_op jit(solution)/shard_map/ppermute | solution.py:746
  117.7 20.4 %collective-permute-start.23 = (bf16[4,2,128,128]{3,2,1,0:T(8,128)(2,1)S(1)}, bf16[4,2,128,128]{3,2,1,0:T(8,128)(2,1)S(1)}, u32[]{:S(2)}, u32[]{:S(2)}) collective-permute-start(bf16[4,2,128,128]{3,2,1,0:T(8,128)(2,1)S(1)} %get-tuple-element.178), channel_id=1, source_target_pairs={{0,2},{1,3},{2,0},{3,1},{4,6},{5,7},{6,4},{7,5},{8,10},{9,11},{10,... | collective-permute-start | bytes 786440 | tf_op jit(solution)/shard_map/ppermute | solution.py:746
  139.3 29.4 %collective-permute-start.24 = (bf16[4,64,640]{2,1,0:T(8,128)(2,1)}, bf16[4,64,640]{2,1,0:T(8,128)(2,1)}, u32[]{:S(2)}, u32[]{:S(2)}) collective-permute-start(bf16[4,64,640]{2,1,0:T(8,128)(2,1)} %get-tuple-element.173), channel_id=1, source_target_pairs={{0,8},{8,0},{16,24},{24,16},{1,9},{9,1},{17,25},{25,17},{2,10},{10... | collective-permute-start | bytes 983048 | tf_op jit(solution)/shard_map/ppermute | solution.py:746
  140.8 27.9 %collective-permute-start.25 = (bf16[4,64,640]{2,1,0:T(8,128)(2,1)}, bf16[4,64,640]{2,1,0:T(8,128)(2,1)}, u32[]{:S(2)}, u32[]{:S(2)}) collective-permute-start(bf16[4,64,640]{2,1,0:T(8,128)(2,1)} %get-tuple-element.172), channel_id=1, source_target_pairs={{0,16},{8,24},{16,0},{24,8},{1,17},{9,25},{17,1},{25,9},{2,18},{10... | collective-permute-start | bytes 983048 | tf_op jit(solution)/shard_map/ppermute | solution.py:746
  141.9 26.9 %collective-permute-start.26 = (bf16[4,64,640]{2,1,0:T(8,128)(2,1)}, bf16[4,64,640]{2,1,0:T(8,128)(2,1)}, u32[]{:S(2)}, u32[]{:S(2)}) collective-permute-start(bf16[4,64,640]{2,1,0:T(8,128)(2,1)} %get-tuple-element.171), channel_id=1, source_target_pairs={{0,24},{8,16},{16,8},{24,0},{1,25},{9,17},{17,9},{25,1},{2,26},{10... | collective-permute-start | bytes 983048 | tf_op jit(solution)/shard_map/ppermute | solution.py:746
  142.8 25.9 %collective-permute-start.27 = (bf16[4,2,128,128]{3,2,1,0:T(8,128)(2,1)}, bf16[4,2,128,128]{3,2,1,0:T(8,128)(2,1)}, u32[]{:S(2)}, u32[]{:S(2)}) collective-permute-start(bf16[4,2,128,128]{3,2,1,0:T(8,128)(2,1)} %get-tuple-element.176), channel_id=1, source_target_pairs={{0,4},{1,5},{2,6},{3,7},{4,0},{5,1},{6,2},{7,3},{8,12},{9,13},{10,... | collective-permute-start | bytes 786440 | tf_op jit(solution)/shard_map/ppermute | solution.py:746
  144.7 24.0 %collective-permute-start.28 = (bf16[4,2,128,128]{3,2,1,0:T(8,128)(2,1)}, bf16[4,2,128,128]{3,2,1,0:T(8,128)(2,1)}, u32[]{:S(2)}, u32[]{:S(2)}) collective-permute-start(bf16[4,2,128,128]{3,2,1,0:T(8,128)(2,1)} %get-tuple-element.175), channel_id=1, source_target_pairs={{0,6},{1,7},{2,4},{3,5},{4,2},{5,3},{6,0},{7,1},{8,14},{9,15},{10,... | collective-permute-start | bytes 786440 | tf_op jit(solution)/shard_map/ppermute | solution.py:746
  170.5 24.4 %collective-permute-start.33 = (bf16[2,64,640]{2,1,0:T(8,128)(2,1)S(1)}, bf16[2,64,640]{2,1,0:T(8,128)(2,1)S(1)}, u32[]{:S(2)}, u32[]{:S(2)}) collective-permute-start(bf16[2,64,640]{2,1,0:T(8,128)(2,1)S(1)} %slice.310), channel_id=1, source_target_pairs={{0,4},{1,5},{2,6},{3,7},{4,0},{5,1},{6,2},{7,3},{8,12},{9,13},{10,... | collective-permute-start | bytes 491528 | tf_op jit(solution)/shard_map/ppermute | solution.py:746
  174.3 20.6 %collective-permute-start.36 = (bf16[16,64,128]{2,1,0:T(8,128)(2,1)S(1)}, bf16[16,64,128]{2,1,0:T(8,128)(2,1)S(1)}, u32[]{:S(2)}, u32[]{:S(2)}) collective-permute-start(bf16[16,64,128]{2,1,0:T(8,128)(2,1)S(1)} %pad_maximum_fusion.15), channel_id=1, source_target_pairs={{0,24},{8,16},{16,8},{24,0},{1,25},{9,17},{17,9},{25,1},{2,26},{10... | collective-permute-start | bytes 786440 | tf_op jit(solution)/shard_map/ppermute | solution.py:746
  176.3 18.5 %collective-permute-start.35 = (bf16[16,64,128]{2,1,0:T(8,128)(2,1)S(1)}, bf16[16,64,128]{2,1,0:T(8,128)(2,1)S(1)}, u32[]{:S(2)}, u32[]{:S(2)}) collective-permute-start(bf16[16,64,128]{2,1,0:T(8,128)(2,1)S(1)} %pad_maximum_fusion.14), channel_id=1, source_target_pairs={{0,16},{8,24},{16,0},{24,8},{1,17},{9,25},{17,1},{25,9},{2,18},{10... | collective-permute-start | bytes 786440 | tf_op jit(solution)/shard_map/ppermute | solution.py:746
  181.5 13.4 %collective-permute-start.34 = (bf16[16,64,128]{2,1,0:T(8,128)(2,1)S(1)}, bf16[16,64,128]{2,1,0:T(8,128)(2,1)S(1)}, u32[]{:S(2)}, u32[]{:S(2)}) collective-permute-start(bf16[16,64,128]{2,1,0:T(8,128)(2,1)S(1)} %pad_maximum_fusion.13), channel_id=1, source_target_pairs={{0,8},{8,0},{16,24},{24,16},{1,9},{9,1},{17,25},{25,17},{2,10},{10... | collective-permute-start | bytes 786440 | tf_op jit(solution)/shard_map/ppermute | solution.py:746
  197.7 11.7 %collective-permute-start.37 = (bf16[256,512]{1,0:T(8,128)(2,1)S(1)}, bf16[256,512]{1,0:T(8,128)(2,1)S(1)}, u32[]{:S(2)}, u32[]{:S(2)}) collective-permute-start(bf16[256,512]{1,0:T(8,128)(2,1)S(1)} %get-tuple-element.193), channel_id=1, source_target_pairs={{0,24},{8,16},{16,8},{24,0},{1,25},{9,17},{17,9},{25,1},{2,26},{10... | collective-permute-start | bytes 786440 | tf_op jit(solution)/shard_map/ppermute | solution.py:746
  199.2 11.2 %collective-permute-start.38 = (bf16[256,512]{1,0:T(8,128)(2,1)S(1)}, bf16[256,512]{1,0:T(8,128)(2,1)S(1)}, u32[]{:S(2)}, u32[]{:S(2)}) collective-permute-start(bf16[256,512]{1,0:T(8,128)(2,1)S(1)} %get-tuple-element.192), channel_id=1, source_target_pairs={{0,16},{8,24},{16,0},{24,8},{1,17},{9,25},{17,1},{25,9},{2,18},{10... | collective-permute-start | bytes 786440 | tf_op jit(solution)/shard_map/ppermute | solution.py:746
  199.7 10.7 %collective-permute-start.39 = (bf16[256,512]{1,0:T(8,128)(2,1)S(1)}, bf16[256,512]{1,0:T(8,128)(2,1)S(1)}, u32[]{:S(2)}, u32[]{:S(2)}) collective-permute-start(bf16[256,512]{1,0:T(8,128)(2,1)S(1)} %get-tuple-element.191), channel_id=1, source_target_pairs={{0,8},{8,0},{16,24},{24,16},{1,9},{9,1},{17,25},{25,17},{2,10},{10... | collective-permute-start | bytes 786440 | tf_op jit(solution)/shard_map/ppermute | solution.py:746
  (48 other events, 369.0 us)

commit v3 on v2

--- a/solution.py
+++ b/solution.py
@@ -11,7 +11,7 @@
 HEADS = 8
 F32 = jnp.float32
 BF16 = jnp.bfloat16
-LIGHT = 2**20
+IN_VMEM = pl.BlockSpec(memory_space=pltpu.VMEM)
 
 
 def nn(left, right):
@@ -28,7 +28,7 @@
 
 def cost(flops, bytes_accessed):
     return pl.CostEstimate(
-        flops=int(flops) // LIGHT, bytes_accessed=int(bytes_accessed) // LIGHT, transcendentals=0
+        flops=int(flops), bytes_accessed=int(bytes_accessed), transcendentals=0
     )
 
 
@@ -78,10 +78,57 @@
             jax.ShapeDtypeStruct((count, 512), BF16),
             jax.ShapeDtypeStruct((count, 128), F32),
         ],
-        compiler_params=params(20),
+        compiler_params=params(12),
         cost_estimate=cost(16 * count * span * 1024, 5 * 2**20),
         name="attend",
     )(q_source, kv_source, kv_source)
+
+
+def attend_row_kernel(chunk, own_ref, out_ref, den_ref):
+    count, width = out_ref.shape
+    lane = lax.broadcasted_iota(jnp.int32, (1, 128), 1)
+    low = lane < 64
+    for start in range(0, count, chunk):
+        at = slice(start, start + chunk)
+        sums = jnp.zeros((chunk, 128), F32)
+        for pair in range(width // 128):
+            col = pair * 128
+            keys = own_ref[:, width + col : width + col + 128]
+            values = own_ref[:, 2 * width + col : 2 * width + col + 128]
+            one = jnp.ones_like(values)
+            q = own_ref[at, col : col + 128] * jnp.asarray(0.125, BF16)
+            zero = jnp.zeros_like(q)
+            left = nn(
+                jnp.exp(nt(jnp.where(low, q, zero), keys)).astype(BF16),
+                jnp.where(low, values, one),
+            )
+            right = nn(
+                jnp.exp(nt(jnp.where(low, zero, q), keys)).astype(BF16),
+                jnp.where(low, one, values),
+            )
+            swapped = jnp.where(low, right, left)
+            den = pltpu.roll(swapped, 64, 1)
+            out_ref[at, col : col + 128] = (jnp.where(low, left, right) / den).astype(BF16)
+            first, second = lane // 16 == 2 * pair, lane // 16 == 2 * pair + 1
+            sums = jnp.where(first, jnp.where(low, den, swapped), sums)
+            sums = jnp.where(second, jnp.where(low, swapped, den), sums)
+        den_ref[at, :] = sums
+
+
+def attend_row(projected):
+    count, width = projected.shape[0], projected.shape[1] // 3
+    return pl.pallas_call(
+        functools.partial(attend_row_kernel, min(256, count)),
+        in_specs=[IN_VMEM],
+        out_specs=[IN_VMEM] * 2,
+        out_shape=[
+            jax.ShapeDtypeStruct((count, width), BF16),
+            jax.ShapeDtypeStruct((count, 128), F32),
+        ],
+        compiler_params=params(12),
+        cost_estimate=cost(16 * count * count * 1024, 5 * 2**20),
+        name="attend_row",
+    )(projected)
 
 
 def head_pair_back(chunk, q_ref, k_ref, v_ref, s_ref, x_ref, dk_ref, dv_ref):
@@ -122,31 +169,42 @@
     dq_ref[...] = head_pair_back(chunk, q_ref, k_ref, v_ref, s_ref, x_ref, dk_ref, dv_ref)
 
 
+def pair_views(col, width, proj_ref, s_ref, x_ref):
+    at = [slice(shift + col, shift + col + 128) for shift in (0, width, 2 * width)]
+    return [proj_ref.at[:, cols] for cols in at] + [s_ref.at[:, at[0]], x_ref.at[:, at[0]]]
+
+
+def attend_back_half_kernel(chunk, proj_ref, s_ref, x_ref, dq_ref, dk_ref, dv_ref):
+    width = s_ref.shape[1]
+    for pair in range(2):
+        col = pair * 128
+        at = slice(col, col + 128)
+        dq_ref[:, at] = head_pair_back(
+            chunk,
+            *pair_views(col, width, proj_ref, s_ref, x_ref),
+            dk_ref.at[:, at],
+            dv_ref.at[:, at],
+        )
+
+
 def attend_back_half(projected, scaled, extra):
     count, width = scaled.shape
-
-    def at(shift):
-        return pl.BlockSpec((count, 128), lambda p: (0, shift + p))
-
     return pl.pallas_call(
-        functools.partial(attend_back_kernel, min(512, count)),
-        grid=(2,),
-        in_specs=[at(0), at(4), at(8), at(0), at(0)],
-        out_specs=[at(0)] * 3,
+        functools.partial(attend_back_half_kernel, min(512, count)),
+        in_specs=[IN_VMEM] * 3,
+        out_specs=[IN_VMEM] * 3,
         out_shape=[jax.ShapeDtypeStruct((count, width // 2), BF16)] * 3,
-        compiler_params=params(20),
+        compiler_params=params(14),
         cost_estimate=cost(16 * count * count * 1024, 6 * 2**20),
         name="attend_back_half",
-    )(projected, projected, projected, scaled, extra)
+    )(projected, scaled, extra)
 
 
 def attend_back_sum_kernel(
     chunk,
     dp_count,
     own_ref,
-    q_ref,
-    k_ref,
-    v_ref,
+    proj_ref,
     s_ref,
     x_ref,
     normed_ref,
@@ -161,16 +219,15 @@
     normed_t,
     joined,
     grad_ref,
-    sem,
+    sems,
 ):
-    step = pl.program_id(0)
-    grad_outs = (mine_out, other_out)
-
-    @pl.when(step == 0)
-    def _():
-        normed_t[...] = normed_ref[...].T
-
-    def weight_part(pair):
+    width = s_ref.shape[1]
+    normed_t[...] = normed_ref[...].T
+
+    def weight_part(pair, refs):
+        cols = slice((pair % 2) * 128, (pair % 2) * 128 + 128)
+        for kind, ref in enumerate(refs):
+            joined[:, kind * 128 : (kind + 1) * 128] = ref[:, cols]
         result = nn(normed_t[...], joined[...]).astype(BF16)
         rows = result.shape[0] // dp_count
         per = grad_ref.shape[3]
@@ -182,58 +239,38 @@
                     d * rows : (d + 1) * rows, kind * 128 : (kind + 1) * 128
                 ]
 
-    for kind, ref in enumerate((dq_first, dk_first, dv_first)):
-        joined[:, kind * 128 : (kind + 1) * 128] = ref[...]
-    weight_part(step)
-    dq = head_pair_back(chunk, q_ref, k_ref, v_ref, s_ref, x_ref, dk_ref, dv_ref)
-    dq_ref[...] = dq
-    joined[:, :128] = dq
-    joined[:, 128:256] = dk_ref[...]
-    joined[:, 256:] = dv_ref[...]
-    weight_part(step + 2)
-
-    @pl.when(step == 1)
-    def _():
-        hand_out(grad_ref, grad_outs, sem)
+    for pair in range(2):
+        weight_part(pair, (dq_first, dk_first, dv_first))
+    for pair in range(2, 4):
+        at = slice((pair - 2) * 128, (pair - 1) * 128)
+        dq_ref[:, at] = head_pair_back(
+            chunk,
+            *pair_views(pair * 128, width, proj_ref, s_ref, x_ref),
+            dk_ref.at[:, at],
+            dv_ref.at[:, at],
+        )
+        weight_part(pair, (dq_ref, dk_ref, dv_ref))
+    hand_out(grad_ref, (mine_out, other_out), sems)
 
 
 def attend_back_sum(own, projected, scaled, extra, normed, first_half, seq_count, dp_count):
     count, width = scaled.shape
     pieces = (2, seq_count, dp_count // 2, 12 // seq_count, width // dp_count, 128)
-
-    def at(shift):
-        return pl.BlockSpec((count, 128), lambda p, own: (0, shift + p))
-
     return pl.pallas_call(
         functools.partial(attend_back_sum_kernel, min(512, count), dp_count),
-        grid_spec=pltpu.PrefetchScalarGridSpec(
-            num_scalar_prefetch=1,
-            grid=(2,),
-            in_specs=[
-                at(2),
-                at(6),
-                at(10),
-                at(2),
-                at(2),
-                pl.BlockSpec((count, width), lambda p, own: (0, 0)),
-                at(0),
-                at(0),
-                at(0),
-            ],
-            out_specs=[at(0)] * 3 + [pl.BlockSpec(memory_space=pl.ANY)] * 2,
-            scratch_shapes=[
-                pltpu.VMEM((width, count), BF16),
-                pltpu.VMEM((count, 384), BF16),
-                pltpu.VMEM(pieces, BF16),
-                pltpu.SemaphoreType.DMA((2,)),
-            ],
-        ),
-        out_shape=[jax.ShapeDtypeStruct((count, width // 2), BF16)] * 3
-        + outs_of(pieces, True),
-        compiler_params=params(24),
+        in_specs=[pl.BlockSpec(memory_space=pltpu.SMEM)] + [IN_VMEM] * 7,
+        out_specs=[IN_VMEM] * 3 + [pl.BlockSpec(memory_space=pl.ANY)] * 2,
+        scratch_shapes=[
+            pltpu.VMEM((width, count), BF16),
+            pltpu.VMEM((count, 384), BF16),
+            pltpu.VMEM(pieces, BF16),
+            pltpu.SemaphoreType.DMA((2,)),
+        ],
+        out_shape=[jax.ShapeDtypeStruct((count, width // 2), BF16)] * 3 + outs_of(pieces, True),
+        compiler_params=params(18),
         cost_estimate=cost(20 * count * count * 1024, 10 * 2**20),
         name="attend_back_sum",
-    )(own, projected, projected, projected, scaled, extra, normed, *first_half)
+    )(own, projected, scaled, extra, normed, *first_half)
 
 
 def attend_back(q_source, kv_source, scaled, extra):
@@ -380,40 +417,37 @@
             jax.ShapeDtypeStruct((count, cols), BF16),
             jax.ShapeDtypeStruct((width, cols), BF16),
         ],
-        compiler_params=params(16),
+        compiler_params=params(12),
         cost_estimate=cost(2 * count * width * cols, 8 * 2**20),
         name="project",
     )(own, hidden, gain, *parts)
 
 
 def rise_kernel(cfg, own_ref, hidden_ref, att_ref, cot_ref, gain_ref, *refs):
-    seq_count, dp_count, split, up_parts, down_parts = cfg
+    seq_count, dp_count, split, chunk, up_parts, down_parts = cfg
     up_sources, refs = refs[:up_parts], refs[up_parts:]
     down_sources, refs = refs[:down_parts], refs[down_parts:]
     outs = 2 if split else 1
     out_ref, normed_ref, scale_ref, slope_ref, w_up, w_down, *refs = refs
     grad_outs, refs = refs[:outs], refs[outs:]
-    (
-        act_ref,
-        cot_t,
-        grad_ref,
-        up_sems,
-        down_sems,
-        out_sem,
-    ) = refs
-    step = pl.program_id(0)
-    chunk, width = hidden_ref.shape
-    count, raised = act_ref.shape
-    steps = count // chunk
-
-    def tokens():
-        at = pl.ds(pl.multiple_of(step * chunk, chunk), chunk)
-        first = hidden_ref[...] + nn(att_ref[...], w_up[:, :width])
+    act_ref, cot_t, grad_ref, up_sems, down_sems, out_sems = refs
+    count, width = hidden_ref.shape
+    raised = act_ref.shape[1]
+    up_copies = fetches(own_ref, up_sources, w_up, up_sems)
+    down_copies = fetches(own_ref, down_sources, w_down, down_sems)
+    launch(up_copies)
+    launch(down_copies)
+    cot_t[...] = cot_ref[...].T
+    finish(up_copies)
+    for row in range(0, count, chunk):
+        at = slice(row, row + chunk)
+        first = hidden_ref[at, :] + nn(att_ref[at, :], w_up[:, :width])
         normed, scale = norm_parts(first)
-        normed_ref[...] = normed
-        scale_ref[...] = jnp.broadcast_to(scale, scale_ref.shape)
+        normed_ref[at, :] = normed
+        scale_ref[at, :] = jnp.broadcast_to(scale, (chunk, scale_ref.shape[1]))
         normed_two = (normed * gain_ref[...]).astype(BF16)
-        cot_t[:, at] = cot_ref[...].T
+        if row == 0:
+            finish(down_copies)
         total = first
         for start in range(0, raised, 512):
             stop = start + 512
@@ -426,85 +460,63 @@
                 0.7978845608028654 + 0.10703222440890037 * square
             )
             act_ref[at, start:stop] = act
-            slope_ref[:, start:stop] = slope.astype(BF16)
+            slope_ref[at, start:stop] = slope.astype(BF16)
             total = total + nn(act, w_down[start:stop, :])
-        out_ref[...] = total.astype(BF16)
-
-    @pl.when(step == 0)
-    def _():
-        copies = fetches(own_ref, up_sources, w_up, up_sems)
-        copies += fetches(own_ref, down_sources, w_down, down_sems)
-        launch(copies)
-        finish(copies)
-
-    pl.when(step < steps)(tokens)
-
-    @pl.when(step == steps)
-    def _():
-        if split:
-            cols = width // seq_count
-            rows = raised // dp_count
-            for d in range(dp_count):
-                result = nn(cot_t[...], act_ref[:, d * rows : (d + 1) * rows]).astype(BF16)
-                for s in range(seq_count):
-                    piece = result[s * cols : (s + 1) * cols, :]
-                    for part in range(rows // 128):
-                        grad_ref[
-                            (d % 2) ^ own_ref[2], (d // 2) ^ own_ref[1], s ^ own_ref[0], part
-                        ] = piece[:, part * 128 : (part + 1) * 128]
-        else:
-            for start in range(0, raised, 512):
-                grad_ref[:, start : start + 512] = nn(
-                    cot_t[...], act_ref[:, start : start + 512]
-                ).astype(BF16)
-        hand_out(grad_ref, grad_outs, out_sem)
+        out_ref[at, :] = total.astype(BF16)
+    if not split:
+        for start in range(0, raised, 512):
+            grad_ref[:, start : start + 512] = nn(
+                cot_t[...], act_ref[:, start : start + 512]
+            ).astype(BF16)
+        hand_out(grad_ref, grad_outs, out_sems)
+        return
+    cols = width // seq_count
+    rows = raised // dp_count
+    copies = []
+    for i in range(dp_count // 2):
+        result = nn(cot_t[...], act_ref[:, 2 * i * rows : 2 * (i + 1) * rows]).astype(BF16)
+        z = i ^ own_ref[1]
+        for s in range(seq_count):
+            piece = result[s * cols : (s + 1) * cols, :]
+            for core in range(2):
+                for part in range(rows // 128):
+                    col = core * rows + part * 128
+                    grad_ref[core ^ own_ref[2], z, s ^ own_ref[0], part] = piece[:, col : col + 128]
+        for core in range(2):
+            copy = pltpu.make_async_copy(
+                grad_ref.at[core, z], grad_outs[core].at[z], out_sems.at[len(copies)]
+            )
+            copies.append(copy)
+            copy.start()
+    finish(copies)
 
 
 def rise(own, hidden, att, cot, gain, up_parts, down_parts, raised, seq_count, dp_count, split):
     count, width = hidden.shape
-    chunk = min(256, count)
-    steps = count // chunk
-
-    def rows(cols):
-        return pl.BlockSpec((chunk, cols), lambda i, own: (jnp.minimum(i, steps - 1), 0))
-
-    def whole(shape):
-        return pl.BlockSpec(shape, lambda i, own: (0, 0), pipeline_mode=pl.Buffered(1))
-
-    anywhere = pl.BlockSpec(memory_space=pl.ANY)
     if split:
         parts = raised // dp_count // 128
         grad_shape = (2, dp_count // 2, seq_count, parts, width // seq_count, 128)
     else:
         grad_shape = (width, raised)
-    cfg = (seq_count, dp_count, split, len(up_parts), len(down_parts))
+    chunk = min(512, count)
+    cfg = (seq_count, dp_count, split, chunk, len(up_parts), len(down_parts))
     grads = outs_of(grad_shape, split)
     up_shape, down_shape = (width, width + raised), (raised, width)
+    anywhere = pl.BlockSpec(memory_space=pl.ANY)
     return pl.pallas_call(
         functools.partial(rise_kernel, cfg),
-        grid_spec=pltpu.PrefetchScalarGridSpec(
-            num_scalar_prefetch=1,
-            grid=(steps + 1,),
-            in_specs=[rows(width), rows(width), rows(width), whole((1, width))]
-            + [anywhere] * (len(up_parts) + len(down_parts)),
-            out_specs=[
-                rows(width),
-                rows(width),
-                rows(128),
-                rows(raised),
-                whole(up_shape),
-                whole(down_shape),
-            ]
-            + [anywhere] * len(grads),
-            scratch_shapes=[
-                pltpu.VMEM((count, raised), BF16),
-                pltpu.VMEM((width, count), BF16),
-                pltpu.VMEM(grad_shape, BF16),
-                pltpu.SemaphoreType.DMA((copies_of(up_parts),)),
-                pltpu.SemaphoreType.DMA((copies_of(down_parts),)),
-                pltpu.SemaphoreType.DMA((2,)),
-            ],
-        ),
+        in_specs=[pl.BlockSpec(memory_space=pltpu.SMEM)]
+        + [IN_VMEM] * 4
+        + [anywhere] * (len(up_parts) + len(down_parts)),
+        out_specs=[IN_VMEM] * 6 + [anywhere] * len(grads),
+        scratch_shapes=[
+            pltpu.VMEM((count, raised), BF16),
+            pltpu.VMEM((width, count), BF16),
+            pltpu.VMEM(grad_shape, BF16),
+            pltpu.SemaphoreType.DMA((copies_of(up_parts),)),
+            pltpu.SemaphoreType.DMA((copies_of(down_parts),)),
+            pltpu.SemaphoreType.DMA((dp_count,)),
+        ],
         out_shape=[
             jax.ShapeDtypeStruct((count, width), BF16),
             jax.ShapeDtypeStruct((count, width), F32),
@@ -514,7 +526,7 @@
             jax.ShapeDtypeStruct(down_shape, BF16),
         ]
         + grads,
-        compiler_params=params(32),
+        compiler_params=params(22),
         cost_estimate=cost(7 * 2**30, 24 * 2**20),
         name="rise",
     )(own, hidden, att, cot, gain, *up_parts, *down_parts)
@@ -538,46 +550,46 @@
     gain_sum_ref,
     *refs,
 ):
-    seq_count, dp_count, split = cfg
+    seq_count, dp_count, split, chunk = cfg
     outs = 2 if split else 1
-    grad_outs, (raise_ref, normed_t, att_t, branch_ref, grad_ref, out_sem) = refs[:outs], refs[outs:]
-    step = pl.program_id(0)
-    chunk, width = cot_ref.shape
-    count, raised = raise_ref.shape
-    steps = count // chunk
-
-    def tokens():
-        at = pl.ds(pl.multiple_of(step * chunk, chunk), chunk)
-        att = att_ref[...]
-        cot = cot_ref[...]
-        normed = normed_ref[...]
-        gain = gain_ref[...]
+    grad_outs, (raise_ref, normed_t, att_t, branch_ref, grad_ref, out_sems) = (
+        refs[:outs],
+        refs[outs:],
+    )
+    count, width = cot_ref.shape
+    raised = raise_ref.shape[1]
+    gain = gain_ref[...]
+    lane = lax.broadcasted_iota(jnp.int32, (128, width), 1)
+    spread = lax.broadcasted_iota(jnp.int32, (128, width), 0) == 16 * (lane // 64)
+    spread = jnp.where(spread, 1.0, 0.0).astype(BF16)
+    row = lax.broadcasted_iota(jnp.int32, (128, 128), 0)
+    col = lax.broadcasted_iota(jnp.int32, (128, 128), 1)
+    swap = jnp.where((row < 64) != (col < 64), 1.0, 0.0).astype(BF16)
+    even = lax.broadcasted_iota(jnp.int32, (1, 128), 1) % 2 == 0
+    gain_sum = jnp.zeros((1, width), F32)
+    att_t[...] = att_ref[...].T
+    for top in range(0, count, chunk):
+        at = slice(top, top + chunk)
+        cot = cot_ref[at, :]
+        normed = normed_ref[at, :]
         normed_t[:, at] = (normed * gain).astype(BF16).T
-        att_t[:, at] = att.T
         back = jnp.zeros((chunk, width), F32)
         for start in range(0, raised, 512):
             stop = start + 512
-            grad_raised = (nt(cot, w_down[start:stop, :]) * slope_ref[:, start:stop]).astype(BF16)
+            grad_raised = (nt(cot, w_down[start:stop, :]) * slope_ref[at, start:stop]).astype(BF16)
             raise_ref[at, start:stop] = grad_raised
             back = back + nt(grad_raised, w_up[:, width + start : width + stop])
-        gain_sum_ref[...] += jnp.sum(back * normed, axis=0, keepdims=True)
-        grad_first = cot.astype(F32) + norm_back(back * gain, normed, scale_ref[:, :1])
-        first_ref[...] = grad_first
+        gain_sum = gain_sum + jnp.sum(back * normed, axis=0, keepdims=True)
+        grad_first = cot.astype(F32) + norm_back(back * gain, normed, scale_ref[at, :1])
+        first_ref[at, :] = grad_first
         branch = grad_first.astype(BF16)
         branch_ref[at, :] = branch
-        inverse = 1.0 / den_ref[...]
-        row = lax.broadcasted_iota(jnp.int32, (128, width), 0)
-        col = lax.broadcasted_iota(jnp.int32, (128, width), 1)
-        spread = jnp.where(row == 16 * (col // 64), 1.0, 0.0).astype(BF16)
+        inverse = 1.0 / den_ref[at, :]
         coarse = inverse.astype(BF16)
         fine = (inverse - coarse.astype(F32)).astype(BF16)
         ratio = nt(branch, w_up[:, :width]) * (nn(coarse, spread) + nn(fine, spread))
-        scaled_ref[...] = ratio.astype(BF16)
-        row = lax.broadcasted_iota(jnp.int32, (128, 128), 0)
-        col = lax.broadcasted_iota(jnp.int32, (128, 128), 1)
-        swap = jnp.where((row < 64) != (col < 64), 1.0, 0.0).astype(BF16)
-        even = lax.broadcasted_iota(jnp.int32, (1, 128), 1) % 2 == 0
-        product = ratio * att
+        scaled_ref[at, :] = ratio.astype(BF16)
+        product = ratio * att_ref[at, :]
         coarse = product.astype(BF16)
         fine = (product - coarse.astype(F32)).astype(BF16)
         for start in range(0, width, 128):
@@ -585,95 +597,69 @@
             offset = nn(coarse[:, start:stop], swap) + nn(fine[:, start:stop], swap)
             upper = offset.astype(BF16)
             lower = (offset - upper.astype(F32)).astype(BF16)
-            extra_ref[:, start:stop] = jnp.where(even, upper, lower)
-
-    @pl.when(step == 0)
-    def _():
-        gain_sum_ref[...] = jnp.zeros_like(gain_sum_ref)
-
-    pl.when(step < steps)(tokens)
-
-    @pl.when(step == steps)
-    def _():
-        if split:
-            cols = raised // seq_count
-            wide = width // seq_count
-            rows = width // dp_count
-            for s in range(seq_count):
-                result = nn(normed_t[...], raise_ref[:, s * cols : (s + 1) * cols]).astype(BF16)
-                for d in range(dp_count):
-                    grad_ref[
-                        (d % 2) ^ own_ref[2], s ^ own_ref[0], (d // 2) ^ own_ref[1], :, wide:
-                    ] = result[d * rows : (d + 1) * rows, :]
-            result = nn(att_t[...], branch_ref[...]).astype(BF16)
-            for s in range(seq_count):
-                for d in range(dp_count):
-                    grad_ref[
-                        (d % 2) ^ own_ref[2], s ^ own_ref[0], (d // 2) ^ own_ref[1], :, :wide
-                    ] = result[d * rows : (d + 1) * rows, s * wide : (s + 1) * wide]
-        else:
-            grad_ref[:, :width] = nn(att_t[...], branch_ref[...]).astype(BF16)
-            for start in range(0, raised, 512):
-                grad_ref[:, width + start : width + start + 512] = nn(
-                    normed_t[...], raise_ref[:, start : start + 512]
-                ).astype(BF16)
-        hand_out(grad_ref, grad_outs, out_sem)
+            extra_ref[at, start:stop] = jnp.where(even, upper, lower)
+    gain_sum_ref[...] = gain_sum
+    if not split:
+        grad_ref[:, :width] = nn(att_t[...], branch_ref[...]).astype(BF16)
+        for start in range(0, raised, 512):
+            grad_ref[:, width + start : width + start + 512] = nn(
+                normed_t[...], raise_ref[:, start : start + 512]
+            ).astype(BF16)
+        hand_out(grad_ref, grad_outs, out_sems)
+        return
+    cols = raised // seq_count
+    wide = width // seq_count
+    rows = width // dp_count
+    copies = []
+
+    def keep(result, s, at):
+        for d in range(dp_count):
+            grad_ref[(d % 2) ^ own_ref[2], s ^ own_ref[0], (d // 2) ^ own_ref[1], :, at] = result[
+                d * rows : (d + 1) * rows, :
+            ]
+
+    result = nn(att_t[...], branch_ref[...]).astype(BF16)
+    for s in range(seq_count):
+        keep(result[:, s * wide : (s + 1) * wide], s, slice(0, wide))
+    for s in range(seq_count):
+        result = nn(normed_t[...], raise_ref[:, s * cols : (s + 1) * cols]).astype(BF16)
+        keep(result, s, slice(wide, wide + cols))
+        for core in range(2):
+            copy = pltpu.make_async_copy(
+                grad_ref.at[core, s ^ own_ref[0]],
+                grad_outs[core].at[s ^ own_ref[0]],
+                out_sems.at[len(copies)],
+            )
+            copies.append(copy)
+            copy.start()
+    finish(copies)
 
 
 def fall(own, cot, slope, normed, scale, att, den, gain, w_up, w_down, seq_count, dp_count, split):
     count, width = cot.shape
     raised = w_down.shape[0]
-    chunk = min(256, count)
-    steps = count // chunk
-
-    def rows(cols):
-        return pl.BlockSpec((chunk, cols), lambda i, own: (jnp.minimum(i, steps - 1), 0))
-
-    def whole(shape):
-        return pl.BlockSpec(shape, lambda i, own: (0, 0), pipeline_mode=pl.Buffered(1))
-
     if split:
         grad_shape = (2, seq_count, dp_count // 2, width // dp_count, (width + raised) // seq_count)
     else:
         grad_shape = (width, width + raised)
-    block = rows(width)
     grads = outs_of(grad_shape, split)
+    cfg = (seq_count, dp_count, split, min(512, count))
 
     def sds(dtype):
         return jax.ShapeDtypeStruct((count, width), dtype)
 
     return pl.pallas_call(
-        functools.partial(fall_kernel, (seq_count, dp_count, split)),
-        grid_spec=pltpu.PrefetchScalarGridSpec(
-            num_scalar_prefetch=1,
-            grid=(steps + 1,),
-            in_specs=[
-                block,
-                rows(raised),
-                block,
-                rows(128),
-                block,
-                rows(128),
-                whole((1, width)),
-                whole(w_up.shape),
-                whole(w_down.shape),
-            ],
-            out_specs=[
-                block,
-                block,
-                block,
-                whole((1, width)),
-            ]
-            + [pl.BlockSpec(memory_space=pl.ANY)] * len(grads),
-            scratch_shapes=[
-                pltpu.VMEM((count, raised), BF16),
-                pltpu.VMEM((width, count), BF16),
-                pltpu.VMEM((width, count), BF16),
-                pltpu.VMEM((count, width), BF16),
-                pltpu.VMEM(grad_shape, BF16),
-                pltpu.SemaphoreType.DMA((2,)),
-            ],
-        ),
+        functools.partial(fall_kernel, cfg),
+        in_specs=[pl.BlockSpec(memory_space=pltpu.SMEM)] + [IN_VMEM] * 9,
+        out_specs=[IN_VMEM] * 4 + [pl.BlockSpec(memory_space=pl.ANY)] * len(grads),
+        scratch_shapes=[
+            pltpu.VMEM((count, raised), BF16),
+            pltpu.VMEM((width, count), BF16),
+            pltpu.VMEM((width, count), BF16),
+            pltpu.VMEM((count, width), BF16),
+            pltpu.VMEM(grad_shape, BF16),
+            pltpu.SemaphoreType.DMA((2 * seq_count,)),
+        ],
         out_shape=[
             sds(F32),
             sds(BF16),
@@ -681,61 +667,46 @@
             jax.ShapeDtypeStruct((1, width), F32),
         ]
         + grads,
-        compiler_params=params(32),
+        compiler_params=params(24),
         cost_estimate=cost(8 * 2**30, 24 * 2**20),
         name="fall",
     )(own, cot, slope, normed, scale, att, den, gain, w_up, w_down)
 
 
-def last_kernel(parts, hidden_ref, first_ref, gain_ref, mask_ref, w_ref, *refs):
-    grads, (out_ref, sums_ref) = refs[:parts], refs[parts:]
-    back = 0.0
-    start = 0
-    for ref in grads:
-        stop = start + ref.shape[1]
-        back = back + nt(ref[...], w_ref[:, start:stop])
-        start = stop
-    normed, scale = norm_parts(hidden_ref[...])
-    grad = first_ref[...] + norm_back(back * gain_ref[...], normed, scale)
-    out_ref[...] = grad.astype(BF16)
-
-    @pl.when(pl.program_id(0) == 0)
-    def _():
-        sums_ref[...] = jnp.zeros_like(sums_ref)
-
-    mask = mask_ref[...].astype(BF16)
-    coarse = grad.astype(BF16)
-    fine = (grad - coarse.astype(F32)).astype(BF16)
-    masked = nn(mask, coarse) + nn(mask, fine)
-    sums_ref[0:1, :] += masked[0:1, :]
-    sums_ref[1:2, :] += jnp.sum(back * normed, axis=0, keepdims=True)
+def last_kernel(chunk, hidden_ref, first_ref, gain_ref, mask_ref, w_ref, *refs):
+    *grads, out_ref, sums_ref = refs
+    masked = gain_sum = 0.0
+    for top in range(0, hidden_ref.shape[0], chunk):
+        at = slice(top, top + chunk)
+        back = 0.0
+        start = 0
+        for ref in grads:
+            stop = start + ref.shape[1]
+            back = back + nt(ref[at, :], w_ref[:, start:stop])
+            start = stop
+        normed, scale = norm_parts(hidden_ref[at, :])
+        grad = first_ref[at, :] + norm_back(back * gain_ref[...], normed, scale)
+        coarse = grad.astype(BF16)
+        out_ref[at, :] = coarse
+        fine = (grad - coarse.astype(F32)).astype(BF16)
+        mask = mask_ref[:, at]
+        masked = masked + nn(mask, coarse) + nn(mask, fine)
+        gain_sum = gain_sum + jnp.sum(back * normed, axis=0, keepdims=True)
+    sums_ref[...] = masked
+    sums_ref[1:2, :] = gain_sum
 
 
 def last(hidden, grad_first, gain, mask, w_qkv, grads):
     count, width = hidden.shape
-    chunk = min(256, count)
-    blk = pl.BlockSpec((chunk, width), lambda i: (i, 0))
-
-    def whole(shape):
-        return pl.BlockSpec(shape, lambda i: (0, 0), pipeline_mode=pl.Buffered(1))
-
     return pl.pallas_call(
-        functools.partial(last_kernel, len(grads)),
-        grid=(count // chunk,),
-        in_specs=[
-            blk,
-            blk,
-            whole((1, width)),
-            pl.BlockSpec((8, chunk), lambda i: (0, i)),
-            whole(w_qkv.shape),
-        ]
-        + [pl.BlockSpec((chunk, g.shape[1]), lambda i: (i, 0)) for g in grads],
-        out_specs=[blk, whole((8, width))],
+        functools.partial(last_kernel, min(512, count)),
+        in_specs=[IN_VMEM] * (5 + len(grads)),
+        out_specs=[IN_VMEM] * 2,
         out_shape=[
             jax.ShapeDtypeStruct((count, width), BF16),
             jax.ShapeDtypeStruct((8, width), F32),
         ],
-        compiler_params=params(16),
+        compiler_params=params(14),
         cost_estimate=cost(6 * count * width * width, 12 * 2**20),
         name="last",
     )(hidden, grad_first, gain, mask, w_qkv, *grads)
@@ -888,10 +859,9 @@
         far = lax.all_gather(
             projected[:, width:], "seq", axis=0, tiled=True, axis_index_groups=groups
         )
-        shift = 0
+        attended, denominators = attend(projected, far, 0)
     else:
-        far, shift = projected, 4
-    attended, denominators = attend(projected, far, shift)
+        attended, denominators = attend_row(projected)
     if split:
         cot, line_up, attended = together(cot, line_up, attended)
         plane_down = jnp.stack([part[segment:] for part in cot])

time: 212 us -> 180 us (0.85); the launches traced: 212 us -> 177 us
  local copies, waits for them, and re-layouts: 25 us -> 11.8 us
  Pallas kernels: 79.3 us -> 68.9 us
  waiting for transfers between devices: 39.4 us -> 34.4 us
  starting transfers between devices: 52.6 us -> 48.6 us
  other arithmetic: 13.8 us -> 11.4 us
    unnamed x74 -> x40, local copies, waits for them, and re-layouts: 15.4 us -> 4.57 us
    pallas_call x5, Pallas kernels: 59.6 us -> 50.4 us  [the longest x1 15.2 us: rise(): pl.pallas_call(functools.partial(rise_kernel, cfg), in_specs=[pl.BlockSpe...]
    ppermute x43, waiting for transfers between devices: 39.4 us -> 34.4 us  [swap_along(): return lax.ppermute(value, axis, [(i, i ^ mask) for i in range(count)])]
    ppermute x43, starting transfers between devices: 52.6 us -> 48.6 us  [swap_along(): return lax.ppermute(value, axis, [(i, i ^ mask) for i in range(count)])]
    convert_element_type x3, other arithmetic: 3.15 us -> 1.02 us  [add_split(): add_up((left[j], right[j])).astype(BF16)]
  transfers between devices with their start and end apart: 43 -> 43, of which waited for: 12 -> 13; matrix products, arithmetic and copies ran while one was open for 9% -> 8% of each run, Pallas kernels for 28% -> 30%
where the time goes in v3:
time: 180 us; the launch traced here: 177 us
  Pallas kernels  68.9 us (38%)
  starting transfers between devices  48.6 us (27%)
  waiting for transfers between devices  34.4 us (19%)
  local copies, waits for them, and re-layouts  11.8 us (7%)
  other arithmetic  11.4 us (6%)
    ppermute x43, starting transfers between devices, swap_along(): return lax.ppermute(value, axis, [(i, i ^ mask) for i in range(count)])  48.6 us
    ppermute x43, waiting for transfers between devices, swap_along(): return lax.ppermute(value, axis, [(i, i ^ mask) for i in range(count)])  34.4 us
    pallas_call x1, Pallas kernels, rise(): pl.pallas_call(functools.partial(rise_kernel, cfg), in_specs=[pl.BlockSpe...  15.2 us
    pallas_call x1, Pallas kernels, attend_back_sum(): pl.pallas_call(functools.partial(attend_back_sum_kernel, min(512, count),...  14.4 us
    pallas_call x1, Pallas kernels, fall(): pl.pallas_call(functools.partial(fall_kernel, cfg), in_specs=[pl.BlockSpe...  12.2 us
    pallas_call x1, Pallas kernels, attend_back_half(): pl.pallas_call(functools.partial(attend_back_half_kernel, min(512, count)...  10.3 us
    pallas_call x1, Pallas kernels, attend_row(): pl.pallas_call(functools.partial(attend_row_kernel, min(256, count)), in_...  9.55 us
    unnamed x40, local copies, waits for them, and re-layouts  4.57 us
  transfers between devices with their start and end apart: 43, of which 13 were waited for; matrix products, arithmetic and copies ran while one was open for 8% of the time, Pallas kernels for 30%

profile of v3, /device:TPU:0, one launch (start us, length us, event | category | flops | bytes accessed | tf_op | source)
XLA Modules:
  0.0 176.8 jit_solution(13555805039433811566)
XLA Ops:
  2.4 3.1 %collective-permute-start.3 = (bf16[64,896]{1,0:T(8,128)(2,1)S(1)}, bf16[64,896]{1,0:T(8,128)(2,1)S(1)}, u32[]{:S(2)}, u32[]{:S(2)}) collective-permute-start(bf16[64,896]{1,0:T(8,128)(2,1)S(1)} %get-tuple-element.225), channel_id=1, source_target_pairs={{0,2},{1,3},{2,0},{3,1},{4,6},{5,7},{6,4},{7,5},{8,10},{9,11},{10,... | collective-permute-start | bytes 344072 | tf_op jit(solution)/shard_map/ppermute | solution.py:717
  5.5 2.6 %collective-permute-start.4 = (bf16[64,896]{1,0:T(8,128)(2,1)S(1)}, bf16[64,896]{1,0:T(8,128)(2,1)S(1)}, u32[]{:S(2)}, u32[]{:S(2)}) collective-permute-start(bf16[64,896]{1,0:T(8,128)(2,1)S(1)} %get-tuple-element.225), channel_id=1, source_target_pairs={{0,4},{1,5},{2,6},{3,7},{4,0},{5,1},{6,2},{7,3},{8,12},{9,13},{10,... | collective-permute-start | bytes 344072 | tf_op jit(solution)/shard_map/ppermute | solution.py:717
  10.2 2.7 %collective-permute-start.2 = (bf16[272,512]{1,0:T(8,128)(2,1)S(1)}, bf16[272,512]{1,0:T(8,128)(2,1)S(1)}, u32[]{:S(2)}, u32[]{:S(2)}) collective-permute-start(bf16[272,512]{1,0:T(8,128)(2,1)S(1)} %get-tuple-element.190), channel_id=1, source_target_pairs={{0,24},{8,16},{16,8},{24,0},{1,25},{9,17},{17,9},{25,1},{2,26},{10... | collective-permute-start | bytes 835592 | tf_op jit(solution)/shard_map/ppermute | solution.py:717
  15.4 1.8 %collective-permute-done.4 = bf16[64,896]{1,0:T(8,128)(2,1)S(1)} collective-permute-done((bf16[64,896]{1,0:T(8,128)(2,1)S(1)}, bf16[64,896]{1,0:T(8,128)(2,1)S(1)}, u32[]{:S(2)}, u32[]{:S(2)}) %collective-permute-start.4) | collective-permute-done | bytes 114720 | tf_op jit(solution)/shard_map/ppermute | solution.py:717
  17.4 1.6 collective-permute-start.6
  18.9 1.5 collective-permute-start.7
  20.5 6.6 %collective-permute-done = bf16[272,512]{1,0:T(8,128)(2,1)S(1)} collective-permute-done((bf16[272,512]{1,0:T(8,128)(2,1)S(1)}, bf16[272,512]{1,0:T(8,128)(2,1)S(1)}, u32[]{:S(2)}, u32[]{:S(2)}) %collective-permute-start) | collective-permute-done | bytes 278560 | tf_op jit(solution)/shard_map/ppermute | solution.py:717
  27.1 1.4 collective-permute-start.8
  29.3 3.6 %collective-permute-start.13 = (bf16[64,2560]{1,0:T(8,128)(2,1)}, bf16[64,2560]{1,0:T(8,128)(2,1)S(1)}, u32[]{:S(2)}, u32[]{:S(2)}) collective-permute-start(bf16[64,2560]{1,0:T(8,128)(2,1)} %pad_maximum_fusion.11), channel_id=1, source_target_pairs={{0,4},{1,5},{2,6},{3,7},{4,0},{5,1},{6,2},{7,3},{8,12},{9,13},{10,... | collective-permute-start | bytes 983048 | tf_op jit(solution)/shard_map/ppermute | solution.py:717
  32.9 1.9 %collective-permute-start.14 = (bf16[64,2560]{1,0:T(8,128)(2,1)}, bf16[64,2560]{1,0:T(8,128)(2,1)S(1)}, u32[]{:S(2)}, u32[]{:S(2)}) collective-permute-start(bf16[64,2560]{1,0:T(8,128)(2,1)} %pad_maximum_fusion.11), channel_id=1, source_target_pairs={{0,6},{1,7},{2,4},{3,5},{4,2},{5,3},{6,0},{7,1},{8,14},{9,15},{10,... | collective-permute-start | bytes 983048 | tf_op jit(solution)/shard_map/ppermute | solution.py:717
  37.4 2.0 %collective-permute-start.11 = (bf16[512,512]{1,0:T(8,128)(2,1)S(1)}, bf16[512,512]{1,0:T(8,128)(2,1)S(1)}, u32[]{:S(2)}, u32[]{:S(2)}) collective-permute-start(bf16[512,512]{1,0:T(8,128)(2,1)S(1)} %get-tuple-element.220), channel_id=1, source_target_pairs={{0,24},{8,16},{16,8},{24,0},{1,25},{9,17},{17,9},{25,1},{2,26},{10... | collective-permute-start | bytes 1572872 | tf_op jit(solution)/shard_map/ppermute | solution.py:717
  39.4 4.1 %project.1 = (bf16[1024,512]{1,0:T(8,128)(2,1)S(1)}, bf16[1024,1536]{1,0:T(8,128)(2,1)S(1)}, bf16[512,1536]{1,0:T(8,128)(2,1)S(1)}) custom-call(s32[3]{0:T(128)S(1)} %pad_add_fusion.own_ref, f32[1024,512]{1,0:T(8,128)S(1)} %multiply_add_fusion.hidden_ref, f32[1,512]{1,0:T(1,128)S(1)} %bitcast.113, bf16[4,4,64,384]{3,2,1,0:T(8,128)(2,1)S(1)} %pad_maximum_fusion.5.refs_0_, ...), custom_call_target="tpu_custom_call" | custom-call | flops 1610612736 | bytes 8388608 | tf_op jit(solution)/shard_map/project/pallas_call | solution.py:401
  45.2 9.6 %attend_row.1 = (bf16[1024,512]{1,0:T(8,128)(2,1)S(1)}, f32[1024,128]{1,0:T(8,128)S(1)}) custom-call(bf16[1024,1536]{1,0:T(8,128)(2,1)S(1)} %get-tuple-element.95.own_ref.proj_ref), custom_call_target="tpu_custom_call" | custom-call | flops 17179869184 | bytes 5242880 | tf_op jit(solution)/shard_map/attend_row/pallas_call | solution.py:120
  56.5 5.4 %collective-permute-done.10 = bf16[512,512]{1,0:T(8,128)(2,1)S(1)} collective-permute-done((bf16[512,512]{1,0:T(8,128)(2,1)S(1)}, bf16[512,512]{1,0:T(8,128)(2,1)S(1)}, u32[]{:S(2)}, u32[]{:S(2)}) %collective-permute-start.10) | collective-permute-done | bytes 524320 | tf_op jit(solution)/shard_map/ppermute | solution.py:717
  67.9 1.3 pad_maximum_fusion.1.cot_ref
  70.4 15.2 %rise.1 = (bf16[1024,512]{1,0:T(8,128)(2,1)S(1)}, f32[1024,512]{1,0:T(8,128)S(1)}, f32[1024,128]{1,0:T(8,128)S(1)}, bf16[1024,2048]{1,0:T(8,128)(2,1)S(1)}, bf16...) custom-call(s32[3]{0:T(128)S(1)} %pad_add_fusion.own_ref, ...), custom_call_target="tpu_custom_call" | custom-call | flops 7516192768 | bytes 25165824 | tf_op jit(solution)/shard_map/rise/pallas_call | solution.py:506
  86.2 1.5 collective-permute-start.19
  89.7 12.2 %fall.1 = (f32[1024,512]{1,0:T(8,128)S(1)}, bf16[1024,512]{1,0:T(8,128)(2,1)S(1)}, bf16[1024,512]{1,0:T(8,128)(2,1)S(1)}, f32[1,512]{1,0:T(1,128)S(1)}, bf16[4,4...) custom-call(s32[3]{0:T(128)S(1)} %pad_add_fusion.own_ref, ...), custom_call_target="tpu_custom_call" | custom-call | flops 8589934592 | bytes 25165824 | tf_op jit(solution)/shard_map/fall/pallas_call | solution.py:651
  102.5 3.0 %collective-permute-start.27 = (bf16[4,2,128,128]{3,2,1,0:T(8,128)(2,1)S(1)}, bf16[4,2,128,128]{3,2,1,0:T(8,128)(2,1)S(1)}, u32[]{:S(2)}, u32[]{:S(2)}) collective-permute-start(bf16[4,2,128,128]{3,2,1,0:T(8,128)(2,1)S(1)} %get-tuple-element.176), channel_id=1, source_target_pairs={{0,4},{1,5},{2,6},{3,7},{4,0},{5,1},{6,2},{7,3},{8,12},{9,13},{10,... | collective-permute-start | bytes 786440 | tf_op jit(solution)/shard_map/ppermute | solution.py:717
  106.8 10.3 %attend_back_half.1 = (bf16[1024,256]{1,0:T(8,128)(2,1)S(1)}, bf16[1024,256]{1,0:T(8,128)(2,1)S(1)}, bf16[1024,256]{1,0:T(8,128)(2,1)S(1)}) custom-call(bf16[1024,1536]{1,0:T(8,128)(2,1)S(1)} %copy-done.7, bf16[1024,512]{1,0:T(8,128)(2,1)S(1)} %get-tuple-element.125.s_ref, bf16[1024,512]{1,0:T(8,128)(2,1)S(1)} %get-tuple-element.126.x_ref), custom_call_target="tpu_custom_call" | custom-call | flops 17179869184 | bytes 6291456 | tf_op jit(solution)/shard_map/attend_back_half/pallas_call | solution.py:192
  117.5 1.5 collective-permute-start.24
  121.0 14.4 %attend_back_sum.1 = (bf16[1024,256]{1,0:T(8,128)(2,1)S(1)}, bf16[1024,256]{1,0:T(8,128)(2,1)S(1)}, bf16[1024,256]{1,0:T(8,128)(2,1)S(1)}, bf16[4,4,3,64,128]{4,...) custom-call(s32[3]{0:T(128)S(1)} %pad_add_fusion.own_ref, bf16[1024,1536]{1,0:T(8,128)(2,1)S(1)} %copy-done.7, ...), custom_call_target="tpu_custom_call" | custom-call | flops 21474836480 | bytes 10485760 | tf_op jit(solution)/shard_map/attend_back_sum/pallas_call | solution.py:259
  136.5 1.4 collective-permute-done.29
  138.2 1.9 %collective-permute-start.36 = (bf16[16,64,128]{2,1,0:T(8,128)(2,1)S(1)}, bf16[16,64,128]{2,1,0:T(8,128)(2,1)S(1)}, u32[]{:S(2)}, u32[]{:S(2)}) collective-permute-start(bf16[16,64,128]{2,1,0:T(8,128)(2,1)S(1)} %pad_maximum_fusion.15), channel_id=1, source_target_pairs={{0,24},{8,16},{16,8},{24,0},{1,25},{9,17},{17,9},{25,1},{2,26},{10... | collective-permute-start | bytes 786440 | tf_op jit(solution)/shard_map/ppermute | solution.py:717
  141.3 3.2 %last.1 = (bf16[1024,512]{1,0:T(8,128)(2,1)S(1)}, f32[8,512]{1,0:T(8,128)S(1)}) custom-call(f32[1024,512]{1,0:T(8,128)S(1)} %multiply_add_fusion.hidden_ref, f32[1024,512]{1,0:T(8,128)S(1)} %get-tuple-element.122.first_ref, f32[1,512]{1,0:T(1,128)S(1)} %bitcast.114, bf16[8,1024]{1,0:T(8,128)(2,1)S(1)} %broadcast_in_dim.34.mask_ref, ...), custom_call_target="tpu_custom_call" | custom-call | flops 1610612736 | bytes 12582912 | tf_op jit(solution)/shard_map/last/pallas_call | solution.py:701
  148.0 6.2 %collective-permute-done.31 = f32[16,512]{1,0:T(8,128)S(1)} collective-permute-done((f32[16,512]{1,0:T(8,128)S(1)}, f32[16,512]{1,0:T(8,128)S(1)}, u32[]{:S(2)}, u32[]{:S(2)}) %collective-permute-start.31) | collective-permute-done | bytes 32800 | tf_op jit(solution)/shard_map/ppermute | solution.py:717
  155.1 3.0 %collective-permute-done.32 = f32[16,512]{1,0:T(8,128)S(1)} collective-permute-done((f32[16,512]{1,0:T(8,128)S(1)}, f32[16,512]{1,0:T(8,128)S(1)}, u32[]{:S(2)}, u32[]{:S(2)}) %collective-permute-start.32) | collective-permute-done | bytes 32800 | tf_op jit(solution)/shard_map/ppermute | solution.py:717
  158.4 1.5 collective-permute-start.42
  160.0 1.7 collective-permute-start.40
  166.1 1.4 collective-permute-done.40
  168.9 2.9 %collective-permute-done.41 = bf16[1,4,64,128]{3,2,1,0:T(8,128)(2,1)S(1)} collective-permute-done((bf16[1,4,64,128]{3,2,1,0:T(8,128)(2,1)S(1)}, bf16[1,4,64,128]{3,2,1,0:T(8,128)(2,1)S(1)}, u32[]{:S(2)}, u32[]{:S(2)}) %collective-permute-start.41) | collective-permute-done | bytes 65568 | tf_op jit(solution)/shard_map/ppermute | solution.py:717
  173.1 2.2 %collective-permute-done.38 = bf16[256,512]{1,0:T(8,128)(2,1)S(1)} collective-permute-done((bf16[256,512]{1,0:T(8,128)(2,1)S(1)}, bf16[256,512]{1,0:T(8,128)(2,1)S(1)}, u32[]{:S(2)}, u32[]{:S(2)}) %collective-permute-start.38) | collective-permute-done | bytes 262176 | tf_op jit(solution)/shard_map/ppermute | solution.py:717
  (177 shorter events, 42.5 us)
Async XLA Ops:
  2.4 12.6 %collective-permute-start.3 = (bf16[64,896]{1,0:T(8,128)(2,1)S(1)}, bf16[64,896]{1,0:T(8,128)(2,1)S(1)}, u32[]{:S(2)}, u32[]{:S(2)}) collective-permute-start(bf16[64,896]{1,0:T(8,128)(2,1)S(1)} %get-tuple-element.225), channel_id=1, source_target_pairs={{0,2},{1,3},{2,0},{3,1},{4,6},{5,7},{6,4},{7,5},{8,10},{9,11},{10,... | collective-permute-start | bytes 344072 | tf_op jit(solution)/shard_map/ppermute | solution.py:717
  5.5 11.7 %collective-permute-start.4 = (bf16[64,896]{1,0:T(8,128)(2,1)S(1)}, bf16[64,896]{1,0:T(8,128)(2,1)S(1)}, u32[]{:S(2)}, u32[]{:S(2)}) collective-permute-start(bf16[64,896]{1,0:T(8,128)(2,1)S(1)} %get-tuple-element.225), channel_id=1, source_target_pairs={{0,4},{1,5},{2,6},{3,7},{4,0},{5,1},{6,2},{7,3},{8,12},{9,13},{10,... | collective-permute-start | bytes 344072 | tf_op jit(solution)/shard_map/ppermute | solution.py:717
  10.2 19.1 %collective-permute-start.2 = (bf16[272,512]{1,0:T(8,128)(2,1)S(1)}, bf16[272,512]{1,0:T(8,128)(2,1)S(1)}, u32[]{:S(2)}, u32[]{:S(2)}) collective-permute-start(bf16[272,512]{1,0:T(8,128)(2,1)S(1)} %get-tuple-element.190), channel_id=1, source_target_pairs={{0,24},{8,16},{16,8},{24,0},{1,25},{9,17},{17,9},{25,1},{2,26},{10... | collective-permute-start | bytes 835592 | tf_op jit(solution)/shard_map/ppermute | solution.py:717
  13.0 15.6 %collective-permute-start.1 = (bf16[272,512]{1,0:T(8,128)(2,1)S(1)}, bf16[272,512]{1,0:T(8,128)(2,1)S(1)}, u32[]{:S(2)}, u32[]{:S(2)}) collective-permute-start(bf16[272,512]{1,0:T(8,128)(2,1)S(1)} %get-tuple-element.189), channel_id=1, source_target_pairs={{0,16},{8,24},{16,0},{24,8},{1,17},{9,25},{17,1},{25,9},{2,18},{10... | collective-permute-start | bytes 835592 | tf_op jit(solution)/shard_map/ppermute | solution.py:717
  15.0 12.0 %collective-permute-start = (bf16[272,512]{1,0:T(8,128)(2,1)S(1)}, bf16[272,512]{1,0:T(8,128)(2,1)S(1)}, u32[]{:S(2)}, u32[]{:S(2)}) collective-permute-start(bf16[272,512]{1,0:T(8,128)(2,1)S(1)} %get-tuple-element.188), channel_id=1, source_target_pairs={{0,8},{8,0},{16,24},{24,16},{1,9},{9,1},{17,25},{25,17},{2,10},{10... | collective-permute-start | bytes 835592 | tf_op jit(solution)/shard_map/ppermute | solution.py:717
  17.4 15.5 %collective-permute-start.6 = (bf16[4,64,384]{2,1,0:T(8,128)(2,1)S(1)}, bf16[4,64,384]{2,1,0:T(8,128)(2,1)S(1)}, u32[]{:S(2)}, u32[]{:S(2)}) collective-permute-start(bf16[4,64,384]{2,1,0:T(8,128)(2,1)S(1)} %get-tuple-element.215), channel_id=1, source_target_pairs={{0,8},{8,0},{16,24},{24,16},{1,9},{9,1},{17,25},{25,17},{2,10},{10... | collective-permute-start | bytes 589832 | tf_op jit(solution)/shard_map/ppermute | solution.py:717
  18.9 15.9 %collective-permute-start.7 = (bf16[4,64,384]{2,1,0:T(8,128)(2,1)S(1)}, bf16[4,64,384]{2,1,0:T(8,128)(2,1)S(1)}, u32[]{:S(2)}, u32[]{:S(2)}) collective-permute-start(bf16[4,64,384]{2,1,0:T(8,128)(2,1)S(1)} %get-tuple-element.215), channel_id=1, source_target_pairs={{0,16},{8,24},{16,0},{24,8},{1,17},{9,25},{17,1},{25,9},{2,18},{10... | collective-permute-start | bytes 589832 | tf_op jit(solution)/shard_map/ppermute | solution.py:717
  28.5 16.1 %collective-permute-start.12 = (bf16[64,2560]{1,0:T(8,128)(2,1)}, bf16[64,2560]{1,0:T(8,128)(2,1)S(1)}, u32[]{:S(2)}, u32[]{:S(2)}) collective-permute-start(bf16[64,2560]{1,0:T(8,128)(2,1)} %pad_maximum_fusion.11), channel_id=1, source_target_pairs={{0,2},{1,3},{2,0},{3,1},{4,6},{5,7},{6,4},{7,5},{8,10},{9,11},{10,... | collective-permute-start | bytes 983048 | tf_op jit(solution)/shard_map/ppermute | solution.py:717
  29.3 27.2 %collective-permute-start.13 = (bf16[64,2560]{1,0:T(8,128)(2,1)}, bf16[64,2560]{1,0:T(8,128)(2,1)S(1)}, u32[]{:S(2)}, u32[]{:S(2)}) collective-permute-start(bf16[64,2560]{1,0:T(8,128)(2,1)} %pad_maximum_fusion.11), channel_id=1, source_target_pairs={{0,4},{1,5},{2,6},{3,7},{4,0},{5,1},{6,2},{7,3},{8,12},{9,13},{10,... | collective-permute-start | bytes 983048 | tf_op jit(solution)/shard_map/ppermute | solution.py:717
  32.9 23.6 %collective-permute-start.14 = (bf16[64,2560]{1,0:T(8,128)(2,1)}, bf16[64,2560]{1,0:T(8,128)(2,1)S(1)}, u32[]{:S(2)}, u32[]{:S(2)}) collective-permute-start(bf16[64,2560]{1,0:T(8,128)(2,1)} %pad_maximum_fusion.11), channel_id=1, source_target_pairs={{0,6},{1,7},{2,4},{3,5},{4,2},{5,3},{6,0},{7,1},{8,14},{9,15},{10,... | collective-permute-start | bytes 983048 | tf_op jit(solution)/shard_map/ppermute | solution.py:717
  36.4 25.6 %collective-permute-start.10 = (bf16[512,512]{1,0:T(8,128)(2,1)S(1)}, bf16[512,512]{1,0:T(8,128)(2,1)S(1)}, u32[]{:S(2)}, u32[]{:S(2)}) collective-permute-start(bf16[512,512]{1,0:T(8,128)(2,1)S(1)} %get-tuple-element.222), channel_id=1, source_target_pairs={{0,16},{8,24},{16,0},{24,8},{1,17},{9,25},{17,1},{25,9},{2,18},{10... | collective-permute-start | bytes 1572872 | tf_op jit(solution)/shard_map/ppermute | solution.py:717
  37.4 24.6 %collective-permute-start.11 = (bf16[512,512]{1,0:T(8,128)(2,1)S(1)}, bf16[512,512]{1,0:T(8,128)(2,1)S(1)}, u32[]{:S(2)}, u32[]{:S(2)}) collective-permute-start(bf16[512,512]{1,0:T(8,128)(2,1)S(1)} %get-tuple-element.220), channel_id=1, source_target_pairs={{0,24},{8,16},{16,8},{24,0},{1,25},{9,17},{17,9},{25,1},{2,26},{10... | collective-permute-start | bytes 1572872 | tf_op jit(solution)/shard_map/ppermute | solution.py:717
  44.6 18.5 %collective-permute-start.9 = (bf16[512,512]{1,0:T(8,128)(2,1)S(1)}, bf16[512,512]{1,0:T(8,128)(2,1)S(1)}, u32[]{:S(2)}, u32[]{:S(2)}) collective-permute-start(bf16[512,512]{1,0:T(8,128)(2,1)S(1)} %get-tuple-element.221), channel_id=1, source_target_pairs={{0,8},{8,0},{16,24},{24,16},{1,9},{9,1},{17,25},{25,17},{2,10},{10... | collective-permute-start | bytes 1572872 | tf_op jit(solution)/shard_map/ppermute | solution.py:717
  85.7 16.3 %collective-permute-start.18 = (bf16[4,4,2,128,128]{4,3,2,1,0:T(8,128)(2,1)S(1)}, bf16[4,4,2,128,128]{4,3,2,1,0:T(8,128)(2,1)S(1)}, u32[]{:S(2)}, u32[]{:S(2)}) collective-permute-start(bf16[4,4,2,128,128]{4,3,2,1,0:T(8,128)(2,1)S(1)} %get-tuple-element.107), channel_id=1, source_target_pairs={{0,1},{1,0},{2,3},{3,2},{4,5},{5,4},{6,7},{7,6},{8,9},{9,8},{10,11... | collective-permute-start | bytes 3145736 | tf_op jit(solution)/shard_map/ppermute | solution.py:717
  86.2 15.7 %collective-permute-start.19 = (bf16[256,512]{1,0:T(8,128)(2,1)S(1)}, bf16[256,512]{1,0:T(8,128)(2,1)S(1)}, u32[]{:S(2)}, u32[]{:S(2)}) collective-permute-start(bf16[256,512]{1,0:T(8,128)(2,1)S(1)} %get-tuple-element.200), channel_id=1, source_target_pairs={{0,8},{8,0},{16,24},{24,16},{1,9},{9,1},{17,25},{25,17},{2,10},{10... | collective-permute-start | bytes 786440 | tf_op jit(solution)/shard_map/ppermute | solution.py:717
  87.7 14.2 %collective-permute-start.20 = (bf16[256,512]{1,0:T(8,128)(2,1)S(1)}, bf16[256,512]{1,0:T(8,128)(2,1)S(1)}, u32[]{:S(2)}, u32[]{:S(2)}) collective-permute-start(bf16[256,512]{1,0:T(8,128)(2,1)S(1)} %get-tuple-element.199), channel_id=1, source_target_pairs={{0,16},{8,24},{16,0},{24,8},{1,17},{9,25},{17,1},{25,9},{2,18},{10... | collective-permute-start | bytes 786440 | tf_op jit(solution)/shard_map/ppermute | solution.py:717
  88.6 13.3 %collective-permute-start.21 = (bf16[256,512]{1,0:T(8,128)(2,1)S(1)}, bf16[256,512]{1,0:T(8,128)(2,1)S(1)}, u32[]{:S(2)}, u32[]{:S(2)}) collective-permute-start(bf16[256,512]{1,0:T(8,128)(2,1)S(1)} %get-tuple-element.198), channel_id=1, source_target_pairs={{0,24},{8,16},{16,8},{24,0},{1,25},{9,17},{17,9},{25,1},{2,26},{10... | collective-permute-start | bytes 786440 | tf_op jit(solution)/shard_map/ppermute | solution.py:717
  102.3 14.7 %collective-permute-start.23 = (bf16[4,2,128,128]{3,2,1,0:T(8,128)(2,1)S(1)}, bf16[4,2,128,128]{3,2,1,0:T(8,128)(2,1)S(1)}, u32[]{:S(2)}, u32[]{:S(2)}) collective-permute-start(bf16[4,2,128,128]{3,2,1,0:T(8,128)(2,1)S(1)} %get-tuple-element.178), channel_id=1, source_target_pairs={{0,2},{1,3},{2,0},{3,1},{4,6},{5,7},{6,4},{7,5},{8,10},{9,11},{10,... | collective-permute-start | bytes 786440 | tf_op jit(solution)/shard_map/ppermute | solution.py:717
  102.4 14.7 %collective-permute-start.22 = (bf16[4,4,64,640]{3,2,1,0:T(8,128)(2,1)S(1)}, bf16[4,4,64,640]{3,2,1,0:T(8,128)(2,1)S(1)}, u32[]{:S(2)}, u32[]{:S(2)}) collective-permute-start(bf16[4,4,64,640]{3,2,1,0:T(8,128)(2,1)S(1)} %get-tuple-element.124), channel_id=1, source_target_pairs={{0,1},{1,0},{2,3},{3,2},{4,5},{5,4},{6,7},{7,6},{8,9},{9,8},{10,11... | collective-permute-start | bytes 3932168 | tf_op jit(solution)/shard_map/ppermute | solution.py:717
  102.5 33.0 %collective-permute-start.27 = (bf16[4,2,128,128]{3,2,1,0:T(8,128)(2,1)S(1)}, bf16[4,2,128,128]{3,2,1,0:T(8,128)(2,1)S(1)}, u32[]{:S(2)}, u32[]{:S(2)}) collective-permute-start(bf16[4,2,128,128]{3,2,1,0:T(8,128)(2,1)S(1)} %get-tuple-element.176), channel_id=1, source_target_pairs={{0,4},{1,5},{2,6},{3,7},{4,0},{5,1},{6,2},{7,3},{8,12},{9,13},{10,... | collective-permute-start | bytes 786440 | tf_op jit(solution)/shard_map/ppermute | solution.py:717
  105.5 30.0 %collective-permute-start.28 = (bf16[4,2,128,128]{3,2,1,0:T(8,128)(2,1)S(1)}, bf16[4,2,128,128]{3,2,1,0:T(8,128)(2,1)S(1)}, u32[]{:S(2)}, u32[]{:S(2)}) collective-permute-start(bf16[4,2,128,128]{3,2,1,0:T(8,128)(2,1)S(1)} %get-tuple-element.175), channel_id=1, source_target_pairs={{0,6},{1,7},{2,4},{3,5},{4,2},{5,3},{6,0},{7,1},{8,14},{9,15},{10,... | collective-permute-start | bytes 786440 | tf_op jit(solution)/shard_map/ppermute | solution.py:717
  117.5 18.0 %collective-permute-start.24 = (bf16[4,64,640]{2,1,0:T(8,128)(2,1)S(1)}, bf16[4,64,640]{2,1,0:T(8,128)(2,1)S(1)}, u32[]{:S(2)}, u32[]{:S(2)}) collective-permute-start(bf16[4,64,640]{2,1,0:T(8,128)(2,1)S(1)} %get-tuple-element.173), channel_id=1, source_target_pairs={{0,8},{8,0},{16,24},{24,16},{1,9},{9,1},{17,25},{25,17},{2,10},{10... | collective-permute-start | bytes 983048 | tf_op jit(solution)/shard_map/ppermute | solution.py:717
  119.0 16.5 %collective-permute-start.25 = (bf16[4,64,640]{2,1,0:T(8,128)(2,1)S(1)}, bf16[4,64,640]{2,1,0:T(8,128)(2,1)S(1)}, u32[]{:S(2)}, u32[]{:S(2)}) collective-permute-start(bf16[4,64,640]{2,1,0:T(8,128)(2,1)S(1)} %get-tuple-element.172), channel_id=1, source_target_pairs={{0,16},{8,24},{16,0},{24,8},{1,17},{9,25},{17,1},{25,9},{2,18},{10... | collective-permute-start | bytes 983048 | tf_op jit(solution)/shard_map/ppermute | solution.py:717
  119.9 15.6 %collective-permute-start.26 = (bf16[4,64,640]{2,1,0:T(8,128)(2,1)S(1)}, bf16[4,64,640]{2,1,0:T(8,128)(2,1)S(1)}, u32[]{:S(2)}, u32[]{:S(2)}) collective-permute-start(bf16[4,64,640]{2,1,0:T(8,128)(2,1)S(1)} %get-tuple-element.171), channel_id=1, source_target_pairs={{0,24},{8,16},{16,8},{24,0},{1,25},{9,17},{17,9},{25,1},{2,26},{10... | collective-permute-start | bytes 983048 | tf_op jit(solution)/shard_map/ppermute | solution.py:717
  135.9 22.1 %collective-permute-start.33 = (bf16[2,64,640]{2,1,0:T(8,128)(2,1)S(1)}, bf16[2,64,640]{2,1,0:T(8,128)(2,1)S(1)}, u32[]{:S(2)}, u32[]{:S(2)}) collective-permute-start(bf16[2,64,640]{2,1,0:T(8,128)(2,1)S(1)} %slice.310), channel_id=1, source_target_pairs={{0,4},{1,5},{2,6},{3,7},{4,0},{5,1},{6,2},{7,3},{8,12},{9,13},{10,... | collective-permute-start | bytes 491528 | tf_op jit(solution)/shard_map/ppermute | solution.py:717
  138.2 19.9 %collective-permute-start.36 = (bf16[16,64,128]{2,1,0:T(8,128)(2,1)S(1)}, bf16[16,64,128]{2,1,0:T(8,128)(2,1)S(1)}, u32[]{:S(2)}, u32[]{:S(2)}) collective-permute-start(bf16[16,64,128]{2,1,0:T(8,128)(2,1)S(1)} %pad_maximum_fusion.15), channel_id=1, source_target_pairs={{0,24},{8,16},{16,8},{24,0},{1,25},{9,17},{17,9},{25,1},{2,26},{10... | collective-permute-start | bytes 786440 | tf_op jit(solution)/shard_map/ppermute | solution.py:717
  140.1 18.0 %collective-permute-start.35 = (bf16[16,64,128]{2,1,0:T(8,128)(2,1)S(1)}, bf16[16,64,128]{2,1,0:T(8,128)(2,1)S(1)}, u32[]{:S(2)}, u32[]{:S(2)}) collective-permute-start(bf16[16,64,128]{2,1,0:T(8,128)(2,1)S(1)} %pad_maximum_fusion.14), channel_id=1, source_target_pairs={{0,16},{8,24},{16,0},{24,8},{1,17},{9,25},{17,1},{25,9},{2,18},{10... | collective-permute-start | bytes 786440 | tf_op jit(solution)/shard_map/ppermute | solution.py:717
  144.7 13.4 %collective-permute-start.34 = (bf16[16,64,128]{2,1,0:T(8,128)(2,1)S(1)}, bf16[16,64,128]{2,1,0:T(8,128)(2,1)S(1)}, u32[]{:S(2)}, u32[]{:S(2)}) collective-permute-start(bf16[16,64,128]{2,1,0:T(8,128)(2,1)S(1)} %pad_maximum_fusion.13), channel_id=1, source_target_pairs={{0,8},{8,0},{16,24},{24,16},{1,9},{9,1},{17,25},{25,17},{2,10},{10... | collective-permute-start | bytes 786440 | tf_op jit(solution)/shard_map/ppermute | solution.py:717
  158.4 9.2 %collective-permute-start.42 = (bf16[1,64,640]{2,1,0:T(8,128)(2,1)S(1)}, bf16[1,64,640]{2,1,0:T(8,128)(2,1)S(1)}, u32[]{:S(2)}, u32[]{:S(2)}) collective-permute-start(bf16[1,64,640]{2,1,0:T(8,128)(2,1)S(1)} %slice.324), channel_id=1, source_target_pairs={{0,2},{1,3},{2,0},{3,1},{4,6},{5,7},{6,4},{7,5},{8,10},{9,11},{10,... | collective-permute-start | bytes 245768 | tf_op jit(solution)/shard_map/ppermute | solution.py:717
  162.5 10.6 %collective-permute-start.37 = (bf16[256,512]{1,0:T(8,128)(2,1)S(1)}, bf16[256,512]{1,0:T(8,128)(2,1)S(1)}, u32[]{:S(2)}, u32[]{:S(2)}) collective-permute-start(bf16[256,512]{1,0:T(8,128)(2,1)S(1)} %get-tuple-element.193), channel_id=1, source_target_pairs={{0,24},{8,16},{16,8},{24,0},{1,25},{9,17},{17,9},{25,1},{2,26},{10... | collective-permute-start | bytes 786440 | tf_op jit(solution)/shard_map/ppermute | solution.py:717
  163.8 11.5 %collective-permute-start.38 = (bf16[256,512]{1,0:T(8,128)(2,1)S(1)}, bf16[256,512]{1,0:T(8,128)(2,1)S(1)}, u32[]{:S(2)}, u32[]{:S(2)}) collective-permute-start(bf16[256,512]{1,0:T(8,128)(2,1)S(1)} %get-tuple-element.192), channel_id=1, source_target_pairs={{0,16},{8,24},{16,0},{24,8},{1,17},{9,25},{17,1},{25,9},{2,18},{10... | collective-permute-start | bytes 786440 | tf_op jit(solution)/shard_map/ppermute | solution.py:717
  164.9 10.5 %collective-permute-start.39 = (bf16[256,512]{1,0:T(8,128)(2,1)S(1)}, bf16[256,512]{1,0:T(8,128)(2,1)S(1)}, u32[]{:S(2)}, u32[]{:S(2)}) collective-permute-start(bf16[256,512]{1,0:T(8,128)(2,1)S(1)} %get-tuple-element.191), channel_id=1, source_target_pairs={{0,8},{8,0},{16,24},{24,16},{1,9},{9,1},{17,25},{25,17},{2,10},{10... | collective-permute-start | bytes 786440 | tf_op jit(solution)/shard_map/ppermute | solution.py:717
  (32 other events, 194.7 us)

commit v4 on v3

--- a/solution.py
+++ b/solution.py
@@ -125,7 +125,7 @@
             jax.ShapeDtypeStruct((count, width), BF16),
             jax.ShapeDtypeStruct((count, 128), F32),
         ],
-        compiler_params=params(12),
+        compiler_params=params(8),
         cost_estimate=cost(16 * count * count * 1024, 5 * 2**20),
         name="attend_row",
     )(projected)
@@ -194,7 +194,7 @@
         in_specs=[IN_VMEM] * 3,
         out_specs=[IN_VMEM] * 3,
         out_shape=[jax.ShapeDtypeStruct((count, width // 2), BF16)] * 3,
-        compiler_params=params(14),
+        compiler_params=params(10),
         cost_estimate=cost(16 * count * count * 1024, 6 * 2**20),
         name="attend_back_half",
     )(projected, scaled, extra)
@@ -267,7 +267,7 @@
             pltpu.SemaphoreType.DMA((2,)),
         ],
         out_shape=[jax.ShapeDtypeStruct((count, width // 2), BF16)] * 3 + outs_of(pieces, True),
-        compiler_params=params(18),
+        compiler_params=params(12),
         cost_estimate=cost(20 * count * count * 1024, 10 * 2**20),
         name="attend_back_sum",
     )(own, projected, scaled, extra, normed, *first_half)
@@ -335,7 +335,11 @@
     return copies
 
 
-def fetches(own_ref, refs, target, sems):
+def fetches(own_ref, refs, target, sems, cols=None):
+    if cols is not None:
+        axes = len(refs[0].shape) - 1
+        refs = [ref.at[(slice(None),) * axes + (cols,)] for ref in refs]
+        target = target.at[:, cols]
     if len(refs) == 2:
         return place_blocks(own_ref, refs, target, sems)
     return [pltpu.make_async_copy(refs[0], target, sems.at[0])]
@@ -374,50 +378,50 @@
     return max(1, count * len(parts))
 
 
-def project_kernel(parts, own_ref, hidden_ref, gain_ref, *refs):
-    sources, (normed_ref, out_ref, whole_ref, sems) = refs[:parts], refs[parts:]
-
-    @pl.when(pl.program_id(0) == 0)
-    def _():
-        launch(fetches(own_ref, sources, whole_ref, sems))
-
-    normed = (norm_parts(hidden_ref[...])[0] * gain_ref[...]).astype(BF16)
-    normed_ref[...] = normed
-
-    @pl.when(pl.program_id(0) == 0)
-    def _():
-        finish(fetches(own_ref, sources, whole_ref, sems))
-
-    out_ref[...] = nn(normed, whole_ref[...]).astype(BF16)
+def project_kernel(chunk, parts, own_ref, hidden_ref, gain_ref, *refs):
+    sources, (normed_out, out_ref, whole_out, normed_ref, whole_ref, sems, out_sems) = (
+        refs[:parts],
+        refs[parts:],
+    )
+    copies = fetches(own_ref, sources, whole_ref, sems)
+    launch(copies)
+    count = hidden_ref.shape[0]
+    for row in range(0, count, chunk):
+        at = slice(row, row + chunk)
+        normed_ref[at, :] = (norm_parts(hidden_ref[at, :])[0] * gain_ref[...]).astype(BF16)
+    finish(copies)
+    copies = [
+        pltpu.make_async_copy(normed_ref, normed_out, out_sems.at[0]),
+        pltpu.make_async_copy(whole_ref, whole_out, out_sems.at[1]),
+    ]
+    launch(copies)
+    for row in range(0, count, chunk):
+        at = slice(row, row + chunk)
+        out_ref[at, :] = nn(normed_ref[at, :], whole_ref[...]).astype(BF16)
+    finish(copies)
 
 
 def project(own, hidden, gain, parts, cols):
     count, width = hidden.shape
-    chunk = min(512, count)
-
-    def rows(cols):
-        return pl.BlockSpec((chunk, cols), lambda i, own: (i, 0))
-
+    in_hbm = pl.BlockSpec(memory_space=pltpu.HBM)
     return pl.pallas_call(
-        functools.partial(project_kernel, len(parts)),
-        grid_spec=pltpu.PrefetchScalarGridSpec(
-            num_scalar_prefetch=1,
-            grid=(count // chunk,),
-            in_specs=[rows(width), pl.BlockSpec((1, width), lambda i, own: (0, 0))]
-            + [pl.BlockSpec(memory_space=pl.ANY)] * len(parts),
-            out_specs=[
-                rows(width),
-                rows(cols),
-                pl.BlockSpec((width, cols), lambda i, own: (0, 0)),
-            ],
-            scratch_shapes=[pltpu.SemaphoreType.DMA((copies_of(parts),))],
-        ),
+        functools.partial(project_kernel, min(512, count), len(parts)),
+        in_specs=[pl.BlockSpec(memory_space=pltpu.SMEM)]
+        + [IN_VMEM] * 2
+        + [pl.BlockSpec(memory_space=pl.ANY)] * len(parts),
+        out_specs=[in_hbm, IN_VMEM, in_hbm],
+        scratch_shapes=[
+            pltpu.VMEM((count, width), BF16),
+            pltpu.VMEM((width, cols), BF16),
+            pltpu.SemaphoreType.DMA((copies_of(parts),)),
+            pltpu.SemaphoreType.DMA((2,)),
+        ],
         out_shape=[
             jax.ShapeDtypeStruct((count, width), BF16),
             jax.ShapeDtypeStruct((count, cols), BF16),
             jax.ShapeDtypeStruct((width, cols), BF16),
         ],
-        compiler_params=params(12),
+        compiler_params=params(10),
         cost_estimate=cost(2 * count * width * cols, 8 * 2**20),
         name="project",
     )(own, hidden, gain, *parts)
@@ -433,12 +437,15 @@
     act_ref, cot_t, grad_ref, up_sems, down_sems, out_sems = refs
     count, width = hidden_ref.shape
     raised = act_ref.shape[1]
-    up_copies = fetches(own_ref, up_sources, w_up, up_sems)
+    up_copies = [
+        fetches(own_ref, up_sources, w_up, up_sems.at[i], slice(start, start + 512))
+        for i, start in enumerate(range(0, width + raised, 512))
+    ]
     down_copies = fetches(own_ref, down_sources, w_down, down_sems)
-    launch(up_copies)
-    launch(down_copies)
+    for copies in up_copies[:2] + [down_copies] + up_copies[2:]:
+        launch(copies)
     cot_t[...] = cot_ref[...].T
-    finish(up_copies)
+    finish(up_copies[0])
     for row in range(0, count, chunk):
         at = slice(row, row + chunk)
         first = hidden_ref[at, :] + nn(att_ref[at, :], w_up[:, :width])
@@ -446,11 +453,11 @@
         normed_ref[at, :] = normed
         scale_ref[at, :] = jnp.broadcast_to(scale, (chunk, scale_ref.shape[1]))
         normed_two = (normed * gain_ref[...]).astype(BF16)
-        if row == 0:
-            finish(down_copies)
         total = first
         for start in range(0, raised, 512):
             stop = start + 512
+            if row == 0:
+                finish(up_copies[1 + start // 512])
             v = nn(normed_two, w_up[:, width + start : width + stop])
             square = v * v
             t = jnp.tanh(v * (0.7978845608028654 + 0.035677408136300125 * square))
@@ -461,6 +468,8 @@
             )
             act_ref[at, start:stop] = act
             slope_ref[at, start:stop] = slope.astype(BF16)
+            if row == 0 and start == 0:
+                finish(down_copies)
             total = total + nn(act, w_down[start:stop, :])
         out_ref[at, :] = total.astype(BF16)
     if not split:
@@ -513,7 +522,7 @@
             pltpu.VMEM((count, raised), BF16),
             pltpu.VMEM((width, count), BF16),
             pltpu.VMEM(grad_shape, BF16),
-            pltpu.SemaphoreType.DMA((copies_of(up_parts),)),
+            pltpu.SemaphoreType.DMA(((width + raised) // 512, copies_of(up_parts))),
             pltpu.SemaphoreType.DMA((copies_of(down_parts),)),
             pltpu.SemaphoreType.DMA((dp_count,)),
         ],
@@ -526,7 +535,7 @@
             jax.ShapeDtypeStruct(down_shape, BF16),
         ]
         + grads,
-        compiler_params=params(22),
+        compiler_params=params(15),
         cost_estimate=cost(7 * 2**30, 24 * 2**20),
         name="rise",
     )(own, hidden, att, cot, gain, *up_parts, *down_parts)
@@ -667,7 +676,7 @@
             jax.ShapeDtypeStruct((1, width), F32),
         ]
         + grads,
-        compiler_params=params(24),
+        compiler_params=params(17),
         cost_estimate=cost(8 * 2**30, 24 * 2**20),
         name="fall",
     )(own, cot, slope, normed, scale, att, den, gain, w_up, w_down)
@@ -706,7 +715,7 @@
             jax.ShapeDtypeStruct((count, width), BF16),
             jax.ShapeDtypeStruct((8, width), F32),
         ],
-        compiler_params=params(14),
+        compiler_params=params(8),
         cost_estimate=cost(6 * count * width * width, 12 * 2**20),
         name="last",
     )(hidden, grad_first, gain, mask, w_qkv, *grads)
@@ -742,6 +751,10 @@
 
 def add_split(left, right):
     return [add_up((left[j], right[j])).astype(BF16) for j in range(left.shape[0])]
+
+
+def both_cores(value):
+    return [value, other_core(value)]
 
 
 def split_first(value):
@@ -801,7 +814,7 @@
     raised = weight_up.shape[1]
     seq_count, dp_count = lax.axis_size("seq"), lax.axis_size("dp")
     outer = seq_count // rows
-    split = outer == 1 and (width // seq_count) % 128 == 0 and (width // dp_count) % 16 == 0
+    split = outer == 1 and (seq_count, dp_count) == (4, 8)
     place = lax.axis_index("seq")
     dp_place = lax.axis_index("dp")
     row = place % rows
@@ -826,30 +839,29 @@
 
     masked = (unmask_order <= timestep[:, None]).astype(BF16)
     masked = jnp.pad(masked[:, None, :], ((0, 0), (0, 15), (0, width - segment)))
-    came = from_plane(by_partner(jnp.concatenate((inputs, masked), axis=1)))
-    block = jnp.concatenate([part[:segment] for part in came]).astype(F32)
-    mask_row = jnp.concatenate([part[segment, :segment] for part in came])
+    came = by_partner(jnp.concatenate((inputs, masked), axis=1))
     up_and_out = jnp.concatenate((weight_out, weight_up), axis=1)
     if split:
         down_rows = weight_down.shape[0] // seq_count
         own_down = lax.dynamic_slice_in_dim(weight_down, place * down_rows, down_rows, 0)
-        own_parts = jnp.concatenate((own_columns(weight_qkv), own_down), axis=1)
-        line = gather_line(own_parts)
+        line = gather_line(jnp.concatenate((own_columns(weight_qkv), own_down), axis=1))
+        came = from_plane(came)
         line, up_and_out = together(line, up_and_out)
         line_up = from_line([up_and_out] * (dp_count // 2))
-        plane_qkv = gather_plane(line[..., : -width])
+        plane_qkv = gather_plane(line[..., :-width])
         line_down = line[..., -width:].reshape(-1, width)
         plane_qkv, line_down, cot = together(plane_qkv, line_down, cotangent)
-        parts_qkv = [plane_qkv, other_core(plane_qkv)]
-        cot = by_partner(cot)
-        cot = from_plane([jnp.concatenate((part, line_down)) for part in cot])
+        parts_qkv = both_cores(plane_qkv)
+        cot = from_plane([jnp.concatenate((part, line_down)) for part in by_partner(cot)])
     else:
-        cot = from_plane(by_partner(cotangent))
+        came, cot = from_plane(came), from_plane(by_partner(cotangent))
         parts_qkv, parts_up, parts_down = (
             [lax.all_gather(weight, "dp", axis=0, tiled=True)]
             for weight in (weight_qkv, up_and_out, weight_down)
         )
 
+    block = jnp.concatenate([part[:segment] for part in came]).astype(F32)
+    mask_row = jnp.concatenate([part[segment, :segment] for part in came])
     hidden = block + mask_row.astype(F32)[:, None] * mask_embed
     normed_one, projected, whole_qkv = project(
         own, hidden, ln1_gain[None, :], parts_qkv, 3 * width
@@ -863,12 +875,12 @@
     else:
         attended, denominators = attend_row(projected)
     if split:
-        cot, line_up, attended = together(cot, line_up, attended)
+        line_up, attended = together(line_up, attended)
+        parts_up = both_cores(jnp.stack(line_up))
+        cot, parts_up[0] = together(cot, parts_up[0])
         plane_down = jnp.stack([part[segment:] for part in cot])
         plane_down = plane_down.reshape(seq_count, dp_count // 2, -1, width)
-        line_up = jnp.stack(line_up)
-        parts_up = [line_up, other_core(line_up)]
-        parts_down = [plane_down, other_core(plane_down)]
+        parts_down = both_cores(plane_down)
     cot = jnp.concatenate([part[:segment] for part in cot])
     outputs, normed, scale, slope, whole_up, whole_down, *grad_down = rise(
         own,
@@ -919,9 +931,9 @@
         line_up = add_up(plane_up).astype(BF16)
         z_half = line_up.shape[0] // 2
         line_came = swap_along(line_up[z_half:], "dp", 2 * z_half)
-        both_qkv, mask_rows = together(both_qkv, mask_rows)
         tall = width // dp_count
         down = add_up(line_down).astype(BF16).reshape(seq_count, -1, tall, 128)
+        both_qkv, mask_rows = together(both_qkv, mask_rows)
         mine_qkv = [part.reshape(-1, tall, 128) for part in add_split(*both_qkv)]
         plane_last = from_plane([jnp.concatenate((mine_qkv[j], down[j])) for j in range(seq_count)])
     else:
@@ -955,32 +967,40 @@
     grad_hidden, sums = last(
         hidden, grad_first, ln1_gain[None, :], mask_rows, whole_qkv, grads
     )
-    vectors = jnp.concatenate((sums[0:2], sum_gain_two, jnp.zeros((13, width), F32)), axis=0)
+    vectors = jnp.concatenate((sums[0:2], sum_gain_two, jnp.zeros((5, width), F32)), axis=0)
     vectors = vectors + other_core(vectors)
-    bit = 1
-    while bit < seq_count:
-        vectors = vectors + swap_along(vectors, "seq", bit)
+    bit = 2
+    while bit < dp_count:
+        vectors = vectors + swap_along(vectors, "dp", bit)
         bit *= 2
     if split:
         grad_hidden, vectors, line_came, plane_last = together(
             grad_hidden, vectors, line_came, plane_last
         )
-        grad_inputs = to_partners(grad_hidden)
-        sum_up = halve_line(add_up((line_up[:z_half], line_came)).astype(BF16))
-        plane = add_up(plane_last)
+        sum_up = add_up((line_up[:z_half], line_came)).astype(BF16)
         kinds = mine_qkv[0].shape[0]
-        sum_down = plane[kinds:].reshape(-1, width // seq_count, 128)
+        sum_qkv = add_up([part[:kinds] for part in plane_last]).astype(BF16)
+        sum_qkv = sum_qkv.reshape((dp_count // 2, -1) + sum_qkv.shape[1:])
+        line_came = swap_along(sum_qkv[z_half:], "dp", 2 * z_half)
+        line_came, plane_last, sum_up = together(line_came, plane_last, sum_up)
+        sum_qkv = halve_line(add_up((sum_qkv[:z_half], line_came)).astype(BF16))
+        sum_up = halve_line(sum_up)
+        sum_down = add_up([part[kinds:] for part in plane_last])
+        sum_down = sum_down.reshape(-1, width // seq_count, 128)
         sum_down = jnp.transpose(sum_down, (0, 2, 1)).reshape(-1, width // seq_count)
-        z_count = dp_count // 2
-        plane = plane[:kinds].astype(BF16).reshape((z_count, -1) + plane.shape[1:])
-        flat = jnp.transpose(vectors.reshape(16, -1, 128), (1, 0, 2)).astype(BF16)
-        flat = jnp.broadcast_to(flat.reshape(1, -1, tall, 128), (z_count, 1, tall, 128))
-        line = halve_line(jnp.concatenate((plane, flat), axis=1))
-        sum_qkv = jnp.transpose(line[:-1], (1, 0, 2)).reshape(tall, -1)
-        vectors = jnp.transpose(line[-1].reshape(-1, 16, 128), (1, 0, 2)).reshape(16, -1)
+        sum_qkv = jnp.transpose(sum_qkv, (1, 0, 2)).reshape(tall, -1)
+    grad_inputs = [grad_hidden[j * segment : (j + 1) * segment] for j in range(rows)]
+    if split:
+        coarse = vectors.astype(BF16)
+        terms = jnp.concatenate((coarse, (vectors - coarse.astype(F32)).astype(BF16)))
+        grad_inputs = [jnp.concatenate((part, terms)) for part in grad_inputs]
+    grad_inputs = from_plane(grad_inputs)
+    if split:
+        vectors = add_up([part[segment:] for part in grad_inputs])
+        vectors = vectors[:8] + vectors[8:]
+        grad_inputs = [part[:segment] for part in grad_inputs]
     else:
-        grad_inputs = to_partners(grad_hidden)
-        vectors = add_up(from_line([vectors] * (dp_count // 2)))
+        vectors = add_up(from_plane([vectors] * seq_count))
     block_width = width // dp_count
     vectors = lax.dynamic_slice_in_dim(vectors, dp_place * block_width, block_width, 1)
     out_cols = width // seq_count

time: 180 us -> 173 us (0.961)
  waiting for transfers between devices: 34.4 us -> 27.6 us
    ppermute x43, waiting for transfers between devices: 34.4 us -> 27.6 us  [swap_along(): return lax.ppermute(value, axis, [(i, i ^ mask) for i in range(count)])]
  transfers between devices with their start and end apart: 43 -> 43, of which waited for: 13 -> 11; matrix products, arithmetic and copies ran while one was open for 8% -> 9% of each run, Pallas kernels for 30% -> 32%
where the time goes in v4:
time: 173 us; the launch traced here: 170 us
  Pallas kernels  68.2 us (39%)
  starting transfers between devices  49.4 us (29%)
  waiting for transfers between devices  27.6 us (16%)
  other arithmetic  12.1 us (7%)
  local copies, waits for them, and re-layouts  11 us (6%)
    ppermute x43, starting transfers between devices, swap_along(): return lax.ppermute(value, axis, [(i, i ^ mask) for i in range(count)])  49.4 us
    ppermute x43, waiting for transfers between devices, swap_along(): return lax.ppermute(value, axis, [(i, i ^ mask) for i in range(count)])  27.6 us
    pallas_call x1, Pallas kernels, rise(): pl.pallas_call(functools.partial(rise_kernel, cfg), in_specs=[pl.BlockSpe...  14.7 us
    pallas_call x1, Pallas kernels, attend_back_sum(): pl.pallas_call(functools.partial(attend_back_sum_kernel, min(512, count),...  14.5 us
    pallas_call x1, Pallas kernels, fall(): pl.pallas_call(functools.partial(fall_kernel, cfg), in_specs=[pl.BlockSpe...  12.2 us
    pallas_call x1, Pallas kernels, attend_back_half(): pl.pallas_call(functools.partial(attend_back_half_kernel, min(512, count)...  10.2 us
    pallas_call x1, Pallas kernels, attend_row(): pl.pallas_call(functools.partial(attend_row_kernel, min(256, count)), in_...  9.56 us
    unnamed x40, local copies, waits for them, and re-layouts  4.6 us
  transfers between devices with their start and end apart: 43, of which 11 were waited for; matrix products, arithmetic and copies ran while one was open for 9% of the time, Pallas kernels for 32%

profile of v4, /device:TPU:0, one launch (start us, length us, event | category | flops | bytes accessed | tf_op | source)
XLA Modules:
  0.0 169.9 jit_solution(11088105718823122306)
XLA Ops:
  2.4 3.1 %collective-permute-start.3 = (bf16[64,896]{1,0:T(8,128)(2,1)S(1)}, bf16[64,896]{1,0:T(8,128)(2,1)S(1)}, u32[]{:S(2)}, u32[]{:S(2)}) collective-permute-start(bf16[64,896]{1,0:T(8,128)(2,1)S(1)} %get-tuple-element.243), channel_id=1, source_target_pairs={{0,2},{1,3},{2,0},{3,1},{4,6},{5,7},{6,4},{7,5},{8,10},{9,11},{10,... | collective-permute-start | bytes 344072 | tf_op jit(solution)/shard_map/ppermute | solution.py:726
  5.5 2.6 %collective-permute-start.4 = (bf16[64,896]{1,0:T(8,128)(2,1)S(1)}, bf16[64,896]{1,0:T(8,128)(2,1)S(1)}, u32[]{:S(2)}, u32[]{:S(2)}) collective-permute-start(bf16[64,896]{1,0:T(8,128)(2,1)S(1)} %get-tuple-element.243), channel_id=1, source_target_pairs={{0,4},{1,5},{2,6},{3,7},{4,0},{5,1},{6,2},{7,3},{8,12},{9,13},{10,... | collective-permute-start | bytes 344072 | tf_op jit(solution)/shard_map/ppermute | solution.py:726
  10.2 2.7 %collective-permute-start.2 = (bf16[272,512]{1,0:T(8,128)(2,1)S(1)}, bf16[272,512]{1,0:T(8,128)(2,1)S(1)}, u32[]{:S(2)}, u32[]{:S(2)}) collective-permute-start(bf16[272,512]{1,0:T(8,128)(2,1)S(1)} %get-tuple-element.206), channel_id=1, source_target_pairs={{0,24},{8,16},{16,8},{24,0},{1,25},{9,17},{17,9},{25,1},{2,26},{10... | collective-permute-start | bytes 835592 | tf_op jit(solution)/shard_map/ppermute | solution.py:726
  15.4 1.8 %collective-permute-done.4 = bf16[64,896]{1,0:T(8,128)(2,1)S(1)} collective-permute-done((bf16[64,896]{1,0:T(8,128)(2,1)S(1)}, bf16[64,896]{1,0:T(8,128)(2,1)S(1)}, u32[]{:S(2)}, u32[]{:S(2)}) %collective-permute-start.4) | collective-permute-done | bytes 114720 | tf_op jit(solution)/shard_map/ppermute | solution.py:726
  17.4 1.6 collective-permute-start.9
  18.9 1.5 collective-permute-start.10
  20.5 6.6 %collective-permute-done = bf16[272,512]{1,0:T(8,128)(2,1)S(1)} collective-permute-done((bf16[272,512]{1,0:T(8,128)(2,1)S(1)}, bf16[272,512]{1,0:T(8,128)(2,1)S(1)}, u32[]{:S(2)}, u32[]{:S(2)}) %collective-permute-start) | collective-permute-done | bytes 278560 | tf_op jit(solution)/shard_map/ppermute | solution.py:726
  27.1 1.4 collective-permute-start.11
  29.3 3.6 %collective-permute-start.7 = (bf16[64,2560]{1,0:T(8,128)(2,1)}, bf16[64,2560]{1,0:T(8,128)(2,1)S(1)}, u32[]{:S(2)}, u32[]{:S(2)}) collective-permute-start(bf16[64,2560]{1,0:T(8,128)(2,1)} %pad_maximum_fusion.17), channel_id=1, source_target_pairs={{0,4},{1,5},{2,6},{3,7},{4,0},{5,1},{6,2},{7,3},{8,12},{9,13},{10,... | collective-permute-start | bytes 983048 | tf_op jit(solution)/shard_map/ppermute | solution.py:726
  32.9 1.9 %collective-permute-start.8 = (bf16[64,2560]{1,0:T(8,128)(2,1)}, bf16[64,2560]{1,0:T(8,128)(2,1)S(1)}, u32[]{:S(2)}, u32[]{:S(2)}) collective-permute-start(bf16[64,2560]{1,0:T(8,128)(2,1)} %pad_maximum_fusion.17), channel_id=1, source_target_pairs={{0,6},{1,7},{2,4},{3,5},{4,2},{5,3},{6,0},{7,1},{8,14},{9,15},{10,... | collective-permute-start | bytes 983048 | tf_op jit(solution)/shard_map/ppermute | solution.py:726
  36.4 1.5 collective-permute-start.13
  38.4 3.9 %project.1 = (bf16[1024,512]{1,0:T(8,128)(2,1)S(1)}, bf16[1024,1536]{1,0:T(8,128)(2,1)S(1)}, bf16[512,1536]{1,0:T(8,128)(2,1)S(1)}) custom-call(s32[3]{0:T(128)S(1)} %pad_add_fusion.own_ref, f32[1024,512]{1,0:T(8,128)S(1)} %multiply_add_fusion.hidden_ref, f32[1,512]{1,0:T(1,128)S(1)} %bitcast.106, bf16[4,4,64,384]{3,2,1,0:T(8,128)(2,1)S(1)} %pad_maximum_fusion.5.refs_0_, ...), custom_call_target="tpu_custom_call" | custom-call | flops 1610612736 | bytes 8388608 | tf_op jit(solution)/shard_map/project/pallas_call | solution.py:407
  43.6 1.9 %collective-permute-start.15 = (bf16[512,512]{1,0:T(8,128)(2,1)S(1)}, bf16[512,512]{1,0:T(8,128)(2,1)S(1)}, u32[]{:S(2)}, u32[]{:S(2)}) collective-permute-start(bf16[512,512]{1,0:T(8,128)(2,1)S(1)} %get-tuple-element.236), channel_id=1, source_target_pairs={{0,24},{8,16},{16,8},{24,0},{1,25},{9,17},{17,9},{25,1},{2,26},{10... | collective-permute-start | bytes 1572872 | tf_op jit(solution)/shard_map/ppermute | solution.py:726
  45.4 9.6 %attend_row.1 = (bf16[1024,512]{1,0:T(8,128)(2,1)S(1)}, f32[1024,128]{1,0:T(8,128)S(1)}) custom-call(bf16[1024,1536]{1,0:T(8,128)(2,1)S(1)} %get-tuple-element.100.own_ref.proj_ref), custom_call_target="tpu_custom_call" | custom-call | flops 17179869184 | bytes 5242880 | tf_op jit(solution)/shard_map/attend_row/pallas_call | solution.py:120
  58.0 5.1 %collective-permute-done.14 = bf16[512,512]{1,0:T(8,128)(2,1)S(1)} collective-permute-done((bf16[512,512]{1,0:T(8,128)(2,1)S(1)}, bf16[512,512]{1,0:T(8,128)(2,1)S(1)}, u32[]{:S(2)}, u32[]{:S(2)}) %collective-permute-start.14) | collective-permute-done | bytes 524320 | tf_op jit(solution)/shard_map/ppermute | solution.py:726
  67.5 1.6 collective-permute-done.17.refs_3_
  69.0 14.7 %rise.1 = (bf16[1024,512]{1,0:T(8,128)(2,1)S(1)}, f32[1024,512]{1,0:T(8,128)S(1)}, f32[1024,128]{1,0:T(8,128)S(1)}, bf16[1024,2048]{1,0:T(8,128)(2,1)S(1)}, bf16...) custom-call(s32[3]{0:T(128)S(1)} %pad_add_fusion.own_ref, ...), custom_call_target="tpu_custom_call" | custom-call | flops 7516192768 | bytes 25165824 | tf_op jit(solution)/shard_map/rise/pallas_call | solution.py:515
  85.8 1.8 %collective-permute-start.21 = (bf16[256,512]{1,0:T(8,128)(2,1)S(1)}, bf16[256,512]{1,0:T(8,128)(2,1)S(1)}, u32[]{:S(2)}, u32[]{:S(2)}) collective-permute-start(bf16[256,512]{1,0:T(8,128)(2,1)S(1)} %get-tuple-element.214), channel_id=1, source_target_pairs={{0,24},{8,16},{16,8},{24,0},{1,25},{9,17},{17,9},{25,1},{2,26},{10... | collective-permute-start | bytes 786440 | tf_op jit(solution)/shard_map/ppermute | solution.py:726
  87.6 12.2 %fall.1 = (f32[1024,512]{1,0:T(8,128)S(1)}, bf16[1024,512]{1,0:T(8,128)(2,1)S(1)}, bf16[1024,512]{1,0:T(8,128)(2,1)S(1)}, f32[1,512]{1,0:T(1,128)S(1)}, bf16[4,4...) custom-call(s32[3]{0:T(128)S(1)} %pad_add_fusion.own_ref, ...), custom_call_target="tpu_custom_call" | custom-call | flops 8589934592 | bytes 25165824 | tf_op jit(solution)/shard_map/fall/pallas_call | solution.py:660
  100.3 2.8 %collective-permute-start.27 = (bf16[4,2,128,128]{3,2,1,0:T(8,128)(2,1)S(1)}, bf16[4,2,128,128]{3,2,1,0:T(8,128)(2,1)S(1)}, u32[]{:S(2)}, u32[]{:S(2)}) collective-permute-start(bf16[4,2,128,128]{3,2,1,0:T(8,128)(2,1)S(1)} %get-tuple-element.192), channel_id=1, source_target_pairs={{0,4},{1,5},{2,6},{3,7},{4,0},{5,1},{6,2},{7,3},{8,12},{9,13},{10,... | collective-permute-start | bytes 786440 | tf_op jit(solution)/shard_map/ppermute | solution.py:726
  103.0 1.5 collective-permute-start.28
  104.6 10.2 %attend_back_half.1 = (bf16[1024,256]{1,0:T(8,128)(2,1)S(1)}, bf16[1024,256]{1,0:T(8,128)(2,1)S(1)}, bf16[1024,256]{1,0:T(8,128)(2,1)S(1)}) custom-call(bf16[1024,1536]{1,0:T(8,128)(2,1)S(1)} %copy-done.7, bf16[1024,512]{1,0:T(8,128)(2,1)S(1)} %get-tuple-element.133.s_ref, bf16[1024,512]{1,0:T(8,128)(2,1)S(1)} %get-tuple-element.134.x_ref), custom_call_target="tpu_custom_call" | custom-call | flops 17179869184 | bytes 6291456 | tf_op jit(solution)/shard_map/attend_back_half/pallas_call | solution.py:192
  117.0 1.7 %collective-permute-start.26 = (bf16[4,64,640]{2,1,0:T(8,128)(2,1)S(1)}, bf16[4,64,640]{2,1,0:T(8,128)(2,1)S(1)}, u32[]{:S(2)}, u32[]{:S(2)}) collective-permute-start(bf16[4,64,640]{2,1,0:T(8,128)(2,1)S(1)} %get-tuple-element.187), channel_id=1, source_target_pairs={{0,24},{8,16},{16,8},{24,0},{1,25},{9,17},{17,9},{25,1},{2,26},{10... | collective-permute-start | bytes 983048 | tf_op jit(solution)/shard_map/ppermute | solution.py:726
  118.8 14.5 %attend_back_sum.1 = (bf16[1024,256]{1,0:T(8,128)(2,1)S(1)}, bf16[1024,256]{1,0:T(8,128)(2,1)S(1)}, bf16[1024,256]{1,0:T(8,128)(2,1)S(1)}, bf16[4,4,3,64,128]{4,...) custom-call(s32[3]{0:T(128)S(1)} %pad_add_fusion.own_ref, bf16[1024,1536]{1,0:T(8,128)(2,1)S(1)} %copy-done.7, ...), custom_call_target="tpu_custom_call" | custom-call | flops 21474836480 | bytes 10485760 | tf_op jit(solution)/shard_map/attend_back_sum/pallas_call | solution.py:259
  134.1 1.6 collective-permute-done.29
  138.5 3.3 %last.1 = (bf16[1024,512]{1,0:T(8,128)(2,1)S(1)}, f32[8,512]{1,0:T(8,128)S(1)}) custom-call(f32[1024,512]{1,0:T(8,128)S(1)} %multiply_add_fusion.hidden_ref, f32[1024,512]{1,0:T(8,128)S(1)} %get-tuple-element.130.first_ref, f32[1,512]{1,0:T(1,128)S(1)} %bitcast.107, bf16[8,1024]{1,0:T(8,128)(2,1)S(1)} %broadcast_in_dim.27.mask_ref, ...), custom_call_target="tpu_custom_call" | custom-call | flops 1610612736 | bytes 12582912 | tf_op jit(solution)/shard_map/last/pallas_call | solution.py:710
  145.5 1.4 collective-permute-done.31
  148.1 3.4 %collective-permute-done.32 = f32[8,512]{1,0:T(8,128)S(1)} collective-permute-done((f32[8,512]{1,0:T(8,128)S(1)}, f32[8,512]{1,0:T(8,128)S(1)}, u32[]{:S(2)}, u32[]{:S(2)}) %collective-permute-start.32) | collective-permute-done | bytes 16416 | tf_op jit(solution)/shard_map/ppermute | solution.py:726
  153.2 1.5 collective-permute-start.37
  156.8 2.1 %collective-permute-done.40 = bf16[2,3,64,128]{3,2,1,0:T(8,128)(2,1)S(1)} collective-permute-done((bf16[2,3,64,128]{3,2,1,0:T(8,128)(2,1)S(1)}, bf16[2,3,64,128]{3,2,1,0:T(8,128)(2,1)S(1)}, u32[]{:S(2)}, u32[]{:S(2)}) %collective-permute-start.40) | collective-permute-done | bytes 98336 | tf_op jit(solution)/shard_map/ppermute | solution.py:726
  159.8 2.1 %collective-permute-start.42 = (bf16[1,64,640]{2,1,0:T(8,128)(2,1)S(1)}, bf16[1,64,640]{2,1,0:T(8,128)(2,1)S(1)}, u32[]{:S(2)}, u32[]{:S(2)}) collective-permute-start(bf16[1,64,640]{2,1,0:T(8,128)(2,1)S(1)} %slice.341), channel_id=1, source_target_pairs={{0,2},{1,3},{2,0},{3,1},{4,6},{5,7},{6,4},{7,5},{8,10},{9,11},{10,... | collective-permute-start | bytes 245768 | tf_op jit(solution)/shard_map/ppermute | solution.py:726
  165.6 2.2 %collective-permute-done.38 = bf16[272,512]{1,0:T(8,128)(2,1)S(1)} collective-permute-done((bf16[272,512]{1,0:T(8,128)(2,1)S(1)}, bf16[272,512]{1,0:T(8,128)(2,1)S(1)}, u32[]{:S(2)}, u32[]{:S(2)}) %collective-permute-start.38) | collective-permute-done | bytes 278560 | tf_op jit(solution)/shard_map/ppermute | solution.py:726
  (175 shorter events, 41.2 us)
Async XLA Ops:
  2.4 12.6 %collective-permute-start.3 = (bf16[64,896]{1,0:T(8,128)(2,1)S(1)}, bf16[64,896]{1,0:T(8,128)(2,1)S(1)}, u32[]{:S(2)}, u32[]{:S(2)}) collective-permute-start(bf16[64,896]{1,0:T(8,128)(2,1)S(1)} %get-tuple-element.243), channel_id=1, source_target_pairs={{0,2},{1,3},{2,0},{3,1},{4,6},{5,7},{6,4},{7,5},{8,10},{9,11},{10,... | collective-permute-start | bytes 344072 | tf_op jit(solution)/shard_map/ppermute | solution.py:726
  5.5 11.7 %collective-permute-start.4 = (bf16[64,896]{1,0:T(8,128)(2,1)S(1)}, bf16[64,896]{1,0:T(8,128)(2,1)S(1)}, u32[]{:S(2)}, u32[]{:S(2)}) collective-permute-start(bf16[64,896]{1,0:T(8,128)(2,1)S(1)} %get-tuple-element.243), channel_id=1, source_target_pairs={{0,4},{1,5},{2,6},{3,7},{4,0},{5,1},{6,2},{7,3},{8,12},{9,13},{10,... | collective-permute-start | bytes 344072 | tf_op jit(solution)/shard_map/ppermute | solution.py:726
  10.2 19.1 %collective-permute-start.2 = (bf16[272,512]{1,0:T(8,128)(2,1)S(1)}, bf16[272,512]{1,0:T(8,128)(2,1)S(1)}, u32[]{:S(2)}, u32[]{:S(2)}) collective-permute-start(bf16[272,512]{1,0:T(8,128)(2,1)S(1)} %get-tuple-element.206), channel_id=1, source_target_pairs={{0,24},{8,16},{16,8},{24,0},{1,25},{9,17},{17,9},{25,1},{2,26},{10... | collective-permute-start | bytes 835592 | tf_op jit(solution)/shard_map/ppermute | solution.py:726
  13.0 15.6 %collective-permute-start.1 = (bf16[272,512]{1,0:T(8,128)(2,1)S(1)}, bf16[272,512]{1,0:T(8,128)(2,1)S(1)}, u32[]{:S(2)}, u32[]{:S(2)}) collective-permute-start(bf16[272,512]{1,0:T(8,128)(2,1)S(1)} %get-tuple-element.205), channel_id=1, source_target_pairs={{0,16},{8,24},{16,0},{24,8},{1,17},{9,25},{17,1},{25,9},{2,18},{10... | collective-permute-start | bytes 835592 | tf_op jit(solution)/shard_map/ppermute | solution.py:726
  15.1 12.0 %collective-permute-start = (bf16[272,512]{1,0:T(8,128)(2,1)S(1)}, bf16[272,512]{1,0:T(8,128)(2,1)S(1)}, u32[]{:S(2)}, u32[]{:S(2)}) collective-permute-start(bf16[272,512]{1,0:T(8,128)(2,1)S(1)} %get-tuple-element.204), channel_id=1, source_target_pairs={{0,8},{8,0},{16,24},{24,16},{1,9},{9,1},{17,25},{25,17},{2,10},{10... | collective-permute-start | bytes 835592 | tf_op jit(solution)/shard_map/ppermute | solution.py:726
  17.4 15.5 %collective-permute-start.9 = (bf16[4,64,384]{2,1,0:T(8,128)(2,1)S(1)}, bf16[4,64,384]{2,1,0:T(8,128)(2,1)S(1)}, u32[]{:S(2)}, u32[]{:S(2)}) collective-permute-start(bf16[4,64,384]{2,1,0:T(8,128)(2,1)S(1)} %get-tuple-element.231), channel_id=1, source_target_pairs={{0,8},{8,0},{16,24},{24,16},{1,9},{9,1},{17,25},{25,17},{2,10},{10... | collective-permute-start | bytes 589832 | tf_op jit(solution)/shard_map/ppermute | solution.py:726
  18.9 15.9 %collective-permute-start.10 = (bf16[4,64,384]{2,1,0:T(8,128)(2,1)S(1)}, bf16[4,64,384]{2,1,0:T(8,128)(2,1)S(1)}, u32[]{:S(2)}, u32[]{:S(2)}) collective-permute-start(bf16[4,64,384]{2,1,0:T(8,128)(2,1)S(1)} %get-tuple-element.231), channel_id=1, source_target_pairs={{0,16},{8,24},{16,0},{24,8},{1,17},{9,25},{17,1},{25,9},{2,18},{10... | collective-permute-start | bytes 589832 | tf_op jit(solution)/shard_map/ppermute | solution.py:726
  28.5 15.0 %collective-permute-start.6 = (bf16[64,2560]{1,0:T(8,128)(2,1)}, bf16[64,2560]{1,0:T(8,128)(2,1)S(1)}, u32[]{:S(2)}, u32[]{:S(2)}) collective-permute-start(bf16[64,2560]{1,0:T(8,128)(2,1)} %pad_maximum_fusion.17), channel_id=1, source_target_pairs={{0,2},{1,3},{2,0},{3,1},{4,6},{5,7},{6,4},{7,5},{8,10},{9,11},{10,... | collective-permute-start | bytes 983048 | tf_op jit(solution)/shard_map/ppermute | solution.py:726
  29.3 27.5 %collective-permute-start.7 = (bf16[64,2560]{1,0:T(8,128)(2,1)}, bf16[64,2560]{1,0:T(8,128)(2,1)S(1)}, u32[]{:S(2)}, u32[]{:S(2)}) collective-permute-start(bf16[64,2560]{1,0:T(8,128)(2,1)} %pad_maximum_fusion.17), channel_id=1, source_target_pairs={{0,4},{1,5},{2,6},{3,7},{4,0},{5,1},{6,2},{7,3},{8,12},{9,13},{10,... | collective-permute-start | bytes 983048 | tf_op jit(solution)/shard_map/ppermute | solution.py:726
  32.9 23.9 %collective-permute-start.8 = (bf16[64,2560]{1,0:T(8,128)(2,1)}, bf16[64,2560]{1,0:T(8,128)(2,1)S(1)}, u32[]{:S(2)}, u32[]{:S(2)}) collective-permute-start(bf16[64,2560]{1,0:T(8,128)(2,1)} %pad_maximum_fusion.17), channel_id=1, source_target_pairs={{0,6},{1,7},{2,4},{3,5},{4,2},{5,3},{6,0},{7,1},{8,14},{9,15},{10,... | collective-permute-start | bytes 983048 | tf_op jit(solution)/shard_map/ppermute | solution.py:726
  36.4 21.6 %collective-permute-start.13 = (bf16[512,512]{1,0:T(8,128)(2,1)S(1)}, bf16[512,512]{1,0:T(8,128)(2,1)S(1)}, u32[]{:S(2)}, u32[]{:S(2)}) collective-permute-start(bf16[512,512]{1,0:T(8,128)(2,1)S(1)} %get-tuple-element.237), channel_id=1, source_target_pairs={{0,8},{8,0},{16,24},{24,16},{1,9},{9,1},{17,25},{25,17},{2,10},{10... | collective-permute-start | bytes 1572872 | tf_op jit(solution)/shard_map/ppermute | solution.py:726
  37.9 25.2 %collective-permute-start.14 = (bf16[512,512]{1,0:T(8,128)(2,1)S(1)}, bf16[512,512]{1,0:T(8,128)(2,1)S(1)}, u32[]{:S(2)}, u32[]{:S(2)}) collective-permute-start(bf16[512,512]{1,0:T(8,128)(2,1)S(1)} %get-tuple-element.238), channel_id=1, source_target_pairs={{0,16},{8,24},{16,0},{24,8},{1,17},{9,25},{17,1},{25,9},{2,18},{10... | collective-permute-start | bytes 1572872 | tf_op jit(solution)/shard_map/ppermute | solution.py:726
  43.6 19.6 %collective-permute-start.15 = (bf16[512,512]{1,0:T(8,128)(2,1)S(1)}, bf16[512,512]{1,0:T(8,128)(2,1)S(1)}, u32[]{:S(2)}, u32[]{:S(2)}) collective-permute-start(bf16[512,512]{1,0:T(8,128)(2,1)S(1)} %get-tuple-element.236), channel_id=1, source_target_pairs={{0,24},{8,16},{16,8},{24,0},{1,25},{9,17},{17,9},{25,1},{2,26},{10... | collective-permute-start | bytes 1572872 | tf_op jit(solution)/shard_map/ppermute | solution.py:726
  57.9 11.1 %collective-permute-start.16 = (bf16[4,64,2560]{2,1,0:T(8,128)(2,1)S(1)}, bf16[4,64,2560]{2,1,0:T(8,128)(2,1)}, u32[]{:S(2)}, u32[]{:S(2)}) collective-permute-start(bf16[4,64,2560]{2,1,0:T(8,128)(2,1)S(1)} %pad_maximum_fusion.refs_0_), channel_id=1, source_target_pairs={{0,1},{1,0},{2,3},{3,2},{4,5},{5,4},{6,7},{7,6},{8,9},{9,8},{10,11... | collective-permute-start | bytes 3932168 | tf_op jit(solution)/shard_map/ppermute | solution.py:726
  83.7 16.1 %collective-permute-start.18 = (bf16[4,4,2,128,128]{4,3,2,1,0:T(8,128)(2,1)S(1)}, bf16[4,4,2,128,128]{4,3,2,1,0:T(8,128)(2,1)S(1)}, u32[]{:S(2)}, u32[]{:S(2)}) collective-permute-start(bf16[4,4,2,128,128]{4,3,2,1,0:T(8,128)(2,1)S(1)} %get-tuple-element.115), channel_id=1, source_target_pairs={{0,1},{1,0},{2,3},{3,2},{4,5},{5,4},{6,7},{7,6},{8,9},{9,8},{10,11... | collective-permute-start | bytes 3145736 | tf_op jit(solution)/shard_map/ppermute | solution.py:726
  84.0 15.8 %collective-permute-start.19 = (bf16[256,512]{1,0:T(8,128)(2,1)S(1)}, bf16[256,512]{1,0:T(8,128)(2,1)S(1)}, u32[]{:S(2)}, u32[]{:S(2)}) collective-permute-start(bf16[256,512]{1,0:T(8,128)(2,1)S(1)} %get-tuple-element.216), channel_id=1, source_target_pairs={{0,8},{8,0},{16,24},{24,16},{1,9},{9,1},{17,25},{25,17},{2,10},{10... | collective-permute-start | bytes 786440 | tf_op jit(solution)/shard_map/ppermute | solution.py:726
  85.0 14.8 %collective-permute-start.20 = (bf16[256,512]{1,0:T(8,128)(2,1)S(1)}, bf16[256,512]{1,0:T(8,128)(2,1)S(1)}, u32[]{:S(2)}, u32[]{:S(2)}) collective-permute-start(bf16[256,512]{1,0:T(8,128)(2,1)S(1)} %get-tuple-element.215), channel_id=1, source_target_pairs={{0,16},{8,24},{16,0},{24,8},{1,17},{9,25},{17,1},{25,9},{2,18},{10... | collective-permute-start | bytes 786440 | tf_op jit(solution)/shard_map/ppermute | solution.py:726
  85.8 14.0 %collective-permute-start.21 = (bf16[256,512]{1,0:T(8,128)(2,1)S(1)}, bf16[256,512]{1,0:T(8,128)(2,1)S(1)}, u32[]{:S(2)}, u32[]{:S(2)}) collective-permute-start(bf16[256,512]{1,0:T(8,128)(2,1)S(1)} %get-tuple-element.214), channel_id=1, source_target_pairs={{0,24},{8,16},{16,8},{24,0},{1,25},{9,17},{17,9},{25,1},{2,26},{10... | collective-permute-start | bytes 786440 | tf_op jit(solution)/shard_map/ppermute | solution.py:726
  100.1 14.7 %collective-permute-start.23 = (bf16[4,2,128,128]{3,2,1,0:T(8,128)(2,1)S(1)}, bf16[4,2,128,128]{3,2,1,0:T(8,128)(2,1)S(1)}, u32[]{:S(2)}, u32[]{:S(2)}) collective-permute-start(bf16[4,2,128,128]{3,2,1,0:T(8,128)(2,1)S(1)} %get-tuple-element.194), channel_id=1, source_target_pairs={{0,2},{1,3},{2,0},{3,1},{4,6},{5,7},{6,4},{7,5},{8,10},{9,11},{10,... | collective-permute-start | bytes 786440 | tf_op jit(solution)/shard_map/ppermute | solution.py:726
  100.2 14.7 %collective-permute-start.22 = (bf16[4,4,64,640]{3,2,1,0:T(8,128)(2,1)S(1)}, bf16[4,4,64,640]{3,2,1,0:T(8,128)(2,1)S(1)}, u32[]{:S(2)}, u32[]{:S(2)}) collective-permute-start(bf16[4,4,64,640]{3,2,1,0:T(8,128)(2,1)S(1)} %get-tuple-element.132), channel_id=1, source_target_pairs={{0,1},{1,0},{2,3},{3,2},{4,5},{5,4},{6,7},{7,6},{8,9},{9,8},{10,11... | collective-permute-start | bytes 3932168 | tf_op jit(solution)/shard_map/ppermute | solution.py:726
  100.3 33.0 %collective-permute-start.27 = (bf16[4,2,128,128]{3,2,1,0:T(8,128)(2,1)S(1)}, bf16[4,2,128,128]{3,2,1,0:T(8,128)(2,1)S(1)}, u32[]{:S(2)}, u32[]{:S(2)}) collective-permute-start(bf16[4,2,128,128]{3,2,1,0:T(8,128)(2,1)S(1)} %get-tuple-element.192), channel_id=1, source_target_pairs={{0,4},{1,5},{2,6},{3,7},{4,0},{5,1},{6,2},{7,3},{8,12},{9,13},{10,... | collective-permute-start | bytes 786440 | tf_op jit(solution)/shard_map/ppermute | solution.py:726
  103.0 30.2 %collective-permute-start.28 = (bf16[4,2,128,128]{3,2,1,0:T(8,128)(2,1)S(1)}, bf16[4,2,128,128]{3,2,1,0:T(8,128)(2,1)S(1)}, u32[]{:S(2)}, u32[]{:S(2)}) collective-permute-start(bf16[4,2,128,128]{3,2,1,0:T(8,128)(2,1)S(1)} %get-tuple-element.191), channel_id=1, source_target_pairs={{0,6},{1,7},{2,4},{3,5},{4,2},{5,3},{6,0},{7,1},{8,14},{9,15},{10,... | collective-permute-start | bytes 786440 | tf_op jit(solution)/shard_map/ppermute | solution.py:726
  115.2 18.0 %collective-permute-start.24 = (bf16[4,64,640]{2,1,0:T(8,128)(2,1)S(1)}, bf16[4,64,640]{2,1,0:T(8,128)(2,1)S(1)}, u32[]{:S(2)}, u32[]{:S(2)}) collective-permute-start(bf16[4,64,640]{2,1,0:T(8,128)(2,1)S(1)} %get-tuple-element.189), channel_id=1, source_target_pairs={{0,8},{8,0},{16,24},{24,16},{1,9},{9,1},{17,25},{25,17},{2,10},{10... | collective-permute-start | bytes 983048 | tf_op jit(solution)/shard_map/ppermute | solution.py:726
  116.2 17.1 %collective-permute-start.25 = (bf16[4,64,640]{2,1,0:T(8,128)(2,1)S(1)}, bf16[4,64,640]{2,1,0:T(8,128)(2,1)S(1)}, u32[]{:S(2)}, u32[]{:S(2)}) collective-permute-start(bf16[4,64,640]{2,1,0:T(8,128)(2,1)S(1)} %get-tuple-element.188), channel_id=1, source_target_pairs={{0,16},{8,24},{16,0},{24,8},{1,17},{9,25},{17,1},{25,9},{2,18},{10... | collective-permute-start | bytes 983048 | tf_op jit(solution)/shard_map/ppermute | solution.py:726
  117.0 16.3 %collective-permute-start.26 = (bf16[4,64,640]{2,1,0:T(8,128)(2,1)S(1)}, bf16[4,64,640]{2,1,0:T(8,128)(2,1)S(1)}, u32[]{:S(2)}, u32[]{:S(2)}) collective-permute-start(bf16[4,64,640]{2,1,0:T(8,128)(2,1)S(1)} %get-tuple-element.187), channel_id=1, source_target_pairs={{0,24},{8,16},{16,8},{24,0},{1,25},{9,17},{17,9},{25,1},{2,26},{10... | collective-permute-start | bytes 983048 | tf_op jit(solution)/shard_map/ppermute | solution.py:726
  133.7 17.8 %collective-permute-start.33 = (bf16[2,64,640]{2,1,0:T(8,128)(2,1)S(1)}, bf16[2,64,640]{2,1,0:T(8,128)(2,1)S(1)}, u32[]{:S(2)}, u32[]{:S(2)}) collective-permute-start(bf16[2,64,640]{2,1,0:T(8,128)(2,1)S(1)} %slice.357), channel_id=1, source_target_pairs={{0,4},{1,5},{2,6},{3,7},{4,0},{5,1},{6,2},{7,3},{8,12},{9,13},{10,... | collective-permute-start | bytes 491528 | tf_op jit(solution)/shard_map/ppermute | solution.py:726
  135.9 15.6 %collective-permute-start.36 = (bf16[16,64,128]{2,1,0:T(8,128)(2,1)S(1)}, bf16[16,64,128]{2,1,0:T(8,128)(2,1)S(1)}, u32[]{:S(2)}, u32[]{:S(2)}) collective-permute-start(bf16[16,64,128]{2,1,0:T(8,128)(2,1)S(1)} %pad_maximum_fusion.21), channel_id=1, source_target_pairs={{0,24},{8,16},{16,8},{24,0},{1,25},{9,17},{17,9},{25,1},{2,26},{10... | collective-permute-start | bytes 786440 | tf_op jit(solution)/shard_map/ppermute | solution.py:726
  137.2 14.3 %collective-permute-start.35 = (bf16[16,64,128]{2,1,0:T(8,128)(2,1)S(1)}, bf16[16,64,128]{2,1,0:T(8,128)(2,1)S(1)}, u32[]{:S(2)}, u32[]{:S(2)}) collective-permute-start(bf16[16,64,128]{2,1,0:T(8,128)(2,1)S(1)} %pad_maximum_fusion.20), channel_id=1, source_target_pairs={{0,16},{8,24},{16,0},{24,8},{1,17},{9,25},{17,1},{25,9},{2,18},{10... | collective-permute-start | bytes 786440 | tf_op jit(solution)/shard_map/ppermute | solution.py:726
  141.9 9.7 %collective-permute-start.34 = (bf16[16,64,128]{2,1,0:T(8,128)(2,1)S(1)}, bf16[16,64,128]{2,1,0:T(8,128)(2,1)S(1)}, u32[]{:S(2)}, u32[]{:S(2)}) collective-permute-start(bf16[16,64,128]{2,1,0:T(8,128)(2,1)S(1)} %pad_maximum_fusion.19), channel_id=1, source_target_pairs={{0,8},{8,0},{16,24},{24,16},{1,9},{9,1},{17,25},{25,17},{2,10},{10... | collective-permute-start | bytes 786440 | tf_op jit(solution)/shard_map/ppermute | solution.py:726
  153.2 12.4 %collective-permute-start.37 = (bf16[272,512]{1,0:T(8,128)(2,1)S(1)}, bf16[272,512]{1,0:T(8,128)(2,1)S(1)}, u32[]{:S(2)}, u32[]{:S(2)}) collective-permute-start(bf16[272,512]{1,0:T(8,128)(2,1)S(1)} %get-tuple-element.248), channel_id=1, source_target_pairs={{0,24},{8,16},{16,8},{24,0},{1,25},{9,17},{17,9},{25,1},{2,26},{10... | collective-permute-start | bytes 835592 | tf_op jit(solution)/shard_map/ppermute | solution.py:726
  154.7 13.1 %collective-permute-start.38 = (bf16[272,512]{1,0:T(8,128)(2,1)S(1)}, bf16[272,512]{1,0:T(8,128)(2,1)S(1)}, u32[]{:S(2)}, u32[]{:S(2)}) collective-permute-start(bf16[272,512]{1,0:T(8,128)(2,1)S(1)} %get-tuple-element.247), channel_id=1, source_target_pairs={{0,16},{8,24},{16,0},{24,8},{1,17},{9,25},{17,1},{25,9},{2,18},{10... | collective-permute-start | bytes 835592 | tf_op jit(solution)/shard_map/ppermute | solution.py:726
  155.8 12.0 %collective-permute-start.39 = (bf16[272,512]{1,0:T(8,128)(2,1)S(1)}, bf16[272,512]{1,0:T(8,128)(2,1)S(1)}, u32[]{:S(2)}, u32[]{:S(2)}) collective-permute-start(bf16[272,512]{1,0:T(8,128)(2,1)S(1)} %get-tuple-element.246), channel_id=1, source_target_pairs={{0,8},{8,0},{16,24},{24,16},{1,9},{9,1},{17,25},{25,17},{2,10},{10... | collective-permute-start | bytes 835592 | tf_op jit(solution)/shard_map/ppermute | solution.py:726
  (32 other events, 188.2 us)

commit v5 on v4

--- a/solution.py
+++ b/solution.py
@@ -417,9 +417,9 @@
             pltpu.SemaphoreType.DMA((2,)),
         ],
         out_shape=[
-            jax.ShapeDtypeStruct((count, width), BF16),
+            pltpu.HBM((count, width), BF16),
             jax.ShapeDtypeStruct((count, cols), BF16),
-            jax.ShapeDtypeStruct((width, cols), BF16),
+            pltpu.HBM((width, cols), BF16),
         ],
         compiler_params=params(10),
         cost_estimate=cost(2 * count * width * cols, 8 * 2**20),
@@ -716,7 +716,7 @@
             jax.ShapeDtypeStruct((8, width), F32),
         ],
         compiler_params=params(8),
-        cost_estimate=cost(6 * count * width * width, 12 * 2**20),
+        cost_estimate=cost(8 * (6 * count * width * width), 8 * (12 * 2**20)),
         name="last",
     )(hidden, grad_first, gain, mask, w_qkv, *grads)
 
@@ -830,12 +830,10 @@
         return from_plane([value[j * segment : (j + 1) * segment] for j in range(rows)])
 
     def by_row(parts):
-        bit = 1
-        while bit < rows:
-            odd = (row & bit) != 0
-            parts = [jnp.where(odd, parts[j ^ bit], parts[j]) for j in range(rows)]
-            bit *= 2
-        return jnp.stack(parts)
+        out = jnp.zeros((rows,) + parts[0].shape, parts[0].dtype)
+        for j in (0, 3, 2, 1) if rows == 4 else range(rows):
+            out = lax.dynamic_update_index_in_dim(out, parts[j], row ^ j, 0)
+        return out
 
     masked = (unmask_order <= timestep[:, None]).astype(BF16)
     masked = jnp.pad(masked[:, None, :], ((0, 0), (0, 15), (0, width - segment)))
@@ -847,7 +845,8 @@
         line = gather_line(jnp.concatenate((own_columns(weight_qkv), own_down), axis=1))
         came = from_plane(came)
         line, up_and_out = together(line, up_and_out)
-        line_up = from_line([up_and_out] * (dp_count // 2))
+        line_up = jnp.stack((up_and_out, swap_along(up_and_out, "dp", 4)))
+        line_up = [line_up, swap_along(line_up, "dp", 2)]
         plane_qkv = gather_plane(line[..., :-width])
         line_down = line[..., -width:].reshape(-1, width)
         plane_qkv, line_down, cot = together(plane_qkv, line_down, cotangent)
@@ -876,7 +875,7 @@
         attended, denominators = attend_row(projected)
     if split:
         line_up, attended = together(line_up, attended)
-        parts_up = both_cores(jnp.stack(line_up))
+        parts_up = both_cores(jnp.stack(line_up, axis=1).reshape((-1,) + up_and_out.shape))
         cot, parts_up[0] = together(cot, parts_up[0])
         plane_down = jnp.stack([part[segment:] for part in cot])
         plane_down = plane_down.reshape(seq_count, dp_count // 2, -1, width)

time: 173 us -> 172 us (level)
  other arithmetic: 12.1 us -> 9.69 us
    another operation x5 -> x2, other arithmetic: 3.54 us -> 1.16 us  [the longest x1 1.03 us: per_device(): line_up = jnp.stack((up_and_out, swap_along(up_and_out, 'dp', 4)))]
    ppermute x43 -> x42, waiting for transfers between devices: 27.6 us -> 29.2 us  [swap_along(): return lax.ppermute(value, axis, [(i, i ^ mask) for i in range(count)])]
    ppermute x43 -> x42, starting transfers between devices: 49.4 us -> 48.9 us  [swap_along(): return lax.ppermute(value, axis, [(i, i ^ mask) for i in range(count)])]
  transfers between devices with their start and end apart: 43 -> 42, of which waited for: 11 -> 16; matrix products, arithmetic and copies ran while one was open for 9% -> 9% of each run, Pallas kernels for 32% -> 32%
where the time goes in v5:
time: 172 us; the launch traced here: 169 us
  Pallas kernels  67.8 us (39%)
  starting transfers between devices  48.9 us (28%)
  waiting for transfers between devices  29.2 us (17%)
  local copies, waits for them, and re-layouts  11.3 us (7%)
  other arithmetic  9.69 us (6%)
  between operations  1.87 us (1%)
    ppermute x42, starting transfers between devices, swap_along(): return lax.ppermute(value, axis, [(i, i ^ mask) for i in range(count)])  48.9 us
    ppermute x42, waiting for transfers between devices, swap_along(): return lax.ppermute(value, axis, [(i, i ^ mask) for i in range(count)])  29.2 us
    pallas_call x1, Pallas kernels, rise(): pl.pallas_call(functools.partial(rise_kernel, cfg), in_specs=[pl.BlockSpe...  14.7 us
    pallas_call x1, Pallas kernels, attend_back_sum(): pl.pallas_call(functools.partial(attend_back_sum_kernel, min(512, count),...  14.4 us
    pallas_call x1, Pallas kernels, fall(): pl.pallas_call(functools.partial(fall_kernel, cfg), in_specs=[pl.BlockSpe...  12.2 us
    pallas_call x1, Pallas kernels, attend_back_half(): pl.pallas_call(functools.partial(attend_back_half_kernel, min(512, count)...  10.3 us
    pallas_call x1, Pallas kernels, attend_row(): pl.pallas_call(functools.partial(attend_row_kernel, min(256, count)), in_...  9.4 us
    unnamed x40, local copies, waits for them, and re-layouts  4.41 us
  transfers between devices with their start and end apart: 42, of which 16 were waited for; matrix products, arithmetic and copies ran while one was open for 9% of the time, Pallas kernels for 32%

profile of v5, /device:TPU:0, one launch (start us, length us, event | category | flops | bytes accessed | tf_op | source)
XLA Modules:
  0.0 168.8 jit_solution(3315038400621573315)
XLA Ops:
  2.4 3.1 %collective-permute-start.3 = (bf16[64,896]{1,0:T(8,128)(2,1)S(1)}, bf16[64,896]{1,0:T(8,128)(2,1)S(1)}, u32[]{:S(2)}, u32[]{:S(2)}) collective-permute-start(bf16[64,896]{1,0:T(8,128)(2,1)S(1)} %get-tuple-element.231), channel_id=1, source_target_pairs={{0,2},{1,3},{2,0},{3,1},{4,6},{5,7},{6,4},{7,5},{8,10},{9,11},{10,... | collective-permute-start | bytes 344072 | tf_op jit(solution)/shard_map/ppermute | solution.py:726
  5.5 2.6 %collective-permute-start.4 = (bf16[64,896]{1,0:T(8,128)(2,1)S(1)}, bf16[64,896]{1,0:T(8,128)(2,1)S(1)}, u32[]{:S(2)}, u32[]{:S(2)}) collective-permute-start(bf16[64,896]{1,0:T(8,128)(2,1)S(1)} %get-tuple-element.231), channel_id=1, source_target_pairs={{0,4},{1,5},{2,6},{3,7},{4,0},{5,1},{6,2},{7,3},{8,12},{9,13},{10,... | collective-permute-start | bytes 344072 | tf_op jit(solution)/shard_map/ppermute | solution.py:726
  10.2 2.7 %collective-permute-start.2 = (bf16[272,512]{1,0:T(8,128)(2,1)S(1)}, bf16[272,512]{1,0:T(8,128)(2,1)S(1)}, u32[]{:S(2)}, u32[]{:S(2)}) collective-permute-start(bf16[272,512]{1,0:T(8,128)(2,1)S(1)} %get-tuple-element.198), channel_id=1, source_target_pairs={{0,24},{8,16},{16,8},{24,0},{1,25},{9,17},{17,9},{25,1},{2,26},{10... | collective-permute-start | bytes 835592 | tf_op jit(solution)/shard_map/ppermute | solution.py:726
  15.4 1.8 %collective-permute-done.4 = bf16[64,896]{1,0:T(8,128)(2,1)S(1)} collective-permute-done((bf16[64,896]{1,0:T(8,128)(2,1)S(1)}, bf16[64,896]{1,0:T(8,128)(2,1)S(1)}, u32[]{:S(2)}, u32[]{:S(2)}) %collective-permute-start.4) | collective-permute-done | bytes 114720 | tf_op jit(solution)/shard_map/ppermute | solution.py:726
  17.4 1.6 collective-permute-start.8
  18.9 1.5 collective-permute-start.9
  20.5 4.6 %collective-permute-done.1 = bf16[272,512]{1,0:T(8,128)(2,1)S(1)} collective-permute-done((bf16[272,512]{1,0:T(8,128)(2,1)S(1)}, bf16[272,512]{1,0:T(8,128)(2,1)S(1)}, u32[]{:S(2)}, u32[]{:S(2)}) %collective-permute-start.1) | collective-permute-done | bytes 278560 | tf_op jit(solution)/shard_map/ppermute | solution.py:726
  25.1 2.5 %collective-permute-start.10 = (bf16[4,64,384]{2,1,0:T(8,128)(2,1)S(1)}, bf16[4,64,384]{2,1,0:T(8,128)(2,1)S(1)}, u32[]{:S(2)}, u32[]{:S(2)}) collective-permute-start(bf16[4,64,384]{2,1,0:T(8,128)(2,1)S(1)} %get-tuple-element.219), channel_id=1, source_target_pairs={{0,24},{8,16},{16,8},{24,0},{1,25},{9,17},{17,9},{25,1},{2,26},{10... | collective-permute-start | bytes 589832 | tf_op jit(solution)/shard_map/ppermute | solution.py:726
  27.6 1.7 %collective-permute-start.6 = (bf16[64,2560]{1,0:T(8,128)(2,1)}, bf16[64,2560]{1,0:T(8,128)(2,1)S(1)}, u32[]{:S(2)}, u32[]{:S(2)}) collective-permute-start(bf16[64,2560]{1,0:T(8,128)(2,1)} %pad_maximum_fusion.16), channel_id=1, source_target_pairs={{0,4},{1,5},{2,6},{3,7},{4,0},{5,1},{6,2},{7,3},{8,12},{9,13},{10,... | collective-permute-start | bytes 983048 | tf_op jit(solution)/shard_map/ppermute | solution.py:726
  30.2 3.2 %collective-permute-done.10 = bf16[4,64,384]{2,1,0:T(8,128)(2,1)S(1)} collective-permute-done((bf16[4,64,384]{2,1,0:T(8,128)(2,1)S(1)}, bf16[4,64,384]{2,1,0:T(8,128)(2,1)S(1)}, u32[]{:S(2)}, u32[]{:S(2)}) %collective-permute-start.10) | collective-permute-done | bytes 196640 | tf_op jit(solution)/shard_map/ppermute | solution.py:726
  34.9 1.6 collective-permute-start.12
  36.5 1.5 collective-permute-start.13
  38.5 5.1 %collective-permute-done.6 = bf16[64,2560]{1,0:T(8,128)(2,1)S(1)} collective-permute-done((bf16[64,2560]{1,0:T(8,128)(2,1)}, bf16[64,2560]{1,0:T(8,128)(2,1)S(1)}, u32[]{:S(2)}, u32[]{:S(2)}) %collective-permute-start.6) | collective-permute-done | bytes 327712 | tf_op jit(solution)/shard_map/ppermute | solution.py:726
  44.7 3.7 %project.1 = (bf16[1024,512]{1,0:T(8,128)(2,1)}, bf16[1024,1536]{1,0:T(8,128)(2,1)S(1)}, bf16[512,1536]{1,0:T(8,128)(2,1)}) custom-call(s32[3]{0:T(128)S(1)} %pad_add_fusion.own_ref, f32[1024,512]{1,0:T(8,128)S(1)} %multiply_add_fusion.hidden_ref, f32[1,512]{1,0:T(1,128)S(1)} %bitcast.117, bf16[4,4,64,384]{3,2,1,0:T(8,128)(2,1)S(1)} %pad_maximum_fusion.3.refs_0_, ...), custom_call_target="tpu_custom_call" | custom-call | flops 1610612736 | bytes 8388608 | tf_op jit(solution)/shard_map/project/pallas_call | solution.py:407
  48.4 9.4 %attend_row.1 = (bf16[1024,512]{1,0:T(8,128)(2,1)S(1)}, f32[1024,128]{1,0:T(8,128)S(1)}) custom-call(bf16[1024,1536]{1,0:T(8,128)(2,1)S(1)} %get-tuple-element.98.own_ref.proj_ref), custom_call_target="tpu_custom_call" | custom-call | flops 17179869184 | bytes 5242880 | tf_op jit(solution)/shard_map/attend_row/pallas_call | solution.py:120
  66.1 1.6 collective-permute-done.16.refs_3_
  67.7 14.7 %rise.1 = (bf16[1024,512]{1,0:T(8,128)(2,1)S(1)}, f32[1024,512]{1,0:T(8,128)S(1)}, f32[1024,128]{1,0:T(8,128)S(1)}, bf16[1024,2048]{1,0:T(8,128)(2,1)S(1)}, bf16...) custom-call(s32[3]{0:T(128)S(1)} %pad_add_fusion.own_ref, ...), custom_call_target="tpu_custom_call" | custom-call | flops 7516192768 | bytes 25165824 | tf_op jit(solution)/shard_map/rise/pallas_call | solution.py:515
  82.7 1.5 collective-permute-start.18
  86.2 12.2 %fall.1 = (f32[1024,512]{1,0:T(8,128)S(1)}, bf16[1024,512]{1,0:T(8,128)(2,1)S(1)}, bf16[1024,512]{1,0:T(8,128)(2,1)S(1)}, f32[1,512]{1,0:T(1,128)S(1)}, bf16[4,4...) custom-call(s32[3]{0:T(128)S(1)} %pad_add_fusion.own_ref, ...), custom_call_target="tpu_custom_call" | custom-call | flops 8589934592 | bytes 25165824 | tf_op jit(solution)/shard_map/fall/pallas_call | solution.py:660
  99.6 3.4 %collective-permute-start.26 = (bf16[4,2,128,128]{3,2,1,0:T(8,128)(2,1)S(1)}, bf16[4,2,128,128]{3,2,1,0:T(8,128)(2,1)S(1)}, u32[]{:S(2)}, u32[]{:S(2)}) collective-permute-start(bf16[4,2,128,128]{3,2,1,0:T(8,128)(2,1)S(1)} %get-tuple-element.188), channel_id=1, source_target_pairs={{0,4},{1,5},{2,6},{3,7},{4,0},{5,1},{6,2},{7,3},{8,12},{9,13},{10,... | collective-permute-start | bytes 786440 | tf_op jit(solution)/shard_map/ppermute | solution.py:726
  103.3 10.3 %attend_back_half.1 = (bf16[1024,256]{1,0:T(8,128)(2,1)S(1)}, bf16[1024,256]{1,0:T(8,128)(2,1)S(1)}, bf16[1024,256]{1,0:T(8,128)(2,1)S(1)}) custom-call(bf16[1024,1536]{1,0:T(8,128)(2,1)S(1)} %copy-done.5, bf16[1024,512]{1,0:T(8,128)(2,1)S(1)} %get-tuple-element.129.s_ref, bf16[1024,512]{1,0:T(8,128)(2,1)S(1)} %get-tuple-element.130.x_ref), custom_call_target="tpu_custom_call" | custom-call | flops 17179869184 | bytes 6291456 | tf_op jit(solution)/shard_map/attend_back_half/pallas_call | solution.py:192
  117.6 14.4 %attend_back_sum.1 = (bf16[1024,256]{1,0:T(8,128)(2,1)S(1)}, bf16[1024,256]{1,0:T(8,128)(2,1)S(1)}, bf16[1024,256]{1,0:T(8,128)(2,1)S(1)}, bf16[4,4,3,64,128]{4,...) custom-call(s32[3]{0:T(128)S(1)} %pad_add_fusion.own_ref, bf16[1024,1536]{1,0:T(8,128)(2,1)S(1)} %copy-done.5, ...), custom_call_target="tpu_custom_call" | custom-call | flops 21474836480 | bytes 10485760 | tf_op jit(solution)/shard_map/attend_back_sum/pallas_call | solution.py:259
  134.7 1.6 collective-permute-start.35
  137.8 3.2 %last.1 = (bf16[1024,512]{1,0:T(8,128)(2,1)S(1)}, f32[8,512]{1,0:T(8,128)S(1)}) custom-call(f32[1024,512]{1,0:T(8,128)S(1)} %multiply_add_fusion.hidden_ref, f32[1024,512]{1,0:T(8,128)S(1)} %get-tuple-element.126.first_ref, f32[1,512]{1,0:T(1,128)S(1)} %bitcast.118, bf16[8,1024]{1,0:T(8,128)(2,1)S(1)} %broadcast_in_dim.56.mask_ref, ...), custom_call_target="tpu_custom_call" | custom-call | flops 12884901888 | bytes 100663296 | tf_op jit(solution)/shard_map/last/pallas_call | solution.py:710
  142.3 2.3 %collective-permute-start.30 = (f32[8,512]{1,0:T(8,128)S(1)}, f32[8,512]{1,0:T(8,128)S(1)}, u32[]{:S(2)}, u32[]{:S(2)}) collective-permute-start(f32[8,512]{1,0:T(8,128)S(1)} %fusion.21), channel_id=1, source_target_pairs={{0,2},{1,3},{2,0},{3,1},{4,6},{5,7},{6,4},{7,5},{8,10},{9,11},{10,... | collective-permute-start | bytes 49160 | tf_op jit(solution)/shard_map/ppermute | solution.py:726
  144.7 1.7 collective-permute-done.30
  146.3 1.8 %collective-permute-start.31 = (f32[8,512]{1,0:T(8,128)S(1)}, f32[8,512]{1,0:T(8,128)S(1)}, u32[]{:S(2)}, u32[]{:S(2)}) collective-permute-start(f32[8,512]{1,0:T(8,128)S(1)} %add.186), channel_id=1, source_target_pairs={{0,4},{1,5},{2,6},{3,7},{4,0},{5,1},{6,2},{7,3},{8,12},{9,13},{10,... | collective-permute-start | bytes 49160 | tf_op jit(solution)/shard_map/ppermute | solution.py:726
  148.1 2.8 %collective-permute-done.31 = f32[8,512]{1,0:T(8,128)S(1)} collective-permute-done((f32[8,512]{1,0:T(8,128)S(1)}, f32[8,512]{1,0:T(8,128)S(1)}, u32[]{:S(2)}, u32[]{:S(2)}) %collective-permute-start.31) | collective-permute-done | bytes 16416 | tf_op jit(solution)/shard_map/ppermute | solution.py:726
  151.2 1.8 %collective-permute-start.39 = (bf16[2,3,64,128]{3,2,1,0:T(8,128)(2,1)S(1)}, bf16[2,3,64,128]{3,2,1,0:T(8,128)(2,1)S(1)}, u32[]{:S(2)}, u32[]{:S(2)}) collective-permute-start(bf16[2,3,64,128]{3,2,1,0:T(8,128)(2,1)S(1)} %bitcast.145), channel_id=1, source_target_pairs={{0,4},{1,5},{2,6},{3,7},{4,0},{5,1},{6,2},{7,3},{8,12},{9,13},{10,... | collective-permute-start | bytes 294920 | tf_op jit(solution)/shard_map/ppermute | solution.py:726
  153.2 1.7 %collective-permute-start.36 = (bf16[272,512]{1,0:T(8,128)(2,1)S(1)}, bf16[272,512]{1,0:T(8,128)(2,1)S(1)}, u32[]{:S(2)}, u32[]{:S(2)}) collective-permute-start(bf16[272,512]{1,0:T(8,128)(2,1)S(1)} %get-tuple-element.236), channel_id=1, source_target_pairs={{0,24},{8,16},{16,8},{24,0},{1,25},{9,17},{17,9},{25,1},{2,26},{10... | collective-permute-start | bytes 835592 | tf_op jit(solution)/shard_map/ppermute | solution.py:726
  156.9 1.5 collective-permute-done.39
  159.9 1.6 collective-permute-start.41
  (181 shorter events, 42.4 us)
Async XLA Ops:
  2.4 12.6 %collective-permute-start.3 = (bf16[64,896]{1,0:T(8,128)(2,1)S(1)}, bf16[64,896]{1,0:T(8,128)(2,1)S(1)}, u32[]{:S(2)}, u32[]{:S(2)}) collective-permute-start(bf16[64,896]{1,0:T(8,128)(2,1)S(1)} %get-tuple-element.231), channel_id=1, source_target_pairs={{0,2},{1,3},{2,0},{3,1},{4,6},{5,7},{6,4},{7,5},{8,10},{9,11},{10,... | collective-permute-start | bytes 344072 | tf_op jit(solution)/shard_map/ppermute | solution.py:726
  5.5 11.7 %collective-permute-start.4 = (bf16[64,896]{1,0:T(8,128)(2,1)S(1)}, bf16[64,896]{1,0:T(8,128)(2,1)S(1)}, u32[]{:S(2)}, u32[]{:S(2)}) collective-permute-start(bf16[64,896]{1,0:T(8,128)(2,1)S(1)} %get-tuple-element.231), channel_id=1, source_target_pairs={{0,4},{1,5},{2,6},{3,7},{4,0},{5,1},{6,2},{7,3},{8,12},{9,13},{10,... | collective-permute-start | bytes 344072 | tf_op jit(solution)/shard_map/ppermute | solution.py:726
  8.1 9.1 %collective-permute-start.5 = (bf16[64,896]{1,0:T(8,128)(2,1)S(1)}, bf16[64,896]{1,0:T(8,128)(2,1)S(1)}, u32[]{:S(2)}, u32[]{:S(2)}) collective-permute-start(bf16[64,896]{1,0:T(8,128)(2,1)S(1)} %get-tuple-element.231), channel_id=1, source_target_pairs={{0,6},{1,7},{2,4},{3,5},{4,2},{5,3},{6,0},{7,1},{8,14},{9,15},{10,... | collective-permute-start | bytes 344072 | tf_op jit(solution)/shard_map/ppermute | solution.py:726
  10.2 17.4 %collective-permute-start.2 = (bf16[272,512]{1,0:T(8,128)(2,1)S(1)}, bf16[272,512]{1,0:T(8,128)(2,1)S(1)}, u32[]{:S(2)}, u32[]{:S(2)}) collective-permute-start(bf16[272,512]{1,0:T(8,128)(2,1)S(1)} %get-tuple-element.198), channel_id=1, source_target_pairs={{0,24},{8,16},{16,8},{24,0},{1,25},{9,17},{17,9},{25,1},{2,26},{10... | collective-permute-start | bytes 835592 | tf_op jit(solution)/shard_map/ppermute | solution.py:726
  12.9 12.1 %collective-permute-start.1 = (bf16[272,512]{1,0:T(8,128)(2,1)S(1)}, bf16[272,512]{1,0:T(8,128)(2,1)S(1)}, u32[]{:S(2)}, u32[]{:S(2)}) collective-permute-start(bf16[272,512]{1,0:T(8,128)(2,1)S(1)} %get-tuple-element.197), channel_id=1, source_target_pairs={{0,16},{8,24},{16,0},{24,8},{1,17},{9,25},{17,1},{25,9},{2,18},{10... | collective-permute-start | bytes 835592 | tf_op jit(solution)/shard_map/ppermute | solution.py:726
  15.0 14.3 %collective-permute-start = (bf16[272,512]{1,0:T(8,128)(2,1)S(1)}, bf16[272,512]{1,0:T(8,128)(2,1)S(1)}, u32[]{:S(2)}, u32[]{:S(2)}) collective-permute-start(bf16[272,512]{1,0:T(8,128)(2,1)S(1)} %get-tuple-element.196), channel_id=1, source_target_pairs={{0,8},{8,0},{16,24},{24,16},{1,9},{9,1},{17,25},{25,17},{2,10},{10... | collective-permute-start | bytes 835592 | tf_op jit(solution)/shard_map/ppermute | solution.py:726
  17.4 12.9 %collective-permute-start.8 = (bf16[4,64,384]{2,1,0:T(8,128)(2,1)S(1)}, bf16[4,64,384]{2,1,0:T(8,128)(2,1)S(1)}, u32[]{:S(2)}, u32[]{:S(2)}) collective-permute-start(bf16[4,64,384]{2,1,0:T(8,128)(2,1)S(1)} %get-tuple-element.219), channel_id=1, source_target_pairs={{0,8},{8,0},{16,24},{24,16},{1,9},{9,1},{17,25},{25,17},{2,10},{10... | collective-permute-start | bytes 589832 | tf_op jit(solution)/shard_map/ppermute | solution.py:726
  18.9 11.3 %collective-permute-start.9 = (bf16[4,64,384]{2,1,0:T(8,128)(2,1)S(1)}, bf16[4,64,384]{2,1,0:T(8,128)(2,1)S(1)}, u32[]{:S(2)}, u32[]{:S(2)}) collective-permute-start(bf16[4,64,384]{2,1,0:T(8,128)(2,1)S(1)} %get-tuple-element.219), channel_id=1, source_target_pairs={{0,16},{8,24},{16,0},{24,8},{1,17},{9,25},{17,1},{25,9},{2,18},{10... | collective-permute-start | bytes 589832 | tf_op jit(solution)/shard_map/ppermute | solution.py:726
  27.6 15.9 %collective-permute-start.6 = (bf16[64,2560]{1,0:T(8,128)(2,1)}, bf16[64,2560]{1,0:T(8,128)(2,1)S(1)}, u32[]{:S(2)}, u32[]{:S(2)}) collective-permute-start(bf16[64,2560]{1,0:T(8,128)(2,1)} %pad_maximum_fusion.16), channel_id=1, source_target_pairs={{0,4},{1,5},{2,6},{3,7},{4,0},{5,1},{6,2},{7,3},{8,12},{9,13},{10,... | collective-permute-start | bytes 983048 | tf_op jit(solution)/shard_map/ppermute | solution.py:726
  33.6 11.1 %collective-permute-start.11 = (bf16[4,4,64,384]{3,2,1,0:T(8,128)(2,1)S(1)}, bf16[4,4,64,384]{3,2,1,0:T(8,128)(2,1)S(1)}, u32[]{:S(2)}, u32[]{:S(2)}) collective-permute-start(bf16[4,4,64,384]{3,2,1,0:T(8,128)(2,1)S(1)} %pad_maximum_fusion.3.refs_0_), channel_id=1, source_target_pairs={{0,1},{1,0},{2,3},{3,2},{4,5},{5,4},{6,7},{7,6},{8,9},{9,8},{10,11... | collective-permute-start | bytes 2359304 | tf_op jit(solution)/shard_map/ppermute | solution.py:726
  34.9 25.7 %collective-permute-start.12 = (bf16[512,512]{1,0:T(8,128)(2,1)S(1)}, bf16[512,512]{1,0:T(8,128)(2,1)S(1)}, u32[]{:S(2)}, u32[]{:S(2)}) collective-permute-start(bf16[512,512]{1,0:T(8,128)(2,1)S(1)} %get-tuple-element.225), channel_id=1, source_target_pairs={{0,8},{8,0},{16,24},{24,16},{1,9},{9,1},{17,25},{25,17},{2,10},{10... | collective-permute-start | bytes 1572872 | tf_op jit(solution)/shard_map/ppermute | solution.py:726
  36.5 25.1 %collective-permute-start.13 = (bf16[512,512]{1,0:T(8,128)(2,1)S(1)}, bf16[512,512]{1,0:T(8,128)(2,1)S(1)}, u32[]{:S(2)}, u32[]{:S(2)}) collective-permute-start(bf16[512,512]{1,0:T(8,128)(2,1)S(1)} %get-tuple-element.226), channel_id=1, source_target_pairs={{0,16},{8,24},{16,0},{24,8},{1,17},{9,25},{17,1},{25,9},{2,18},{10... | collective-permute-start | bytes 1572872 | tf_op jit(solution)/shard_map/ppermute | solution.py:726
  38.0 23.6 %collective-permute-start.14 = (bf16[512,512]{1,0:T(8,128)(2,1)S(1)}, bf16[512,512]{1,0:T(8,128)(2,1)S(1)}, u32[]{:S(2)}, u32[]{:S(2)}) collective-permute-start(bf16[512,512]{1,0:T(8,128)(2,1)S(1)} %get-tuple-element.224), channel_id=1, source_target_pairs={{0,24},{8,16},{16,8},{24,0},{1,25},{9,17},{17,9},{25,1},{2,26},{10... | collective-permute-start | bytes 1572872 | tf_op jit(solution)/shard_map/ppermute | solution.py:726
  44.6 15.7 %collective-permute-start.7 = (bf16[2,64,2560]{2,1,0:T(8,128)(2,1)S(1)}, bf16[2,64,2560]{2,1,0:T(8,128)(2,1)S(1)}, u32[]{:S(2)}, u32[]{:S(2)}) collective-permute-start(bf16[2,64,2560]{2,1,0:T(8,128)(2,1)S(1)} %pad_maximum_fusion.8), channel_id=1, source_target_pairs={{0,2},{1,3},{2,0},{3,1},{4,6},{5,7},{6,4},{7,5},{8,10},{9,11},{10,... | collective-permute-start | bytes 1966088 | tf_op jit(solution)/shard_map/ppermute | solution.py:726
  82.4 16.1 %collective-permute-start.17 = (bf16[4,4,2,128,128]{4,3,2,1,0:T(8,128)(2,1)S(1)}, bf16[4,4,2,128,128]{4,3,2,1,0:T(8,128)(2,1)S(1)}, u32[]{:S(2)}, u32[]{:S(2)}) collective-permute-start(bf16[4,4,2,128,128]{4,3,2,1,0:T(8,128)(2,1)S(1)} %get-tuple-element.111), channel_id=1, source_target_pairs={{0,1},{1,0},{2,3},{3,2},{4,5},{5,4},{6,7},{7,6},{8,9},{9,8},{10,11... | collective-permute-start | bytes 3145736 | tf_op jit(solution)/shard_map/ppermute | solution.py:726
  82.7 15.8 %collective-permute-start.18 = (bf16[256,512]{1,0:T(8,128)(2,1)S(1)}, bf16[256,512]{1,0:T(8,128)(2,1)S(1)}, u32[]{:S(2)}, u32[]{:S(2)}) collective-permute-start(bf16[256,512]{1,0:T(8,128)(2,1)S(1)} %get-tuple-element.204), channel_id=1, source_target_pairs={{0,8},{8,0},{16,24},{24,16},{1,9},{9,1},{17,25},{25,17},{2,10},{10... | collective-permute-start | bytes 786440 | tf_op jit(solution)/shard_map/ppermute | solution.py:726
  84.1 14.3 %collective-permute-start.19 = (bf16[256,512]{1,0:T(8,128)(2,1)S(1)}, bf16[256,512]{1,0:T(8,128)(2,1)S(1)}, u32[]{:S(2)}, u32[]{:S(2)}) collective-permute-start(bf16[256,512]{1,0:T(8,128)(2,1)S(1)} %get-tuple-element.203), channel_id=1, source_target_pairs={{0,16},{8,24},{16,0},{24,8},{1,17},{9,25},{17,1},{25,9},{2,18},{10... | collective-permute-start | bytes 786440 | tf_op jit(solution)/shard_map/ppermute | solution.py:726
  84.8 13.7 %collective-permute-start.20 = (bf16[256,512]{1,0:T(8,128)(2,1)S(1)}, bf16[256,512]{1,0:T(8,128)(2,1)S(1)}, u32[]{:S(2)}, u32[]{:S(2)}) collective-permute-start(bf16[256,512]{1,0:T(8,128)(2,1)S(1)} %get-tuple-element.202), channel_id=1, source_target_pairs={{0,24},{8,16},{16,8},{24,0},{1,25},{9,17},{17,9},{25,1},{2,26},{10... | collective-permute-start | bytes 786440 | tf_op jit(solution)/shard_map/ppermute | solution.py:726
  98.8 14.9 %collective-permute-start.22 = (bf16[4,2,128,128]{3,2,1,0:T(8,128)(2,1)S(1)}, bf16[4,2,128,128]{3,2,1,0:T(8,128)(2,1)S(1)}, u32[]{:S(2)}, u32[]{:S(2)}) collective-permute-start(bf16[4,2,128,128]{3,2,1,0:T(8,128)(2,1)S(1)} %get-tuple-element.190), channel_id=1, source_target_pairs={{0,2},{1,3},{2,0},{3,1},{4,6},{5,7},{6,4},{7,5},{8,10},{9,11},{10,... | collective-permute-start | bytes 786440 | tf_op jit(solution)/shard_map/ppermute | solution.py:726
  99.6 14.1 %collective-permute-start.21 = (bf16[4,4,64,640]{3,2,1,0:T(8,128)(2,1)S(1)}, bf16[4,4,64,640]{3,2,1,0:T(8,128)(2,1)S(1)}, u32[]{:S(2)}, u32[]{:S(2)}) collective-permute-start(bf16[4,4,64,640]{3,2,1,0:T(8,128)(2,1)S(1)} %get-tuple-element.128), channel_id=1, source_target_pairs={{0,1},{1,0},{2,3},{3,2},{4,5},{5,4},{6,7},{7,6},{8,9},{9,8},{10,11... | collective-permute-start | bytes 3932168 | tf_op jit(solution)/shard_map/ppermute | solution.py:726
  99.6 32.5 %collective-permute-start.26 = (bf16[4,2,128,128]{3,2,1,0:T(8,128)(2,1)S(1)}, bf16[4,2,128,128]{3,2,1,0:T(8,128)(2,1)S(1)}, u32[]{:S(2)}, u32[]{:S(2)}) collective-permute-start(bf16[4,2,128,128]{3,2,1,0:T(8,128)(2,1)S(1)} %get-tuple-element.188), channel_id=1, source_target_pairs={{0,4},{1,5},{2,6},{3,7},{4,0},{5,1},{6,2},{7,3},{8,12},{9,13},{10,... | collective-permute-start | bytes 786440 | tf_op jit(solution)/shard_map/ppermute | solution.py:726
  103.0 29.1 %collective-permute-start.27 = (bf16[4,2,128,128]{3,2,1,0:T(8,128)(2,1)S(1)}, bf16[4,2,128,128]{3,2,1,0:T(8,128)(2,1)S(1)}, u32[]{:S(2)}, u32[]{:S(2)}) collective-permute-start(bf16[4,2,128,128]{3,2,1,0:T(8,128)(2,1)S(1)} %get-tuple-element.187), channel_id=1, source_target_pairs={{0,6},{1,7},{2,4},{3,5},{4,2},{5,3},{6,0},{7,1},{8,14},{9,15},{10,... | collective-permute-start | bytes 786440 | tf_op jit(solution)/shard_map/ppermute | solution.py:726
  114.1 18.0 %collective-permute-start.23 = (bf16[4,64,640]{2,1,0:T(8,128)(2,1)S(1)}, bf16[4,64,640]{2,1,0:T(8,128)(2,1)S(1)}, u32[]{:S(2)}, u32[]{:S(2)}) collective-permute-start(bf16[4,64,640]{2,1,0:T(8,128)(2,1)S(1)} %get-tuple-element.185), channel_id=1, source_target_pairs={{0,8},{8,0},{16,24},{24,16},{1,9},{9,1},{17,25},{25,17},{2,10},{10... | collective-permute-start | bytes 983048 | tf_op jit(solution)/shard_map/ppermute | solution.py:726
  115.5 16.5 %collective-permute-start.24 = (bf16[4,64,640]{2,1,0:T(8,128)(2,1)S(1)}, bf16[4,64,640]{2,1,0:T(8,128)(2,1)S(1)}, u32[]{:S(2)}, u32[]{:S(2)}) collective-permute-start(bf16[4,64,640]{2,1,0:T(8,128)(2,1)S(1)} %get-tuple-element.184), channel_id=1, source_target_pairs={{0,16},{8,24},{16,0},{24,8},{1,17},{9,25},{17,1},{25,9},{2,18},{10... | collective-permute-start | bytes 983048 | tf_op jit(solution)/shard_map/ppermute | solution.py:726
  116.2 15.9 %collective-permute-start.25 = (bf16[4,64,640]{2,1,0:T(8,128)(2,1)S(1)}, bf16[4,64,640]{2,1,0:T(8,128)(2,1)S(1)}, u32[]{:S(2)}, u32[]{:S(2)}) collective-permute-start(bf16[4,64,640]{2,1,0:T(8,128)(2,1)S(1)} %get-tuple-element.183), channel_id=1, source_target_pairs={{0,24},{8,16},{16,8},{24,0},{1,25},{9,17},{17,9},{25,1},{2,26},{10... | collective-permute-start | bytes 983048 | tf_op jit(solution)/shard_map/ppermute | solution.py:726
  132.4 18.6 %collective-permute-start.32 = (bf16[2,64,640]{2,1,0:T(8,128)(2,1)S(1)}, bf16[2,64,640]{2,1,0:T(8,128)(2,1)S(1)}, u32[]{:S(2)}, u32[]{:S(2)}) collective-permute-start(bf16[2,64,640]{2,1,0:T(8,128)(2,1)S(1)} %slice.357), channel_id=1, source_target_pairs={{0,4},{1,5},{2,6},{3,7},{4,0},{5,1},{6,2},{7,3},{8,12},{9,13},{10,... | collective-permute-start | bytes 491528 | tf_op jit(solution)/shard_map/ppermute | solution.py:726
  134.7 16.3 %collective-permute-start.35 = (bf16[16,64,128]{2,1,0:T(8,128)(2,1)S(1)}, bf16[16,64,128]{2,1,0:T(8,128)(2,1)S(1)}, u32[]{:S(2)}, u32[]{:S(2)}) collective-permute-start(bf16[16,64,128]{2,1,0:T(8,128)(2,1)S(1)} %pad_maximum_fusion.20), channel_id=1, source_target_pairs={{0,24},{8,16},{16,8},{24,0},{1,25},{9,17},{17,9},{25,1},{2,26},{10... | collective-permute-start | bytes 786440 | tf_op jit(solution)/shard_map/ppermute | solution.py:726
  136.3 14.7 %collective-permute-start.34 = (bf16[16,64,128]{2,1,0:T(8,128)(2,1)S(1)}, bf16[16,64,128]{2,1,0:T(8,128)(2,1)S(1)}, u32[]{:S(2)}, u32[]{:S(2)}) collective-permute-start(bf16[16,64,128]{2,1,0:T(8,128)(2,1)S(1)} %pad_maximum_fusion.19), channel_id=1, source_target_pairs={{0,16},{8,24},{16,0},{24,8},{1,17},{9,25},{17,1},{25,9},{2,18},{10... | collective-permute-start | bytes 786440 | tf_op jit(solution)/shard_map/ppermute | solution.py:726
  141.1 9.9 %collective-permute-start.33 = (bf16[16,64,128]{2,1,0:T(8,128)(2,1)S(1)}, bf16[16,64,128]{2,1,0:T(8,128)(2,1)S(1)}, u32[]{:S(2)}, u32[]{:S(2)}) collective-permute-start(bf16[16,64,128]{2,1,0:T(8,128)(2,1)S(1)} %pad_maximum_fusion.18), channel_id=1, source_target_pairs={{0,8},{8,0},{16,24},{24,16},{1,9},{9,1},{17,25},{25,17},{2,10},{10... | collective-permute-start | bytes 786440 | tf_op jit(solution)/shard_map/ppermute | solution.py:726
  153.2 12.5 %collective-permute-start.36 = (bf16[272,512]{1,0:T(8,128)(2,1)S(1)}, bf16[272,512]{1,0:T(8,128)(2,1)S(1)}, u32[]{:S(2)}, u32[]{:S(2)}) collective-permute-start(bf16[272,512]{1,0:T(8,128)(2,1)S(1)} %get-tuple-element.236), channel_id=1, source_target_pairs={{0,24},{8,16},{16,8},{24,0},{1,25},{9,17},{17,9},{25,1},{2,26},{10... | collective-permute-start | bytes 835592 | tf_op jit(solution)/shard_map/ppermute | solution.py:726
  154.9 11.9 %collective-permute-start.37 = (bf16[272,512]{1,0:T(8,128)(2,1)S(1)}, bf16[272,512]{1,0:T(8,128)(2,1)S(1)}, u32[]{:S(2)}, u32[]{:S(2)}) collective-permute-start(bf16[272,512]{1,0:T(8,128)(2,1)S(1)} %get-tuple-element.235), channel_id=1, source_target_pairs={{0,16},{8,24},{16,0},{24,8},{1,17},{9,25},{17,1},{25,9},{2,18},{10... | collective-permute-start | bytes 835592 | tf_op jit(solution)/shard_map/ppermute | solution.py:726
  155.7 11.2 %collective-permute-start.38 = (bf16[272,512]{1,0:T(8,128)(2,1)S(1)}, bf16[272,512]{1,0:T(8,128)(2,1)S(1)}, u32[]{:S(2)}, u32[]{:S(2)}) collective-permute-start(bf16[272,512]{1,0:T(8,128)(2,1)S(1)} %get-tuple-element.234), channel_id=1, source_target_pairs={{0,8},{8,0},{16,24},{24,16},{1,9},{9,1},{17,25},{25,17},{2,10},{10... | collective-permute-start | bytes 835592 | tf_op jit(solution)/shard_map/ppermute | solution.py:726
  (31 other events, 191.9 us)

commit v6 on v5

--- a/solution.py
+++ b/solution.py
@@ -194,7 +194,7 @@
         in_specs=[IN_VMEM] * 3,
         out_specs=[IN_VMEM] * 3,
         out_shape=[jax.ShapeDtypeStruct((count, width // 2), BF16)] * 3,
-        compiler_params=params(10),
+        compiler_params=params(9),
         cost_estimate=cost(16 * count * count * 1024, 6 * 2**20),
         name="attend_back_half",
     )(projected, scaled, extra)
@@ -267,7 +267,7 @@
             pltpu.SemaphoreType.DMA((2,)),
         ],
         out_shape=[jax.ShapeDtypeStruct((count, width // 2), BF16)] * 3 + outs_of(pieces, True),
-        compiler_params=params(12),
+        compiler_params=params(11),
         cost_estimate=cost(20 * count * count * 1024, 10 * 2**20),
         name="attend_back_sum",
     )(own, projected, scaled, extra, normed, *first_half)
@@ -422,7 +422,7 @@
             pltpu.HBM((width, cols), BF16),
         ],
         compiler_params=params(10),
-        cost_estimate=cost(2 * count * width * cols, 8 * 2**20),
+        cost_estimate=cost(4 * (2 * count * width * cols), 4 * (8 * 2**20)),
         name="project",
     )(own, hidden, gain, *parts)
 
@@ -535,7 +535,7 @@
             jax.ShapeDtypeStruct(down_shape, BF16),
         ]
         + grads,
-        compiler_params=params(15),
+        compiler_params=params(12),
         cost_estimate=cost(7 * 2**30, 24 * 2**20),
         name="rise",
     )(own, hidden, att, cot, gain, *up_parts, *down_parts)
@@ -676,8 +676,8 @@
             jax.ShapeDtypeStruct((1, width), F32),
         ]
         + grads,
-        compiler_params=params(17),
-        cost_estimate=cost(8 * 2**30, 24 * 2**20),
+        compiler_params=params(14),
+        cost_estimate=cost(4 * (8 * 2**30), 4 * (24 * 2**20)),
         name="fall",
     )(own, cot, slope, normed, scale, att, den, gain, w_up, w_down)
 
@@ -849,7 +849,7 @@
         line_up = [line_up, swap_along(line_up, "dp", 2)]
         plane_qkv = gather_plane(line[..., :-width])
         line_down = line[..., -width:].reshape(-1, width)
-        plane_qkv, line_down, cot = together(plane_qkv, line_down, cotangent)
+        cot = cotangent
         parts_qkv = both_cores(plane_qkv)
         cot = from_plane([jnp.concatenate((part, line_down)) for part in by_partner(cot)])
     else:

time: 172 us -> 171 us (level)
  waiting for transfers between devices: 29.2 us -> 24.2 us
  local copies, waits for them, and re-layouts: 11.3 us -> 13.9 us
    ppermute x42, waiting for transfers between devices: 29.2 us -> 24.2 us  [swap_along(): return lax.ppermute(value, axis, [(i, i ^ mask) for i in range(count)])]
    slice x4, local copies, waits for them, and re-layouts: 0.79 us -> 2.7 us  [per_device(): block = jnp.concatenate([part[:segment] for part in came]).astype(F32)]
    unnamed x40 -> x38, local copies, waits for them, and re-layouts: 4.41 us -> 3.74 us
  transfers between devices with their start and end apart: 42 -> 42, of which waited for: 16 -> 16; matrix products, arithmetic and copies ran while one was open for 9% -> 10% of each run, Pallas kernels for 32% -> 32%
where the time goes in v6:
time: 171 us; the launch traced here: 168 us
  Pallas kernels  67.9 us (40%)
  starting transfers between devices  50.5 us (30%)
  waiting for transfers between devices  24.2 us (14%)
  local copies, waits for them, and re-layouts  13.9 us (8%)
  other arithmetic  9.57 us (6%)
  between operations  1.92 us (1%)
    ppermute x42, starting transfers between devices, swap_along(): return lax.ppermute(value, axis, [(i, i ^ mask) for i in range(count)])  50.5 us
    ppermute x42, waiting for transfers between devices, swap_along(): return lax.ppermute(value, axis, [(i, i ^ mask) for i in range(count)])  24.2 us
    pallas_call x1, Pallas kernels, rise(): pl.pallas_call(functools.partial(rise_kernel, cfg), in_specs=[pl.BlockSpe...  14.7 us
    pallas_call x1, Pallas kernels, attend_back_sum(): pl.pallas_call(functools.partial(attend_back_sum_kernel, min(512, count),...  14.4 us
    pallas_call x1, Pallas kernels, fall(): pl.pallas_call(functools.partial(fall_kernel, cfg), in_specs=[pl.BlockSpe...  12.2 us
    pallas_call x1, Pallas kernels, attend_back_half(): pl.pallas_call(functools.partial(attend_back_half_kernel, min(512, count)...  10.3 us
    pallas_call x1, Pallas kernels, attend_row(): pl.pallas_call(functools.partial(attend_row_kernel, min(256, count)), in_...  9.4 us
    unnamed x38, local copies, waits for them, and re-layouts  3.74 us
  transfers between devices with their start and end apart: 42, of which 16 were waited for; matrix products, arithmetic and copies ran while one was open for 10% of the time, Pallas kernels for 32%

profile of v6, /device:TPU:0, one launch (start us, length us, event | category | flops | bytes accessed | tf_op | source)
XLA Modules:
  0.0 167.9 jit_solution(8266419951741731665)
XLA Ops:
  3.1 3.0 %collective-permute-start.3 = (bf16[64,896]{1,0:T(8,128)(2,1)}, bf16[64,896]{1,0:T(8,128)(2,1)S(1)}, u32[]{:S(2)}, u32[]{:S(2)}) collective-permute-start(bf16[64,896]{1,0:T(8,128)(2,1)} %get-tuple-element.225), channel_id=1, source_target_pairs={{0,2},{1,3},{2,0},{3,1},{4,6},{5,7},{6,4},{7,5},{8,10},{9,11},{10,... | collective-permute-start | bytes 344072 | tf_op jit(solution)/shard_map/ppermute | solution.py:726
  6.1 2.6 %collective-permute-start.4 = (bf16[64,896]{1,0:T(8,128)(2,1)}, bf16[64,896]{1,0:T(8,128)(2,1)S(1)}, u32[]{:S(2)}, u32[]{:S(2)}) collective-permute-start(bf16[64,896]{1,0:T(8,128)(2,1)} %get-tuple-element.225), channel_id=1, source_target_pairs={{0,4},{1,5},{2,6},{3,7},{4,0},{5,1},{6,2},{7,3},{8,12},{9,13},{10,... | collective-permute-start | bytes 344072 | tf_op jit(solution)/shard_map/ppermute | solution.py:726
  9.5 2.1 %fusion.6 = (bf16[1,272,512]{2,1,0:T(8,128)(2,1)S(1)}, bf16[272,512]{1,0:T(8,128)(2,1)}, bf16[272,512]{1,0:T(8,128)(2,1)}, bf16[272,512]{1,0:T(8,128)(2,1)}) fusion(s32[]{:T(128)S(6)} %select_n.54, bf16[4,256,512]{2,1,0:T(8,128)(2,1)} %param.11, bf16[4,16,512]{2,1,0:T(8,128)(2,1)S(1)} %pad_convert_fusion, s32[]{:T(128)S(6)} %select_n.55, s32[]{:T(128)S(6)} %select_n.56, ...), kind=kLoop, calls=%fused_computation.48 | loop fusion | flops 2228224 | bytes 2228240 | tf_op jit(solution)/shard_map/concatenate | solution.py:840
  11.7 2.7 %collective-permute-start.2 = (bf16[272,512]{1,0:T(8,128)(2,1)}, bf16[272,512]{1,0:T(8,128)(2,1)}, u32[]{:S(2)}, u32[]{:S(2)}) collective-permute-start(bf16[272,512]{1,0:T(8,128)(2,1)} %get-tuple-element.192), channel_id=1, source_target_pairs={{0,24},{8,16},{16,8},{24,0},{1,25},{9,17},{17,9},{25,1},{2,26},{10... | collective-permute-start | bytes 835592 | tf_op jit(solution)/shard_map/ppermute | solution.py:726
  16.2 1.8 %collective-permute-done.4 = bf16[64,896]{1,0:T(8,128)(2,1)S(1)} collective-permute-done((bf16[64,896]{1,0:T(8,128)(2,1)}, bf16[64,896]{1,0:T(8,128)(2,1)S(1)}, u32[]{:S(2)}, u32[]{:S(2)}) %collective-permute-start.4) | collective-permute-done | bytes 114720 | tf_op jit(solution)/shard_map/ppermute | solution.py:726
  18.1 1.6 collective-permute-start.8
  22.5 2.6 %collective-permute-start.10 = (bf16[4,64,384]{2,1,0:T(8,128)(2,1)S(1)}, bf16[4,64,384]{2,1,0:T(8,128)(2,1)S(1)}, u32[]{:S(2)}, u32[]{:S(2)}) collective-permute-start(bf16[4,64,384]{2,1,0:T(8,128)(2,1)S(1)} %get-tuple-element.213), channel_id=1, source_target_pairs={{0,24},{8,16},{16,8},{24,0},{1,25},{9,17},{17,9},{25,1},{2,26},{10... | collective-permute-start | bytes 589832 | tf_op jit(solution)/shard_map/ppermute | solution.py:726
  26.8 1.6 collective-permute-start.6
  29.1 3.7 %collective-permute-done.8 = bf16[4,64,384]{2,1,0:T(8,128)(2,1)S(1)} collective-permute-done((bf16[4,64,384]{2,1,0:T(8,128)(2,1)S(1)}, bf16[4,64,384]{2,1,0:T(8,128)(2,1)S(1)}, u32[]{:S(2)}, u32[]{:S(2)}) %collective-permute-start.8) | collective-permute-done | bytes 196640 | tf_op jit(solution)/shard_map/ppermute | solution.py:726
  34.9 2.0 %collective-permute-done.10 = bf16[4,64,384]{2,1,0:T(8,128)(2,1)S(1)} collective-permute-done((bf16[4,64,384]{2,1,0:T(8,128)(2,1)S(1)}, bf16[4,64,384]{2,1,0:T(8,128)(2,1)S(1)}, u32[]{:S(2)}, u32[]{:S(2)}) %collective-permute-start.10) | collective-permute-done | bytes 196640 | tf_op jit(solution)/shard_map/ppermute | solution.py:726
  36.8 2.6 %collective-permute-start.14 = (bf16[512,512]{1,0:T(8,128)(2,1)S(1)}, bf16[512,512]{1,0:T(8,128)(2,1)S(1)}, u32[]{:S(2)}, u32[]{:S(2)}) collective-permute-start(bf16[512,512]{1,0:T(8,128)(2,1)S(1)} %get-tuple-element.218), channel_id=1, source_target_pairs={{0,24},{8,16},{16,8},{24,0},{1,25},{9,17},{17,9},{25,1},{2,26},{10... | collective-permute-start | bytes 1572872 | tf_op jit(solution)/shard_map/ppermute | solution.py:726
  42.0 2.3 %collective-permute-done.6 = bf16[64,2560]{1,0:T(8,128)(2,1)S(1)} collective-permute-done((bf16[64,2560]{1,0:T(8,128)(2,1)S(1)}, bf16[64,2560]{1,0:T(8,128)(2,1)S(1)}, u32[]{:S(2)}, u32[]{:S(2)}) %collective-permute-start.6) | collective-permute-done | bytes 327712 | tf_op jit(solution)/shard_map/ppermute | solution.py:726
  44.4 3.7 %project.1 = (bf16[1024,512]{1,0:T(8,128)(2,1)}, bf16[1024,1536]{1,0:T(8,128)(2,1)S(1)}, bf16[512,1536]{1,0:T(8,128)(2,1)}) custom-call(s32[3]{0:T(128)S(1)} %pad_add_fusion.own_ref, f32[1024,512]{1,0:T(8,128)S(1)} %multiply_add_fusion.hidden_ref, f32[1,512]{1,0:T(1,128)S(1)} %bitcast.117, bf16[4,4,64,384]{3,2,1,0:T(8,128)(2,1)S(1)} %pad_maximum_fusion.3.refs_0_, ...), custom_call_target="tpu_custom_call" | custom-call | flops 6442450944 | bytes 33554432 | tf_op jit(solution)/shard_map/project/pallas_call | solution.py:407
  48.2 9.4 %attend_row.1 = (bf16[1024,512]{1,0:T(8,128)(2,1)S(1)}, f32[1024,128]{1,0:T(8,128)S(1)}) custom-call(bf16[1024,1536]{1,0:T(8,128)(2,1)S(1)} %get-tuple-element.94.own_ref.proj_ref), custom_call_target="tpu_custom_call" | custom-call | flops 17179869184 | bytes 5242880 | tf_op jit(solution)/shard_map/attend_row/pallas_call | solution.py:120
  66.7 14.7 %rise.1 = (bf16[1024,512]{1,0:T(8,128)(2,1)S(1)}, f32[1024,512]{1,0:T(8,128)S(1)}, f32[1024,128]{1,0:T(8,128)S(1)}, bf16[1024,2048]{1,0:T(8,128)(2,1)S(1)}, bf16...) custom-call(s32[3]{0:T(128)S(1)} %pad_add_fusion.own_ref, ...), custom_call_target="tpu_custom_call" | custom-call | flops 7516192768 | bytes 25165824 | tf_op jit(solution)/shard_map/rise/pallas_call | solution.py:515
  81.4 1.6 collective-permute-start.18
  83.1 1.9 %collective-permute-start.20 = (bf16[256,512]{1,0:T(8,128)(2,1)S(1)}, bf16[256,512]{1,0:T(8,128)(2,1)S(1)}, u32[]{:S(2)}, u32[]{:S(2)}) collective-permute-start(bf16[256,512]{1,0:T(8,128)(2,1)S(1)} %get-tuple-element.196), channel_id=1, source_target_pairs={{0,24},{8,16},{16,8},{24,0},{1,25},{9,17},{17,9},{25,1},{2,26},{10... | collective-permute-start | bytes 786440 | tf_op jit(solution)/shard_map/ppermute | solution.py:726
  85.0 12.2 %fall.1 = (f32[1024,512]{1,0:T(8,128)S(1)}, bf16[1024,512]{1,0:T(8,128)(2,1)S(1)}, bf16[1024,512]{1,0:T(8,128)(2,1)S(1)}, f32[1,512]{1,0:T(1,128)S(1)}, bf16[4,4...) custom-call(s32[3]{0:T(128)S(1)} %pad_add_fusion.own_ref, ...), custom_call_target="tpu_custom_call" | custom-call | flops 34359738368 | bytes 100663296 | tf_op jit(solution)/shard_map/fall/pallas_call | solution.py:660
  99.1 2.8 %collective-permute-start.26 = (bf16[4,2,128,128]{3,2,1,0:T(8,128)(2,1)S(1)}, bf16[4,2,128,128]{3,2,1,0:T(8,128)(2,1)S(1)}, u32[]{:S(2)}, u32[]{:S(2)}) collective-permute-start(bf16[4,2,128,128]{3,2,1,0:T(8,128)(2,1)S(1)} %get-tuple-element.182), channel_id=1, source_target_pairs={{0,4},{1,5},{2,6},{3,7},{4,0},{5,1},{6,2},{7,3},{8,12},{9,13},{10,... | collective-permute-start | bytes 786440 | tf_op jit(solution)/shard_map/ppermute | solution.py:726
  102.3 10.3 %attend_back_half.1 = (bf16[1024,256]{1,0:T(8,128)(2,1)S(1)}, bf16[1024,256]{1,0:T(8,128)(2,1)S(1)}, bf16[1024,256]{1,0:T(8,128)(2,1)S(1)}) custom-call(bf16[1024,1536]{1,0:T(8,128)(2,1)S(1)} %copy-done.5, bf16[1024,512]{1,0:T(8,128)(2,1)S(1)} %get-tuple-element.123.s_ref, bf16[1024,512]{1,0:T(8,128)(2,1)S(1)} %get-tuple-element.124.x_ref), custom_call_target="tpu_custom_call" | custom-call | flops 17179869184 | bytes 6291456 | tf_op jit(solution)/shard_map/attend_back_half/pallas_call | solution.py:192
  113.1 1.6 collective-permute-start.23
  114.8 1.9 %collective-permute-start.25 = (bf16[4,64,640]{2,1,0:T(8,128)(2,1)S(1)}, bf16[4,64,640]{2,1,0:T(8,128)(2,1)S(1)}, u32[]{:S(2)}, u32[]{:S(2)}) collective-permute-start(bf16[4,64,640]{2,1,0:T(8,128)(2,1)S(1)} %get-tuple-element.177), channel_id=1, source_target_pairs={{0,24},{8,16},{16,8},{24,0},{1,25},{9,17},{17,9},{25,1},{2,26},{10... | collective-permute-start | bytes 983048 | tf_op jit(solution)/shard_map/ppermute | solution.py:726
  116.7 14.4 %attend_back_sum.1 = (bf16[1024,256]{1,0:T(8,128)(2,1)S(1)}, bf16[1024,256]{1,0:T(8,128)(2,1)S(1)}, bf16[1024,256]{1,0:T(8,128)(2,1)S(1)}, bf16[4,4,3,64,128]{4,...) custom-call(s32[3]{0:T(128)S(1)} %pad_add_fusion.own_ref, bf16[1024,1536]{1,0:T(8,128)(2,1)S(1)} %copy-done.5, ...), custom_call_target="tpu_custom_call" | custom-call | flops 21474836480 | bytes 10485760 | tf_op jit(solution)/shard_map/attend_back_sum/pallas_call | solution.py:259
  135.0 2.0 %collective-permute-start.34 = (bf16[16,64,128]{2,1,0:T(8,128)(2,1)S(1)}, bf16[16,64,128]{2,1,0:T(8,128)(2,1)S(1)}, u32[]{:S(2)}, u32[]{:S(2)}) collective-permute-start(bf16[16,64,128]{2,1,0:T(8,128)(2,1)S(1)} %pad_maximum_fusion.19), channel_id=1, source_target_pairs={{0,16},{8,24},{16,0},{24,8},{1,17},{9,25},{17,1},{25,9},{2,18},{10... | collective-permute-start | bytes 786440 | tf_op jit(solution)/shard_map/ppermute | solution.py:726
  136.9 3.3 %last.1 = (bf16[1024,512]{1,0:T(8,128)(2,1)S(1)}, f32[8,512]{1,0:T(8,128)S(1)}) custom-call(f32[1024,512]{1,0:T(8,128)S(1)} %multiply_add_fusion.hidden_ref, f32[1024,512]{1,0:T(8,128)S(1)} %get-tuple-element.120.first_ref, f32[1,512]{1,0:T(1,128)S(1)} %bitcast.118, bf16[8,1024]{1,0:T(8,128)(2,1)S(1)} %broadcast_in_dim.56.mask_ref, ...), custom_call_target="tpu_custom_call" | custom-call | flops 12884901888 | bytes 100663296 | tf_op jit(solution)/shard_map/last/pallas_call | solution.py:710
  141.6 2.2 %collective-permute-start.30 = (f32[8,512]{1,0:T(8,128)S(1)}, f32[8,512]{1,0:T(8,128)S(1)}, u32[]{:S(2)}, u32[]{:S(2)}) collective-permute-start(f32[8,512]{1,0:T(8,128)S(1)} %fusion.21), channel_id=1, source_target_pairs={{0,2},{1,3},{2,0},{3,1},{4,6},{5,7},{6,4},{7,5},{8,10},{9,11},{10,... | collective-permute-start | bytes 49160 | tf_op jit(solution)/shard_map/ppermute | solution.py:726
  143.8 1.7 %collective-permute-done.30 = f32[8,512]{1,0:T(8,128)S(1)} collective-permute-done((f32[8,512]{1,0:T(8,128)S(1)}, f32[8,512]{1,0:T(8,128)S(1)}, u32[]{:S(2)}, u32[]{:S(2)}) %collective-permute-start.30) | collective-permute-done | bytes 16416 | tf_op jit(solution)/shard_map/ppermute | solution.py:726
  145.5 1.8 %collective-permute-start.31 = (f32[8,512]{1,0:T(8,128)S(1)}, f32[8,512]{1,0:T(8,128)S(1)}, u32[]{:S(2)}, u32[]{:S(2)}) collective-permute-start(f32[8,512]{1,0:T(8,128)S(1)} %add.186), channel_id=1, source_target_pairs={{0,4},{1,5},{2,6},{3,7},{4,0},{5,1},{6,2},{7,3},{8,12},{9,13},{10,... | collective-permute-start | bytes 49160 | tf_op jit(solution)/shard_map/ppermute | solution.py:726
  147.3 2.8 %collective-permute-done.31 = f32[8,512]{1,0:T(8,128)S(1)} collective-permute-done((f32[8,512]{1,0:T(8,128)S(1)}, f32[8,512]{1,0:T(8,128)S(1)}, u32[]{:S(2)}, u32[]{:S(2)}) %collective-permute-start.31) | collective-permute-done | bytes 16416 | tf_op jit(solution)/shard_map/ppermute | solution.py:726
  150.3 1.8 %collective-permute-start.39 = (bf16[2,3,64,128]{3,2,1,0:T(8,128)(2,1)S(1)}, bf16[2,3,64,128]{3,2,1,0:T(8,128)(2,1)S(1)}, u32[]{:S(2)}, u32[]{:S(2)}) collective-permute-start(bf16[2,3,64,128]{3,2,1,0:T(8,128)(2,1)S(1)} %bitcast.146), channel_id=1, source_target_pairs={{0,4},{1,5},{2,6},{3,7},{4,0},{5,1},{6,2},{7,3},{8,12},{9,13},{10,... | collective-permute-start | bytes 294920 | tf_op jit(solution)/shard_map/ppermute | solution.py:726
  156.4 1.8 %collective-permute-start.40 = (bf16[1,3,64,128]{3,2,1,0:T(8,128)(2,1)S(1)}, bf16[1,3,64,128]{3,2,1,0:T(8,128)(2,1)S(1)}, u32[]{:S(2)}, u32[]{:S(2)}) collective-permute-start(bf16[1,3,64,128]{3,2,1,0:T(8,128)(2,1)S(1)} %slice.374), channel_id=1, source_target_pairs={{0,2},{1,3},{2,0},{3,1},{4,6},{5,7},{6,4},{7,5},{8,10},{9,11},{10,... | collective-permute-start | bytes 147464 | tf_op jit(solution)/shard_map/ppermute | solution.py:726
  161.2 2.3 %collective-permute-done.41 = bf16[1,64,640]{2,1,0:T(8,128)(2,1)S(1)} collective-permute-done((bf16[1,64,640]{2,1,0:T(8,128)(2,1)S(1)}, bf16[1,64,640]{2,1,0:T(8,128)(2,1)S(1)}, u32[]{:S(2)}, u32[]{:S(2)}) %collective-permute-start.41) | collective-permute-done | bytes 81952 | tf_op jit(solution)/shard_map/ppermute | solution.py:726
  (178 shorter events, 43.3 us)
Async XLA Ops:
  3.1 12.8 %collective-permute-start.3 = (bf16[64,896]{1,0:T(8,128)(2,1)}, bf16[64,896]{1,0:T(8,128)(2,1)S(1)}, u32[]{:S(2)}, u32[]{:S(2)}) collective-permute-start(bf16[64,896]{1,0:T(8,128)(2,1)} %get-tuple-element.225), channel_id=1, source_target_pairs={{0,2},{1,3},{2,0},{3,1},{4,6},{5,7},{6,4},{7,5},{8,10},{9,11},{10,... | collective-permute-start | bytes 344072 | tf_op jit(solution)/shard_map/ppermute | solution.py:726
  6.1 11.9 %collective-permute-start.4 = (bf16[64,896]{1,0:T(8,128)(2,1)}, bf16[64,896]{1,0:T(8,128)(2,1)S(1)}, u32[]{:S(2)}, u32[]{:S(2)}) collective-permute-start(bf16[64,896]{1,0:T(8,128)(2,1)} %get-tuple-element.225), channel_id=1, source_target_pairs={{0,4},{1,5},{2,6},{3,7},{4,0},{5,1},{6,2},{7,3},{8,12},{9,13},{10,... | collective-permute-start | bytes 344072 | tf_op jit(solution)/shard_map/ppermute | solution.py:726
  8.7 9.3 %collective-permute-start.5 = (bf16[64,896]{1,0:T(8,128)(2,1)}, bf16[64,896]{1,0:T(8,128)(2,1)S(1)}, u32[]{:S(2)}, u32[]{:S(2)}) collective-permute-start(bf16[64,896]{1,0:T(8,128)(2,1)} %get-tuple-element.225), channel_id=1, source_target_pairs={{0,6},{1,7},{2,4},{3,5},{4,2},{5,3},{6,0},{7,1},{8,14},{9,15},{10,... | collective-permute-start | bytes 344072 | tf_op jit(solution)/shard_map/ppermute | solution.py:726
  11.7 10.9 %collective-permute-start.2 = (bf16[272,512]{1,0:T(8,128)(2,1)}, bf16[272,512]{1,0:T(8,128)(2,1)}, u32[]{:S(2)}, u32[]{:S(2)}) collective-permute-start(bf16[272,512]{1,0:T(8,128)(2,1)} %get-tuple-element.192), channel_id=1, source_target_pairs={{0,24},{8,16},{16,8},{24,0},{1,25},{9,17},{17,9},{25,1},{2,26},{10... | collective-permute-start | bytes 835592 | tf_op jit(solution)/shard_map/ppermute | solution.py:726
  14.3 12.4 %collective-permute-start.1 = (bf16[272,512]{1,0:T(8,128)(2,1)}, bf16[272,512]{1,0:T(8,128)(2,1)}, u32[]{:S(2)}, u32[]{:S(2)}) collective-permute-start(bf16[272,512]{1,0:T(8,128)(2,1)} %get-tuple-element.191), channel_id=1, source_target_pairs={{0,16},{8,24},{16,0},{24,8},{1,17},{9,25},{17,1},{25,9},{2,18},{10... | collective-permute-start | bytes 835592 | tf_op jit(solution)/shard_map/ppermute | solution.py:726
  15.8 23.7 %collective-permute-start = (bf16[272,512]{1,0:T(8,128)(2,1)}, bf16[272,512]{1,0:T(8,128)(2,1)S(1)}, u32[]{:S(2)}, u32[]{:S(2)}) collective-permute-start(bf16[272,512]{1,0:T(8,128)(2,1)} %get-tuple-element.190), channel_id=1, source_target_pairs={{0,8},{8,0},{16,24},{24,16},{1,9},{9,1},{17,25},{25,17},{2,10},{10... | collective-permute-start | bytes 835592 | tf_op jit(solution)/shard_map/ppermute | solution.py:726
  18.1 14.7 %collective-permute-start.8 = (bf16[4,64,384]{2,1,0:T(8,128)(2,1)S(1)}, bf16[4,64,384]{2,1,0:T(8,128)(2,1)S(1)}, u32[]{:S(2)}, u32[]{:S(2)}) collective-permute-start(bf16[4,64,384]{2,1,0:T(8,128)(2,1)S(1)} %get-tuple-element.213), channel_id=1, source_target_pairs={{0,8},{8,0},{16,24},{24,16},{1,9},{9,1},{17,25},{25,17},{2,10},{10... | collective-permute-start | bytes 589832 | tf_op jit(solution)/shard_map/ppermute | solution.py:726
  19.7 14.6 %collective-permute-start.9 = (bf16[4,64,384]{2,1,0:T(8,128)(2,1)S(1)}, bf16[4,64,384]{2,1,0:T(8,128)(2,1)S(1)}, u32[]{:S(2)}, u32[]{:S(2)}) collective-permute-start(bf16[4,64,384]{2,1,0:T(8,128)(2,1)S(1)} %get-tuple-element.213), channel_id=1, source_target_pairs={{0,16},{8,24},{16,0},{24,8},{1,17},{9,25},{17,1},{25,9},{2,18},{10... | collective-permute-start | bytes 589832 | tf_op jit(solution)/shard_map/ppermute | solution.py:726
  22.5 14.3 %collective-permute-start.10 = (bf16[4,64,384]{2,1,0:T(8,128)(2,1)S(1)}, bf16[4,64,384]{2,1,0:T(8,128)(2,1)S(1)}, u32[]{:S(2)}, u32[]{:S(2)}) collective-permute-start(bf16[4,64,384]{2,1,0:T(8,128)(2,1)S(1)} %get-tuple-element.213), channel_id=1, source_target_pairs={{0,24},{8,16},{16,8},{24,0},{1,25},{9,17},{17,9},{25,1},{2,26},{10... | collective-permute-start | bytes 589832 | tf_op jit(solution)/shard_map/ppermute | solution.py:726
  26.8 17.5 %collective-permute-start.6 = (bf16[64,2560]{1,0:T(8,128)(2,1)S(1)}, bf16[64,2560]{1,0:T(8,128)(2,1)S(1)}, u32[]{:S(2)}, u32[]{:S(2)}) collective-permute-start(bf16[64,2560]{1,0:T(8,128)(2,1)S(1)} %pad_maximum_fusion.16), channel_id=1, source_target_pairs={{0,4},{1,5},{2,6},{3,7},{4,0},{5,1},{6,2},{7,3},{8,12},{9,13},{10,... | collective-permute-start | bytes 983048 | tf_op jit(solution)/shard_map/ppermute | solution.py:726
  32.9 27.6 %collective-permute-start.12 = (bf16[512,512]{1,0:T(8,128)(2,1)S(1)}, bf16[512,512]{1,0:T(8,128)(2,1)S(1)}, u32[]{:S(2)}, u32[]{:S(2)}) collective-permute-start(bf16[512,512]{1,0:T(8,128)(2,1)S(1)} %get-tuple-element.219), channel_id=1, source_target_pairs={{0,8},{8,0},{16,24},{24,16},{1,9},{9,1},{17,25},{25,17},{2,10},{10... | collective-permute-start | bytes 1572872 | tf_op jit(solution)/shard_map/ppermute | solution.py:726
  34.3 26.1 %collective-permute-start.13 = (bf16[512,512]{1,0:T(8,128)(2,1)S(1)}, bf16[512,512]{1,0:T(8,128)(2,1)S(1)}, u32[]{:S(2)}, u32[]{:S(2)}) collective-permute-start(bf16[512,512]{1,0:T(8,128)(2,1)S(1)} %get-tuple-element.220), channel_id=1, source_target_pairs={{0,16},{8,24},{16,0},{24,8},{1,17},{9,25},{17,1},{25,9},{2,18},{10... | collective-permute-start | bytes 1572872 | tf_op jit(solution)/shard_map/ppermute | solution.py:726
  36.8 23.6 %collective-permute-start.14 = (bf16[512,512]{1,0:T(8,128)(2,1)S(1)}, bf16[512,512]{1,0:T(8,128)(2,1)S(1)}, u32[]{:S(2)}, u32[]{:S(2)}) collective-permute-start(bf16[512,512]{1,0:T(8,128)(2,1)S(1)} %get-tuple-element.218), channel_id=1, source_target_pairs={{0,24},{8,16},{16,8},{24,0},{1,25},{9,17},{17,9},{25,1},{2,26},{10... | collective-permute-start | bytes 1572872 | tf_op jit(solution)/shard_map/ppermute | solution.py:726
  44.3 15.8 %collective-permute-start.7 = (bf16[2,64,2560]{2,1,0:T(8,128)(2,1)S(1)}, bf16[2,64,2560]{2,1,0:T(8,128)(2,1)S(1)}, u32[]{:S(2)}, u32[]{:S(2)}) collective-permute-start(bf16[2,64,2560]{2,1,0:T(8,128)(2,1)S(1)} %pad_maximum_fusion.8), channel_id=1, source_target_pairs={{0,2},{1,3},{2,0},{3,1},{4,6},{5,7},{6,4},{7,5},{8,10},{9,11},{10,... | collective-permute-start | bytes 1966088 | tf_op jit(solution)/shard_map/ppermute | solution.py:726
  81.4 15.8 %collective-permute-start.18 = (bf16[256,512]{1,0:T(8,128)(2,1)S(1)}, bf16[256,512]{1,0:T(8,128)(2,1)S(1)}, u32[]{:S(2)}, u32[]{:S(2)}) collective-permute-start(bf16[256,512]{1,0:T(8,128)(2,1)S(1)} %get-tuple-element.198), channel_id=1, source_target_pairs={{0,8},{8,0},{16,24},{24,16},{1,9},{9,1},{17,25},{25,17},{2,10},{10... | collective-permute-start | bytes 786440 | tf_op jit(solution)/shard_map/ppermute | solution.py:726
  83.0 14.2 %collective-permute-start.19 = (bf16[256,512]{1,0:T(8,128)(2,1)S(1)}, bf16[256,512]{1,0:T(8,128)(2,1)S(1)}, u32[]{:S(2)}, u32[]{:S(2)}) collective-permute-start(bf16[256,512]{1,0:T(8,128)(2,1)S(1)} %get-tuple-element.197), channel_id=1, source_target_pairs={{0,16},{8,24},{16,0},{24,8},{1,17},{9,25},{17,1},{25,9},{2,18},{10... | collective-permute-start | bytes 786440 | tf_op jit(solution)/shard_map/ppermute | solution.py:726
  83.1 14.1 %collective-permute-start.20 = (bf16[256,512]{1,0:T(8,128)(2,1)S(1)}, bf16[256,512]{1,0:T(8,128)(2,1)S(1)}, u32[]{:S(2)}, u32[]{:S(2)}) collective-permute-start(bf16[256,512]{1,0:T(8,128)(2,1)S(1)} %get-tuple-element.196), channel_id=1, source_target_pairs={{0,24},{8,16},{16,8},{24,0},{1,25},{9,17},{17,9},{25,1},{2,26},{10... | collective-permute-start | bytes 786440 | tf_op jit(solution)/shard_map/ppermute | solution.py:726
  85.0 12.2 %collective-permute-start.17 = (bf16[4,4,2,128,128]{4,3,2,1,0:T(8,128)(2,1)S(1)}, bf16[4,4,2,128,128]{4,3,2,1,0:T(8,128)(2,1)S(1)}, u32[]{:S(2)}, u32[]{:S(2)}) collective-permute-start(bf16[4,4,2,128,128]{4,3,2,1,0:T(8,128)(2,1)S(1)} %get-tuple-element.105), channel_id=1, source_target_pairs={{0,1},{1,0},{2,3},{3,2},{4,5},{5,4},{6,7},{7,6},{8,9},{9,8},{10,11... | collective-permute-start | bytes 3145736 | tf_op jit(solution)/shard_map/ppermute | solution.py:726
  97.6 15.1 %collective-permute-start.22 = (bf16[4,2,128,128]{3,2,1,0:T(8,128)(2,1)S(1)}, bf16[4,2,128,128]{3,2,1,0:T(8,128)(2,1)S(1)}, u32[]{:S(2)}, u32[]{:S(2)}) collective-permute-start(bf16[4,2,128,128]{3,2,1,0:T(8,128)(2,1)S(1)} %get-tuple-element.184), channel_id=1, source_target_pairs={{0,2},{1,3},{2,0},{3,1},{4,6},{5,7},{6,4},{7,5},{8,10},{9,11},{10,... | collective-permute-start | bytes 786440 | tf_op jit(solution)/shard_map/ppermute | solution.py:726
  98.9 13.8 %collective-permute-start.21 = (bf16[4,4,64,640]{3,2,1,0:T(8,128)(2,1)S(1)}, bf16[4,4,64,640]{3,2,1,0:T(8,128)(2,1)S(1)}, u32[]{:S(2)}, u32[]{:S(2)}) collective-permute-start(bf16[4,4,64,640]{3,2,1,0:T(8,128)(2,1)S(1)} %get-tuple-element.122), channel_id=1, source_target_pairs={{0,1},{1,0},{2,3},{3,2},{4,5},{5,4},{6,7},{7,6},{8,9},{9,8},{10,11... | collective-permute-start | bytes 3932168 | tf_op jit(solution)/shard_map/ppermute | solution.py:726
  99.1 32.0 %collective-permute-start.26 = (bf16[4,2,128,128]{3,2,1,0:T(8,128)(2,1)S(1)}, bf16[4,2,128,128]{3,2,1,0:T(8,128)(2,1)S(1)}, u32[]{:S(2)}, u32[]{:S(2)}) collective-permute-start(bf16[4,2,128,128]{3,2,1,0:T(8,128)(2,1)S(1)} %get-tuple-element.182), channel_id=1, source_target_pairs={{0,4},{1,5},{2,6},{3,7},{4,0},{5,1},{6,2},{7,3},{8,12},{9,13},{10,... | collective-permute-start | bytes 786440 | tf_op jit(solution)/shard_map/ppermute | solution.py:726
  101.9 29.2 %collective-permute-start.27 = (bf16[4,2,128,128]{3,2,1,0:T(8,128)(2,1)S(1)}, bf16[4,2,128,128]{3,2,1,0:T(8,128)(2,1)S(1)}, u32[]{:S(2)}, u32[]{:S(2)}) collective-permute-start(bf16[4,2,128,128]{3,2,1,0:T(8,128)(2,1)S(1)} %get-tuple-element.181), channel_id=1, source_target_pairs={{0,6},{1,7},{2,4},{3,5},{4,2},{5,3},{6,0},{7,1},{8,14},{9,15},{10,... | collective-permute-start | bytes 786440 | tf_op jit(solution)/shard_map/ppermute | solution.py:726
  113.1 18.0 %collective-permute-start.23 = (bf16[4,64,640]{2,1,0:T(8,128)(2,1)S(1)}, bf16[4,64,640]{2,1,0:T(8,128)(2,1)S(1)}, u32[]{:S(2)}, u32[]{:S(2)}) collective-permute-start(bf16[4,64,640]{2,1,0:T(8,128)(2,1)S(1)} %get-tuple-element.179), channel_id=1, source_target_pairs={{0,8},{8,0},{16,24},{24,16},{1,9},{9,1},{17,25},{25,17},{2,10},{10... | collective-permute-start | bytes 983048 | tf_op jit(solution)/shard_map/ppermute | solution.py:726
  114.7 16.5 %collective-permute-start.24 = (bf16[4,64,640]{2,1,0:T(8,128)(2,1)S(1)}, bf16[4,64,640]{2,1,0:T(8,128)(2,1)S(1)}, u32[]{:S(2)}, u32[]{:S(2)}) collective-permute-start(bf16[4,64,640]{2,1,0:T(8,128)(2,1)S(1)} %get-tuple-element.178), channel_id=1, source_target_pairs={{0,16},{8,24},{16,0},{24,8},{1,17},{9,25},{17,1},{25,9},{2,18},{10... | collective-permute-start | bytes 983048 | tf_op jit(solution)/shard_map/ppermute | solution.py:726
  114.8 16.4 %collective-permute-start.25 = (bf16[4,64,640]{2,1,0:T(8,128)(2,1)S(1)}, bf16[4,64,640]{2,1,0:T(8,128)(2,1)S(1)}, u32[]{:S(2)}, u32[]{:S(2)}) collective-permute-start(bf16[4,64,640]{2,1,0:T(8,128)(2,1)S(1)} %get-tuple-element.177), channel_id=1, source_target_pairs={{0,24},{8,16},{16,8},{24,0},{1,25},{9,17},{17,9},{25,1},{2,26},{10... | collective-permute-start | bytes 983048 | tf_op jit(solution)/shard_map/ppermute | solution.py:726
  131.5 18.7 %collective-permute-start.32 = (bf16[2,64,640]{2,1,0:T(8,128)(2,1)S(1)}, bf16[2,64,640]{2,1,0:T(8,128)(2,1)S(1)}, u32[]{:S(2)}, u32[]{:S(2)}) collective-permute-start(bf16[2,64,640]{2,1,0:T(8,128)(2,1)S(1)} %slice.357), channel_id=1, source_target_pairs={{0,4},{1,5},{2,6},{3,7},{4,0},{5,1},{6,2},{7,3},{8,12},{9,13},{10,... | collective-permute-start | bytes 491528 | tf_op jit(solution)/shard_map/ppermute | solution.py:726
  133.8 16.3 %collective-permute-start.35 = (bf16[16,64,128]{2,1,0:T(8,128)(2,1)S(1)}, bf16[16,64,128]{2,1,0:T(8,128)(2,1)S(1)}, u32[]{:S(2)}, u32[]{:S(2)}) collective-permute-start(bf16[16,64,128]{2,1,0:T(8,128)(2,1)S(1)} %pad_maximum_fusion.20), channel_id=1, source_target_pairs={{0,24},{8,16},{16,8},{24,0},{1,25},{9,17},{17,9},{25,1},{2,26},{10... | collective-permute-start | bytes 786440 | tf_op jit(solution)/shard_map/ppermute | solution.py:726
  135.0 15.2 %collective-permute-start.34 = (bf16[16,64,128]{2,1,0:T(8,128)(2,1)S(1)}, bf16[16,64,128]{2,1,0:T(8,128)(2,1)S(1)}, u32[]{:S(2)}, u32[]{:S(2)}) collective-permute-start(bf16[16,64,128]{2,1,0:T(8,128)(2,1)S(1)} %pad_maximum_fusion.19), channel_id=1, source_target_pairs={{0,16},{8,24},{16,0},{24,8},{1,17},{9,25},{17,1},{25,9},{2,18},{10... | collective-permute-start | bytes 786440 | tf_op jit(solution)/shard_map/ppermute | solution.py:726
  140.3 9.8 %collective-permute-start.33 = (bf16[16,64,128]{2,1,0:T(8,128)(2,1)S(1)}, bf16[16,64,128]{2,1,0:T(8,128)(2,1)S(1)}, u32[]{:S(2)}, u32[]{:S(2)}) collective-permute-start(bf16[16,64,128]{2,1,0:T(8,128)(2,1)S(1)} %pad_maximum_fusion.18), channel_id=1, source_target_pairs={{0,8},{8,0},{16,24},{24,16},{1,9},{9,1},{17,25},{25,17},{2,10},{10... | collective-permute-start | bytes 786440 | tf_op jit(solution)/shard_map/ppermute | solution.py:726
  152.3 12.5 %collective-permute-start.36 = (bf16[272,512]{1,0:T(8,128)(2,1)S(1)}, bf16[272,512]{1,0:T(8,128)(2,1)S(1)}, u32[]{:S(2)}, u32[]{:S(2)}) collective-permute-start(bf16[272,512]{1,0:T(8,128)(2,1)S(1)} %get-tuple-element.230), channel_id=1, source_target_pairs={{0,24},{8,16},{16,8},{24,0},{1,25},{9,17},{17,9},{25,1},{2,26},{10... | collective-permute-start | bytes 835592 | tf_op jit(solution)/shard_map/ppermute | solution.py:726
  153.9 12.1 %collective-permute-start.37 = (bf16[272,512]{1,0:T(8,128)(2,1)S(1)}, bf16[272,512]{1,0:T(8,128)(2,1)S(1)}, u32[]{:S(2)}, u32[]{:S(2)}) collective-permute-start(bf16[272,512]{1,0:T(8,128)(2,1)S(1)} %get-tuple-element.229), channel_id=1, source_target_pairs={{0,16},{8,24},{16,0},{24,8},{1,17},{9,25},{17,1},{25,9},{2,18},{10... | collective-permute-start | bytes 835592 | tf_op jit(solution)/shard_map/ppermute | solution.py:726
  154.8 11.2 %collective-permute-start.38 = (bf16[272,512]{1,0:T(8,128)(2,1)S(1)}, bf16[272,512]{1,0:T(8,128)(2,1)S(1)}, u32[]{:S(2)}, u32[]{:S(2)}) collective-permute-start(bf16[272,512]{1,0:T(8,128)(2,1)S(1)} %get-tuple-element.228), channel_id=1, source_target_pairs={{0,8},{8,0},{16,24},{24,16},{1,9},{9,1},{17,25},{25,17},{2,10},{10... | collective-permute-start | bytes 835592 | tf_op jit(solution)/shard_map/ppermute | solution.py:726
  (29 other events, 168.4 us)

commit v7 on v6

--- a/solution.py
+++ b/solution.py
@@ -224,23 +224,23 @@
     width = s_ref.shape[1]
     normed_t[...] = normed_ref[...].T
 
-    def weight_part(pair, refs):
-        cols = slice((pair % 2) * 128, (pair % 2) * 128 + 128)
+    def weight_part(pairs, refs):
         for kind, ref in enumerate(refs):
-            joined[:, kind * 128 : (kind + 1) * 128] = ref[:, cols]
+            joined[:, kind * 256 : (kind + 1) * 256] = ref[...]
         result = nn(normed_t[...], joined[...]).astype(BF16)
         rows = result.shape[0] // dp_count
         per = grad_ref.shape[3]
         for kind in range(3):
-            block = pair + 4 * kind
-            col, part = (block // per) ^ own_ref[0], block % per
-            for d in range(dp_count):
-                grad_ref[(d % 2) ^ own_ref[2], col, (d // 2) ^ own_ref[1], part] = result[
-                    d * rows : (d + 1) * rows, kind * 128 : (kind + 1) * 128
-                ]
-
-    for pair in range(2):
-        weight_part(pair, (dq_first, dk_first, dv_first))
+            for i, pair in enumerate(pairs):
+                block = pair + 4 * kind
+                col, part = (block // per) ^ own_ref[0], block % per
+                at = slice(kind * 256 + i * 128, kind * 256 + (i + 1) * 128)
+                for d in range(dp_count):
+                    grad_ref[(d % 2) ^ own_ref[2], col, (d // 2) ^ own_ref[1], part] = result[
+                        d * rows : (d + 1) * rows, at
+                    ]
+
+    weight_part((0, 1), (dq_first, dk_first, dv_first))
     for pair in range(2, 4):
         at = slice((pair - 2) * 128, (pair - 1) * 128)
         dq_ref[:, at] = head_pair_back(
@@ -249,7 +249,7 @@
             dk_ref.at[:, at],
             dv_ref.at[:, at],
         )
-        weight_part(pair, (dq_ref, dk_ref, dv_ref))
+    weight_part((2, 3), (dq_ref, dk_ref, dv_ref))
     hand_out(grad_ref, (mine_out, other_out), sems)
 
 
@@ -262,12 +262,12 @@
         out_specs=[IN_VMEM] * 3 + [pl.BlockSpec(memory_space=pl.ANY)] * 2,
         scratch_shapes=[
             pltpu.VMEM((width, count), BF16),
-            pltpu.VMEM((count, 384), BF16),
+            pltpu.VMEM((count, 768), BF16),
             pltpu.VMEM(pieces, BF16),
             pltpu.SemaphoreType.DMA((2,)),
         ],
         out_shape=[jax.ShapeDtypeStruct((count, width // 2), BF16)] * 3 + outs_of(pieces, True),
-        compiler_params=params(11),
+        compiler_params=params(13),
         cost_estimate=cost(20 * count * count * 1024, 10 * 2**20),
         name="attend_back_sum",
     )(own, projected, scaled, extra, normed, *first_half)

time: 171 us -> 170 us (level)
  transfers between devices with their start and end apart: 42 -> 42, of which waited for: 16 -> 17; matrix products, arithmetic and copies ran while one was open for 10% -> 10% of each run, Pallas kernels for 32% -> 31%
where the time goes in v7:
time: 170 us; the launch traced here: 167 us
  Pallas kernels  67.1 us (39%)
  starting transfers between devices  50.3 us (30%)
  waiting for transfers between devices  24.4 us (14%)
  local copies, waits for them, and re-layouts  13.9 us (8%)
  other arithmetic  9.56 us (6%)
  between operations  1.9 us (1%)
    ppermute x42, starting transfers between devices, swap_along(): return lax.ppermute(value, axis, [(i, i ^ mask) for i in range(count)])  50.3 us
    ppermute x42, waiting for transfers between devices, swap_along(): return lax.ppermute(value, axis, [(i, i ^ mask) for i in range(count)])  24.4 us
    pallas_call x1, Pallas kernels, rise(): pl.pallas_call(functools.partial(rise_kernel, cfg), in_specs=[pl.BlockSpe...  14.7 us
    pallas_call x1, Pallas kernels, attend_back_sum(): pl.pallas_call(functools.partial(attend_back_sum_kernel, min(512, count),...  13.7 us
    pallas_call x1, Pallas kernels, fall(): pl.pallas_call(functools.partial(fall_kernel, cfg), in_specs=[pl.BlockSpe...  12.2 us
    pallas_call x1, Pallas kernels, attend_back_half(): pl.pallas_call(functools.partial(attend_back_half_kernel, min(512, count)...  10.2 us
    pallas_call x1, Pallas kernels, attend_row(): pl.pallas_call(functools.partial(attend_row_kernel, min(256, count)), in_...  9.4 us
    unnamed x38, local copies, waits for them, and re-layouts  3.74 us
  transfers between devices with their start and end apart: 42, of which 17 were waited for; matrix products, arithmetic and copies ran while one was open for 10% of the time, Pallas kernels for 31%

profile of v7, /device:TPU:0, one launch (start us, length us, event | category | flops | bytes accessed | tf_op | source)
XLA Modules:
  0.0 167.2 jit_solution(11467998815276181936)
XLA Ops:
  3.1 3.0 %collective-permute-start.3 = (bf16[64,896]{1,0:T(8,128)(2,1)}, bf16[64,896]{1,0:T(8,128)(2,1)S(1)}, u32[]{:S(2)}, u32[]{:S(2)}) collective-permute-start(bf16[64,896]{1,0:T(8,128)(2,1)} %get-tuple-element.225), channel_id=1, source_target_pairs={{0,2},{1,3},{2,0},{3,1},{4,6},{5,7},{6,4},{7,5},{8,10},{9,11},{10,... | collective-permute-start | bytes 344072 | tf_op jit(solution)/shard_map/ppermute | solution.py:726
  6.1 2.6 %collective-permute-start.4 = (bf16[64,896]{1,0:T(8,128)(2,1)}, bf16[64,896]{1,0:T(8,128)(2,1)S(1)}, u32[]{:S(2)}, u32[]{:S(2)}) collective-permute-start(bf16[64,896]{1,0:T(8,128)(2,1)} %get-tuple-element.225), channel_id=1, source_target_pairs={{0,4},{1,5},{2,6},{3,7},{4,0},{5,1},{6,2},{7,3},{8,12},{9,13},{10,... | collective-permute-start | bytes 344072 | tf_op jit(solution)/shard_map/ppermute | solution.py:726
  9.5 2.1 %fusion.6 = (bf16[1,272,512]{2,1,0:T(8,128)(2,1)S(1)}, bf16[272,512]{1,0:T(8,128)(2,1)}, bf16[272,512]{1,0:T(8,128)(2,1)}, bf16[272,512]{1,0:T(8,128)(2,1)}) fusion(s32[]{:T(128)S(6)} %select_n.54, bf16[4,256,512]{2,1,0:T(8,128)(2,1)} %param.11, bf16[4,16,512]{2,1,0:T(8,128)(2,1)S(1)} %pad_convert_fusion, s32[]{:T(128)S(6)} %select_n.55, s32[]{:T(128)S(6)} %select_n.56, ...), kind=kLoop, calls=%fused_computation.48 | loop fusion | flops 2228224 | bytes 2228240 | tf_op jit(solution)/shard_map/concatenate | solution.py:840
  11.7 2.7 %collective-permute-start.2 = (bf16[272,512]{1,0:T(8,128)(2,1)}, bf16[272,512]{1,0:T(8,128)(2,1)}, u32[]{:S(2)}, u32[]{:S(2)}) collective-permute-start(bf16[272,512]{1,0:T(8,128)(2,1)} %get-tuple-element.192), channel_id=1, source_target_pairs={{0,24},{8,16},{16,8},{24,0},{1,25},{9,17},{17,9},{25,1},{2,26},{10... | collective-permute-start | bytes 835592 | tf_op jit(solution)/shard_map/ppermute | solution.py:726
  16.2 1.8 %collective-permute-done.4 = bf16[64,896]{1,0:T(8,128)(2,1)S(1)} collective-permute-done((bf16[64,896]{1,0:T(8,128)(2,1)}, bf16[64,896]{1,0:T(8,128)(2,1)S(1)}, u32[]{:S(2)}, u32[]{:S(2)}) %collective-permute-start.4) | collective-permute-done | bytes 114720 | tf_op jit(solution)/shard_map/ppermute | solution.py:726
  18.1 1.6 collective-permute-start.8
  22.5 2.6 %collective-permute-start.10 = (bf16[4,64,384]{2,1,0:T(8,128)(2,1)S(1)}, bf16[4,64,384]{2,1,0:T(8,128)(2,1)S(1)}, u32[]{:S(2)}, u32[]{:S(2)}) collective-permute-start(bf16[4,64,384]{2,1,0:T(8,128)(2,1)S(1)} %get-tuple-element.213), channel_id=1, source_target_pairs={{0,24},{8,16},{16,8},{24,0},{1,25},{9,17},{17,9},{25,1},{2,26},{10... | collective-permute-start | bytes 589832 | tf_op jit(solution)/shard_map/ppermute | solution.py:726
  26.8 1.6 collective-permute-start.6
  29.1 3.7 %collective-permute-done.8 = bf16[4,64,384]{2,1,0:T(8,128)(2,1)S(1)} collective-permute-done((bf16[4,64,384]{2,1,0:T(8,128)(2,1)S(1)}, bf16[4,64,384]{2,1,0:T(8,128)(2,1)S(1)}, u32[]{:S(2)}, u32[]{:S(2)}) %collective-permute-start.8) | collective-permute-done | bytes 196640 | tf_op jit(solution)/shard_map/ppermute | solution.py:726
  34.9 2.0 %collective-permute-done.10 = bf16[4,64,384]{2,1,0:T(8,128)(2,1)S(1)} collective-permute-done((bf16[4,64,384]{2,1,0:T(8,128)(2,1)S(1)}, bf16[4,64,384]{2,1,0:T(8,128)(2,1)S(1)}, u32[]{:S(2)}, u32[]{:S(2)}) %collective-permute-start.10) | collective-permute-done | bytes 196640 | tf_op jit(solution)/shard_map/ppermute | solution.py:726
  36.8 2.6 %collective-permute-start.14 = (bf16[512,512]{1,0:T(8,128)(2,1)S(1)}, bf16[512,512]{1,0:T(8,128)(2,1)S(1)}, u32[]{:S(2)}, u32[]{:S(2)}) collective-permute-start(bf16[512,512]{1,0:T(8,128)(2,1)S(1)} %get-tuple-element.218), channel_id=1, source_target_pairs={{0,24},{8,16},{16,8},{24,0},{1,25},{9,17},{17,9},{25,1},{2,26},{10... | collective-permute-start | bytes 1572872 | tf_op jit(solution)/shard_map/ppermute | solution.py:726
  42.0 2.3 %collective-permute-done.6 = bf16[64,2560]{1,0:T(8,128)(2,1)S(1)} collective-permute-done((bf16[64,2560]{1,0:T(8,128)(2,1)S(1)}, bf16[64,2560]{1,0:T(8,128)(2,1)S(1)}, u32[]{:S(2)}, u32[]{:S(2)}) %collective-permute-start.6) | collective-permute-done | bytes 327712 | tf_op jit(solution)/shard_map/ppermute | solution.py:726
  44.4 3.7 %project.1 = (bf16[1024,512]{1,0:T(8,128)(2,1)}, bf16[1024,1536]{1,0:T(8,128)(2,1)S(1)}, bf16[512,1536]{1,0:T(8,128)(2,1)}) custom-call(s32[3]{0:T(128)S(1)} %pad_add_fusion.own_ref, f32[1024,512]{1,0:T(8,128)S(1)} %multiply_add_fusion.hidden_ref, f32[1,512]{1,0:T(1,128)S(1)} %bitcast.117, bf16[4,4,64,384]{3,2,1,0:T(8,128)(2,1)S(1)} %pad_maximum_fusion.3.refs_0_, ...), custom_call_target="tpu_custom_call" | custom-call | flops 6442450944 | bytes 33554432 | tf_op jit(solution)/shard_map/project/pallas_call | solution.py:407
  48.2 9.4 %attend_row.1 = (bf16[1024,512]{1,0:T(8,128)(2,1)S(1)}, f32[1024,128]{1,0:T(8,128)S(1)}) custom-call(bf16[1024,1536]{1,0:T(8,128)(2,1)S(1)} %get-tuple-element.94.own_ref.proj_ref), custom_call_target="tpu_custom_call" | custom-call | flops 17179869184 | bytes 5242880 | tf_op jit(solution)/shard_map/attend_row/pallas_call | solution.py:120
  66.7 14.7 %rise.1 = (bf16[1024,512]{1,0:T(8,128)(2,1)S(1)}, f32[1024,512]{1,0:T(8,128)S(1)}, f32[1024,128]{1,0:T(8,128)S(1)}, bf16[1024,2048]{1,0:T(8,128)(2,1)S(1)}, bf16...) custom-call(s32[3]{0:T(128)S(1)} %pad_add_fusion.own_ref, ...), custom_call_target="tpu_custom_call" | custom-call | flops 7516192768 | bytes 25165824 | tf_op jit(solution)/shard_map/rise/pallas_call | solution.py:515
  81.4 1.6 collective-permute-start.18
  83.1 1.9 %collective-permute-start.20 = (bf16[256,512]{1,0:T(8,128)(2,1)S(1)}, bf16[256,512]{1,0:T(8,128)(2,1)S(1)}, u32[]{:S(2)}, u32[]{:S(2)}) collective-permute-start(bf16[256,512]{1,0:T(8,128)(2,1)S(1)} %get-tuple-element.196), channel_id=1, source_target_pairs={{0,24},{8,16},{16,8},{24,0},{1,25},{9,17},{17,9},{25,1},{2,26},{10... | collective-permute-start | bytes 786440 | tf_op jit(solution)/shard_map/ppermute | solution.py:726
  85.0 12.2 %fall.1 = (f32[1024,512]{1,0:T(8,128)S(1)}, bf16[1024,512]{1,0:T(8,128)(2,1)S(1)}, bf16[1024,512]{1,0:T(8,128)(2,1)S(1)}, f32[1,512]{1,0:T(1,128)S(1)}, bf16[4,4...) custom-call(s32[3]{0:T(128)S(1)} %pad_add_fusion.own_ref, ...), custom_call_target="tpu_custom_call" | custom-call | flops 34359738368 | bytes 100663296 | tf_op jit(solution)/shard_map/fall/pallas_call | solution.py:660
  99.1 2.8 %collective-permute-start.26 = (bf16[4,2,128,128]{3,2,1,0:T(8,128)(2,1)S(1)}, bf16[4,2,128,128]{3,2,1,0:T(8,128)(2,1)S(1)}, u32[]{:S(2)}, u32[]{:S(2)}) collective-permute-start(bf16[4,2,128,128]{3,2,1,0:T(8,128)(2,1)S(1)} %get-tuple-element.182), channel_id=1, source_target_pairs={{0,4},{1,5},{2,6},{3,7},{4,0},{5,1},{6,2},{7,3},{8,12},{9,13},{10,... | collective-permute-start | bytes 786440 | tf_op jit(solution)/shard_map/ppermute | solution.py:726
  102.2 10.2 %attend_back_half.1 = (bf16[1024,256]{1,0:T(8,128)(2,1)S(1)}, bf16[1024,256]{1,0:T(8,128)(2,1)S(1)}, bf16[1024,256]{1,0:T(8,128)(2,1)S(1)}) custom-call(bf16[1024,1536]{1,0:T(8,128)(2,1)S(1)} %copy-done.5, bf16[1024,512]{1,0:T(8,128)(2,1)S(1)} %get-tuple-element.123.s_ref, bf16[1024,512]{1,0:T(8,128)(2,1)S(1)} %get-tuple-element.124.x_ref), custom_call_target="tpu_custom_call" | custom-call | flops 17179869184 | bytes 6291456 | tf_op jit(solution)/shard_map/attend_back_half/pallas_call | solution.py:192
  113.1 1.6 collective-permute-start.23
  114.7 1.9 %collective-permute-start.25 = (bf16[4,64,640]{2,1,0:T(8,128)(2,1)S(1)}, bf16[4,64,640]{2,1,0:T(8,128)(2,1)S(1)}, u32[]{:S(2)}, u32[]{:S(2)}) collective-permute-start(bf16[4,64,640]{2,1,0:T(8,128)(2,1)S(1)} %get-tuple-element.177), channel_id=1, source_target_pairs={{0,24},{8,16},{16,8},{24,0},{1,25},{9,17},{17,9},{25,1},{2,26},{10... | collective-permute-start | bytes 983048 | tf_op jit(solution)/shard_map/ppermute | solution.py:726
  116.6 13.7 %attend_back_sum.1 = (bf16[1024,256]{1,0:T(8,128)(2,1)S(1)}, bf16[1024,256]{1,0:T(8,128)(2,1)S(1)}, bf16[1024,256]{1,0:T(8,128)(2,1)S(1)}, bf16[4,4,3,64,128]{4,...) custom-call(s32[3]{0:T(128)S(1)} %pad_add_fusion.own_ref, bf16[1024,1536]{1,0:T(8,128)(2,1)S(1)} %copy-done.5, ...), custom_call_target="tpu_custom_call" | custom-call | flops 21474836480 | bytes 10485760 | tf_op jit(solution)/shard_map/attend_back_sum/pallas_call | solution.py:259
  133.3 1.6 collective-permute-start.35
  136.1 3.2 %last.1 = (bf16[1024,512]{1,0:T(8,128)(2,1)S(1)}, f32[8,512]{1,0:T(8,128)S(1)}) custom-call(f32[1024,512]{1,0:T(8,128)S(1)} %multiply_add_fusion.hidden_ref, f32[1024,512]{1,0:T(8,128)S(1)} %get-tuple-element.120.first_ref, f32[1,512]{1,0:T(1,128)S(1)} %bitcast.118, bf16[8,1024]{1,0:T(8,128)(2,1)S(1)} %broadcast_in_dim.56.mask_ref, ...), custom_call_target="tpu_custom_call" | custom-call | flops 12884901888 | bytes 100663296 | tf_op jit(solution)/shard_map/last/pallas_call | solution.py:710
  140.7 2.2 %collective-permute-start.30 = (f32[8,512]{1,0:T(8,128)S(1)}, f32[8,512]{1,0:T(8,128)S(1)}, u32[]{:S(2)}, u32[]{:S(2)}) collective-permute-start(f32[8,512]{1,0:T(8,128)S(1)} %fusion.21), channel_id=1, source_target_pairs={{0,2},{1,3},{2,0},{3,1},{4,6},{5,7},{6,4},{7,5},{8,10},{9,11},{10,... | collective-permute-start | bytes 49160 | tf_op jit(solution)/shard_map/ppermute | solution.py:726
  143.0 1.7 %collective-permute-done.30 = f32[8,512]{1,0:T(8,128)S(1)} collective-permute-done((f32[8,512]{1,0:T(8,128)S(1)}, f32[8,512]{1,0:T(8,128)S(1)}, u32[]{:S(2)}, u32[]{:S(2)}) %collective-permute-start.30) | collective-permute-done | bytes 16416 | tf_op jit(solution)/shard_map/ppermute | solution.py:726
  144.7 1.8 %collective-permute-start.31 = (f32[8,512]{1,0:T(8,128)S(1)}, f32[8,512]{1,0:T(8,128)S(1)}, u32[]{:S(2)}, u32[]{:S(2)}) collective-permute-start(f32[8,512]{1,0:T(8,128)S(1)} %add.186), channel_id=1, source_target_pairs={{0,4},{1,5},{2,6},{3,7},{4,0},{5,1},{6,2},{7,3},{8,12},{9,13},{10,... | collective-permute-start | bytes 49160 | tf_op jit(solution)/shard_map/ppermute | solution.py:726
  146.5 2.8 %collective-permute-done.31 = f32[8,512]{1,0:T(8,128)S(1)} collective-permute-done((f32[8,512]{1,0:T(8,128)S(1)}, f32[8,512]{1,0:T(8,128)S(1)}, u32[]{:S(2)}, u32[]{:S(2)}) %collective-permute-start.31) | collective-permute-done | bytes 16416 | tf_op jit(solution)/shard_map/ppermute | solution.py:726
  149.5 1.8 %collective-permute-start.39 = (bf16[2,3,64,128]{3,2,1,0:T(8,128)(2,1)S(1)}, bf16[2,3,64,128]{3,2,1,0:T(8,128)(2,1)S(1)}, u32[]{:S(2)}, u32[]{:S(2)}) collective-permute-start(bf16[2,3,64,128]{3,2,1,0:T(8,128)(2,1)S(1)} %bitcast.146), channel_id=1, source_target_pairs={{0,4},{1,5},{2,6},{3,7},{4,0},{5,1},{6,2},{7,3},{8,12},{9,13},{10,... | collective-permute-start | bytes 294920 | tf_op jit(solution)/shard_map/ppermute | solution.py:726
  155.2 1.7 %collective-permute-done.39 = bf16[2,3,64,128]{3,2,1,0:T(8,128)(2,1)S(1)} collective-permute-done((bf16[2,3,64,128]{3,2,1,0:T(8,128)(2,1)S(1)}, bf16[2,3,64,128]{3,2,1,0:T(8,128)(2,1)S(1)}, u32[]{:S(2)}, u32[]{:S(2)}) %collective-permute-start.39) | collective-permute-done | bytes 98336 | tf_op jit(solution)/shard_map/ppermute | solution.py:726
  158.2 1.8 %collective-permute-start.41 = (bf16[1,64,640]{2,1,0:T(8,128)(2,1)S(1)}, bf16[1,64,640]{2,1,0:T(8,128)(2,1)S(1)}, u32[]{:S(2)}, u32[]{:S(2)}) collective-permute-start(bf16[1,64,640]{2,1,0:T(8,128)(2,1)S(1)} %slice.341), channel_id=1, source_target_pairs={{0,2},{1,3},{2,0},{3,1},{4,6},{5,7},{6,4},{7,5},{8,10},{9,11},{10,... | collective-permute-start | bytes 245768 | tf_op jit(solution)/shard_map/ppermute | solution.py:726
  (178 shorter events, 44.4 us)
Async XLA Ops:
  3.1 12.8 %collective-permute-start.3 = (bf16[64,896]{1,0:T(8,128)(2,1)}, bf16[64,896]{1,0:T(8,128)(2,1)S(1)}, u32[]{:S(2)}, u32[]{:S(2)}) collective-permute-start(bf16[64,896]{1,0:T(8,128)(2,1)} %get-tuple-element.225), channel_id=1, source_target_pairs={{0,2},{1,3},{2,0},{3,1},{4,6},{5,7},{6,4},{7,5},{8,10},{9,11},{10,... | collective-permute-start | bytes 344072 | tf_op jit(solution)/shard_map/ppermute | solution.py:726
  6.1 11.9 %collective-permute-start.4 = (bf16[64,896]{1,0:T(8,128)(2,1)}, bf16[64,896]{1,0:T(8,128)(2,1)S(1)}, u32[]{:S(2)}, u32[]{:S(2)}) collective-permute-start(bf16[64,896]{1,0:T(8,128)(2,1)} %get-tuple-element.225), channel_id=1, source_target_pairs={{0,4},{1,5},{2,6},{3,7},{4,0},{5,1},{6,2},{7,3},{8,12},{9,13},{10,... | collective-permute-start | bytes 344072 | tf_op jit(solution)/shard_map/ppermute | solution.py:726
  8.7 9.3 %collective-permute-start.5 = (bf16[64,896]{1,0:T(8,128)(2,1)}, bf16[64,896]{1,0:T(8,128)(2,1)S(1)}, u32[]{:S(2)}, u32[]{:S(2)}) collective-permute-start(bf16[64,896]{1,0:T(8,128)(2,1)} %get-tuple-element.225), channel_id=1, source_target_pairs={{0,6},{1,7},{2,4},{3,5},{4,2},{5,3},{6,0},{7,1},{8,14},{9,15},{10,... | collective-permute-start | bytes 344072 | tf_op jit(solution)/shard_map/ppermute | solution.py:726
  11.7 10.9 %collective-permute-start.2 = (bf16[272,512]{1,0:T(8,128)(2,1)}, bf16[272,512]{1,0:T(8,128)(2,1)}, u32[]{:S(2)}, u32[]{:S(2)}) collective-permute-start(bf16[272,512]{1,0:T(8,128)(2,1)} %get-tuple-element.192), channel_id=1, source_target_pairs={{0,24},{8,16},{16,8},{24,0},{1,25},{9,17},{17,9},{25,1},{2,26},{10... | collective-permute-start | bytes 835592 | tf_op jit(solution)/shard_map/ppermute | solution.py:726
  14.3 12.4 %collective-permute-start.1 = (bf16[272,512]{1,0:T(8,128)(2,1)}, bf16[272,512]{1,0:T(8,128)(2,1)}, u32[]{:S(2)}, u32[]{:S(2)}) collective-permute-start(bf16[272,512]{1,0:T(8,128)(2,1)} %get-tuple-element.191), channel_id=1, source_target_pairs={{0,16},{8,24},{16,0},{24,8},{1,17},{9,25},{17,1},{25,9},{2,18},{10... | collective-permute-start | bytes 835592 | tf_op jit(solution)/shard_map/ppermute | solution.py:726
  15.8 23.7 %collective-permute-start = (bf16[272,512]{1,0:T(8,128)(2,1)}, bf16[272,512]{1,0:T(8,128)(2,1)S(1)}, u32[]{:S(2)}, u32[]{:S(2)}) collective-permute-start(bf16[272,512]{1,0:T(8,128)(2,1)} %get-tuple-element.190), channel_id=1, source_target_pairs={{0,8},{8,0},{16,24},{24,16},{1,9},{9,1},{17,25},{25,17},{2,10},{10... | collective-permute-start | bytes 835592 | tf_op jit(solution)/shard_map/ppermute | solution.py:726
  18.1 14.7 %collective-permute-start.8 = (bf16[4,64,384]{2,1,0:T(8,128)(2,1)S(1)}, bf16[4,64,384]{2,1,0:T(8,128)(2,1)S(1)}, u32[]{:S(2)}, u32[]{:S(2)}) collective-permute-start(bf16[4,64,384]{2,1,0:T(8,128)(2,1)S(1)} %get-tuple-element.213), channel_id=1, source_target_pairs={{0,8},{8,0},{16,24},{24,16},{1,9},{9,1},{17,25},{25,17},{2,10},{10... | collective-permute-start | bytes 589832 | tf_op jit(solution)/shard_map/ppermute | solution.py:726
  19.7 14.6 %collective-permute-start.9 = (bf16[4,64,384]{2,1,0:T(8,128)(2,1)S(1)}, bf16[4,64,384]{2,1,0:T(8,128)(2,1)S(1)}, u32[]{:S(2)}, u32[]{:S(2)}) collective-permute-start(bf16[4,64,384]{2,1,0:T(8,128)(2,1)S(1)} %get-tuple-element.213), channel_id=1, source_target_pairs={{0,16},{8,24},{16,0},{24,8},{1,17},{9,25},{17,1},{25,9},{2,18},{10... | collective-permute-start | bytes 589832 | tf_op jit(solution)/shard_map/ppermute | solution.py:726
  22.5 14.3 %collective-permute-start.10 = (bf16[4,64,384]{2,1,0:T(8,128)(2,1)S(1)}, bf16[4,64,384]{2,1,0:T(8,128)(2,1)S(1)}, u32[]{:S(2)}, u32[]{:S(2)}) collective-permute-start(bf16[4,64,384]{2,1,0:T(8,128)(2,1)S(1)} %get-tuple-element.213), channel_id=1, source_target_pairs={{0,24},{8,16},{16,8},{24,0},{1,25},{9,17},{17,9},{25,1},{2,26},{10... | collective-permute-start | bytes 589832 | tf_op jit(solution)/shard_map/ppermute | solution.py:726
  26.8 17.5 %collective-permute-start.6 = (bf16[64,2560]{1,0:T(8,128)(2,1)S(1)}, bf16[64,2560]{1,0:T(8,128)(2,1)S(1)}, u32[]{:S(2)}, u32[]{:S(2)}) collective-permute-start(bf16[64,2560]{1,0:T(8,128)(2,1)S(1)} %pad_maximum_fusion.16), channel_id=1, source_target_pairs={{0,4},{1,5},{2,6},{3,7},{4,0},{5,1},{6,2},{7,3},{8,12},{9,13},{10,... | collective-permute-start | bytes 983048 | tf_op jit(solution)/shard_map/ppermute | solution.py:726
  32.9 27.6 %collective-permute-start.12 = (bf16[512,512]{1,0:T(8,128)(2,1)S(1)}, bf16[512,512]{1,0:T(8,128)(2,1)S(1)}, u32[]{:S(2)}, u32[]{:S(2)}) collective-permute-start(bf16[512,512]{1,0:T(8,128)(2,1)S(1)} %get-tuple-element.219), channel_id=1, source_target_pairs={{0,8},{8,0},{16,24},{24,16},{1,9},{9,1},{17,25},{25,17},{2,10},{10... | collective-permute-start | bytes 1572872 | tf_op jit(solution)/shard_map/ppermute | solution.py:726
  34.3 26.1 %collective-permute-start.13 = (bf16[512,512]{1,0:T(8,128)(2,1)S(1)}, bf16[512,512]{1,0:T(8,128)(2,1)S(1)}, u32[]{:S(2)}, u32[]{:S(2)}) collective-permute-start(bf16[512,512]{1,0:T(8,128)(2,1)S(1)} %get-tuple-element.220), channel_id=1, source_target_pairs={{0,16},{8,24},{16,0},{24,8},{1,17},{9,25},{17,1},{25,9},{2,18},{10... | collective-permute-start | bytes 1572872 | tf_op jit(solution)/shard_map/ppermute | solution.py:726
  36.8 23.6 %collective-permute-start.14 = (bf16[512,512]{1,0:T(8,128)(2,1)S(1)}, bf16[512,512]{1,0:T(8,128)(2,1)S(1)}, u32[]{:S(2)}, u32[]{:S(2)}) collective-permute-start(bf16[512,512]{1,0:T(8,128)(2,1)S(1)} %get-tuple-element.218), channel_id=1, source_target_pairs={{0,24},{8,16},{16,8},{24,0},{1,25},{9,17},{17,9},{25,1},{2,26},{10... | collective-permute-start | bytes 1572872 | tf_op jit(solution)/shard_map/ppermute | solution.py:726
  44.3 15.8 %collective-permute-start.7 = (bf16[2,64,2560]{2,1,0:T(8,128)(2,1)S(1)}, bf16[2,64,2560]{2,1,0:T(8,128)(2,1)S(1)}, u32[]{:S(2)}, u32[]{:S(2)}) collective-permute-start(bf16[2,64,2560]{2,1,0:T(8,128)(2,1)S(1)} %pad_maximum_fusion.8), channel_id=1, source_target_pairs={{0,2},{1,3},{2,0},{3,1},{4,6},{5,7},{6,4},{7,5},{8,10},{9,11},{10,... | collective-permute-start | bytes 1966088 | tf_op jit(solution)/shard_map/ppermute | solution.py:726
  81.4 15.8 %collective-permute-start.18 = (bf16[256,512]{1,0:T(8,128)(2,1)S(1)}, bf16[256,512]{1,0:T(8,128)(2,1)S(1)}, u32[]{:S(2)}, u32[]{:S(2)}) collective-permute-start(bf16[256,512]{1,0:T(8,128)(2,1)S(1)} %get-tuple-element.198), channel_id=1, source_target_pairs={{0,8},{8,0},{16,24},{24,16},{1,9},{9,1},{17,25},{25,17},{2,10},{10... | collective-permute-start | bytes 786440 | tf_op jit(solution)/shard_map/ppermute | solution.py:726
  83.0 14.2 %collective-permute-start.19 = (bf16[256,512]{1,0:T(8,128)(2,1)S(1)}, bf16[256,512]{1,0:T(8,128)(2,1)S(1)}, u32[]{:S(2)}, u32[]{:S(2)}) collective-permute-start(bf16[256,512]{1,0:T(8,128)(2,1)S(1)} %get-tuple-element.197), channel_id=1, source_target_pairs={{0,16},{8,24},{16,0},{24,8},{1,17},{9,25},{17,1},{25,9},{2,18},{10... | collective-permute-start | bytes 786440 | tf_op jit(solution)/shard_map/ppermute | solution.py:726
  83.1 14.1 %collective-permute-start.20 = (bf16[256,512]{1,0:T(8,128)(2,1)S(1)}, bf16[256,512]{1,0:T(8,128)(2,1)S(1)}, u32[]{:S(2)}, u32[]{:S(2)}) collective-permute-start(bf16[256,512]{1,0:T(8,128)(2,1)S(1)} %get-tuple-element.196), channel_id=1, source_target_pairs={{0,24},{8,16},{16,8},{24,0},{1,25},{9,17},{17,9},{25,1},{2,26},{10... | collective-permute-start | bytes 786440 | tf_op jit(solution)/shard_map/ppermute | solution.py:726
  85.0 12.2 %collective-permute-start.17 = (bf16[4,4,2,128,128]{4,3,2,1,0:T(8,128)(2,1)S(1)}, bf16[4,4,2,128,128]{4,3,2,1,0:T(8,128)(2,1)S(1)}, u32[]{:S(2)}, u32[]{:S(2)}) collective-permute-start(bf16[4,4,2,128,128]{4,3,2,1,0:T(8,128)(2,1)S(1)} %get-tuple-element.105), channel_id=1, source_target_pairs={{0,1},{1,0},{2,3},{3,2},{4,5},{5,4},{6,7},{7,6},{8,9},{9,8},{10,11... | collective-permute-start | bytes 3145736 | tf_op jit(solution)/shard_map/ppermute | solution.py:726
  97.6 15.1 %collective-permute-start.22 = (bf16[4,2,128,128]{3,2,1,0:T(8,128)(2,1)S(1)}, bf16[4,2,128,128]{3,2,1,0:T(8,128)(2,1)S(1)}, u32[]{:S(2)}, u32[]{:S(2)}) collective-permute-start(bf16[4,2,128,128]{3,2,1,0:T(8,128)(2,1)S(1)} %get-tuple-element.184), channel_id=1, source_target_pairs={{0,2},{1,3},{2,0},{3,1},{4,6},{5,7},{6,4},{7,5},{8,10},{9,11},{10,... | collective-permute-start | bytes 786440 | tf_op jit(solution)/shard_map/ppermute | solution.py:726
  98.8 13.8 %collective-permute-start.21 = (bf16[4,4,64,640]{3,2,1,0:T(8,128)(2,1)S(1)}, bf16[4,4,64,640]{3,2,1,0:T(8,128)(2,1)S(1)}, u32[]{:S(2)}, u32[]{:S(2)}) collective-permute-start(bf16[4,4,64,640]{3,2,1,0:T(8,128)(2,1)S(1)} %get-tuple-element.122), channel_id=1, source_target_pairs={{0,1},{1,0},{2,3},{3,2},{4,5},{5,4},{6,7},{7,6},{8,9},{9,8},{10,11... | collective-permute-start | bytes 3932168 | tf_op jit(solution)/shard_map/ppermute | solution.py:726
  99.1 31.2 %collective-permute-start.26 = (bf16[4,2,128,128]{3,2,1,0:T(8,128)(2,1)S(1)}, bf16[4,2,128,128]{3,2,1,0:T(8,128)(2,1)S(1)}, u32[]{:S(2)}, u32[]{:S(2)}) collective-permute-start(bf16[4,2,128,128]{3,2,1,0:T(8,128)(2,1)S(1)} %get-tuple-element.182), channel_id=1, source_target_pairs={{0,4},{1,5},{2,6},{3,7},{4,0},{5,1},{6,2},{7,3},{8,12},{9,13},{10,... | collective-permute-start | bytes 786440 | tf_op jit(solution)/shard_map/ppermute | solution.py:726
  101.9 28.4 %collective-permute-start.27 = (bf16[4,2,128,128]{3,2,1,0:T(8,128)(2,1)S(1)}, bf16[4,2,128,128]{3,2,1,0:T(8,128)(2,1)S(1)}, u32[]{:S(2)}, u32[]{:S(2)}) collective-permute-start(bf16[4,2,128,128]{3,2,1,0:T(8,128)(2,1)S(1)} %get-tuple-element.181), channel_id=1, source_target_pairs={{0,6},{1,7},{2,4},{3,5},{4,2},{5,3},{6,0},{7,1},{8,14},{9,15},{10,... | collective-permute-start | bytes 786440 | tf_op jit(solution)/shard_map/ppermute | solution.py:726
  113.1 17.2 %collective-permute-start.23 = (bf16[4,64,640]{2,1,0:T(8,128)(2,1)S(1)}, bf16[4,64,640]{2,1,0:T(8,128)(2,1)S(1)}, u32[]{:S(2)}, u32[]{:S(2)}) collective-permute-start(bf16[4,64,640]{2,1,0:T(8,128)(2,1)S(1)} %get-tuple-element.179), channel_id=1, source_target_pairs={{0,8},{8,0},{16,24},{24,16},{1,9},{9,1},{17,25},{25,17},{2,10},{10... | collective-permute-start | bytes 983048 | tf_op jit(solution)/shard_map/ppermute | solution.py:726
  114.6 16.1 %collective-permute-start.24 = (bf16[4,64,640]{2,1,0:T(8,128)(2,1)S(1)}, bf16[4,64,640]{2,1,0:T(8,128)(2,1)S(1)}, u32[]{:S(2)}, u32[]{:S(2)}) collective-permute-start(bf16[4,64,640]{2,1,0:T(8,128)(2,1)S(1)} %get-tuple-element.178), channel_id=1, source_target_pairs={{0,16},{8,24},{16,0},{24,8},{1,17},{9,25},{17,1},{25,9},{2,18},{10... | collective-permute-start | bytes 983048 | tf_op jit(solution)/shard_map/ppermute | solution.py:726
  114.7 16.0 %collective-permute-start.25 = (bf16[4,64,640]{2,1,0:T(8,128)(2,1)S(1)}, bf16[4,64,640]{2,1,0:T(8,128)(2,1)S(1)}, u32[]{:S(2)}, u32[]{:S(2)}) collective-permute-start(bf16[4,64,640]{2,1,0:T(8,128)(2,1)S(1)} %get-tuple-element.177), channel_id=1, source_target_pairs={{0,24},{8,16},{16,8},{24,0},{1,25},{9,17},{17,9},{25,1},{2,26},{10... | collective-permute-start | bytes 983048 | tf_op jit(solution)/shard_map/ppermute | solution.py:726
  130.9 18.4 %collective-permute-start.32 = (bf16[2,64,640]{2,1,0:T(8,128)(2,1)S(1)}, bf16[2,64,640]{2,1,0:T(8,128)(2,1)S(1)}, u32[]{:S(2)}, u32[]{:S(2)}) collective-permute-start(bf16[2,64,640]{2,1,0:T(8,128)(2,1)S(1)} %slice.357), channel_id=1, source_target_pairs={{0,4},{1,5},{2,6},{3,7},{4,0},{5,1},{6,2},{7,3},{8,12},{9,13},{10,... | collective-permute-start | bytes 491528 | tf_op jit(solution)/shard_map/ppermute | solution.py:726
  133.3 16.0 %collective-permute-start.35 = (bf16[16,64,128]{2,1,0:T(8,128)(2,1)S(1)}, bf16[16,64,128]{2,1,0:T(8,128)(2,1)S(1)}, u32[]{:S(2)}, u32[]{:S(2)}) collective-permute-start(bf16[16,64,128]{2,1,0:T(8,128)(2,1)S(1)} %pad_maximum_fusion.20), channel_id=1, source_target_pairs={{0,24},{8,16},{16,8},{24,0},{1,25},{9,17},{17,9},{25,1},{2,26},{10... | collective-permute-start | bytes 786440 | tf_op jit(solution)/shard_map/ppermute | solution.py:726
  134.9 14.4 %collective-permute-start.34 = (bf16[16,64,128]{2,1,0:T(8,128)(2,1)S(1)}, bf16[16,64,128]{2,1,0:T(8,128)(2,1)S(1)}, u32[]{:S(2)}, u32[]{:S(2)}) collective-permute-start(bf16[16,64,128]{2,1,0:T(8,128)(2,1)S(1)} %pad_maximum_fusion.19), channel_id=1, source_target_pairs={{0,16},{8,24},{16,0},{24,8},{1,17},{9,25},{17,1},{25,9},{2,18},{10... | collective-permute-start | bytes 786440 | tf_op jit(solution)/shard_map/ppermute | solution.py:726
  139.5 9.8 %collective-permute-start.33 = (bf16[16,64,128]{2,1,0:T(8,128)(2,1)S(1)}, bf16[16,64,128]{2,1,0:T(8,128)(2,1)S(1)}, u32[]{:S(2)}, u32[]{:S(2)}) collective-permute-start(bf16[16,64,128]{2,1,0:T(8,128)(2,1)S(1)} %pad_maximum_fusion.18), channel_id=1, source_target_pairs={{0,8},{8,0},{16,24},{24,16},{1,9},{9,1},{17,25},{25,17},{2,10},{10... | collective-permute-start | bytes 786440 | tf_op jit(solution)/shard_map/ppermute | solution.py:726
  151.5 12.5 %collective-permute-start.36 = (bf16[272,512]{1,0:T(8,128)(2,1)S(1)}, bf16[272,512]{1,0:T(8,128)(2,1)S(1)}, u32[]{:S(2)}, u32[]{:S(2)}) collective-permute-start(bf16[272,512]{1,0:T(8,128)(2,1)S(1)} %get-tuple-element.230), channel_id=1, source_target_pairs={{0,24},{8,16},{16,8},{24,0},{1,25},{9,17},{17,9},{25,1},{2,26},{10... | collective-permute-start | bytes 835592 | tf_op jit(solution)/shard_map/ppermute | solution.py:726
  153.0 12.2 %collective-permute-start.37 = (bf16[272,512]{1,0:T(8,128)(2,1)S(1)}, bf16[272,512]{1,0:T(8,128)(2,1)S(1)}, u32[]{:S(2)}, u32[]{:S(2)}) collective-permute-start(bf16[272,512]{1,0:T(8,128)(2,1)S(1)} %get-tuple-element.229), channel_id=1, source_target_pairs={{0,16},{8,24},{16,0},{24,8},{1,17},{9,25},{17,1},{25,9},{2,18},{10... | collective-permute-start | bytes 835592 | tf_op jit(solution)/shard_map/ppermute | solution.py:726
  154.0 11.3 %collective-permute-start.38 = (bf16[272,512]{1,0:T(8,128)(2,1)S(1)}, bf16[272,512]{1,0:T(8,128)(2,1)S(1)}, u32[]{:S(2)}, u32[]{:S(2)}) collective-permute-start(bf16[272,512]{1,0:T(8,128)(2,1)S(1)} %get-tuple-element.228), channel_id=1, source_target_pairs={{0,8},{8,0},{16,24},{24,16},{1,9},{9,1},{17,25},{25,17},{2,10},{10... | collective-permute-start | bytes 835592 | tf_op jit(solution)/shard_map/ppermute | solution.py:726
  (29 other events, 169.6 us)

commit v8 on v7

--- a/solution.py
+++ b/solution.py
@@ -593,10 +593,10 @@
         first_ref[at, :] = grad_first
         branch = grad_first.astype(BF16)
         branch_ref[at, :] = branch
-        inverse = 1.0 / den_ref[at, :]
-        coarse = inverse.astype(BF16)
-        fine = (inverse - coarse.astype(F32)).astype(BF16)
-        ratio = nt(branch, w_up[:, :width]) * (nn(coarse, spread) + nn(fine, spread))
+        den = den_ref[at, :]
+        coarse = den.astype(BF16)
+        fine = (den - coarse.astype(F32)).astype(BF16)
+        ratio = nt(branch, w_up[:, :width]) / (nn(coarse, spread) + nn(fine, spread))
         scaled_ref[at, :] = ratio.astype(BF16)
         product = ratio * att_ref[at, :]
         coarse = product.astype(BF16)

time: 170 us -> 170 us (level)
  no operation moved by 1% of the time
where the time goes in v8:
time: 170 us; the launch traced here: 167 us
  Pallas kernels  67.1 us (39%)
  starting transfers between devices  50.3 us (30%)
  waiting for transfers between devices  24.4 us (14%)
  local copies, waits for them, and re-layouts  13.9 us (8%)
  other arithmetic  9.56 us (6%)
  between operations  1.9 us (1%)
    ppermute x42, starting transfers between devices, swap_along(): return lax.ppermute(value, axis, [(i, i ^ mask) for i in range(count)])  50.3 us
    ppermute x42, waiting for transfers between devices, swap_along(): return lax.ppermute(value, axis, [(i, i ^ mask) for i in range(count)])  24.4 us
    pallas_call x1, Pallas kernels, rise(): pl.pallas_call(functools.partial(rise_kernel, cfg), in_specs=[pl.BlockSpe...  14.7 us
    pallas_call x1, Pallas kernels, attend_back_sum(): pl.pallas_call(functools.partial(attend_back_sum_kernel, min(512, count),...  13.7 us
    pallas_call x1, Pallas kernels, fall(): pl.pallas_call(functools.partial(fall_kernel, cfg), in_specs=[pl.BlockSpe...  12.2 us
    pallas_call x1, Pallas kernels, attend_back_half(): pl.pallas_call(functools.partial(attend_back_half_kernel, min(512, count)...  10.2 us
    pallas_call x1, Pallas kernels, attend_row(): pl.pallas_call(functools.partial(attend_row_kernel, min(256, count)), in_...  9.4 us
    unnamed x38, local copies, waits for them, and re-layouts  3.74 us
  transfers between devices with their start and end apart: 42, of which 17 were waited for; matrix products, arithmetic and copies ran while one was open for 10% of the time, Pallas kernels for 31%

profile of v8, /device:TPU:0, one launch (start us, length us, event | category | flops | bytes accessed | tf_op | source)
XLA Modules:
  0.0 167.3 jit_solution(15979496804237300354)
XLA Ops:
  3.1 3.0 %collective-permute-start.3 = (bf16[64,896]{1,0:T(8,128)(2,1)}, bf16[64,896]{1,0:T(8,128)(2,1)S(1)}, u32[]{:S(2)}, u32[]{:S(2)}) collective-permute-start(bf16[64,896]{1,0:T(8,128)(2,1)} %get-tuple-element.225), channel_id=1, source_target_pairs={{0,2},{1,3},{2,0},{3,1},{4,6},{5,7},{6,4},{7,5},{8,10},{9,11},{10,... | collective-permute-start | bytes 344072 | tf_op jit(solution)/shard_map/ppermute | solution.py:726
  6.1 2.6 %collective-permute-start.4 = (bf16[64,896]{1,0:T(8,128)(2,1)}, bf16[64,896]{1,0:T(8,128)(2,1)S(1)}, u32[]{:S(2)}, u32[]{:S(2)}) collective-permute-start(bf16[64,896]{1,0:T(8,128)(2,1)} %get-tuple-element.225), channel_id=1, source_target_pairs={{0,4},{1,5},{2,6},{3,7},{4,0},{5,1},{6,2},{7,3},{8,12},{9,13},{10,... | collective-permute-start | bytes 344072 | tf_op jit(solution)/shard_map/ppermute | solution.py:726
  9.5 2.1 %fusion.6 = (bf16[1,272,512]{2,1,0:T(8,128)(2,1)S(1)}, bf16[272,512]{1,0:T(8,128)(2,1)}, bf16[272,512]{1,0:T(8,128)(2,1)}, bf16[272,512]{1,0:T(8,128)(2,1)}) fusion(s32[]{:T(128)S(6)} %select_n.54, bf16[4,256,512]{2,1,0:T(8,128)(2,1)} %param.11, bf16[4,16,512]{2,1,0:T(8,128)(2,1)S(1)} %pad_convert_fusion, s32[]{:T(128)S(6)} %select_n.55, s32[]{:T(128)S(6)} %select_n.56, ...), kind=kLoop, calls=%fused_computation.48 | loop fusion | flops 2228224 | bytes 2228240 | tf_op jit(solution)/shard_map/concatenate | solution.py:840
  11.7 2.7 %collective-permute-start.2 = (bf16[272,512]{1,0:T(8,128)(2,1)}, bf16[272,512]{1,0:T(8,128)(2,1)}, u32[]{:S(2)}, u32[]{:S(2)}) collective-permute-start(bf16[272,512]{1,0:T(8,128)(2,1)} %get-tuple-element.192), channel_id=1, source_target_pairs={{0,24},{8,16},{16,8},{24,0},{1,25},{9,17},{17,9},{25,1},{2,26},{10... | collective-permute-start | bytes 835592 | tf_op jit(solution)/shard_map/ppermute | solution.py:726
  16.2 1.8 %collective-permute-done.4 = bf16[64,896]{1,0:T(8,128)(2,1)S(1)} collective-permute-done((bf16[64,896]{1,0:T(8,128)(2,1)}, bf16[64,896]{1,0:T(8,128)(2,1)S(1)}, u32[]{:S(2)}, u32[]{:S(2)}) %collective-permute-start.4) | collective-permute-done | bytes 114720 | tf_op jit(solution)/shard_map/ppermute | solution.py:726
  18.1 1.6 collective-permute-start.8
  22.5 2.6 %collective-permute-start.10 = (bf16[4,64,384]{2,1,0:T(8,128)(2,1)S(1)}, bf16[4,64,384]{2,1,0:T(8,128)(2,1)S(1)}, u32[]{:S(2)}, u32[]{:S(2)}) collective-permute-start(bf16[4,64,384]{2,1,0:T(8,128)(2,1)S(1)} %get-tuple-element.213), channel_id=1, source_target_pairs={{0,24},{8,16},{16,8},{24,0},{1,25},{9,17},{17,9},{25,1},{2,26},{10... | collective-permute-start | bytes 589832 | tf_op jit(solution)/shard_map/ppermute | solution.py:726
  26.8 1.6 collective-permute-start.6
  29.1 3.7 %collective-permute-done.8 = bf16[4,64,384]{2,1,0:T(8,128)(2,1)S(1)} collective-permute-done((bf16[4,64,384]{2,1,0:T(8,128)(2,1)S(1)}, bf16[4,64,384]{2,1,0:T(8,128)(2,1)S(1)}, u32[]{:S(2)}, u32[]{:S(2)}) %collective-permute-start.8) | collective-permute-done | bytes 196640 | tf_op jit(solution)/shard_map/ppermute | solution.py:726
  34.9 2.0 %collective-permute-done.10 = bf16[4,64,384]{2,1,0:T(8,128)(2,1)S(1)} collective-permute-done((bf16[4,64,384]{2,1,0:T(8,128)(2,1)S(1)}, bf16[4,64,384]{2,1,0:T(8,128)(2,1)S(1)}, u32[]{:S(2)}, u32[]{:S(2)}) %collective-permute-start.10) | collective-permute-done | bytes 196640 | tf_op jit(solution)/shard_map/ppermute | solution.py:726
  36.8 2.6 %collective-permute-start.14 = (bf16[512,512]{1,0:T(8,128)(2,1)S(1)}, bf16[512,512]{1,0:T(8,128)(2,1)S(1)}, u32[]{:S(2)}, u32[]{:S(2)}) collective-permute-start(bf16[512,512]{1,0:T(8,128)(2,1)S(1)} %get-tuple-element.218), channel_id=1, source_target_pairs={{0,24},{8,16},{16,8},{24,0},{1,25},{9,17},{17,9},{25,1},{2,26},{10... | collective-permute-start | bytes 1572872 | tf_op jit(solution)/shard_map/ppermute | solution.py:726
  42.0 2.3 %collective-permute-done.6 = bf16[64,2560]{1,0:T(8,128)(2,1)S(1)} collective-permute-done((bf16[64,2560]{1,0:T(8,128)(2,1)S(1)}, bf16[64,2560]{1,0:T(8,128)(2,1)S(1)}, u32[]{:S(2)}, u32[]{:S(2)}) %collective-permute-start.6) | collective-permute-done | bytes 327712 | tf_op jit(solution)/shard_map/ppermute | solution.py:726
  44.4 3.7 %project.1 = (bf16[1024,512]{1,0:T(8,128)(2,1)}, bf16[1024,1536]{1,0:T(8,128)(2,1)S(1)}, bf16[512,1536]{1,0:T(8,128)(2,1)}) custom-call(s32[3]{0:T(128)S(1)} %pad_add_fusion.own_ref, f32[1024,512]{1,0:T(8,128)S(1)} %multiply_add_fusion.hidden_ref, f32[1,512]{1,0:T(1,128)S(1)} %bitcast.117, bf16[4,4,64,384]{3,2,1,0:T(8,128)(2,1)S(1)} %pad_maximum_fusion.3.refs_0_, ...), custom_call_target="tpu_custom_call" | custom-call | flops 6442450944 | bytes 33554432 | tf_op jit(solution)/shard_map/project/pallas_call | solution.py:407
  48.2 9.4 %attend_row.1 = (bf16[1024,512]{1,0:T(8,128)(2,1)S(1)}, f32[1024,128]{1,0:T(8,128)S(1)}) custom-call(bf16[1024,1536]{1,0:T(8,128)(2,1)S(1)} %get-tuple-element.94.own_ref.proj_ref), custom_call_target="tpu_custom_call" | custom-call | flops 17179869184 | bytes 5242880 | tf_op jit(solution)/shard_map/attend_row/pallas_call | solution.py:120
  66.7 14.7 %rise.1 = (bf16[1024,512]{1,0:T(8,128)(2,1)S(1)}, f32[1024,512]{1,0:T(8,128)S(1)}, f32[1024,128]{1,0:T(8,128)S(1)}, bf16[1024,2048]{1,0:T(8,128)(2,1)S(1)}, bf16...) custom-call(s32[3]{0:T(128)S(1)} %pad_add_fusion.own_ref, ...), custom_call_target="tpu_custom_call" | custom-call | flops 7516192768 | bytes 25165824 | tf_op jit(solution)/shard_map/rise/pallas_call | solution.py:515
  81.4 1.6 collective-permute-start.18
  83.1 1.9 %collective-permute-start.20 = (bf16[256,512]{1,0:T(8,128)(2,1)S(1)}, bf16[256,512]{1,0:T(8,128)(2,1)S(1)}, u32[]{:S(2)}, u32[]{:S(2)}) collective-permute-start(bf16[256,512]{1,0:T(8,128)(2,1)S(1)} %get-tuple-element.196), channel_id=1, source_target_pairs={{0,24},{8,16},{16,8},{24,0},{1,25},{9,17},{17,9},{25,1},{2,26},{10... | collective-permute-start | bytes 786440 | tf_op jit(solution)/shard_map/ppermute | solution.py:726
  85.0 12.2 %fall.1 = (f32[1024,512]{1,0:T(8,128)S(1)}, bf16[1024,512]{1,0:T(8,128)(2,1)S(1)}, bf16[1024,512]{1,0:T(8,128)(2,1)S(1)}, f32[1,512]{1,0:T(1,128)S(1)}, bf16[4,4...) custom-call(s32[3]{0:T(128)S(1)} %pad_add_fusion.own_ref, ...), custom_call_target="tpu_custom_call" | custom-call | flops 34359738368 | bytes 100663296 | tf_op jit(solution)/shard_map/fall/pallas_call | solution.py:660
  99.1 2.8 %collective-permute-start.26 = (bf16[4,2,128,128]{3,2,1,0:T(8,128)(2,1)S(1)}, bf16[4,2,128,128]{3,2,1,0:T(8,128)(2,1)S(1)}, u32[]{:S(2)}, u32[]{:S(2)}) collective-permute-start(bf16[4,2,128,128]{3,2,1,0:T(8,128)(2,1)S(1)} %get-tuple-element.182), channel_id=1, source_target_pairs={{0,4},{1,5},{2,6},{3,7},{4,0},{5,1},{6,2},{7,3},{8,12},{9,13},{10,... | collective-permute-start | bytes 786440 | tf_op jit(solution)/shard_map/ppermute | solution.py:726
  102.3 10.2 %attend_back_half.1 = (bf16[1024,256]{1,0:T(8,128)(2,1)S(1)}, bf16[1024,256]{1,0:T(8,128)(2,1)S(1)}, bf16[1024,256]{1,0:T(8,128)(2,1)S(1)}) custom-call(bf16[1024,1536]{1,0:T(8,128)(2,1)S(1)} %copy-done.5, bf16[1024,512]{1,0:T(8,128)(2,1)S(1)} %get-tuple-element.123.s_ref, bf16[1024,512]{1,0:T(8,128)(2,1)S(1)} %get-tuple-element.124.x_ref), custom_call_target="tpu_custom_call" | custom-call | flops 17179869184 | bytes 6291456 | tf_op jit(solution)/shard_map/attend_back_half/pallas_call | solution.py:192
  113.1 1.6 collective-permute-start.23
  114.8 1.9 %collective-permute-start.25 = (bf16[4,64,640]{2,1,0:T(8,128)(2,1)S(1)}, bf16[4,64,640]{2,1,0:T(8,128)(2,1)S(1)}, u32[]{:S(2)}, u32[]{:S(2)}) collective-permute-start(bf16[4,64,640]{2,1,0:T(8,128)(2,1)S(1)} %get-tuple-element.177), channel_id=1, source_target_pairs={{0,24},{8,16},{16,8},{24,0},{1,25},{9,17},{17,9},{25,1},{2,26},{10... | collective-permute-start | bytes 983048 | tf_op jit(solution)/shard_map/ppermute | solution.py:726
  116.7 13.7 %attend_back_sum.1 = (bf16[1024,256]{1,0:T(8,128)(2,1)S(1)}, bf16[1024,256]{1,0:T(8,128)(2,1)S(1)}, bf16[1024,256]{1,0:T(8,128)(2,1)S(1)}, bf16[4,4,3,64,128]{4,...) custom-call(s32[3]{0:T(128)S(1)} %pad_add_fusion.own_ref, bf16[1024,1536]{1,0:T(8,128)(2,1)S(1)} %copy-done.5, ...), custom_call_target="tpu_custom_call" | custom-call | flops 21474836480 | bytes 10485760 | tf_op jit(solution)/shard_map/attend_back_sum/pallas_call | solution.py:259
  133.4 1.6 collective-permute-start.35
  136.2 3.2 %last.1 = (bf16[1024,512]{1,0:T(8,128)(2,1)S(1)}, f32[8,512]{1,0:T(8,128)S(1)}) custom-call(f32[1024,512]{1,0:T(8,128)S(1)} %multiply_add_fusion.hidden_ref, f32[1024,512]{1,0:T(8,128)S(1)} %get-tuple-element.120.first_ref, f32[1,512]{1,0:T(1,128)S(1)} %bitcast.118, bf16[8,1024]{1,0:T(8,128)(2,1)S(1)} %broadcast_in_dim.56.mask_ref, ...), custom_call_target="tpu_custom_call" | custom-call | flops 12884901888 | bytes 100663296 | tf_op jit(solution)/shard_map/last/pallas_call | solution.py:710
  140.8 2.2 %collective-permute-start.30 = (f32[8,512]{1,0:T(8,128)S(1)}, f32[8,512]{1,0:T(8,128)S(1)}, u32[]{:S(2)}, u32[]{:S(2)}) collective-permute-start(f32[8,512]{1,0:T(8,128)S(1)} %fusion.21), channel_id=1, source_target_pairs={{0,2},{1,3},{2,0},{3,1},{4,6},{5,7},{6,4},{7,5},{8,10},{9,11},{10,... | collective-permute-start | bytes 49160 | tf_op jit(solution)/shard_map/ppermute | solution.py:726
  143.0 1.7 %collective-permute-done.30 = f32[8,512]{1,0:T(8,128)S(1)} collective-permute-done((f32[8,512]{1,0:T(8,128)S(1)}, f32[8,512]{1,0:T(8,128)S(1)}, u32[]{:S(2)}, u32[]{:S(2)}) %collective-permute-start.30) | collective-permute-done | bytes 16416 | tf_op jit(solution)/shard_map/ppermute | solution.py:726
  144.7 1.8 %collective-permute-start.31 = (f32[8,512]{1,0:T(8,128)S(1)}, f32[8,512]{1,0:T(8,128)S(1)}, u32[]{:S(2)}, u32[]{:S(2)}) collective-permute-start(f32[8,512]{1,0:T(8,128)S(1)} %add.186), channel_id=1, source_target_pairs={{0,4},{1,5},{2,6},{3,7},{4,0},{5,1},{6,2},{7,3},{8,12},{9,13},{10,... | collective-permute-start | bytes 49160 | tf_op jit(solution)/shard_map/ppermute | solution.py:726
  146.5 2.8 %collective-permute-done.31 = f32[8,512]{1,0:T(8,128)S(1)} collective-permute-done((f32[8,512]{1,0:T(8,128)S(1)}, f32[8,512]{1,0:T(8,128)S(1)}, u32[]{:S(2)}, u32[]{:S(2)}) %collective-permute-start.31) | collective-permute-done | bytes 16416 | tf_op jit(solution)/shard_map/ppermute | solution.py:726
  149.6 1.8 %collective-permute-start.39 = (bf16[2,3,64,128]{3,2,1,0:T(8,128)(2,1)S(1)}, bf16[2,3,64,128]{3,2,1,0:T(8,128)(2,1)S(1)}, u32[]{:S(2)}, u32[]{:S(2)}) collective-permute-start(bf16[2,3,64,128]{3,2,1,0:T(8,128)(2,1)S(1)} %bitcast.146), channel_id=1, source_target_pairs={{0,4},{1,5},{2,6},{3,7},{4,0},{5,1},{6,2},{7,3},{8,12},{9,13},{10,... | collective-permute-start | bytes 294920 | tf_op jit(solution)/shard_map/ppermute | solution.py:726
  155.3 1.7 %collective-permute-done.39 = bf16[2,3,64,128]{3,2,1,0:T(8,128)(2,1)S(1)} collective-permute-done((bf16[2,3,64,128]{3,2,1,0:T(8,128)(2,1)S(1)}, bf16[2,3,64,128]{3,2,1,0:T(8,128)(2,1)S(1)}, u32[]{:S(2)}, u32[]{:S(2)}) %collective-permute-start.39) | collective-permute-done | bytes 98336 | tf_op jit(solution)/shard_map/ppermute | solution.py:726
  158.2 1.8 %collective-permute-start.41 = (bf16[1,64,640]{2,1,0:T(8,128)(2,1)S(1)}, bf16[1,64,640]{2,1,0:T(8,128)(2,1)S(1)}, u32[]{:S(2)}, u32[]{:S(2)}) collective-permute-start(bf16[1,64,640]{2,1,0:T(8,128)(2,1)S(1)} %slice.341), channel_id=1, source_target_pairs={{0,2},{1,3},{2,0},{3,1},{4,6},{5,7},{6,4},{7,5},{8,10},{9,11},{10,... | collective-permute-start | bytes 245768 | tf_op jit(solution)/shard_map/ppermute | solution.py:726
  (178 shorter events, 44.5 us)
Async XLA Ops:
  3.1 12.8 %collective-permute-start.3 = (bf16[64,896]{1,0:T(8,128)(2,1)}, bf16[64,896]{1,0:T(8,128)(2,1)S(1)}, u32[]{:S(2)}, u32[]{:S(2)}) collective-permute-start(bf16[64,896]{1,0:T(8,128)(2,1)} %get-tuple-element.225), channel_id=1, source_target_pairs={{0,2},{1,3},{2,0},{3,1},{4,6},{5,7},{6,4},{7,5},{8,10},{9,11},{10,... | collective-permute-start | bytes 344072 | tf_op jit(solution)/shard_map/ppermute | solution.py:726
  6.1 11.9 %collective-permute-start.4 = (bf16[64,896]{1,0:T(8,128)(2,1)}, bf16[64,896]{1,0:T(8,128)(2,1)S(1)}, u32[]{:S(2)}, u32[]{:S(2)}) collective-permute-start(bf16[64,896]{1,0:T(8,128)(2,1)} %get-tuple-element.225), channel_id=1, source_target_pairs={{0,4},{1,5},{2,6},{3,7},{4,0},{5,1},{6,2},{7,3},{8,12},{9,13},{10,... | collective-permute-start | bytes 344072 | tf_op jit(solution)/shard_map/ppermute | solution.py:726
  8.7 9.3 %collective-permute-start.5 = (bf16[64,896]{1,0:T(8,128)(2,1)}, bf16[64,896]{1,0:T(8,128)(2,1)S(1)}, u32[]{:S(2)}, u32[]{:S(2)}) collective-permute-start(bf16[64,896]{1,0:T(8,128)(2,1)} %get-tuple-element.225), channel_id=1, source_target_pairs={{0,6},{1,7},{2,4},{3,5},{4,2},{5,3},{6,0},{7,1},{8,14},{9,15},{10,... | collective-permute-start | bytes 344072 | tf_op jit(solution)/shard_map/ppermute | solution.py:726
  11.7 10.9 %collective-permute-start.2 = (bf16[272,512]{1,0:T(8,128)(2,1)}, bf16[272,512]{1,0:T(8,128)(2,1)}, u32[]{:S(2)}, u32[]{:S(2)}) collective-permute-start(bf16[272,512]{1,0:T(8,128)(2,1)} %get-tuple-element.192), channel_id=1, source_target_pairs={{0,24},{8,16},{16,8},{24,0},{1,25},{9,17},{17,9},{25,1},{2,26},{10... | collective-permute-start | bytes 835592 | tf_op jit(solution)/shard_map/ppermute | solution.py:726
  14.3 12.4 %collective-permute-start.1 = (bf16[272,512]{1,0:T(8,128)(2,1)}, bf16[272,512]{1,0:T(8,128)(2,1)}, u32[]{:S(2)}, u32[]{:S(2)}) collective-permute-start(bf16[272,512]{1,0:T(8,128)(2,1)} %get-tuple-element.191), channel_id=1, source_target_pairs={{0,16},{8,24},{16,0},{24,8},{1,17},{9,25},{17,1},{25,9},{2,18},{10... | collective-permute-start | bytes 835592 | tf_op jit(solution)/shard_map/ppermute | solution.py:726
  15.8 23.7 %collective-permute-start = (bf16[272,512]{1,0:T(8,128)(2,1)}, bf16[272,512]{1,0:T(8,128)(2,1)S(1)}, u32[]{:S(2)}, u32[]{:S(2)}) collective-permute-start(bf16[272,512]{1,0:T(8,128)(2,1)} %get-tuple-element.190), channel_id=1, source_target_pairs={{0,8},{8,0},{16,24},{24,16},{1,9},{9,1},{17,25},{25,17},{2,10},{10... | collective-permute-start | bytes 835592 | tf_op jit(solution)/shard_map/ppermute | solution.py:726
  18.1 14.7 %collective-permute-start.8 = (bf16[4,64,384]{2,1,0:T(8,128)(2,1)S(1)}, bf16[4,64,384]{2,1,0:T(8,128)(2,1)S(1)}, u32[]{:S(2)}, u32[]{:S(2)}) collective-permute-start(bf16[4,64,384]{2,1,0:T(8,128)(2,1)S(1)} %get-tuple-element.213), channel_id=1, source_target_pairs={{0,8},{8,0},{16,24},{24,16},{1,9},{9,1},{17,25},{25,17},{2,10},{10... | collective-permute-start | bytes 589832 | tf_op jit(solution)/shard_map/ppermute | solution.py:726
  19.7 14.6 %collective-permute-start.9 = (bf16[4,64,384]{2,1,0:T(8,128)(2,1)S(1)}, bf16[4,64,384]{2,1,0:T(8,128)(2,1)S(1)}, u32[]{:S(2)}, u32[]{:S(2)}) collective-permute-start(bf16[4,64,384]{2,1,0:T(8,128)(2,1)S(1)} %get-tuple-element.213), channel_id=1, source_target_pairs={{0,16},{8,24},{16,0},{24,8},{1,17},{9,25},{17,1},{25,9},{2,18},{10... | collective-permute-start | bytes 589832 | tf_op jit(solution)/shard_map/ppermute | solution.py:726
  22.5 14.3 %collective-permute-start.10 = (bf16[4,64,384]{2,1,0:T(8,128)(2,1)S(1)}, bf16[4,64,384]{2,1,0:T(8,128)(2,1)S(1)}, u32[]{:S(2)}, u32[]{:S(2)}) collective-permute-start(bf16[4,64,384]{2,1,0:T(8,128)(2,1)S(1)} %get-tuple-element.213), channel_id=1, source_target_pairs={{0,24},{8,16},{16,8},{24,0},{1,25},{9,17},{17,9},{25,1},{2,26},{10... | collective-permute-start | bytes 589832 | tf_op jit(solution)/shard_map/ppermute | solution.py:726
  26.8 17.5 %collective-permute-start.6 = (bf16[64,2560]{1,0:T(8,128)(2,1)S(1)}, bf16[64,2560]{1,0:T(8,128)(2,1)S(1)}, u32[]{:S(2)}, u32[]{:S(2)}) collective-permute-start(bf16[64,2560]{1,0:T(8,128)(2,1)S(1)} %pad_maximum_fusion.16), channel_id=1, source_target_pairs={{0,4},{1,5},{2,6},{3,7},{4,0},{5,1},{6,2},{7,3},{8,12},{9,13},{10,... | collective-permute-start | bytes 983048 | tf_op jit(solution)/shard_map/ppermute | solution.py:726
  32.9 27.6 %collective-permute-start.12 = (bf16[512,512]{1,0:T(8,128)(2,1)S(1)}, bf16[512,512]{1,0:T(8,128)(2,1)S(1)}, u32[]{:S(2)}, u32[]{:S(2)}) collective-permute-start(bf16[512,512]{1,0:T(8,128)(2,1)S(1)} %get-tuple-element.219), channel_id=1, source_target_pairs={{0,8},{8,0},{16,24},{24,16},{1,9},{9,1},{17,25},{25,17},{2,10},{10... | collective-permute-start | bytes 1572872 | tf_op jit(solution)/shard_map/ppermute | solution.py:726
  34.3 26.1 %collective-permute-start.13 = (bf16[512,512]{1,0:T(8,128)(2,1)S(1)}, bf16[512,512]{1,0:T(8,128)(2,1)S(1)}, u32[]{:S(2)}, u32[]{:S(2)}) collective-permute-start(bf16[512,512]{1,0:T(8,128)(2,1)S(1)} %get-tuple-element.220), channel_id=1, source_target_pairs={{0,16},{8,24},{16,0},{24,8},{1,17},{9,25},{17,1},{25,9},{2,18},{10... | collective-permute-start | bytes 1572872 | tf_op jit(solution)/shard_map/ppermute | solution.py:726
  36.8 23.6 %collective-permute-start.14 = (bf16[512,512]{1,0:T(8,128)(2,1)S(1)}, bf16[512,512]{1,0:T(8,128)(2,1)S(1)}, u32[]{:S(2)}, u32[]{:S(2)}) collective-permute-start(bf16[512,512]{1,0:T(8,128)(2,1)S(1)} %get-tuple-element.218), channel_id=1, source_target_pairs={{0,24},{8,16},{16,8},{24,0},{1,25},{9,17},{17,9},{25,1},{2,26},{10... | collective-permute-start | bytes 1572872 | tf_op jit(solution)/shard_map/ppermute | solution.py:726
  44.3 15.8 %collective-permute-start.7 = (bf16[2,64,2560]{2,1,0:T(8,128)(2,1)S(1)}, bf16[2,64,2560]{2,1,0:T(8,128)(2,1)S(1)}, u32[]{:S(2)}, u32[]{:S(2)}) collective-permute-start(bf16[2,64,2560]{2,1,0:T(8,128)(2,1)S(1)} %pad_maximum_fusion.8), channel_id=1, source_target_pairs={{0,2},{1,3},{2,0},{3,1},{4,6},{5,7},{6,4},{7,5},{8,10},{9,11},{10,... | collective-permute-start | bytes 1966088 | tf_op jit(solution)/shard_map/ppermute | solution.py:726
  81.4 15.8 %collective-permute-start.18 = (bf16[256,512]{1,0:T(8,128)(2,1)S(1)}, bf16[256,512]{1,0:T(8,128)(2,1)S(1)}, u32[]{:S(2)}, u32[]{:S(2)}) collective-permute-start(bf16[256,512]{1,0:T(8,128)(2,1)S(1)} %get-tuple-element.198), channel_id=1, source_target_pairs={{0,8},{8,0},{16,24},{24,16},{1,9},{9,1},{17,25},{25,17},{2,10},{10... | collective-permute-start | bytes 786440 | tf_op jit(solution)/shard_map/ppermute | solution.py:726
  83.0 14.2 %collective-permute-start.19 = (bf16[256,512]{1,0:T(8,128)(2,1)S(1)}, bf16[256,512]{1,0:T(8,128)(2,1)S(1)}, u32[]{:S(2)}, u32[]{:S(2)}) collective-permute-start(bf16[256,512]{1,0:T(8,128)(2,1)S(1)} %get-tuple-element.197), channel_id=1, source_target_pairs={{0,16},{8,24},{16,0},{24,8},{1,17},{9,25},{17,1},{25,9},{2,18},{10... | collective-permute-start | bytes 786440 | tf_op jit(solution)/shard_map/ppermute | solution.py:726
  83.1 14.1 %collective-permute-start.20 = (bf16[256,512]{1,0:T(8,128)(2,1)S(1)}, bf16[256,512]{1,0:T(8,128)(2,1)S(1)}, u32[]{:S(2)}, u32[]{:S(2)}) collective-permute-start(bf16[256,512]{1,0:T(8,128)(2,1)S(1)} %get-tuple-element.196), channel_id=1, source_target_pairs={{0,24},{8,16},{16,8},{24,0},{1,25},{9,17},{17,9},{25,1},{2,26},{10... | collective-permute-start | bytes 786440 | tf_op jit(solution)/shard_map/ppermute | solution.py:726
  85.0 12.3 %collective-permute-start.17 = (bf16[4,4,2,128,128]{4,3,2,1,0:T(8,128)(2,1)S(1)}, bf16[4,4,2,128,128]{4,3,2,1,0:T(8,128)(2,1)S(1)}, u32[]{:S(2)}, u32[]{:S(2)}) collective-permute-start(bf16[4,4,2,128,128]{4,3,2,1,0:T(8,128)(2,1)S(1)} %get-tuple-element.105), channel_id=1, source_target_pairs={{0,1},{1,0},{2,3},{3,2},{4,5},{5,4},{6,7},{7,6},{8,9},{9,8},{10,11... | collective-permute-start | bytes 3145736 | tf_op jit(solution)/shard_map/ppermute | solution.py:726
  97.6 15.1 %collective-permute-start.22 = (bf16[4,2,128,128]{3,2,1,0:T(8,128)(2,1)S(1)}, bf16[4,2,128,128]{3,2,1,0:T(8,128)(2,1)S(1)}, u32[]{:S(2)}, u32[]{:S(2)}) collective-permute-start(bf16[4,2,128,128]{3,2,1,0:T(8,128)(2,1)S(1)} %get-tuple-element.184), channel_id=1, source_target_pairs={{0,2},{1,3},{2,0},{3,1},{4,6},{5,7},{6,4},{7,5},{8,10},{9,11},{10,... | collective-permute-start | bytes 786440 | tf_op jit(solution)/shard_map/ppermute | solution.py:726
  98.9 13.8 %collective-permute-start.21 = (bf16[4,4,64,640]{3,2,1,0:T(8,128)(2,1)S(1)}, bf16[4,4,64,640]{3,2,1,0:T(8,128)(2,1)S(1)}, u32[]{:S(2)}, u32[]{:S(2)}) collective-permute-start(bf16[4,4,64,640]{3,2,1,0:T(8,128)(2,1)S(1)} %get-tuple-element.122), channel_id=1, source_target_pairs={{0,1},{1,0},{2,3},{3,2},{4,5},{5,4},{6,7},{7,6},{8,9},{9,8},{10,11... | collective-permute-start | bytes 3932168 | tf_op jit(solution)/shard_map/ppermute | solution.py:726
  99.1 31.2 %collective-permute-start.26 = (bf16[4,2,128,128]{3,2,1,0:T(8,128)(2,1)S(1)}, bf16[4,2,128,128]{3,2,1,0:T(8,128)(2,1)S(1)}, u32[]{:S(2)}, u32[]{:S(2)}) collective-permute-start(bf16[4,2,128,128]{3,2,1,0:T(8,128)(2,1)S(1)} %get-tuple-element.182), channel_id=1, source_target_pairs={{0,4},{1,5},{2,6},{3,7},{4,0},{5,1},{6,2},{7,3},{8,12},{9,13},{10,... | collective-permute-start | bytes 786440 | tf_op jit(solution)/shard_map/ppermute | solution.py:726
  101.9 28.5 %collective-permute-start.27 = (bf16[4,2,128,128]{3,2,1,0:T(8,128)(2,1)S(1)}, bf16[4,2,128,128]{3,2,1,0:T(8,128)(2,1)S(1)}, u32[]{:S(2)}, u32[]{:S(2)}) collective-permute-start(bf16[4,2,128,128]{3,2,1,0:T(8,128)(2,1)S(1)} %get-tuple-element.181), channel_id=1, source_target_pairs={{0,6},{1,7},{2,4},{3,5},{4,2},{5,3},{6,0},{7,1},{8,14},{9,15},{10,... | collective-permute-start | bytes 786440 | tf_op jit(solution)/shard_map/ppermute | solution.py:726
  113.1 17.2 %collective-permute-start.23 = (bf16[4,64,640]{2,1,0:T(8,128)(2,1)S(1)}, bf16[4,64,640]{2,1,0:T(8,128)(2,1)S(1)}, u32[]{:S(2)}, u32[]{:S(2)}) collective-permute-start(bf16[4,64,640]{2,1,0:T(8,128)(2,1)S(1)} %get-tuple-element.179), channel_id=1, source_target_pairs={{0,8},{8,0},{16,24},{24,16},{1,9},{9,1},{17,25},{25,17},{2,10},{10... | collective-permute-start | bytes 983048 | tf_op jit(solution)/shard_map/ppermute | solution.py:726
  114.7 16.1 %collective-permute-start.24 = (bf16[4,64,640]{2,1,0:T(8,128)(2,1)S(1)}, bf16[4,64,640]{2,1,0:T(8,128)(2,1)S(1)}, u32[]{:S(2)}, u32[]{:S(2)}) collective-permute-start(bf16[4,64,640]{2,1,0:T(8,128)(2,1)S(1)} %get-tuple-element.178), channel_id=1, source_target_pairs={{0,16},{8,24},{16,0},{24,8},{1,17},{9,25},{17,1},{25,9},{2,18},{10... | collective-permute-start | bytes 983048 | tf_op jit(solution)/shard_map/ppermute | solution.py:726
  114.8 16.0 %collective-permute-start.25 = (bf16[4,64,640]{2,1,0:T(8,128)(2,1)S(1)}, bf16[4,64,640]{2,1,0:T(8,128)(2,1)S(1)}, u32[]{:S(2)}, u32[]{:S(2)}) collective-permute-start(bf16[4,64,640]{2,1,0:T(8,128)(2,1)S(1)} %get-tuple-element.177), channel_id=1, source_target_pairs={{0,24},{8,16},{16,8},{24,0},{1,25},{9,17},{17,9},{25,1},{2,26},{10... | collective-permute-start | bytes 983048 | tf_op jit(solution)/shard_map/ppermute | solution.py:726
  131.0 18.4 %collective-permute-start.32 = (bf16[2,64,640]{2,1,0:T(8,128)(2,1)S(1)}, bf16[2,64,640]{2,1,0:T(8,128)(2,1)S(1)}, u32[]{:S(2)}, u32[]{:S(2)}) collective-permute-start(bf16[2,64,640]{2,1,0:T(8,128)(2,1)S(1)} %slice.357), channel_id=1, source_target_pairs={{0,4},{1,5},{2,6},{3,7},{4,0},{5,1},{6,2},{7,3},{8,12},{9,13},{10,... | collective-permute-start | bytes 491528 | tf_op jit(solution)/shard_map/ppermute | solution.py:726
  133.4 16.0 %collective-permute-start.35 = (bf16[16,64,128]{2,1,0:T(8,128)(2,1)S(1)}, bf16[16,64,128]{2,1,0:T(8,128)(2,1)S(1)}, u32[]{:S(2)}, u32[]{:S(2)}) collective-permute-start(bf16[16,64,128]{2,1,0:T(8,128)(2,1)S(1)} %pad_maximum_fusion.20), channel_id=1, source_target_pairs={{0,24},{8,16},{16,8},{24,0},{1,25},{9,17},{17,9},{25,1},{2,26},{10... | collective-permute-start | bytes 786440 | tf_op jit(solution)/shard_map/ppermute | solution.py:726
  135.0 14.4 %collective-permute-start.34 = (bf16[16,64,128]{2,1,0:T(8,128)(2,1)S(1)}, bf16[16,64,128]{2,1,0:T(8,128)(2,1)S(1)}, u32[]{:S(2)}, u32[]{:S(2)}) collective-permute-start(bf16[16,64,128]{2,1,0:T(8,128)(2,1)S(1)} %pad_maximum_fusion.19), channel_id=1, source_target_pairs={{0,16},{8,24},{16,0},{24,8},{1,17},{9,25},{17,1},{25,9},{2,18},{10... | collective-permute-start | bytes 786440 | tf_op jit(solution)/shard_map/ppermute | solution.py:726
  139.6 9.8 %collective-permute-start.33 = (bf16[16,64,128]{2,1,0:T(8,128)(2,1)S(1)}, bf16[16,64,128]{2,1,0:T(8,128)(2,1)S(1)}, u32[]{:S(2)}, u32[]{:S(2)}) collective-permute-start(bf16[16,64,128]{2,1,0:T(8,128)(2,1)S(1)} %pad_maximum_fusion.18), channel_id=1, source_target_pairs={{0,8},{8,0},{16,24},{24,16},{1,9},{9,1},{17,25},{25,17},{2,10},{10... | collective-permute-start | bytes 786440 | tf_op jit(solution)/shard_map/ppermute | solution.py:726
  151.6 12.5 %collective-permute-start.36 = (bf16[272,512]{1,0:T(8,128)(2,1)S(1)}, bf16[272,512]{1,0:T(8,128)(2,1)S(1)}, u32[]{:S(2)}, u32[]{:S(2)}) collective-permute-start(bf16[272,512]{1,0:T(8,128)(2,1)S(1)} %get-tuple-element.230), channel_id=1, source_target_pairs={{0,24},{8,16},{16,8},{24,0},{1,25},{9,17},{17,9},{25,1},{2,26},{10... | collective-permute-start | bytes 835592 | tf_op jit(solution)/shard_map/ppermute | solution.py:726
  153.1 12.2 %collective-permute-start.37 = (bf16[272,512]{1,0:T(8,128)(2,1)S(1)}, bf16[272,512]{1,0:T(8,128)(2,1)S(1)}, u32[]{:S(2)}, u32[]{:S(2)}) collective-permute-start(bf16[272,512]{1,0:T(8,128)(2,1)S(1)} %get-tuple-element.229), channel_id=1, source_target_pairs={{0,16},{8,24},{16,0},{24,8},{1,17},{9,25},{17,1},{25,9},{2,18},{10... | collective-permute-start | bytes 835592 | tf_op jit(solution)/shard_map/ppermute | solution.py:726
  154.0 11.2 %collective-permute-start.38 = (bf16[272,512]{1,0:T(8,128)(2,1)S(1)}, bf16[272,512]{1,0:T(8,128)(2,1)S(1)}, u32[]{:S(2)}, u32[]{:S(2)}) collective-permute-start(bf16[272,512]{1,0:T(8,128)(2,1)S(1)} %get-tuple-element.228), channel_id=1, source_target_pairs={{0,8},{8,0},{16,24},{24,16},{1,9},{9,1},{17,25},{25,17},{2,10},{10... | collective-permute-start | bytes 835592 | tf_op jit(solution)/shard_map/ppermute | solution.py:726
  (29 other events, 169.6 us)

commit v9 on v8

--- a/solution.py
+++ b/solution.py
@@ -571,9 +571,11 @@
     lane = lax.broadcasted_iota(jnp.int32, (128, width), 1)
     spread = lax.broadcasted_iota(jnp.int32, (128, width), 0) == 16 * (lane // 64)
     spread = jnp.where(spread, 1.0, 0.0).astype(BF16)
+    spread = jnp.concatenate((spread, spread))
     row = lax.broadcasted_iota(jnp.int32, (128, 128), 0)
     col = lax.broadcasted_iota(jnp.int32, (128, 128), 1)
     swap = jnp.where((row < 64) != (col < 64), 1.0, 0.0).astype(BF16)
+    swap = jnp.concatenate((swap, swap))
     even = lax.broadcasted_iota(jnp.int32, (1, 128), 1) % 2 == 0
     gain_sum = jnp.zeros((1, width), F32)
     att_t[...] = att_ref[...].T
@@ -596,14 +598,16 @@
         den = den_ref[at, :]
         coarse = den.astype(BF16)
         fine = (den - coarse.astype(F32)).astype(BF16)
-        ratio = nt(branch, w_up[:, :width]) / (nn(coarse, spread) + nn(fine, spread))
+        terms = jnp.concatenate((coarse, fine), axis=1)
+        ratio = nt(branch, w_up[:, :width]) / nn(terms, spread)
         scaled_ref[at, :] = ratio.astype(BF16)
         product = ratio * att_ref[at, :]
         coarse = product.astype(BF16)
         fine = (product - coarse.astype(F32)).astype(BF16)
         for start in range(0, width, 128):
             stop = start + 128
-            offset = nn(coarse[:, start:stop], swap) + nn(fine[:, start:stop], swap)
+            terms = jnp.concatenate((coarse[:, start:stop], fine[:, start:stop]), axis=1)
+            offset = nn(terms, swap)
             upper = offset.astype(BF16)
             lower = (offset - upper.astype(F32)).astype(BF16)
             extra_ref[at, start:stop] = jnp.where(even, upper, lower)

time: 170 us -> 170 us (level)
  transfers between devices with their start and end apart: 42 -> 42, of which waited for: 17 -> 18; matrix products, arithmetic and copies ran while one was open for 10% -> 10% of each run, Pallas kernels for 31% -> 31%
where the time goes in v9:
time: 170 us; the launch traced here: 167 us
  Pallas kernels  66.7 us (39%)
  starting transfers between devices  50.3 us (30%)
  waiting for transfers between devices  24.5 us (14%)
  local copies, waits for them, and re-layouts  13.9 us (8%)
  other arithmetic  9.56 us (6%)
  between operations  1.88 us (1%)
    ppermute x42, starting transfers between devices, swap_along(): return lax.ppermute(value, axis, [(i, i ^ mask) for i in range(count)])  50.3 us
    ppermute x42, waiting for transfers between devices, swap_along(): return lax.ppermute(value, axis, [(i, i ^ mask) for i in range(count)])  24.5 us
    pallas_call x1, Pallas kernels, rise(): pl.pallas_call(functools.partial(rise_kernel, cfg), in_specs=[pl.BlockSpe...  14.7 us
    pallas_call x1, Pallas kernels, attend_back_sum(): pl.pallas_call(functools.partial(attend_back_sum_kernel, min(512, count),...  13.7 us
    pallas_call x1, Pallas kernels, fall(): pl.pallas_call(functools.partial(fall_kernel, cfg), in_specs=[pl.BlockSpe...  11.8 us
    pallas_call x1, Pallas kernels, attend_back_half(): pl.pallas_call(functools.partial(attend_back_half_kernel, min(512, count)...  10.2 us
    pallas_call x1, Pallas kernels, attend_row(): pl.pallas_call(functools.partial(attend_row_kernel, min(256, count)), in_...  9.4 us
    unnamed x38, local copies, waits for them, and re-layouts  3.74 us
  transfers between devices with their start and end apart: 42, of which 18 were waited for; matrix products, arithmetic and copies ran while one was open for 10% of the time, Pallas kernels for 31%

profile of v9, /device:TPU:0, one launch (start us, length us, event | category | flops | bytes accessed | tf_op | source)
XLA Modules:
  0.0 166.8 jit_solution(16318560565473143042)
XLA Ops:
  3.1 3.0 %collective-permute-start.3 = (bf16[64,896]{1,0:T(8,128)(2,1)}, bf16[64,896]{1,0:T(8,128)(2,1)S(1)}, u32[]{:S(2)}, u32[]{:S(2)}) collective-permute-start(bf16[64,896]{1,0:T(8,128)(2,1)} %get-tuple-element.225), channel_id=1, source_target_pairs={{0,2},{1,3},{2,0},{3,1},{4,6},{5,7},{6,4},{7,5},{8,10},{9,11},{10,... | collective-permute-start | bytes 344072 | tf_op jit(solution)/shard_map/ppermute | solution.py:730
  6.1 2.6 %collective-permute-start.4 = (bf16[64,896]{1,0:T(8,128)(2,1)}, bf16[64,896]{1,0:T(8,128)(2,1)S(1)}, u32[]{:S(2)}, u32[]{:S(2)}) collective-permute-start(bf16[64,896]{1,0:T(8,128)(2,1)} %get-tuple-element.225), channel_id=1, source_target_pairs={{0,4},{1,5},{2,6},{3,7},{4,0},{5,1},{6,2},{7,3},{8,12},{9,13},{10,... | collective-permute-start | bytes 344072 | tf_op jit(solution)/shard_map/ppermute | solution.py:730
  9.5 2.1 %fusion.6 = (bf16[1,272,512]{2,1,0:T(8,128)(2,1)S(1)}, bf16[272,512]{1,0:T(8,128)(2,1)}, bf16[272,512]{1,0:T(8,128)(2,1)}, bf16[272,512]{1,0:T(8,128)(2,1)}) fusion(s32[]{:T(128)S(6)} %select_n.54, bf16[4,256,512]{2,1,0:T(8,128)(2,1)} %param.11, bf16[4,16,512]{2,1,0:T(8,128)(2,1)S(1)} %pad_convert_fusion, s32[]{:T(128)S(6)} %select_n.55, s32[]{:T(128)S(6)} %select_n.56, ...), kind=kLoop, calls=%fused_computation.48 | loop fusion | flops 2228224 | bytes 2228240 | tf_op jit(solution)/shard_map/concatenate | solution.py:844
  11.7 2.7 %collective-permute-start.2 = (bf16[272,512]{1,0:T(8,128)(2,1)}, bf16[272,512]{1,0:T(8,128)(2,1)}, u32[]{:S(2)}, u32[]{:S(2)}) collective-permute-start(bf16[272,512]{1,0:T(8,128)(2,1)} %get-tuple-element.192), channel_id=1, source_target_pairs={{0,24},{8,16},{16,8},{24,0},{1,25},{9,17},{17,9},{25,1},{2,26},{10... | collective-permute-start | bytes 835592 | tf_op jit(solution)/shard_map/ppermute | solution.py:730
  16.2 1.8 %collective-permute-done.4 = bf16[64,896]{1,0:T(8,128)(2,1)S(1)} collective-permute-done((bf16[64,896]{1,0:T(8,128)(2,1)}, bf16[64,896]{1,0:T(8,128)(2,1)S(1)}, u32[]{:S(2)}, u32[]{:S(2)}) %collective-permute-start.4) | collective-permute-done | bytes 114720 | tf_op jit(solution)/shard_map/ppermute | solution.py:730
  18.1 1.6 collective-permute-start.8
  22.5 2.6 %collective-permute-start.10 = (bf16[4,64,384]{2,1,0:T(8,128)(2,1)S(1)}, bf16[4,64,384]{2,1,0:T(8,128)(2,1)S(1)}, u32[]{:S(2)}, u32[]{:S(2)}) collective-permute-start(bf16[4,64,384]{2,1,0:T(8,128)(2,1)S(1)} %get-tuple-element.213), channel_id=1, source_target_pairs={{0,24},{8,16},{16,8},{24,0},{1,25},{9,17},{17,9},{25,1},{2,26},{10... | collective-permute-start | bytes 589832 | tf_op jit(solution)/shard_map/ppermute | solution.py:730
  26.8 1.6 collective-permute-start.6
  29.1 3.7 %collective-permute-done.8 = bf16[4,64,384]{2,1,0:T(8,128)(2,1)S(1)} collective-permute-done((bf16[4,64,384]{2,1,0:T(8,128)(2,1)S(1)}, bf16[4,64,384]{2,1,0:T(8,128)(2,1)S(1)}, u32[]{:S(2)}, u32[]{:S(2)}) %collective-permute-start.8) | collective-permute-done | bytes 196640 | tf_op jit(solution)/shard_map/ppermute | solution.py:730
  34.9 2.0 %collective-permute-done.10 = bf16[4,64,384]{2,1,0:T(8,128)(2,1)S(1)} collective-permute-done((bf16[4,64,384]{2,1,0:T(8,128)(2,1)S(1)}, bf16[4,64,384]{2,1,0:T(8,128)(2,1)S(1)}, u32[]{:S(2)}, u32[]{:S(2)}) %collective-permute-start.10) | collective-permute-done | bytes 196640 | tf_op jit(solution)/shard_map/ppermute | solution.py:730
  36.8 2.6 %collective-permute-start.14 = (bf16[512,512]{1,0:T(8,128)(2,1)S(1)}, bf16[512,512]{1,0:T(8,128)(2,1)S(1)}, u32[]{:S(2)}, u32[]{:S(2)}) collective-permute-start(bf16[512,512]{1,0:T(8,128)(2,1)S(1)} %get-tuple-element.218), channel_id=1, source_target_pairs={{0,24},{8,16},{16,8},{24,0},{1,25},{9,17},{17,9},{25,1},{2,26},{10... | collective-permute-start | bytes 1572872 | tf_op jit(solution)/shard_map/ppermute | solution.py:730
  42.0 2.3 %collective-permute-done.6 = bf16[64,2560]{1,0:T(8,128)(2,1)S(1)} collective-permute-done((bf16[64,2560]{1,0:T(8,128)(2,1)S(1)}, bf16[64,2560]{1,0:T(8,128)(2,1)S(1)}, u32[]{:S(2)}, u32[]{:S(2)}) %collective-permute-start.6) | collective-permute-done | bytes 327712 | tf_op jit(solution)/shard_map/ppermute | solution.py:730
  44.4 3.7 %project.1 = (bf16[1024,512]{1,0:T(8,128)(2,1)}, bf16[1024,1536]{1,0:T(8,128)(2,1)S(1)}, bf16[512,1536]{1,0:T(8,128)(2,1)}) custom-call(s32[3]{0:T(128)S(1)} %pad_add_fusion.own_ref, f32[1024,512]{1,0:T(8,128)S(1)} %multiply_add_fusion.hidden_ref, f32[1,512]{1,0:T(1,128)S(1)} %bitcast.117, bf16[4,4,64,384]{3,2,1,0:T(8,128)(2,1)S(1)} %pad_maximum_fusion.3.refs_0_, ...), custom_call_target="tpu_custom_call" | custom-call | flops 6442450944 | bytes 33554432 | tf_op jit(solution)/shard_map/project/pallas_call | solution.py:407
  48.2 9.4 %attend_row.1 = (bf16[1024,512]{1,0:T(8,128)(2,1)S(1)}, f32[1024,128]{1,0:T(8,128)S(1)}) custom-call(bf16[1024,1536]{1,0:T(8,128)(2,1)S(1)} %get-tuple-element.94.own_ref.proj_ref), custom_call_target="tpu_custom_call" | custom-call | flops 17179869184 | bytes 5242880 | tf_op jit(solution)/shard_map/attend_row/pallas_call | solution.py:120
  66.7 14.7 %rise.1 = (bf16[1024,512]{1,0:T(8,128)(2,1)S(1)}, f32[1024,512]{1,0:T(8,128)S(1)}, f32[1024,128]{1,0:T(8,128)S(1)}, bf16[1024,2048]{1,0:T(8,128)(2,1)S(1)}, bf16...) custom-call(s32[3]{0:T(128)S(1)} %pad_add_fusion.own_ref, ...), custom_call_target="tpu_custom_call" | custom-call | flops 7516192768 | bytes 25165824 | tf_op jit(solution)/shard_map/rise/pallas_call | solution.py:515
  81.4 1.6 collective-permute-start.18
  83.1 1.9 %collective-permute-start.20 = (bf16[256,512]{1,0:T(8,128)(2,1)S(1)}, bf16[256,512]{1,0:T(8,128)(2,1)S(1)}, u32[]{:S(2)}, u32[]{:S(2)}) collective-permute-start(bf16[256,512]{1,0:T(8,128)(2,1)S(1)} %get-tuple-element.196), channel_id=1, source_target_pairs={{0,24},{8,16},{16,8},{24,0},{1,25},{9,17},{17,9},{25,1},{2,26},{10... | collective-permute-start | bytes 786440 | tf_op jit(solution)/shard_map/ppermute | solution.py:730
  85.0 11.8 %fall.1 = (f32[1024,512]{1,0:T(8,128)S(1)}, bf16[1024,512]{1,0:T(8,128)(2,1)S(1)}, bf16[1024,512]{1,0:T(8,128)(2,1)S(1)}, f32[1,512]{1,0:T(1,128)S(1)}, bf16[4,4...) custom-call(s32[3]{0:T(128)S(1)} %pad_add_fusion.own_ref, ...), custom_call_target="tpu_custom_call" | custom-call | flops 34359738368 | bytes 100663296 | tf_op jit(solution)/shard_map/fall/pallas_call | solution.py:664
  98.7 2.8 %collective-permute-start.26 = (bf16[4,2,128,128]{3,2,1,0:T(8,128)(2,1)S(1)}, bf16[4,2,128,128]{3,2,1,0:T(8,128)(2,1)S(1)}, u32[]{:S(2)}, u32[]{:S(2)}) collective-permute-start(bf16[4,2,128,128]{3,2,1,0:T(8,128)(2,1)S(1)} %get-tuple-element.182), channel_id=1, source_target_pairs={{0,4},{1,5},{2,6},{3,7},{4,0},{5,1},{6,2},{7,3},{8,12},{9,13},{10,... | collective-permute-start | bytes 786440 | tf_op jit(solution)/shard_map/ppermute | solution.py:730
  101.9 10.2 %attend_back_half.1 = (bf16[1024,256]{1,0:T(8,128)(2,1)S(1)}, bf16[1024,256]{1,0:T(8,128)(2,1)S(1)}, bf16[1024,256]{1,0:T(8,128)(2,1)S(1)}) custom-call(bf16[1024,1536]{1,0:T(8,128)(2,1)S(1)} %copy-done.5, bf16[1024,512]{1,0:T(8,128)(2,1)S(1)} %get-tuple-element.123.s_ref, bf16[1024,512]{1,0:T(8,128)(2,1)S(1)} %get-tuple-element.124.x_ref), custom_call_target="tpu_custom_call" | custom-call | flops 17179869184 | bytes 6291456 | tf_op jit(solution)/shard_map/attend_back_half/pallas_call | solution.py:192
  112.7 1.6 collective-permute-start.23
  114.6 1.6 collective-permute-start.25
  116.2 13.7 %attend_back_sum.1 = (bf16[1024,256]{1,0:T(8,128)(2,1)S(1)}, bf16[1024,256]{1,0:T(8,128)(2,1)S(1)}, bf16[1024,256]{1,0:T(8,128)(2,1)S(1)}, bf16[4,4,3,64,128]{4,...) custom-call(s32[3]{0:T(128)S(1)} %pad_add_fusion.own_ref, bf16[1024,1536]{1,0:T(8,128)(2,1)S(1)} %copy-done.5, ...), custom_call_target="tpu_custom_call" | custom-call | flops 21474836480 | bytes 10485760 | tf_op jit(solution)/shard_map/attend_back_sum/pallas_call | solution.py:259
  133.0 1.6 collective-permute-start.35
  135.8 3.2 %last.1 = (bf16[1024,512]{1,0:T(8,128)(2,1)S(1)}, f32[8,512]{1,0:T(8,128)S(1)}) custom-call(f32[1024,512]{1,0:T(8,128)S(1)} %multiply_add_fusion.hidden_ref, f32[1024,512]{1,0:T(8,128)S(1)} %get-tuple-element.120.first_ref, f32[1,512]{1,0:T(1,128)S(1)} %bitcast.118, bf16[8,1024]{1,0:T(8,128)(2,1)S(1)} %broadcast_in_dim.56.mask_ref, ...), custom_call_target="tpu_custom_call" | custom-call | flops 12884901888 | bytes 100663296 | tf_op jit(solution)/shard_map/last/pallas_call | solution.py:714
  140.3 2.2 %collective-permute-start.30 = (f32[8,512]{1,0:T(8,128)S(1)}, f32[8,512]{1,0:T(8,128)S(1)}, u32[]{:S(2)}, u32[]{:S(2)}) collective-permute-start(f32[8,512]{1,0:T(8,128)S(1)} %fusion.21), channel_id=1, source_target_pairs={{0,2},{1,3},{2,0},{3,1},{4,6},{5,7},{6,4},{7,5},{8,10},{9,11},{10,... | collective-permute-start | bytes 49160 | tf_op jit(solution)/shard_map/ppermute | solution.py:730
  142.6 1.7 %collective-permute-done.30 = f32[8,512]{1,0:T(8,128)S(1)} collective-permute-done((f32[8,512]{1,0:T(8,128)S(1)}, f32[8,512]{1,0:T(8,128)S(1)}, u32[]{:S(2)}, u32[]{:S(2)}) %collective-permute-start.30) | collective-permute-done | bytes 16416 | tf_op jit(solution)/shard_map/ppermute | solution.py:730
  144.3 1.8 %collective-permute-start.31 = (f32[8,512]{1,0:T(8,128)S(1)}, f32[8,512]{1,0:T(8,128)S(1)}, u32[]{:S(2)}, u32[]{:S(2)}) collective-permute-start(f32[8,512]{1,0:T(8,128)S(1)} %add.186), channel_id=1, source_target_pairs={{0,4},{1,5},{2,6},{3,7},{4,0},{5,1},{6,2},{7,3},{8,12},{9,13},{10,... | collective-permute-start | bytes 49160 | tf_op jit(solution)/shard_map/ppermute | solution.py:730
  146.1 2.8 %collective-permute-done.31 = f32[8,512]{1,0:T(8,128)S(1)} collective-permute-done((f32[8,512]{1,0:T(8,128)S(1)}, f32[8,512]{1,0:T(8,128)S(1)}, u32[]{:S(2)}, u32[]{:S(2)}) %collective-permute-start.31) | collective-permute-done | bytes 16416 | tf_op jit(solution)/shard_map/ppermute | solution.py:730
  149.1 1.8 %collective-permute-start.39 = (bf16[2,3,64,128]{3,2,1,0:T(8,128)(2,1)S(1)}, bf16[2,3,64,128]{3,2,1,0:T(8,128)(2,1)S(1)}, u32[]{:S(2)}, u32[]{:S(2)}) collective-permute-start(bf16[2,3,64,128]{3,2,1,0:T(8,128)(2,1)S(1)} %bitcast.146), channel_id=1, source_target_pairs={{0,4},{1,5},{2,6},{3,7},{4,0},{5,1},{6,2},{7,3},{8,12},{9,13},{10,... | collective-permute-start | bytes 294920 | tf_op jit(solution)/shard_map/ppermute | solution.py:730
  154.9 1.7 %collective-permute-done.39 = bf16[2,3,64,128]{3,2,1,0:T(8,128)(2,1)S(1)} collective-permute-done((bf16[2,3,64,128]{3,2,1,0:T(8,128)(2,1)S(1)}, bf16[2,3,64,128]{3,2,1,0:T(8,128)(2,1)S(1)}, u32[]{:S(2)}, u32[]{:S(2)}) %collective-permute-start.39) | collective-permute-done | bytes 98336 | tf_op jit(solution)/shard_map/ppermute | solution.py:730
  157.8 1.8 %collective-permute-start.41 = (bf16[1,64,640]{2,1,0:T(8,128)(2,1)S(1)}, bf16[1,64,640]{2,1,0:T(8,128)(2,1)S(1)}, u32[]{:S(2)}, u32[]{:S(2)}) collective-permute-start(bf16[1,64,640]{2,1,0:T(8,128)(2,1)S(1)} %slice.341), channel_id=1, source_target_pairs={{0,2},{1,3},{2,0},{3,1},{4,6},{5,7},{6,4},{7,5},{8,10},{9,11},{10,... | collective-permute-start | bytes 245768 | tf_op jit(solution)/shard_map/ppermute | solution.py:730
  (178 shorter events, 44.7 us)
Async XLA Ops:
  3.1 12.8 %collective-permute-start.3 = (bf16[64,896]{1,0:T(8,128)(2,1)}, bf16[64,896]{1,0:T(8,128)(2,1)S(1)}, u32[]{:S(2)}, u32[]{:S(2)}) collective-permute-start(bf16[64,896]{1,0:T(8,128)(2,1)} %get-tuple-element.225), channel_id=1, source_target_pairs={{0,2},{1,3},{2,0},{3,1},{4,6},{5,7},{6,4},{7,5},{8,10},{9,11},{10,... | collective-permute-start | bytes 344072 | tf_op jit(solution)/shard_map/ppermute | solution.py:730
  6.1 11.9 %collective-permute-start.4 = (bf16[64,896]{1,0:T(8,128)(2,1)}, bf16[64,896]{1,0:T(8,128)(2,1)S(1)}, u32[]{:S(2)}, u32[]{:S(2)}) collective-permute-start(bf16[64,896]{1,0:T(8,128)(2,1)} %get-tuple-element.225), channel_id=1, source_target_pairs={{0,4},{1,5},{2,6},{3,7},{4,0},{5,1},{6,2},{7,3},{8,12},{9,13},{10,... | collective-permute-start | bytes 344072 | tf_op jit(solution)/shard_map/ppermute | solution.py:730
  8.7 9.3 %collective-permute-start.5 = (bf16[64,896]{1,0:T(8,128)(2,1)}, bf16[64,896]{1,0:T(8,128)(2,1)S(1)}, u32[]{:S(2)}, u32[]{:S(2)}) collective-permute-start(bf16[64,896]{1,0:T(8,128)(2,1)} %get-tuple-element.225), channel_id=1, source_target_pairs={{0,6},{1,7},{2,4},{3,5},{4,2},{5,3},{6,0},{7,1},{8,14},{9,15},{10,... | collective-permute-start | bytes 344072 | tf_op jit(solution)/shard_map/ppermute | solution.py:730
  11.7 10.9 %collective-permute-start.2 = (bf16[272,512]{1,0:T(8,128)(2,1)}, bf16[272,512]{1,0:T(8,128)(2,1)}, u32[]{:S(2)}, u32[]{:S(2)}) collective-permute-start(bf16[272,512]{1,0:T(8,128)(2,1)} %get-tuple-element.192), channel_id=1, source_target_pairs={{0,24},{8,16},{16,8},{24,0},{1,25},{9,17},{17,9},{25,1},{2,26},{10... | collective-permute-start | bytes 835592 | tf_op jit(solution)/shard_map/ppermute | solution.py:730
  14.3 12.4 %collective-permute-start.1 = (bf16[272,512]{1,0:T(8,128)(2,1)}, bf16[272,512]{1,0:T(8,128)(2,1)}, u32[]{:S(2)}, u32[]{:S(2)}) collective-permute-start(bf16[272,512]{1,0:T(8,128)(2,1)} %get-tuple-element.191), channel_id=1, source_target_pairs={{0,16},{8,24},{16,0},{24,8},{1,17},{9,25},{17,1},{25,9},{2,18},{10... | collective-permute-start | bytes 835592 | tf_op jit(solution)/shard_map/ppermute | solution.py:730
  15.8 23.7 %collective-permute-start = (bf16[272,512]{1,0:T(8,128)(2,1)}, bf16[272,512]{1,0:T(8,128)(2,1)S(1)}, u32[]{:S(2)}, u32[]{:S(2)}) collective-permute-start(bf16[272,512]{1,0:T(8,128)(2,1)} %get-tuple-element.190), channel_id=1, source_target_pairs={{0,8},{8,0},{16,24},{24,16},{1,9},{9,1},{17,25},{25,17},{2,10},{10... | collective-permute-start | bytes 835592 | tf_op jit(solution)/shard_map/ppermute | solution.py:730
  18.1 14.7 %collective-permute-start.8 = (bf16[4,64,384]{2,1,0:T(8,128)(2,1)S(1)}, bf16[4,64,384]{2,1,0:T(8,128)(2,1)S(1)}, u32[]{:S(2)}, u32[]{:S(2)}) collective-permute-start(bf16[4,64,384]{2,1,0:T(8,128)(2,1)S(1)} %get-tuple-element.213), channel_id=1, source_target_pairs={{0,8},{8,0},{16,24},{24,16},{1,9},{9,1},{17,25},{25,17},{2,10},{10... | collective-permute-start | bytes 589832 | tf_op jit(solution)/shard_map/ppermute | solution.py:730
  19.7 14.6 %collective-permute-start.9 = (bf16[4,64,384]{2,1,0:T(8,128)(2,1)S(1)}, bf16[4,64,384]{2,1,0:T(8,128)(2,1)S(1)}, u32[]{:S(2)}, u32[]{:S(2)}) collective-permute-start(bf16[4,64,384]{2,1,0:T(8,128)(2,1)S(1)} %get-tuple-element.213), channel_id=1, source_target_pairs={{0,16},{8,24},{16,0},{24,8},{1,17},{9,25},{17,1},{25,9},{2,18},{10... | collective-permute-start | bytes 589832 | tf_op jit(solution)/shard_map/ppermute | solution.py:730
  22.5 14.3 %collective-permute-start.10 = (bf16[4,64,384]{2,1,0:T(8,128)(2,1)S(1)}, bf16[4,64,384]{2,1,0:T(8,128)(2,1)S(1)}, u32[]{:S(2)}, u32[]{:S(2)}) collective-permute-start(bf16[4,64,384]{2,1,0:T(8,128)(2,1)S(1)} %get-tuple-element.213), channel_id=1, source_target_pairs={{0,24},{8,16},{16,8},{24,0},{1,25},{9,17},{17,9},{25,1},{2,26},{10... | collective-permute-start | bytes 589832 | tf_op jit(solution)/shard_map/ppermute | solution.py:730
  26.8 17.5 %collective-permute-start.6 = (bf16[64,2560]{1,0:T(8,128)(2,1)S(1)}, bf16[64,2560]{1,0:T(8,128)(2,1)S(1)}, u32[]{:S(2)}, u32[]{:S(2)}) collective-permute-start(bf16[64,2560]{1,0:T(8,128)(2,1)S(1)} %pad_maximum_fusion.16), channel_id=1, source_target_pairs={{0,4},{1,5},{2,6},{3,7},{4,0},{5,1},{6,2},{7,3},{8,12},{9,13},{10,... | collective-permute-start | bytes 983048 | tf_op jit(solution)/shard_map/ppermute | solution.py:730
  32.9 27.6 %collective-permute-start.12 = (bf16[512,512]{1,0:T(8,128)(2,1)S(1)}, bf16[512,512]{1,0:T(8,128)(2,1)S(1)}, u32[]{:S(2)}, u32[]{:S(2)}) collective-permute-start(bf16[512,512]{1,0:T(8,128)(2,1)S(1)} %get-tuple-element.219), channel_id=1, source_target_pairs={{0,8},{8,0},{16,24},{24,16},{1,9},{9,1},{17,25},{25,17},{2,10},{10... | collective-permute-start | bytes 1572872 | tf_op jit(solution)/shard_map/ppermute | solution.py:730
  34.3 26.1 %collective-permute-start.13 = (bf16[512,512]{1,0:T(8,128)(2,1)S(1)}, bf16[512,512]{1,0:T(8,128)(2,1)S(1)}, u32[]{:S(2)}, u32[]{:S(2)}) collective-permute-start(bf16[512,512]{1,0:T(8,128)(2,1)S(1)} %get-tuple-element.220), channel_id=1, source_target_pairs={{0,16},{8,24},{16,0},{24,8},{1,17},{9,25},{17,1},{25,9},{2,18},{10... | collective-permute-start | bytes 1572872 | tf_op jit(solution)/shard_map/ppermute | solution.py:730
  36.8 23.6 %collective-permute-start.14 = (bf16[512,512]{1,0:T(8,128)(2,1)S(1)}, bf16[512,512]{1,0:T(8,128)(2,1)S(1)}, u32[]{:S(2)}, u32[]{:S(2)}) collective-permute-start(bf16[512,512]{1,0:T(8,128)(2,1)S(1)} %get-tuple-element.218), channel_id=1, source_target_pairs={{0,24},{8,16},{16,8},{24,0},{1,25},{9,17},{17,9},{25,1},{2,26},{10... | collective-permute-start | bytes 1572872 | tf_op jit(solution)/shard_map/ppermute | solution.py:730
  44.3 15.8 %collective-permute-start.7 = (bf16[2,64,2560]{2,1,0:T(8,128)(2,1)S(1)}, bf16[2,64,2560]{2,1,0:T(8,128)(2,1)S(1)}, u32[]{:S(2)}, u32[]{:S(2)}) collective-permute-start(bf16[2,64,2560]{2,1,0:T(8,128)(2,1)S(1)} %pad_maximum_fusion.8), channel_id=1, source_target_pairs={{0,2},{1,3},{2,0},{3,1},{4,6},{5,7},{6,4},{7,5},{8,10},{9,11},{10,... | collective-permute-start | bytes 1966088 | tf_op jit(solution)/shard_map/ppermute | solution.py:730
  81.4 15.4 %collective-permute-start.18 = (bf16[256,512]{1,0:T(8,128)(2,1)S(1)}, bf16[256,512]{1,0:T(8,128)(2,1)S(1)}, u32[]{:S(2)}, u32[]{:S(2)}) collective-permute-start(bf16[256,512]{1,0:T(8,128)(2,1)S(1)} %get-tuple-element.198), channel_id=1, source_target_pairs={{0,8},{8,0},{16,24},{24,16},{1,9},{9,1},{17,25},{25,17},{2,10},{10... | collective-permute-start | bytes 786440 | tf_op jit(solution)/shard_map/ppermute | solution.py:730
  83.0 13.9 %collective-permute-start.19 = (bf16[256,512]{1,0:T(8,128)(2,1)S(1)}, bf16[256,512]{1,0:T(8,128)(2,1)S(1)}, u32[]{:S(2)}, u32[]{:S(2)}) collective-permute-start(bf16[256,512]{1,0:T(8,128)(2,1)S(1)} %get-tuple-element.197), channel_id=1, source_target_pairs={{0,16},{8,24},{16,0},{24,8},{1,17},{9,25},{17,1},{25,9},{2,18},{10... | collective-permute-start | bytes 786440 | tf_op jit(solution)/shard_map/ppermute | solution.py:730
  83.1 13.8 %collective-permute-start.20 = (bf16[256,512]{1,0:T(8,128)(2,1)S(1)}, bf16[256,512]{1,0:T(8,128)(2,1)S(1)}, u32[]{:S(2)}, u32[]{:S(2)}) collective-permute-start(bf16[256,512]{1,0:T(8,128)(2,1)S(1)} %get-tuple-element.196), channel_id=1, source_target_pairs={{0,24},{8,16},{16,8},{24,0},{1,25},{9,17},{17,9},{25,1},{2,26},{10... | collective-permute-start | bytes 786440 | tf_op jit(solution)/shard_map/ppermute | solution.py:730
  85.0 11.9 %collective-permute-start.17 = (bf16[4,4,2,128,128]{4,3,2,1,0:T(8,128)(2,1)S(1)}, bf16[4,4,2,128,128]{4,3,2,1,0:T(8,128)(2,1)S(1)}, u32[]{:S(2)}, u32[]{:S(2)}) collective-permute-start(bf16[4,4,2,128,128]{4,3,2,1,0:T(8,128)(2,1)S(1)} %get-tuple-element.105), channel_id=1, source_target_pairs={{0,1},{1,0},{2,3},{3,2},{4,5},{5,4},{6,7},{7,6},{8,9},{9,8},{10,11... | collective-permute-start | bytes 3145736 | tf_op jit(solution)/shard_map/ppermute | solution.py:730
  97.3 15.0 %collective-permute-start.22 = (bf16[4,2,128,128]{3,2,1,0:T(8,128)(2,1)S(1)}, bf16[4,2,128,128]{3,2,1,0:T(8,128)(2,1)S(1)}, u32[]{:S(2)}, u32[]{:S(2)}) collective-permute-start(bf16[4,2,128,128]{3,2,1,0:T(8,128)(2,1)S(1)} %get-tuple-element.184), channel_id=1, source_target_pairs={{0,2},{1,3},{2,0},{3,1},{4,6},{5,7},{6,4},{7,5},{8,10},{9,11},{10,... | collective-permute-start | bytes 786440 | tf_op jit(solution)/shard_map/ppermute | solution.py:730
  98.5 13.8 %collective-permute-start.21 = (bf16[4,4,64,640]{3,2,1,0:T(8,128)(2,1)S(1)}, bf16[4,4,64,640]{3,2,1,0:T(8,128)(2,1)S(1)}, u32[]{:S(2)}, u32[]{:S(2)}) collective-permute-start(bf16[4,4,64,640]{3,2,1,0:T(8,128)(2,1)S(1)} %get-tuple-element.122), channel_id=1, source_target_pairs={{0,1},{1,0},{2,3},{3,2},{4,5},{5,4},{6,7},{7,6},{8,9},{9,8},{10,11... | collective-permute-start | bytes 3932168 | tf_op jit(solution)/shard_map/ppermute | solution.py:730
  98.7 31.2 %collective-permute-start.26 = (bf16[4,2,128,128]{3,2,1,0:T(8,128)(2,1)S(1)}, bf16[4,2,128,128]{3,2,1,0:T(8,128)(2,1)S(1)}, u32[]{:S(2)}, u32[]{:S(2)}) collective-permute-start(bf16[4,2,128,128]{3,2,1,0:T(8,128)(2,1)S(1)} %get-tuple-element.182), channel_id=1, source_target_pairs={{0,4},{1,5},{2,6},{3,7},{4,0},{5,1},{6,2},{7,3},{8,12},{9,13},{10,... | collective-permute-start | bytes 786440 | tf_op jit(solution)/shard_map/ppermute | solution.py:730
  101.5 28.4 %collective-permute-start.27 = (bf16[4,2,128,128]{3,2,1,0:T(8,128)(2,1)S(1)}, bf16[4,2,128,128]{3,2,1,0:T(8,128)(2,1)S(1)}, u32[]{:S(2)}, u32[]{:S(2)}) collective-permute-start(bf16[4,2,128,128]{3,2,1,0:T(8,128)(2,1)S(1)} %get-tuple-element.181), channel_id=1, source_target_pairs={{0,6},{1,7},{2,4},{3,5},{4,2},{5,3},{6,0},{7,1},{8,14},{9,15},{10,... | collective-permute-start | bytes 786440 | tf_op jit(solution)/shard_map/ppermute | solution.py:730
  112.7 17.2 %collective-permute-start.23 = (bf16[4,64,640]{2,1,0:T(8,128)(2,1)S(1)}, bf16[4,64,640]{2,1,0:T(8,128)(2,1)S(1)}, u32[]{:S(2)}, u32[]{:S(2)}) collective-permute-start(bf16[4,64,640]{2,1,0:T(8,128)(2,1)S(1)} %get-tuple-element.179), channel_id=1, source_target_pairs={{0,8},{8,0},{16,24},{24,16},{1,9},{9,1},{17,25},{25,17},{2,10},{10... | collective-permute-start | bytes 983048 | tf_op jit(solution)/shard_map/ppermute | solution.py:730
  114.3 16.1 %collective-permute-start.24 = (bf16[4,64,640]{2,1,0:T(8,128)(2,1)S(1)}, bf16[4,64,640]{2,1,0:T(8,128)(2,1)S(1)}, u32[]{:S(2)}, u32[]{:S(2)}) collective-permute-start(bf16[4,64,640]{2,1,0:T(8,128)(2,1)S(1)} %get-tuple-element.178), channel_id=1, source_target_pairs={{0,16},{8,24},{16,0},{24,8},{1,17},{9,25},{17,1},{25,9},{2,18},{10... | collective-permute-start | bytes 983048 | tf_op jit(solution)/shard_map/ppermute | solution.py:730
  114.6 15.7 %collective-permute-start.25 = (bf16[4,64,640]{2,1,0:T(8,128)(2,1)S(1)}, bf16[4,64,640]{2,1,0:T(8,128)(2,1)S(1)}, u32[]{:S(2)}, u32[]{:S(2)}) collective-permute-start(bf16[4,64,640]{2,1,0:T(8,128)(2,1)S(1)} %get-tuple-element.177), channel_id=1, source_target_pairs={{0,24},{8,16},{16,8},{24,0},{1,25},{9,17},{17,9},{25,1},{2,26},{10... | collective-permute-start | bytes 983048 | tf_op jit(solution)/shard_map/ppermute | solution.py:730
  130.6 18.4 %collective-permute-start.32 = (bf16[2,64,640]{2,1,0:T(8,128)(2,1)S(1)}, bf16[2,64,640]{2,1,0:T(8,128)(2,1)S(1)}, u32[]{:S(2)}, u32[]{:S(2)}) collective-permute-start(bf16[2,64,640]{2,1,0:T(8,128)(2,1)S(1)} %slice.357), channel_id=1, source_target_pairs={{0,4},{1,5},{2,6},{3,7},{4,0},{5,1},{6,2},{7,3},{8,12},{9,13},{10,... | collective-permute-start | bytes 491528 | tf_op jit(solution)/shard_map/ppermute | solution.py:730
  133.0 16.0 %collective-permute-start.35 = (bf16[16,64,128]{2,1,0:T(8,128)(2,1)S(1)}, bf16[16,64,128]{2,1,0:T(8,128)(2,1)S(1)}, u32[]{:S(2)}, u32[]{:S(2)}) collective-permute-start(bf16[16,64,128]{2,1,0:T(8,128)(2,1)S(1)} %pad_maximum_fusion.20), channel_id=1, source_target_pairs={{0,24},{8,16},{16,8},{24,0},{1,25},{9,17},{17,9},{25,1},{2,26},{10... | collective-permute-start | bytes 786440 | tf_op jit(solution)/shard_map/ppermute | solution.py:730
  134.5 14.4 %collective-permute-start.34 = (bf16[16,64,128]{2,1,0:T(8,128)(2,1)S(1)}, bf16[16,64,128]{2,1,0:T(8,128)(2,1)S(1)}, u32[]{:S(2)}, u32[]{:S(2)}) collective-permute-start(bf16[16,64,128]{2,1,0:T(8,128)(2,1)S(1)} %pad_maximum_fusion.19), channel_id=1, source_target_pairs={{0,16},{8,24},{16,0},{24,8},{1,17},{9,25},{17,1},{25,9},{2,18},{10... | collective-permute-start | bytes 786440 | tf_op jit(solution)/shard_map/ppermute | solution.py:730
  139.1 9.8 %collective-permute-start.33 = (bf16[16,64,128]{2,1,0:T(8,128)(2,1)S(1)}, bf16[16,64,128]{2,1,0:T(8,128)(2,1)S(1)}, u32[]{:S(2)}, u32[]{:S(2)}) collective-permute-start(bf16[16,64,128]{2,1,0:T(8,128)(2,1)S(1)} %pad_maximum_fusion.18), channel_id=1, source_target_pairs={{0,8},{8,0},{16,24},{24,16},{1,9},{9,1},{17,25},{25,17},{2,10},{10... | collective-permute-start | bytes 786440 | tf_op jit(solution)/shard_map/ppermute | solution.py:730
  151.1 12.5 %collective-permute-start.36 = (bf16[272,512]{1,0:T(8,128)(2,1)S(1)}, bf16[272,512]{1,0:T(8,128)(2,1)S(1)}, u32[]{:S(2)}, u32[]{:S(2)}) collective-permute-start(bf16[272,512]{1,0:T(8,128)(2,1)S(1)} %get-tuple-element.230), channel_id=1, source_target_pairs={{0,24},{8,16},{16,8},{24,0},{1,25},{9,17},{17,9},{25,1},{2,26},{10... | collective-permute-start | bytes 835592 | tf_op jit(solution)/shard_map/ppermute | solution.py:730
  152.7 12.2 %collective-permute-start.37 = (bf16[272,512]{1,0:T(8,128)(2,1)S(1)}, bf16[272,512]{1,0:T(8,128)(2,1)S(1)}, u32[]{:S(2)}, u32[]{:S(2)}) collective-permute-start(bf16[272,512]{1,0:T(8,128)(2,1)S(1)} %get-tuple-element.229), channel_id=1, source_target_pairs={{0,16},{8,24},{16,0},{24,8},{1,17},{9,25},{17,1},{25,9},{2,18},{10... | collective-permute-start | bytes 835592 | tf_op jit(solution)/shard_map/ppermute | solution.py:730
  153.6 11.3 %collective-permute-start.38 = (bf16[272,512]{1,0:T(8,128)(2,1)S(1)}, bf16[272,512]{1,0:T(8,128)(2,1)S(1)}, u32[]{:S(2)}, u32[]{:S(2)}) collective-permute-start(bf16[272,512]{1,0:T(8,128)(2,1)S(1)} %get-tuple-element.228), channel_id=1, source_target_pairs={{0,8},{8,0},{16,24},{24,16},{1,9},{9,1},{17,25},{25,17},{2,10},{10... | collective-permute-start | bytes 835592 | tf_op jit(solution)/shard_map/ppermute | solution.py:730
  (29 other events, 169.6 us)
